TPU v7x, 32 devices: a whole 2x2x4 slice. The times are simulated.
32 devices in a mesh: tok: 8 (over z, y), grp: 4 (over x, core).
Axes of the slice: x: 2, y: 2, z: 4, core: 2. Of those that a mesh axis runs over, the one named last changes fastest.
Arguments:
- tokens: bfloat16 [12288, 1024], P(('tok', 'grp')), may hold values from -6 to 6
- norm_gain: float32 [1024], replicated, may hold values from 0.25 to 1.75
- input_weight: bfloat16 [1024, 3072], P('tok', 'grp')
- output_weight: bfloat16 [1024, 1024], P('tok', 'grp'), may hold values from -2 to 2
- segment_ids: int32 [12288], replicated, may hold values from 0 to 23, never falling along the last dimension, each value on 1 to 1024 neighbouring positions
- page_owner: int32 [3072, 1], P(('tok', 'grp')), may hold values from 0 to 7; in each aligned block of 96 rows (0 to 95, 96 to 191, ...) at most 24 rows name the same one
Outputs:
- attended: bfloat16 [12288, 1024], P(('tok', 'grp'))
- cache_pages: bfloat16 [6144, 8192], P(('tok', 'grp'))
Inputs may be any that keep to these rules, and one draw needn't show every extreme that they name: `segment_ids`: segment ids never fall along the pack; every id occurs on 1 to 1024 consecutive tokens, and some document has exactly 1024 tokens. `page_owner`: within the 96 pages of one device no owner is named more than 24 times, and in some device one owner is named exactly 24 times.
All inputs are finite; a program needn't handle non-finite values.
Results may differ from a plain program's by a relative error of at most 0.0089.
Values may be sent and summed in bfloat16 or wider, within the bound.
No kernel may reach another device: no remote copies, remote signals or barrier semaphores. Data moves between devices by JAX's collectives and lax.ppermute only.
A program may use at most 128 MiB of HBM per device.

v0:
```python
import functools
import math

import jax
import jax.numpy as jnp
from jax import lax
from jax.experimental import pallas as pl
from jax.experimental.pallas import tpu as pltpu
from jax.sharding import PartitionSpec as P

H = 16
SPAN = 1024
PAGE = 4
HEAD_DIM = 64

NEG_FILL = -1e30
ROPE_BASE = 160000.0
EPSILON = 1e-05
TILE = 256
PARTS = 3
PAIR = 2
ONES_ROWS = 16
HEAD_ROWS = HEAD_DIM + ONES_ROWS
EXTRA_ROWS = 16
KEYS = 512
SCALE = HEAD_DIM ** (-0.5) * math.log2(math.e)
VMEM_LIMIT = 60 * 1024 * 1024
PARAMS = pltpu.CompilerParams(vmem_limit_bytes=VMEM_LIMIT)


def flipped(value, axis, bit):
    count = lax.axis_size(axis)
    return lax.ppermute(value, axis, [(source, source ^ bit) for source in range(count)])


def shifted(value, axis, steps):
    count = lax.axis_size(axis)
    initial, last = (max(0, -steps), min(count, count - steps))
    return lax.ppermute(value, axis, [(source, source + steps) for source in range(initial, last)])


def doubled(value, axis, bit, low):
    other = flipped(value, axis, bit)
    first = (lax.axis_index(axis) & bit) == 0
    pair = jnp.stack([jnp.where(first, value, other), jnp.where(first, other, value)], axis=low)
    return pair.reshape((-1,) + value.shape[1:])


def norm_kernel(capacity, tokens, gain, owner_row, normed, owners):
    rows = tokens.shape[0]
    values = tokens[...].astype(jnp.float32)
    centred = values - jnp.mean(values, axis=-1, keepdims=True)
    spread = jnp.mean(jnp.square(centred), axis=-1, keepdims=True)
    normed[:rows, :] = (centred * lax.rsqrt(spread + EPSILON) * gain[...]).astype(jnp.bfloat16)
    pages = owner_row.shape[1]
    owners[...] = jnp.full(owners.shape, -1.0, jnp.float32)
    owners[:1, :pages] = owner_row[...].astype(jnp.float32)
    lanes = owners.shape[1]
    across = jnp.broadcast_to(owners[:1, :], (lanes, lanes))
    earlier = lax.broadcasted_iota(jnp.int32, (lanes, lanes), 0) < lax.broadcasted_iota(
        jnp.int32, (lanes, lanes), 1
    )
    same = (across.T == across) & earlier
    ranks = jnp.sum(jnp.where(same, 1.0, 0.0), axis=0, keepdims=True)
    slots = owners[:1, :] * capacity + ranks
    normed[rows:, :] = jnp.zeros((EXTRA_ROWS, normed.shape[1]), jnp.bfloat16)
    normed[rows:, :lanes] = jnp.broadcast_to(slots, (EXTRA_ROWS, lanes)).astype(jnp.bfloat16)


def layer_norm(tokens, gain, owners, capacity):
    rows, width = tokens.shape
    lanes = -(-owners.shape[0] // 128) * 128
    return pl.pallas_call(
        functools.partial(norm_kernel, capacity),
        out_shape=jax.ShapeDtypeStruct((rows + EXTRA_ROWS, width), jnp.bfloat16),
        scratch_shapes=[pltpu.VMEM((8, lanes), jnp.float32)],
        compiler_params=PARAMS,
        name="layer_norm",
    )(tokens, gain, owners[None, :])


def project_kernel(first, layout, weight_count, peers, capacity, meta, *refs):
    operands = 1 + max(entry[0] for pieces in layout for entry in pieces)
    tokens = refs[:operands]
    weights = refs[operands : operands + weight_count]
    cosine, sine = refs[operands + weight_count : operands + weight_count + 2]
    query_out, pair_out, send_out, blocks, weight, page_source, sems = refs[-7:]
    step = pl.program_id(0)
    steps = len(layout)
    rows = query_out.shape[0]
    width = query_out.shape[1]
    shard = weights[0].shape[0] // 2

    def arrivals(number):
        return [
            pltpu.make_async_copy(
                tokens[operand],
                blocks.at[number, pl.ds(offset, count), :],
                sems.at[number, place],
            )
            for place, (operand, offset, count) in enumerate(layout[number])
        ]

    @pl.when(step == 0)
    def _():
        for number in range(steps):
            for copy in arrivals(number):
                copy.start()
        for plane in range(weight_count):
            for low in range(2):
                row = pl.multiple_of((meta[1] ^ (2 * plane + low)) * shard, shard)
                for number in range(PARTS):
                    column = pl.multiple_of(meta[2 + number] * width, width)
                    weight[pl.ds(row, shard), number * width : (number + 1) * width] = weights[
                        plane
                    ][low * shard : (low + 1) * shard, pl.ds(column, width)]

    for number in range(steps):

        @pl.when(step == number)
        def _():
            for copy in arrivals(number):
                copy.wait()

    joined = jnp.dot(blocks[step, :rows, :], weight[...], preferred_element_type=jnp.float32)
    cosines = jnp.concatenate([cosine[...]] * 4, axis=0).T
    sines = jnp.concatenate([-sine[...], sine[...]] * 2, axis=0).T
    first_half = lax.rem(lax.broadcasted_iota(jnp.int32, (rows, width), 1), HEAD_DIM) < (
        HEAD_DIM // 2
    )

    def rotate(values):
        partner = jnp.where(
            first_half,
            pltpu.roll(values, width - HEAD_DIM // 2, 1),
            pltpu.roll(values, HEAD_DIM // 2, 1),
        )
        return (values * cosines + partner * sines).astype(jnp.bfloat16)

    query_out[...] = rotate(joined[:, :width])
    keys = rotate(joined[:, width : 2 * width])
    values = joined[:, 2 * width :].astype(jnp.bfloat16)
    pair_out[:, :width] = keys
    pair_out[:, width:] = values
    page_source[0] = keys.astype(jnp.float32)
    page_source[1] = values.astype(jnp.float32)

    pages = rows // PAGE
    slot_count = peers * capacity
    slots = blocks[step, rows : rows + EXTRA_ROWS, :128].astype(jnp.float32)[:1, :pages]
    chosen = (
        lax.broadcasted_iota(jnp.int32, (slot_count, pages), 0).astype(jnp.float32) == slots
    ).astype(jnp.bfloat16)
    for turn in range(PAGE):
        page_part = jnp.concatenate(
            [
                page_source[half, pl.ds(turn, pages, stride=PAGE), :].astype(jnp.bfloat16)
                for half in range(2)
            ],
            axis=1,
        )
        placed = jnp.dot(chosen, page_part, preferred_element_type=jnp.float32)
        columns = slice(turn * 2 * width, (turn + 1) * 2 * width)
        for peer in range(peers):
            send_out[peer, 0, :, columns] = placed[
                peer * capacity : (peer + 1) * capacity
            ].astype(jnp.bfloat16)


def project(meta, first, layout, operands, weights, cosine, sine, rows, blocks, peers, capacity, into):
    steps = len(layout)
    model_width = operands[0].shape[1]
    group_rows = rows * blocks
    width = weights[0].shape[1] // PARTS
    members = blocks // PAIR
    whole = lambda shape: pl.BlockSpec(shape, lambda i, m: (0,) * len(shape))
    place = lambda i, m: m[0] ^ (first + i)
    table = pl.BlockSpec((HEAD_DIM // 2, rows), lambda i, m: (0, place(i, m)))
    send_shape = (peers, members, capacity, 2 * PAGE * width)
    return pl.pallas_call(
        functools.partial(project_kernel, first, layout, len(weights), peers, capacity),
        grid_spec=pltpu.PrefetchScalarGridSpec(
            num_scalar_prefetch=1,
            grid=(steps,),
            in_specs=[pl.BlockSpec(memory_space=pl.ANY)] * len(operands)
            + [whole(weights[0].shape)] * len(weights)
            + [table, table]
            + [pl.BlockSpec(memory_space=pl.ANY)] * len(into),
            out_specs=[
                pl.BlockSpec((rows, width), lambda i, m: (place(i, m), 0)),
                pl.BlockSpec((rows, 2 * width), lambda i, m: (place(i, m), 0)),
                pl.BlockSpec(
                    (peers, 1) + send_shape[2:], lambda i, m: (0, place(i, m) % members, 0, 0)
                ),
            ],
            scratch_shapes=[
                pltpu.VMEM((steps, rows + EXTRA_ROWS, model_width), jnp.bfloat16),
                pltpu.VMEM((model_width, PARTS * width), jnp.bfloat16),
                pltpu.VMEM((2, rows, width), jnp.float32),
                pltpu.SemaphoreType.DMA((steps, 2)),
            ],
        ),
        out_shape=[
            jax.ShapeDtypeStruct((group_rows, width), jnp.bfloat16),
            jax.ShapeDtypeStruct((group_rows, 2 * width), jnp.bfloat16),
            jax.ShapeDtypeStruct(send_shape, jnp.bfloat16),
        ],
        input_output_aliases={
            1 + len(operands) + len(weights) + 2 + number: number for number in range(len(into))
        },
        compiler_params=PARAMS,
        cost_estimate=pl.CostEstimate(
            flops=2 * steps * rows * model_width * PARTS * width,
            bytes_accessed=(3 * steps) << 19,
            transcendentals=0,
        ),
        name="project",
    )(meta, *operands, *weights, cosine, sine, *into)


def mask_heads(queries, masked):
    head_of_lane = lax.broadcasted_iota(jnp.int32, queries.shape, 1) // HEAD_DIM
    for head in range(masked.shape[0]):
        masked[head] = jnp.where(head_of_lane == head, queries[...], jnp.zeros((), jnp.bfloat16))


def with_ones(values):
    turned = values.T
    ones = jnp.ones((ONES_ROWS, values.shape[0]), values.dtype)
    rows = []
    for head in range(values.shape[1] // HEAD_DIM):
        rows += [turned[head * HEAD_DIM : (head + 1) * HEAD_DIM], ones]
    return jnp.concatenate(rows, axis=0)


def sweep(begin, end, base, pairs, values_of, masked, starts, ends, total, peaks):
    width = pairs.shape[1] // 2
    held = pairs.shape[0] // TILE
    begin = jnp.maximum(begin, base)
    end = jnp.minimum(end, base + held)
    last = jnp.minimum(ends, end * TILE)

    def one(number, peaks):
        wanted = begin + number * (KEYS // TILE)
        block = jnp.minimum(wanted, base + held - KEYS // TILE)
        row = pl.multiple_of((block - base) * TILE, TILE)
        keys = pairs[pl.ds(row, KEYS), :width]
        values = values_of(row)
        index = block * TILE + lax.broadcasted_iota(jnp.int32, (KEYS, TILE), 0)
        allowed = (index >= jnp.maximum(starts, wanted * TILE)) & (index < last)
        new_peaks = []
        for head, old_peak in enumerate(peaks):
            scores = lax.dot_general(
                keys, masked[head], (((1,), (1,)), ((), ())), preferred_element_type=jnp.float32
            )
            scores = jnp.where(allowed, scores * SCALE, NEG_FILL)
            peak = jnp.maximum(old_peak, jnp.max(scores, axis=0, keepdims=True))
            fade = jnp.exp2(old_peak - peak)
            weights = jnp.exp2(scores - peak).astype(jnp.bfloat16)
            own = slice(head * HEAD_ROWS, (head + 1) * HEAD_ROWS)
            total[own, :] = total[own, :] * fade + jnp.dot(
                values[own, :], weights, preferred_element_type=jnp.float32
            )
            new_peaks.append(peak)
        return tuple(new_peaks)

    steps = jnp.maximum(end - begin + KEYS // TILE - 1, 0) // (KEYS // TILE)
    return lax.fori_loop(0, steps, one, peaks)


def attend_kernel(ranges, queries, starts, ends, pairs, total, peak_out, masked, values):
    step = pl.program_id(0)
    width = queries.shape[1]
    heads = width // HEAD_DIM
    per_span = SPAN // TILE

    @pl.when(step == 0)
    def _():
        for number in range(pairs.shape[0] // TILE):
            rows = slice(number * TILE, (number + 1) * TILE)
            values[:, rows] = with_ones(pairs[rows, width:])

    mask_heads(queries, masked)
    total[...] = jnp.zeros_like(total)
    peaks = sweep(
        ranges[2 * step],
        ranges[2 * step + 1],
        per_span,
        pairs,
        lambda row: values[:, pl.ds(row, KEYS)],
        masked,
        starts[...],
        ends[...],
        total.at[0],
        tuple(jnp.full((1, TILE), NEG_FILL, jnp.float32) for _ in range(heads)),
    )
    for head in range(heads):
        peak_out[0, head : head + 1, :] = peaks[head]


def finish_kernel(meta, queries, starts, ends, before, after, total, peak_in, *refs):
    outs = refs[:-3]
    masked, sums, mixed = refs[-3:]
    step = pl.program_id(0)
    width = queries.shape[1]
    heads = width // HEAD_DIM
    per_span = SPAN // TILE
    own_tiles = pl.num_programs(0)
    sums[...] = total[0]
    begin, end = meta[1 + 2 * step], meta[2 + 2 * step]

    @pl.when((begin < per_span) | (end > per_span + own_tiles))
    def _():
        mask_heads(queries, masked)
        peaks = tuple(peak_in[0, head : head + 1, :] for head in range(heads))
        for chunk, base in ((before, 0), (after, per_span + own_tiles)):
            peaks = sweep(
                begin,
                end,
                base,
                chunk,
                lambda row: with_ones(chunk[pl.ds(row, KEYS), width:]),
                masked,
                starts[...],
                ends[...],
                sums,
                peaks,
            )

    parts = []
    for head in range(heads):
        row = head * HEAD_ROWS
        parts.append(sums[row : row + HEAD_DIM, :] / sums[row + HEAD_DIM : row + HEAD_DIM + 1, :])
    tile_rows = pl.ds(pl.multiple_of(step * TILE, TILE), TILE)
    mixed[tile_rows, :] = jnp.concatenate(parts, axis=0).T.astype(jnp.bfloat16)

    @pl.when(step == own_tiles - 1)
    def _():
        rows = outs[0].shape[0]
        for distance, out in enumerate(outs):
            out[...] = mixed[pl.ds(pl.multiple_of((meta[0] ^ distance) * rows, 128), rows), :]


def attend_specs(width, held):
    spec = lambda shape, index: pl.BlockSpec(shape, lambda i, m: index(i))
    return [
        spec((TILE, width), lambda i: (i, 0)),
        spec((1, TILE), lambda i: (0, i)),
        spec((1, TILE), lambda i: (0, i)),
    ] + [spec((rows, 2 * width), lambda i: (0, 0)) for rows in held]


def attend_local(ranges, queries, starts, ends, pairs):
    group_rows, width = queries.shape
    heads = width // HEAD_DIM
    tiles = group_rows // TILE
    return pl.pallas_call(
        attend_kernel,
        grid_spec=pltpu.PrefetchScalarGridSpec(
            num_scalar_prefetch=1,
            grid=(tiles,),
            in_specs=attend_specs(width, (group_rows,)),
            out_specs=[
                pl.BlockSpec((1, heads * HEAD_ROWS, TILE), lambda i, m: (i, 0, 0)),
                pl.BlockSpec((1, 8, TILE), lambda i, m: (i, 0, 0)),
            ],
            scratch_shapes=[
                pltpu.VMEM((heads, TILE, width), jnp.bfloat16),
                pltpu.VMEM((heads * HEAD_ROWS, group_rows), jnp.bfloat16),
            ],
        ),
        out_shape=[
            jax.ShapeDtypeStruct((tiles, heads * HEAD_ROWS, TILE), jnp.float32),
            jax.ShapeDtypeStruct((tiles, 8, TILE), jnp.float32),
        ],
        compiler_params=PARAMS,
        cost_estimate=pl.CostEstimate(
            flops=16 * group_rows * 1024 * width,
            bytes_accessed=5 << 20,
            transcendentals=group_rows * 1024 * heads,
        ),
        name="attend_local",
    )(ranges, queries, starts, ends, pairs)


def attend_finish(meta, queries, starts, ends, before, after, total, peaks, rows):
    group_rows, width = queries.shape
    heads = width // HEAD_DIM
    tiles = group_rows // TILE
    members = group_rows // rows
    return pl.pallas_call(
        finish_kernel,
        grid_spec=pltpu.PrefetchScalarGridSpec(
            num_scalar_prefetch=1,
            grid=(tiles,),
            in_specs=attend_specs(width, (SPAN, SPAN))
            + [
                pl.BlockSpec((1,) + total.shape[1:], lambda i, m: (i, 0, 0)),
                pl.BlockSpec((1,) + peaks.shape[1:], lambda i, m: (i, 0, 0)),
            ],
            out_specs=[pl.BlockSpec((rows, width), lambda i, m: (0, 0))] * members,
            scratch_shapes=[
                pltpu.VMEM((heads, TILE, width), jnp.bfloat16),
                pltpu.VMEM(total.shape[1:], jnp.float32),
                pltpu.VMEM((group_rows, width), jnp.bfloat16),
            ],
        ),
        out_shape=[jax.ShapeDtypeStruct((rows, width), jnp.bfloat16)] * members,
        compiler_params=PARAMS,
        cost_estimate=pl.CostEstimate(
            flops=4 * group_rows * 1024 * width,
            bytes_accessed=5 << 20,
            transcendentals=group_rows * 256 * heads,
        ),
        name="attend_finish",
    )(meta, queries, starts, ends, before, after, total, peaks)


def output_kernel(members, meta, *refs):
    parts, weight, result, mixed = refs[:members], refs[members], refs[-2], refs[-1]
    width = parts[0].shape[1]

    @pl.when(pl.program_id(0) == 0)
    def _():
        for distance in range(members):
            source = meta[0] ^ distance
            head_pair = PAIR * (source % (members // PAIR)) + source // (members // PAIR)
            columns = pl.ds(pl.multiple_of(head_pair * width, width), width)
            mixed[:, columns] = parts[distance][...]

    result[...] = jnp.dot(
        mixed[...], weight[...], preferred_element_type=jnp.float32
    ).astype(jnp.bfloat16)


def output_projection(meta, parts, weight):
    rows, width = parts[0].shape
    depth = width * len(parts)
    tile = weight.shape[1]
    steps = weight.shape[0] // depth
    return pl.pallas_call(
        functools.partial(output_kernel, len(parts)),
        grid_spec=pltpu.PrefetchScalarGridSpec(
            num_scalar_prefetch=1,
            grid=(steps,),
            in_specs=[pl.BlockSpec((rows, width), lambda i, m: (0, 0))] * len(parts)
            + [pl.BlockSpec((depth, tile), lambda i, m: (i, 0))],
            out_specs=pl.BlockSpec((rows, tile), lambda i, m: (0, i)),
            scratch_shapes=[pltpu.VMEM((rows, depth), jnp.bfloat16)],
        ),
        out_shape=jax.ShapeDtypeStruct((rows, steps * tile), jnp.bfloat16),
        compiler_params=PARAMS,
        cost_estimate=pl.CostEstimate(
            flops=2 * rows * depth * steps * tile, bytes_accessed=4 << 20, transcendentals=0
        ),
        name="output_projection",
    )(meta, *parts, weight)


def unpack_kernel(own_row, other_row, pages):
    _, pair, members, capacity, part = own_row.shape
    width = part // (2 * PAGE)
    for source in range(pair):
        for low in range(pair):
            received = own_row if source == low else other_row
            for high in range(members):
                for turn in range(2 * PAGE):
                    start = (turn * pair * members + PAIR * high + low) * width
                    pages[source, :, start : start + width] = received[
                        0, low, high, :, turn * width : (turn + 1) * width
                    ]


def unpack(own_row, other_row):
    planes, pair, members, capacity, part = own_row.shape
    block = pl.BlockSpec((1,) + own_row.shape[1:], lambda i: (i, 0, 0, 0, 0))
    return pl.pallas_call(
        unpack_kernel,
        grid=(planes,),
        in_specs=[block, block],
        out_specs=pl.BlockSpec((pair, capacity, pair * members * part), lambda i: (i, 0, 0)),
        out_shape=jax.ShapeDtypeStruct(
            (planes * pair, capacity, pair * members * part), jnp.bfloat16
        ),
        compiler_params=pltpu.CompilerParams(vmem_limit_bytes=24 * 1024 * 1024),
        cost_estimate=pl.CostEstimate(flops=0, bytes_accessed=6 << 20, transcendentals=0),
        name="unpack",
    )(own_row, other_row)


def rope_tables(positions):
    half_dim = HEAD_DIM // 2
    inverse = 1.0 / ROPE_BASE ** (jnp.arange(half_dim, dtype=jnp.float32) * 2.0 / HEAD_DIM)
    angles = inverse[:, None] * positions.astype(jnp.float32)[None, :]
    return jnp.cos(angles), jnp.sin(angles)


def document_bounds(window_ids, rows, blocks):
    reach = SPAN + rows
    firsts = jnp.arange(blocks, dtype=jnp.int32)[:, None] * rows
    own = window_ids[SPAN : SPAN + rows * blocks].reshape(blocks, rows)
    behind = jnp.stack([window_ids[k * rows : k * rows + reach] for k in range(blocks)])
    ahead = jnp.stack(
        [window_ids[SPAN + k * rows : SPAN + k * rows + reach] for k in range(blocks)]
    )
    starts = jnp.sum((behind[:, None, :] < own[:, :, None]).astype(jnp.int32), axis=2) + firsts
    ends = (
        jnp.sum((ahead[:, None, :] <= own[:, :, None]).astype(jnp.int32), axis=2)
        + firsts
        + SPAN
    )
    return starts.reshape(-1), ends.reshape(-1)


def per_device(tokens, norm_gain, input_weight, output_weight, segment_ids, page_owner):
    rows, model_width = tokens.shape
    peers, members = lax.axis_size("tok"), lax.axis_size("grp")
    place, column = lax.axis_index("tok"), lax.axis_index("grp")
    low = place % PAIR
    blocks = PAIR * members
    member = low * members + column
    group_rows = rows * blocks
    width = model_width // blocks
    pages = rows // PAGE

    flat = peers * members
    owners = page_owner[:, 0]
    capacity = max(2, (2 * pages + peers - 1) // peers)
    halves = []
    for parity in range(PAIR):
        pieces = []
        for number in range(PARTS):
            start = number * PAIR * width
            choices = [input_weight[:, start : start + width], input_weight[:, start + width : start + 2 * width]]
            piece = jnp.where((low ^ parity) == 0, choices[0], choices[1])
            route = []
            for source in range(flat):
                row, column_from = divmod(source, members)
                target = (row ^ parity) * members + (PARTS * column_from + number) % members
                route.append((source, target))
            pieces.append(lax.ppermute(piece, ("tok", "grp"), route))
        halves.append(jnp.concatenate(pieces, axis=1))
    plane = jnp.concatenate(halves, axis=0)
    own = layer_norm(tokens, norm_gain[None, :], owners, capacity)
    own, plane = lax.optimization_barrier((own, plane))
    planes = {0: plane}
    bit = peers // 2
    while bit > 1:
        for distance in list(planes):
            planes[distance ^ bit] = flipped(planes[distance], "tok", bit)
        bit //= 2
    weights = [planes[distance] for distance in range(0, peers, 2)]

    across, along = flipped(own, "grp", 2), flipped(own, "tok", 1)
    held = rows + EXTRA_ROWS
    half = rows // 2
    corner_top = flipped(across[:half], "tok", 1)
    corner_bottom = flipped(along[half:], "grp", 2)
    near_blocks = [own, flipped(own, "grp", 1), across, flipped(across, "grp", 1)]
    near_layout = [[(number, 0, held)] for number in range(4)]

    last_weight = output_weight
    bit = PAIR
    while bit < peers:
        last_weight = doubled(last_weight, "tok", bit, 0)
        bit *= 2
    last_weight = last_weight.reshape((peers // PAIR,) + output_weight.shape)
    last_weight = doubled(last_weight, "tok", 1, 1).reshape(model_width, output_weight.shape[1])

    first_row = place // PAIR * group_rows
    padded_ids = jnp.concatenate(
        [
            jnp.full((SPAN,), -1, jnp.int32),
            segment_ids,
            jnp.full((SPAN,), 1 << 30, jnp.int32),
        ]
    )
    window_ids = lax.dynamic_slice_in_dim(padded_ids, first_row, group_rows + 2 * SPAN, 0)
    starts, ends = document_bounds(window_ids, rows, blocks)
    positions = SPAN + jnp.arange(group_rows, dtype=jnp.int32) - starts
    cosine, sine = rope_tables(positions)
    ranges = jnp.stack(
        [starts[::TILE] // TILE, (ends[TILE - 1 :: TILE] + TILE - 1) // TILE], axis=1
    ).reshape(-1)

    order = [
        (number * members + column) % PARTS for number in range(PARTS)
    ]
    meta = jnp.stack([member, place] + order).astype(jnp.int32)
    sizes = (weights, cosine, sine, rows, blocks, peers, capacity)

    def to_owners(send):
        received = lax.all_to_all(
            send.reshape((flat,) + send.shape[2:]),
            ("tok", "grp"),
            split_axis=0,
            concat_axis=0,
            tiled=True,
        )
        return received.reshape((peers // PAIR, PAIR, members) + send.shape[2:])

    queries, pairs, send = project(meta, 0, near_layout, near_blocks, *sizes, ())
    own_row = to_owners(send)
    corner_top, corner_bottom, queries = lax.optimization_barrier(
        (corner_top, corner_bottom, queries)
    )
    far_blocks = [along, flipped(along, "grp", 1), corner_top, corner_bottom]
    far_blocks += [flipped(corner_top, "grp", 1), flipped(corner_bottom, "grp", 1)]
    far_layout = [[(0, 0, held)], [(1, 0, held)]]
    far_layout += [[(number, 0, half), (number + 1, half, held - half)] for number in (2, 4)]
    queries, pairs, send = project(meta, 4, far_layout, far_blocks, *sizes, (queries, pairs))
    before = shifted(pairs[group_rows - SPAN :], "tok", PAIR)
    after = shifted(pairs[:SPAN], "tok", -PAIR)
    other_row = to_owners(send)

    last_weight, pairs = lax.optimization_barrier((last_weight, pairs))
    last_weight = doubled(last_weight[None], "grp", 2, 0)

    bounds = (starts[None, :], ends[None, :])
    total, peaks = attend_local(ranges, queries, *bounds, pairs)
    last_weight, total = lax.optimization_barrier((last_weight, total))
    last_weight = doubled(last_weight, "grp", 1, 1).reshape(members * model_width, -1)
    own_member = member[None].astype(jnp.int32)
    mixed = attend_finish(
        jnp.concatenate([own_member, ranges]),
        queries,
        *bounds,
        before,
        after,
        total,
        peaks,
        rows,
    )
    parts = [mixed[0]] + [
        lax.ppermute(
            mixed[distance],
            ("tok", "grp"),
            [(source, source ^ distance) for source in range(flat)],
        )
        for distance in range(1, blocks)
    ]
    attended = output_projection(own_member, parts, last_weight)

    cache_pages = unpack(own_row, other_row).reshape(
        peers * capacity, 2 * PAGE * model_width
    )
    return attended, cache_pages


def solution(mesh):
    placed = (
        P(("tok", "grp"), None),
        P(),
        P("tok", "grp"),
        P("tok", "grp"),
        P(),
        P(("tok", "grp"), None),
    )
    return jax.shard_map(
        per_device,
        mesh=mesh,
        in_specs=placed,
        out_specs=(P(("tok", "grp"), None), P(("tok", "grp"), None)),
        check_vma=False,
    )
```

profile of v0, /device:TPU:17, one launch (start us, length us, event | category | flops | bytes accessed | tf_op | source)
XLA Modules:
  0.0 217.3 jit_solution(12299061201715180855)
XLA Ops:
  2.8 2.0 collective-permute-start.4
  6.7 1.7 collective-permute-start.1
  9.2 2.4 %collective-permute-start = (bf16[128,128]{1,0:T(8,128)(2,1)S(1)}, bf16[128,128]{1,0:T(8,128)(2,1)S(1)}, u32[]{:S(2)}, u32[]{:S(2)}) collective-permute-start(bf16[128,128]{1,0:T(8,128)(2,1)S(1)} %get-tuple-element.64), channel_id=1, source_target_pairs={{0,0},{1,3},{2,2},{3,1},{4,4},{5,7},{6,6},{7,5},{8,8},{9,11},{10,1... | collective-permute-start | bytes 98312 | tf_op jit(solution)/shard_map/ppermute | solution.py:541
  11.9 2.6 %layer_norm.1.refs_0_ = bf16[400,1024]{1,0:T(8,128)(2,1)} custom-call(bf16[384,1024]{1,0:T(8,128)(2,1)} %tokens.1, f32[1,1024]{1,0:T(1,128)} %bitcast.76, s32[1,96]{1,0:T(1,128)} %bitcast.77), custom_call_target="tpu_custom_call" | custom-call | tf_op jit(solution)/shard_map/layer_norm/pallas_call | solution.py:73
  15.8 3.9 %convert_reduce_fusion.1 = (s32[8,384]{1,0:T(8,128)S(1)}, s32[8,384]{1,0:T(8,128)S(1)}) fusion(s32[8,384]{1,0:T(8,128)S(1)} %lt.39, s32[8,1408]{1,0:T(8,128)S(1)} %stack.132, s32[8,1408]{1,0:T(8,128)S(1)} %stack.142), kind=kLoop, calls=%fused_computation.1 | loop fusion | flops 25946112 | bytes 126976 | tf_op jit(solution)/shard_map/reduce_sum | solution.py:506
  19.9 13.8 %collective-permute-done.8.refs_2_ = bf16[400,1024]{1,0:T(8,128)(2,1)S(1)} collective-permute-done((bf16[400,1024]{1,0:T(8,128)(2,1)}, bf16[400,1024]{1,0:T(8,128)(2,1)S(1)}, u32[]{:S(2)}, u32[]{:S(2)}) %collective-permute-start.8) | collective-permute-done | bytes 819232 | tf_op jit(solution)/shard_map/ppermute | solution.py:33
  33.8 1.4 collective-permute-start.13
  35.3 2.3 %multiply_sine_fusion = (f32[32,3072]{1,0:T(8,128)}, f32[32,3072]{1,0:T(8,128)}) fusion(f32[3072]{0:T(1024)S(1)} %subtract_convert_fusion, f32[32]{0:T(128)S(1)} %negate_power_fusion), kind=kLoop, calls=%fused_computation.6 | loop fusion | flops 98304 | bytes 798848 | tf_op jit(solution)/shard_map/sin | solution.py:495
  38.3 1.6 collective-permute-done.13.refs_5_.refs_7_
  39.8 4.2 %collective-permute-done.15.refs_7_.refs_9_ = bf16[256,384]{1,0:T(8,128)(2,1)S(1)} collective-permute-done((bf16[256,384]{1,0:T(8,128)(2,1)S(1)}, bf16[256,384]{1,0:T(8,128)(2,1)S(1)}, u32[]{:S(2)}, u32[]{:S(2)}) %collective-permute-start.15) | collective-permute-done | bytes 196640 | tf_op jit(solution)/shard_map/ppermute | solution.py:33
  45.3 8.2 %project.2 = (bf16[3072,128]{1,0:T(8,128)(2,1)}, bf16[3072,256]{1,0:T(8,128)(2,1)}, bf16[8,4,24,1024]{3,2,1,0:T(8,128)(2,1)}) custom-call(s32[5]{0:T(128)} %stack.149.meta, bf16[400,1024]{1,0:T(8,128)(2,1)} %layer_norm.1.refs_0_, bf16[400,1024]{1,0:T(8,128)(2,1)} %copy-done.5, bf16[400,1024]{1,0:T(8,128)(2,1)} %copy-done.3, bf16[400,1024]{1,0:T(8,128)(2,1)} %copy-done.6, ...), custom_call_target="tpu_custom_call" | custom-call | flops 1207959552 | bytes 6291456 | tf_op jit(solution)/shard_map/project/pallas_call | solution.py:180
  53.5 6.2 %all-to-all-start = ((bf16[32,24,1024]{2,1,0:T(8,128)(2,1)}), bf16[32,24,1024]{2,1,0:T(8,128)(2,1)S(1)}, u32[]{:S(2)}, u32[]{:S(2)}) async-start(bf16[32,24,1024]{2,1,0:T(8,128)(2,1)} %bitcast.66), calls=%async_computation | async-start | bytes 3145728 | tf_op jit(solution)/shard_map/all_to_all | solution.py:593
  62.3 1.8 slice.139
  64.3 32.3 %collective-permute-done.6.refs_0_ = bf16[400,1024]{1,0:T(8,128)(2,1)S(1)} collective-permute-done((bf16[400,1024]{1,0:T(8,128)(2,1)S(1)}, bf16[400,1024]{1,0:T(8,128)(2,1)S(1)}, u32[]{:S(2)}, u32[]{:S(2)}) %collective-permute-start.6) | collective-permute-done | bytes 819232 | tf_op jit(solution)/shard_map/ppermute | solution.py:33
  99.4 5.8 %collective-permute-done.9.refs_2_ = bf16[192,1024]{1,0:T(8,128)(2,1)} collective-permute-done((bf16[192,1024]{1,0:T(8,128)(2,1)}, bf16[192,1024]{1,0:T(8,128)(2,1)}, u32[]{:S(2)}, u32[]{:S(2)}) %collective-permute-start.9) | collective-permute-done | bytes 393248 | tf_op jit(solution)/shard_map/ppermute | solution.py:33
  105.2 2.6 %collective-permute-done.10.refs_3_ = bf16[208,1024]{1,0:T(8,128)(2,1)} collective-permute-done((bf16[208,1024]{1,0:T(8,128)(2,1)S(1)}, bf16[208,1024]{1,0:T(8,128)(2,1)}, u32[]{:S(2)}, u32[]{:S(2)}) %collective-permute-start.10) | collective-permute-done | bytes 426016 | tf_op jit(solution)/shard_map/ppermute | solution.py:33
  107.7 1.3 collective-permute-start.16
  109.3 1.4 collective-permute-done.16.refs_4_
  112.2 8.2 %project.3 = (bf16[3072,128]{1,0:T(8,128)(2,1)}, bf16[3072,256]{1,0:T(8,128)(2,1)}, bf16[8,4,24,1024]{3,2,1,0:T(8,128)(2,1)}) custom-call(s32[5]{0:T(128)} %stack.149.meta, bf16[400,1024]{1,0:T(8,128)(2,1)} %copy-done.2, bf16[400,1024]{1,0:T(8,128)(2,1)} %collective-permute-done.7.refs_1_, ...), custom_call_target="tpu_custom_call", output_to_operand_aliasing={{0}: (13, {}), {1}: (14, {})} | custom-call | flops 1207959552 | bytes 6291456 | tf_op jit(solution)/shard_map/project/pallas_call | solution.py:180
  120.4 5.1 %all-to-all-start.1 = ((bf16[32,24,1024]{2,1,0:T(8,128)(2,1)}), bf16[32,24,1024]{2,1,0:T(8,128)(2,1)S(1)}, u32[]{:S(2)}, u32[]{:S(2)}) async-start(bf16[32,24,1024]{2,1,0:T(8,128)(2,1)} %bitcast.65), calls=%async_computation.1 | async-start | bytes 3145728 | tf_op jit(solution)/shard_map/all_to_all | solution.py:593
  129.8 28.1 %attend_local.1 = (f32[12,160,256]{2,1,0:T(8,128)}, f32[12,8,256]{2,1,0:T(8,128)}) custom-call(s32[24]{0:T(128)} %reshape.109.ranges, bf16[3072,128]{1,0:T(8,128)(2,1)} %get-tuple-element.34.queries, s32[1,3072]{1,0:T(1,128)} %bitcast.72, s32[1,3072]{1,0:T(1,128)} %bitcast.74, bf16[3072,256]{1,0:T(8,128)(2,1)} %get-tuple-element.37.pairs), custom_call_target="tpu_custom_call" | custom-call | flops 6442450944 | bytes 5242880 | tf_op jit(solution)/shard_map/attend_local/pallas_call | solution.py:357
  161.9 5.9 %collective-permute-start.18 = (bf16[1024,256]{1,0:T(8,128)(2,1)}, bf16[1024,256]{1,0:T(8,128)(2,1)}, u32[]{:S(2)}, u32[]{:S(2)}) collective-permute-start(bf16[1024,256]{1,0:T(8,128)(2,1)} %get-tuple-element.57), channel_id=1, source_target_pairs={{0,8},{4,12},{8,16},{12,20},{16,24},{20,28},{1,9},{5,13},{9,17},{1... | collective-permute-start | bytes 1572872 | tf_op jit(solution)/shard_map/ppermute | solution.py:39
  167.9 4.8 %collective-permute-start.19 = (bf16[1024,256]{1,0:T(8,128)(2,1)}, bf16[1024,256]{1,0:T(8,128)(2,1)}, u32[]{:S(2)}, u32[]{:S(2)}) collective-permute-start(bf16[1024,256]{1,0:T(8,128)(2,1)} %get-tuple-element.56), channel_id=1, source_target_pairs={{8,0},{12,4},{16,8},{20,12},{24,16},{28,20},{9,1},{13,5},{17,9},{2... | collective-permute-start | bytes 1572872 | tf_op jit(solution)/shard_map/ppermute | solution.py:39
  173.4 9.8 %collective-permute-done.18.before = bf16[1024,256]{1,0:T(8,128)(2,1)} collective-permute-done((bf16[1024,256]{1,0:T(8,128)(2,1)}, bf16[1024,256]{1,0:T(8,128)(2,1)}, u32[]{:S(2)}, u32[]{:S(2)}) %collective-permute-start.18) | collective-permute-done | bytes 524320 | tf_op jit(solution)/shard_map/ppermute | solution.py:39
  184.2 11.7 %attend_finish.1 = (bf16[384,128]{1,0:T(8,128)(2,1)}, bf16[384,128]{1,0:T(8,128)(2,1)}, bf16[384,128]{1,0:T(8,128)(2,1)}, bf16[384,128]{1,0:T(8,128)(2,1)}, bf16...) custom-call(s32[25]{0:T(128)} %pad_add_fusion.1.meta, ...), custom_call_target="tpu_custom_call" | custom-call | flops 1610612736 | bytes 5242880 | tf_op jit(solution)/shard_map/attend_finish/pallas_call | solution.py:391
  197.0 1.4 collective-permute-start.26
  200.2 1.7 select_bitcast_fusion.1
  203.2 1.5 collective-permute-start.30
  204.7 1.5 pad_maximum_fusion
  207.3 2.3 %collective-permute-done.30.refs_7_ = bf16[384,128]{1,0:T(8,128)(2,1)S(1)} collective-permute-done((bf16[384,128]{1,0:T(8,128)(2,1)S(1)}, bf16[384,128]{1,0:T(8,128)(2,1)S(1)}, u32[]{:S(2)}, u32[]{:S(2)}) %collective-permute-start.30) | collective-permute-done | bytes 98336 | tf_op jit(solution)/shard_map/ppermute | solution.py:635
  210.2 4.7 %output_projection.1 = bf16[384,1024]{1,0:T(8,128)(2,1)} custom-call(s32[1]{0:T(128)} %bitcast.meta, bf16[384,128]{1,0:T(8,128)(2,1)} %get-tuple-element.41.refs_0_, bf16[384,128]{1,0:T(8,128)(2,1)} %copy-done.12, bf16[384,128]{1,0:T(8,128)(2,1)} %copy-done.13, bf16[384,128]{1,0:T(8,128)(2,1)} %copy-done.14, bf16[384,128]{1,0:T(8,128)(2,1)} %copy-done.15, ...), custom_call_target="tpu_custom_call" | custom-call | flops 805306368 | bytes 4194304 | tf_op jit(solution)/shard_map/output_projection/pallas_call | solution.py:441
  214.8 2.5 %unpack.1 = bf16[8,24,8192]{2,1,0:T(8,128)(2,1)} custom-call(bf16[4,2,4,24,1024]{4,3,2,1,0:T(8,128)(2,1)S(1)} %bitcast.59, bf16[4,2,4,24,1024]{4,3,2,1,0:T(8,128)(2,1)S(1)} %bitcast.60), custom_call_target="tpu_custom_call" | custom-call | bytes 6291456 | tf_op jit(solution)/shard_map/unpack/pallas_call | solution.py:477
  (146 shorter events, 31.2 us)
Async XLA Ops:
  1.5 7.7 %collective-permute-start.5 = (bf16[128,128]{1,0:T(8,128)(2,1)S(1)}, bf16[128,128]{1,0:T(8,128)(2,1)S(1)}, u32[]{:S(2)}, u32[]{:S(2)}) collective-permute-start(bf16[128,128]{1,0:T(8,128)(2,1)S(1)} %get-tuple-element.67), channel_id=1, source_target_pairs={{0,6},{1,5},{2,4},{3,7},{4,2},{5,1},{6,0},{7,3},{8,14},{9,13},{10,... | collective-permute-start | bytes 98312 | tf_op jit(solution)/shard_map/ppermute | solution.py:541
  2.8 11.9 %collective-permute-start.4 = (bf16[128,128]{1,0:T(8,128)(2,1)S(1)}, bf16[128,128]{1,0:T(8,128)(2,1)S(1)}, u32[]{:S(2)}, u32[]{:S(2)}) collective-permute-start(bf16[128,128]{1,0:T(8,128)(2,1)S(1)} %get-tuple-element.65), channel_id=1, source_target_pairs={{0,5},{1,4},{2,7},{3,6},{4,1},{5,0},{6,3},{7,2},{8,13},{9,12},{10,... | collective-permute-start | bytes 98312 | tf_op jit(solution)/shard_map/ppermute | solution.py:541
  4.8 9.9 %collective-permute-start.3 = (bf16[128,128]{1,0:T(8,128)(2,1)S(1)}, bf16[128,128]{1,0:T(8,128)(2,1)S(1)}, u32[]{:S(2)}, u32[]{:S(2)}) collective-permute-start(bf16[128,128]{1,0:T(8,128)(2,1)S(1)} %get-tuple-element.66), channel_id=1, source_target_pairs={{0,4},{1,7},{2,6},{3,5},{4,0},{5,3},{6,2},{7,1},{8,12},{9,15},{10,... | collective-permute-start | bytes 98312 | tf_op jit(solution)/shard_map/ppermute | solution.py:541
  6.0 8.7 %collective-permute-start.2 = (bf16[128,128]{1,0:T(8,128)(2,1)S(1)}, bf16[128,128]{1,0:T(8,128)(2,1)S(1)}, u32[]{:S(2)}, u32[]{:S(2)}) collective-permute-start(bf16[128,128]{1,0:T(8,128)(2,1)S(1)} %get-tuple-element.69), channel_id=1, source_target_pairs={{0,2},{1,1},{2,0},{3,3},{4,6},{5,5},{6,4},{7,7},{8,10},{9,9},{10,8... | collective-permute-start | bytes 98312 | tf_op jit(solution)/shard_map/ppermute | solution.py:541
  6.7 8.0 %collective-permute-start.1 = (bf16[128,128]{1,0:T(8,128)(2,1)S(1)}, bf16[128,128]{1,0:T(8,128)(2,1)S(1)}, u32[]{:S(2)}, u32[]{:S(2)}) collective-permute-start(bf16[128,128]{1,0:T(8,128)(2,1)S(1)} %get-tuple-element.68), channel_id=1, source_target_pairs={{0,1},{1,0},{2,3},{3,2},{4,5},{5,4},{6,7},{7,6},{8,9},{9,8},{10,11... | collective-permute-start | bytes 98312 | tf_op jit(solution)/shard_map/ppermute | solution.py:541
  9.2 5.5 %collective-permute-start = (bf16[128,128]{1,0:T(8,128)(2,1)S(1)}, bf16[128,128]{1,0:T(8,128)(2,1)S(1)}, u32[]{:S(2)}, u32[]{:S(2)}) collective-permute-start(bf16[128,128]{1,0:T(8,128)(2,1)S(1)} %get-tuple-element.64), channel_id=1, source_target_pairs={{0,0},{1,3},{2,2},{3,1},{4,4},{5,7},{6,6},{7,5},{8,8},{9,11},{10,1... | collective-permute-start | bytes 98312 | tf_op jit(solution)/shard_map/ppermute | solution.py:541
  14.8 19.0 %collective-permute-start.8 = (bf16[400,1024]{1,0:T(8,128)(2,1)}, bf16[400,1024]{1,0:T(8,128)(2,1)S(1)}, u32[]{:S(2)}, u32[]{:S(2)}) collective-permute-start(bf16[400,1024]{1,0:T(8,128)(2,1)} %layer_norm.1.refs_0_), channel_id=1, source_target_pairs={{0,2},{1,3},{2,0},{3,1},{4,6},{5,7},{6,4},{7,5},{8,10},{9,11},{10,... | collective-permute-start | bytes 2457608 | tf_op jit(solution)/shard_map/ppermute | solution.py:33
  19.8 24.3 %collective-permute-start.11 = (bf16[400,1024]{1,0:T(8,128)(2,1)}, bf16[400,1024]{1,0:T(8,128)(2,1)S(1)}, u32[]{:S(2)}, u32[]{:S(2)}) collective-permute-start(bf16[400,1024]{1,0:T(8,128)(2,1)} %layer_norm.1.refs_0_), channel_id=1, source_target_pairs={{0,1},{1,0},{2,3},{3,2},{4,5},{5,4},{6,7},{7,6},{8,9},{9,8},{10,11... | collective-permute-start | bytes 2457608 | tf_op jit(solution)/shard_map/ppermute | solution.py:33
  19.8 15.3 %collective-permute-start.14 = (bf16[256,384]{1,0:T(8,128)(2,1)S(1)}, bf16[256,384]{1,0:T(8,128)(2,1)S(1)}, u32[]{:S(2)}, u32[]{:S(2)}) collective-permute-start(bf16[256,384]{1,0:T(8,128)(2,1)S(1)} %maximum_maximum_fusion.refs_4_.refs_6_), channel_id=1, source_target_pairs={{0,16},{4,20},{8,24},{12,28},{16,0},{20,4},{24,8},{28,12},{1,17},{... | collective-permute-start | bytes 589832 | tf_op jit(solution)/shard_map/ppermute | solution.py:33
  33.8 10.3 %collective-permute-start.12 = (bf16[400,1024]{1,0:T(8,128)(2,1)S(1)}, bf16[400,1024]{1,0:T(8,128)(2,1)S(1)}, u32[]{:S(2)}, u32[]{:S(2)}) collective-permute-start(bf16[400,1024]{1,0:T(8,128)(2,1)S(1)} %collective-permute-done.8.refs_2_), channel_id=1, source_target_pairs={{0,1},{1,0},{2,3},{3,2},{4,5},{5,4},{6,7},{7,6},{8,9},{9,8},{10,11... | collective-permute-start | bytes 2457608 | tf_op jit(solution)/shard_map/ppermute | solution.py:33
  33.8 6.0 %collective-permute-start.13 = (bf16[256,384]{1,0:T(8,128)(2,1)S(1)}, bf16[256,384]{1,0:T(8,128)(2,1)S(1)}, u32[]{:S(2)}, u32[]{:S(2)}) collective-permute-start(bf16[256,384]{1,0:T(8,128)(2,1)S(1)} %maximum_maximum_fusion.refs_4_.refs_6_), channel_id=1, source_target_pairs={{0,8},{4,12},{8,0},{12,4},{16,24},{20,28},{24,16},{28,20},{1,9},{5... | collective-permute-start | bytes 589832 | tf_op jit(solution)/shard_map/ppermute | solution.py:33
  35.1 8.9 %collective-permute-start.15 = (bf16[256,384]{1,0:T(8,128)(2,1)S(1)}, bf16[256,384]{1,0:T(8,128)(2,1)S(1)}, u32[]{:S(2)}, u32[]{:S(2)}) collective-permute-start(bf16[256,384]{1,0:T(8,128)(2,1)S(1)} %collective-permute-done.14.refs_6_.refs_8_), channel_id=1, source_target_pairs={{0,8},{4,12},{8,0},{12,4},{16,24},{20,28},{24,16},{28,20},{1,9},{5... | collective-permute-start | bytes 589832 | tf_op jit(solution)/shard_map/ppermute | solution.py:33
  53.5 66.8 %all-to-all-start = ((bf16[32,24,1024]{2,1,0:T(8,128)(2,1)}), bf16[32,24,1024]{2,1,0:T(8,128)(2,1)S(1)}, u32[]{:S(2)}, u32[]{:S(2)}) async-start(bf16[32,24,1024]{2,1,0:T(8,128)(2,1)} %bitcast.66), calls=%async_computation | async-start | bytes 3145728 | tf_op jit(solution)/shard_map/all_to_all | solution.py:593
  59.8 36.9 %collective-permute-start.6 = (bf16[400,1024]{1,0:T(8,128)(2,1)S(1)}, bf16[400,1024]{1,0:T(8,128)(2,1)S(1)}, u32[]{:S(2)}, u32[]{:S(2)}) collective-permute-start(bf16[400,1024]{1,0:T(8,128)(2,1)S(1)} %copy-done.1), channel_id=1, source_target_pairs={{0,4},{4,0},{8,12},{12,8},{16,20},{20,16},{24,28},{28,24},{1,5},{5... | collective-permute-start | bytes 2457608 | tf_op jit(solution)/shard_map/ppermute | solution.py:33
  61.1 36.9 %collective-permute-start.20 = (bf16[128,256]{1,0:T(8,128)(2,1)S(1)}, bf16[128,256]{1,0:T(8,128)(2,1)S(1)}, u32[]{:S(2)}, u32[]{:S(2)}) collective-permute-start(bf16[128,256]{1,0:T(8,128)(2,1)S(1)} %copy-done.19), channel_id=1, source_target_pairs={{0,8},{4,12},{8,0},{12,4},{16,24},{20,28},{24,16},{28,20},{1,9},{5... | collective-permute-start | bytes 196616 | tf_op jit(solution)/shard_map/ppermute | solution.py:33
  64.1 41.1 %collective-permute-start.9 = (bf16[192,1024]{1,0:T(8,128)(2,1)}, bf16[192,1024]{1,0:T(8,128)(2,1)}, u32[]{:S(2)}, u32[]{:S(2)}) collective-permute-start(bf16[192,1024]{1,0:T(8,128)(2,1)} %slice.139), channel_id=1, source_target_pairs={{0,4},{4,0},{8,12},{12,8},{16,20},{20,16},{24,28},{28,24},{1,5},{5... | collective-permute-start | bytes 1179656 | tf_op jit(solution)/shard_map/ppermute | solution.py:33
  96.7 11.1 %collective-permute-start.10 = (bf16[208,1024]{1,0:T(8,128)(2,1)S(1)}, bf16[208,1024]{1,0:T(8,128)(2,1)}, u32[]{:S(2)}, u32[]{:S(2)}) collective-permute-start(bf16[208,1024]{1,0:T(8,128)(2,1)S(1)} %slice.140), channel_id=1, source_target_pairs={{0,2},{1,3},{2,0},{3,1},{4,6},{5,7},{6,4},{7,5},{8,10},{9,11},{10,... | collective-permute-start | bytes 1277960 | tf_op jit(solution)/shard_map/ppermute | solution.py:33
  98.0 11.3 %collective-permute-start.7 = (bf16[400,1024]{1,0:T(8,128)(2,1)S(1)}, bf16[400,1024]{1,0:T(8,128)(2,1)}, u32[]{:S(2)}, u32[]{:S(2)}) collective-permute-start(bf16[400,1024]{1,0:T(8,128)(2,1)S(1)} %collective-permute-done.6.refs_0_), channel_id=1, source_target_pairs={{0,1},{1,0},{2,3},{3,2},{4,5},{5,4},{6,7},{7,6},{8,9},{9,8},{10,11... | collective-permute-start | bytes 2457608 | tf_op jit(solution)/shard_map/ppermute | solution.py:33
  98.8 10.3 %collective-permute-start.21 = (bf16[256,256]{1,0:T(8,128)(2,1)S(1)}, bf16[256,256]{1,0:T(8,128)(2,1)S(1)}, u32[]{:S(2)}, u32[]{:S(2)}) collective-permute-start(bf16[256,256]{1,0:T(8,128)(2,1)S(1)} %bitcast.69), channel_id=1, source_target_pairs={{0,16},{4,20},{8,24},{12,28},{16,0},{20,4},{24,8},{28,12},{1,17},{... | collective-permute-start | bytes 393224 | tf_op jit(solution)/shard_map/ppermute | solution.py:33
  109.2 18.4 %collective-permute-start.22 = (bf16[4,128,256]{2,1,0:T(8,128)(2,1)S(1)}, bf16[4,128,256]{2,1,0:T(8,128)(2,1)}, u32[]{:S(2)}, u32[]{:S(2)}) collective-permute-start(bf16[4,128,256]{2,1,0:T(8,128)(2,1)S(1)} %bitcast.67), channel_id=1, source_target_pairs={{0,4},{4,0},{8,12},{12,8},{16,20},{20,16},{24,28},{28,24},{1,5},{5... | collective-permute-start | bytes 786440 | tf_op jit(solution)/shard_map/ppermute | solution.py:33
  120.4 94.5 %all-to-all-start.1 = ((bf16[32,24,1024]{2,1,0:T(8,128)(2,1)}), bf16[32,24,1024]{2,1,0:T(8,128)(2,1)S(1)}, u32[]{:S(2)}, u32[]{:S(2)}) async-start(bf16[32,24,1024]{2,1,0:T(8,128)(2,1)} %bitcast.65), calls=%async_computation.1 | async-start | bytes 3145728 | tf_op jit(solution)/shard_map/all_to_all | solution.py:593
  128.6 29.4 %collective-permute-start.23 = (bf16[1,1024,256]{2,1,0:T(8,128)(2,1)S(1)}, bf16[1,1024,256]{2,1,0:T(8,128)(2,1)}, u32[]{:S(2)}, u32[]{:S(2)}) collective-permute-start(bf16[1,1024,256]{2,1,0:T(8,128)(2,1)S(1)} %bitcast.63), channel_id=1, source_target_pairs={{0,2},{1,3},{2,0},{3,1},{4,6},{5,7},{6,4},{7,5},{8,10},{9,11},{10,... | collective-permute-start | bytes 1572872 | tf_op jit(solution)/shard_map/ppermute | solution.py:33
  160.3 39.3 %collective-permute-start.31 = (bf16[2,1024,256]{2,1,0:T(8,128)(2,1)}, bf16[2,1024,256]{2,1,0:T(8,128)(2,1)}, u32[]{:S(2)}, u32[]{:S(2)}) collective-permute-start(bf16[2,1024,256]{2,1,0:T(8,128)(2,1)} %maximum_bitcast_fusion), channel_id=1, source_target_pairs={{0,1},{1,0},{2,3},{3,2},{4,5},{5,4},{6,7},{7,6},{8,9},{9,8},{10,11... | collective-permute-start | bytes 3145736 | tf_op jit(solution)/shard_map/ppermute | solution.py:33
  161.9 21.3 %collective-permute-start.18 = (bf16[1024,256]{1,0:T(8,128)(2,1)}, bf16[1024,256]{1,0:T(8,128)(2,1)}, u32[]{:S(2)}, u32[]{:S(2)}) collective-permute-start(bf16[1024,256]{1,0:T(8,128)(2,1)} %get-tuple-element.57), channel_id=1, source_target_pairs={{0,8},{4,12},{8,16},{12,20},{16,24},{20,28},{1,9},{5,13},{9,17},{1... | collective-permute-start | bytes 1572872 | tf_op jit(solution)/shard_map/ppermute | solution.py:39
  167.9 16.3 %collective-permute-start.19 = (bf16[1024,256]{1,0:T(8,128)(2,1)}, bf16[1024,256]{1,0:T(8,128)(2,1)}, u32[]{:S(2)}, u32[]{:S(2)}) collective-permute-start(bf16[1024,256]{1,0:T(8,128)(2,1)} %get-tuple-element.56), channel_id=1, source_target_pairs={{8,0},{12,4},{16,8},{20,12},{24,16},{28,20},{9,1},{13,5},{17,9},{2... | collective-permute-start | bytes 1572872 | tf_op jit(solution)/shard_map/ppermute | solution.py:39
  195.9 6.0 %collective-permute-start.24 = (bf16[384,128]{1,0:T(8,128)(2,1)}, bf16[384,128]{1,0:T(8,128)(2,1)S(1)}, u32[]{:S(2)}, u32[]{:S(2)}) collective-permute-start(bf16[384,128]{1,0:T(8,128)(2,1)} %get-tuple-element.42), channel_id=1, source_target_pairs={{0,1},{1,0},{2,3},{3,2},{4,5},{5,4},{6,7},{7,6},{8,9},{9,8},{10,11... | collective-permute-start | bytes 294920 | tf_op jit(solution)/shard_map/ppermute | solution.py:635
  196.7 6.5 %collective-permute-start.25 = (bf16[384,128]{1,0:T(8,128)(2,1)}, bf16[384,128]{1,0:T(8,128)(2,1)S(1)}, u32[]{:S(2)}, u32[]{:S(2)}) collective-permute-start(bf16[384,128]{1,0:T(8,128)(2,1)} %get-tuple-element.43), channel_id=1, source_target_pairs={{0,2},{1,3},{2,0},{3,1},{4,6},{5,7},{6,4},{7,5},{8,10},{9,11},{10,... | collective-permute-start | bytes 294920 | tf_op jit(solution)/shard_map/ppermute | solution.py:635
  197.0 9.2 %collective-permute-start.26 = (bf16[384,128]{1,0:T(8,128)(2,1)}, bf16[384,128]{1,0:T(8,128)(2,1)S(1)}, u32[]{:S(2)}, u32[]{:S(2)}) collective-permute-start(bf16[384,128]{1,0:T(8,128)(2,1)} %get-tuple-element.44), channel_id=1, source_target_pairs={{0,3},{1,2},{2,1},{3,0},{4,7},{5,6},{6,5},{7,4},{8,11},{9,10},{10,... | collective-permute-start | bytes 294920 | tf_op jit(solution)/shard_map/ppermute | solution.py:635
  198.4 7.8 %collective-permute-start.27 = (bf16[384,128]{1,0:T(8,128)(2,1)}, bf16[384,128]{1,0:T(8,128)(2,1)S(1)}, u32[]{:S(2)}, u32[]{:S(2)}) collective-permute-start(bf16[384,128]{1,0:T(8,128)(2,1)} %get-tuple-element.45), channel_id=1, source_target_pairs={{0,4},{1,5},{2,6},{3,7},{4,0},{5,1},{6,2},{7,3},{8,12},{9,13},{10,... | collective-permute-start | bytes 294920 | tf_op jit(solution)/shard_map/ppermute | solution.py:635
  199.6 6.6 %collective-permute-start.28 = (bf16[384,128]{1,0:T(8,128)(2,1)}, bf16[384,128]{1,0:T(8,128)(2,1)S(1)}, u32[]{:S(2)}, u32[]{:S(2)}) collective-permute-start(bf16[384,128]{1,0:T(8,128)(2,1)} %get-tuple-element.46), channel_id=1, source_target_pairs={{0,5},{1,4},{2,7},{3,6},{4,1},{5,0},{6,3},{7,2},{8,13},{9,12},{10,... | collective-permute-start | bytes 294920 | tf_op jit(solution)/shard_map/ppermute | solution.py:635
  201.9 5.3 %collective-permute-start.29 = (bf16[384,128]{1,0:T(8,128)(2,1)S(1)}, bf16[384,128]{1,0:T(8,128)(2,1)S(1)}, u32[]{:S(2)}, u32[]{:S(2)}) collective-permute-start(bf16[384,128]{1,0:T(8,128)(2,1)S(1)} %copy-done.22), channel_id=1, source_target_pairs={{0,6},{1,7},{2,4},{3,5},{4,2},{5,3},{6,0},{7,1},{8,14},{9,15},{10,... | collective-permute-start | bytes 294920 | tf_op jit(solution)/shard_map/ppermute | solution.py:635
  203.2 6.3 %collective-permute-start.30 = (bf16[384,128]{1,0:T(8,128)(2,1)S(1)}, bf16[384,128]{1,0:T(8,128)(2,1)S(1)}, u32[]{:S(2)}, u32[]{:S(2)}) collective-permute-start(bf16[384,128]{1,0:T(8,128)(2,1)S(1)} %copy-done.21), channel_id=1, source_target_pairs={{0,7},{1,6},{2,5},{3,4},{4,3},{5,2},{6,1},{7,0},{8,15},{9,14},{10,... | collective-permute-start | bytes 294920 | tf_op jit(solution)/shard_map/ppermute | solution.py:635
  (25 other events, 133.5 us)
where the time goes:
time: 222 us; the launch traced here: 217 us
  waiting for transfers between devices  76.5 us (34%)
  Pallas kernels  66 us (30%)
  starting transfers between devices  49.7 us (22%)
  other arithmetic  15.2 us (7%)
  local copies, waits for them, and re-layouts  8.73 us (4%)
    ppermute x17, waiting for transfers between devices, flipped(): lax.ppermute(value, axis, [(source, source ^ bit) for source in range(cou...  62.3 us
    pallas_call x1, Pallas kernels, attend_local(): pl.pallas_call(attend_kernel, grid_spec=pltpu.PrefetchScalarGridSpec(num_...  28.1 us
    pallas_call x2, Pallas kernels, project(): pl.pallas_call(functools.partial(project_kernel, first, layout, len(weigh...  16.4 us
    pallas_call x1, Pallas kernels, attend_finish(): pl.pallas_call(finish_kernel, grid_spec=pltpu.PrefetchScalarGridSpec(num_...  11.7 us
    all_to_all x2, starting transfers between devices, to_owners(): lax.all_to_all(send.reshape((flat,) + send.shape[2:]), ('tok', 'grp'), sp...  11.4 us
    ppermute x17, starting transfers between devices, flipped(): lax.ppermute(value, axis, [(source, source ^ bit) for source in range(cou...  11.2 us
    ppermute x2, waiting for transfers between devices, shifted(): lax.ppermute(value, axis, [(source, source + steps) for source in range(i...  10.8 us
    ppermute x2, starting transfers between devices, shifted(): lax.ppermute(value, axis, [(source, source + steps) for source in range(i...  10.8 us
  transfers between devices with their start and end apart: 34, of which 12 were waited for; matrix products, arithmetic and copies ran while one was open for 9% of the time, Pallas kernels for 25%

commit v1 on v0

--- a/solution.py
+++ b/solution.py
@@ -46,12 +46,15 @@
     return pair.reshape((-1,) + value.shape[1:])
 
 
-def norm_kernel(capacity, tokens, gain, owner_row, normed, owners):
-    rows = tokens.shape[0]
+def norm_kernel(capacity, tokens, gain, owner_row, top, bottom, owners):
+    half = top.shape[0]
+    rest = tokens.shape[0] - half
     values = tokens[...].astype(jnp.float32)
     centred = values - jnp.mean(values, axis=-1, keepdims=True)
     spread = jnp.mean(jnp.square(centred), axis=-1, keepdims=True)
-    normed[:rows, :] = (centred * lax.rsqrt(spread + EPSILON) * gain[...]).astype(jnp.bfloat16)
+    normed = (centred * lax.rsqrt(spread + EPSILON) * gain[...]).astype(jnp.bfloat16)
+    top[...] = normed[:half]
+    bottom[:rest, :] = normed[half:]
     pages = owner_row.shape[1]
     owners[...] = jnp.full(owners.shape, -1.0, jnp.float32)
     owners[:1, :pages] = owner_row[...].astype(jnp.float32)
@@ -63,8 +66,8 @@
     same = (across.T == across) & earlier
     ranks = jnp.sum(jnp.where(same, 1.0, 0.0), axis=0, keepdims=True)
     slots = owners[:1, :] * capacity + ranks
-    normed[rows:, :] = jnp.zeros((EXTRA_ROWS, normed.shape[1]), jnp.bfloat16)
-    normed[rows:, :lanes] = jnp.broadcast_to(slots, (EXTRA_ROWS, lanes)).astype(jnp.bfloat16)
+    bottom[rest:, :] = jnp.zeros((EXTRA_ROWS, bottom.shape[1]), jnp.bfloat16)
+    bottom[rest:, :lanes] = jnp.broadcast_to(slots, (EXTRA_ROWS, lanes)).astype(jnp.bfloat16)
 
 
 def layer_norm(tokens, gain, owners, capacity):
@@ -72,7 +75,10 @@
     lanes = -(-owners.shape[0] // 128) * 128
     return pl.pallas_call(
         functools.partial(norm_kernel, capacity),
-        out_shape=jax.ShapeDtypeStruct((rows + EXTRA_ROWS, width), jnp.bfloat16),
+        out_shape=[
+            jax.ShapeDtypeStruct((rows // 2, width), jnp.bfloat16),
+            jax.ShapeDtypeStruct((rows // 2 + EXTRA_ROWS, width), jnp.bfloat16),
+        ],
         scratch_shapes=[pltpu.VMEM((8, lanes), jnp.float32)],
         compiler_params=PARAMS,
         name="layer_norm",
@@ -541,8 +547,8 @@
             pieces.append(lax.ppermute(piece, ("tok", "grp"), route))
         halves.append(jnp.concatenate(pieces, axis=1))
     plane = jnp.concatenate(halves, axis=0)
-    own = layer_norm(tokens, norm_gain[None, :], owners, capacity)
-    own, plane = lax.optimization_barrier((own, plane))
+    top, bottom = layer_norm(tokens, norm_gain[None, :], owners, capacity)
+    top, bottom, plane = lax.optimization_barrier((top, bottom, plane))
     planes = {0: plane}
     bit = peers // 2
     while bit > 1:
@@ -551,13 +557,17 @@
         bit //= 2
     weights = [planes[distance] for distance in range(0, peers, 2)]
 
-    across, along = flipped(own, "grp", 2), flipped(own, "tok", 1)
-    held = rows + EXTRA_ROWS
-    half = rows // 2
-    corner_top = flipped(across[:half], "tok", 1)
-    corner_bottom = flipped(along[half:], "grp", 2)
-    near_blocks = [own, flipped(own, "grp", 1), across, flipped(across, "grp", 1)]
-    near_layout = [[(number, 0, held)] for number in range(4)]
+    across_top, along_bottom = flipped(top, "grp", 2), flipped(bottom, "tok", 1)
+    across_bottom, along_top = flipped(bottom, "grp", 2), flipped(top, "tok", 1)
+    near_blocks = [top, bottom, flipped(top, "grp", 1), flipped(bottom, "grp", 1)]
+    near_blocks += [across_top, across_bottom]
+    near_blocks += [flipped(across_top, "grp", 1), flipped(across_bottom, "grp", 1)]
+    far_blocks = [along_top, along_bottom]
+    far_blocks += [flipped(along_top, "grp", 1), flipped(along_bottom, "grp", 1)]
+    half, held = rows // 2, rows + EXTRA_ROWS
+    layout = [
+        [(2 * number, 0, half), (2 * number + 1, half, held - half)] for number in range(4)
+    ]
 
     last_weight = output_weight
     bit = PAIR
@@ -565,6 +575,15 @@
         last_weight = doubled(last_weight, "tok", bit, 0)
         bit *= 2
     last_weight = last_weight.reshape((peers // PAIR,) + output_weight.shape)
+    near_blocks, far_blocks, weights, last_weight = lax.optimization_barrier(
+        (near_blocks, far_blocks, weights, last_weight)
+    )
+    corners = [
+        flipped(near_blocks[4], "tok", 1),
+        flipped(far_blocks[1], "grp", 2),
+        flipped(near_blocks[6], "tok", 1),
+        flipped(far_blocks[3], "grp", 2),
+    ]
     last_weight = doubled(last_weight, "tok", 1, 1).reshape(model_width, output_weight.shape[1])
 
     first_row = place // PAIR * group_rows
@@ -599,26 +618,22 @@
         )
         return received.reshape((peers // PAIR, PAIR, members) + send.shape[2:])
 
-    queries, pairs, send = project(meta, 0, near_layout, near_blocks, *sizes, ())
+    queries, pairs, send = project(meta, 0, layout, near_blocks, *sizes, ())
+    send, corners, last_weight = lax.optimization_barrier((send, corners, last_weight))
     own_row = to_owners(send)
-    corner_top, corner_bottom, queries = lax.optimization_barrier(
-        (corner_top, corner_bottom, queries)
-    )
-    far_blocks = [along, flipped(along, "grp", 1), corner_top, corner_bottom]
-    far_blocks += [flipped(corner_top, "grp", 1), flipped(corner_bottom, "grp", 1)]
-    far_layout = [[(0, 0, held)], [(1, 0, held)]]
-    far_layout += [[(number, 0, half), (number + 1, half, held - half)] for number in (2, 4)]
-    queries, pairs, send = project(meta, 4, far_layout, far_blocks, *sizes, (queries, pairs))
+    queries, pairs, send = project(
+        meta, 4, layout, far_blocks + corners, *sizes, (queries, pairs)
+    )
+    other_row = to_owners(send)
     before = shifted(pairs[group_rows - SPAN :], "tok", PAIR)
     after = shifted(pairs[:SPAN], "tok", -PAIR)
-    other_row = to_owners(send)
-
-    last_weight, pairs = lax.optimization_barrier((last_weight, pairs))
     last_weight = doubled(last_weight[None], "grp", 2, 0)
 
     bounds = (starts[None, :], ends[None, :])
     total, peaks = attend_local(ranges, queries, *bounds, pairs)
-    last_weight, total = lax.optimization_barrier((last_weight, total))
+    last_weight, before, after, total, peaks = lax.optimization_barrier(
+        (last_weight, before, after, total, peaks)
+    )
     last_weight = doubled(last_weight, "grp", 1, 1).reshape(members * model_width, -1)
     own_member = member[None].astype(jnp.int32)
     mixed = attend_finish(

time: 222 us -> 214 us (0.964)
  waiting for transfers between devices: 76.5 us -> 56.4 us
  starting transfers between devices: 49.7 us -> 57.8 us
  Pallas kernels: 66 us -> 72.8 us
    ppermute x17 -> x22, waiting for transfers between devices: 62.3 us -> 25.2 us  [flipped(): lax.ppermute(value, axis, [(source, source ^ bit) for source in range(cou...]
    all_to_all x2, waiting for transfers between devices: 0.01 us -> 27.8 us  [to_owners(): lax.all_to_all(send.reshape((flat,) + send.shape[2:]), ('tok', 'grp'), sp...]
    ppermute x17 -> x22, starting transfers between devices: 11.2 us -> 22.2 us  [flipped(): lax.ppermute(value, axis, [(source, source ^ bit) for source in range(cou...]
    ppermute x2, waiting for transfers between devices: 10.8 us -> 0.11 us  [shifted(): lax.ppermute(value, axis, [(source, source + steps) for source in range(i...]
    pallas_call x1, Pallas kernels: 28.1 us -> 33.8 us  [attend_local(): pl.pallas_call(attend_kernel, grid_spec=pltpu.PrefetchScalarGridSpec(num_...]
    ppermute x2, starting transfers between devices: 10.8 us -> 5.45 us  [shifted(): lax.ppermute(value, axis, [(source, source + steps) for source in range(i...]
    all_to_all x2, starting transfers between devices: 11.4 us -> 14.1 us  [to_owners(): lax.all_to_all(send.reshape((flat,) + send.shape[2:]), ('tok', 'grp'), sp...]
  transfers between devices with their start and end apart: 34 -> 39, of which waited for: 12 -> 12; matrix products, arithmetic and copies ran while one was open for 9% -> 10% of each run, Pallas kernels for 25% -> 33%
where the time goes in v1:
time: 214 us; the launch traced here: 211 us
  Pallas kernels  72.8 us (34%)
  starting transfers between devices  57.8 us (27%)
  waiting for transfers between devices  56.4 us (26%)
  other arithmetic  15.9 us (7%)
  local copies, waits for them, and re-layouts  6.78 us (3%)
    pallas_call x1, Pallas kernels, attend_local(): pl.pallas_call(attend_kernel, grid_spec=pltpu.PrefetchScalarGridSpec(num_...  33.8 us
    all_to_all x2, waiting for transfers between devices, to_owners(): lax.all_to_all(send.reshape((flat,) + send.shape[2:]), ('tok', 'grp'), sp...  27.8 us
    ppermute x22, waiting for transfers between devices, flipped(): lax.ppermute(value, axis, [(source, source ^ bit) for source in range(cou...  25.2 us
    ppermute x22, starting transfers between devices, flipped(): lax.ppermute(value, axis, [(source, source ^ bit) for source in range(cou...  22.2 us
    pallas_call x2, Pallas kernels, project(): pl.pallas_call(functools.partial(project_kernel, first, layout, len(weigh...  16.5 us
    all_to_all x2, starting transfers between devices, to_owners(): lax.all_to_all(send.reshape((flat,) + send.shape[2:]), ('tok', 'grp'), sp...  14.1 us
    pallas_call x1, Pallas kernels, attend_finish(): pl.pallas_call(finish_kernel, grid_spec=pltpu.PrefetchScalarGridSpec(num_...  12.8 us
    ppermute x6, starting transfers between devices, per_device(): pieces.append(lax.ppermute(piece, ('tok', 'grp'), route))  9.34 us
  transfers between devices with their start and end apart: 39, of which 12 were waited for; matrix products, arithmetic and copies ran while one was open for 10% of the time, Pallas kernels for 33%

profile of v1, /device:TPU:17, one launch (start us, length us, event | category | flops | bytes accessed | tf_op | source)
XLA Modules:
  0.0 211.0 jit_solution(11572690198798065817)
XLA Ops:
  2.8 2.0 collective-permute-start.4
  6.7 1.7 collective-permute-start.1
  9.2 2.4 %collective-permute-start = (bf16[128,128]{1,0:T(8,128)(2,1)S(1)}, bf16[128,128]{1,0:T(8,128)(2,1)S(1)}, u32[]{:S(2)}, u32[]{:S(2)}) collective-permute-start(bf16[128,128]{1,0:T(8,128)(2,1)S(1)} %get-tuple-element.112), channel_id=1, source_target_pairs={{0,0},{1,3},{2,2},{3,1},{4,4},{5,7},{6,6},{7,5},{8,8},{9,11},{10,1... | collective-permute-start | bytes 98312 | tf_op jit(solution)/shard_map/ppermute | solution.py:547
  11.9 2.5 %layer_norm.1 = (bf16[192,1024]{1,0:T(8,128)(2,1)}, bf16[208,1024]{1,0:T(8,128)(2,1)}) custom-call(bf16[384,1024]{1,0:T(8,128)(2,1)} %tokens.1, f32[1,1024]{1,0:T(1,128)} %bitcast.75, s32[1,96]{1,0:T(1,128)} %bitcast.76), custom_call_target="tpu_custom_call" | custom-call | tf_op jit(solution)/shard_map/layer_norm/pallas_call | solution.py:76
  16.3 2.4 %collective-permute-done.19 = bf16[128,256]{1,0:T(8,128)(2,1)S(1)} collective-permute-done((bf16[128,256]{1,0:T(8,128)(2,1)}, bf16[128,256]{1,0:T(8,128)(2,1)S(1)}, u32[]{:S(2)}, u32[]{:S(2)}) %collective-permute-start.19) | collective-permute-done | bytes 65568 | tf_op jit(solution)/shard_map/ppermute | solution.py:33
  18.9 3.9 %convert_reduce_fusion.1 = (s32[8,384]{1,0:T(8,128)S(1)}, s32[8,384]{1,0:T(8,128)S(1)}) fusion(s32[8,384]{1,0:T(8,128)S(1)} %lt.39, s32[8,1408]{1,0:T(8,128)S(1)} %stack.132, s32[8,1408]{1,0:T(8,128)S(1)} %stack.142), kind=kLoop, calls=%fused_computation.1 | loop fusion | flops 25946112 | bytes 126976 | tf_op jit(solution)/shard_map/reduce_sum | solution.py:512
  22.8 5.5 %collective-permute-start.8 = (bf16[192,1024]{1,0:T(8,128)(2,1)}, bf16[192,1024]{1,0:T(8,128)(2,1)}, u32[]{:S(2)}, u32[]{:S(2)}) collective-permute-start(bf16[192,1024]{1,0:T(8,128)(2,1)} %get-tuple-element.60.refs_0_), channel_id=1, source_target_pairs={{0,2},{1,3},{2,0},{3,1},{4,6},{5,7},{6,4},{7,5},{8,10},{9,11},{10,... | collective-permute-start | bytes 1179656 | tf_op jit(solution)/shard_map/ppermute | solution.py:33
  28.3 2.0 collective-permute-done.20
  32.6 3.8 %collective-permute-start.18 = (bf16[256,384]{1,0:T(8,128)(2,1)S(1)}, bf16[256,384]{1,0:T(8,128)(2,1)S(1)}, u32[]{:S(2)}, u32[]{:S(2)}) collective-permute-start(bf16[256,384]{1,0:T(8,128)(2,1)S(1)} %collective-permute-done.17.refs_10_), channel_id=1, source_target_pairs={{0,8},{4,12},{8,0},{12,4},{16,24},{20,28},{24,16},{28,20},{1,9},{5... | collective-permute-start | bytes 589832 | tf_op jit(solution)/shard_map/ppermute | solution.py:33
  37.6 3.6 %collective-permute-done.12.refs_0_ = bf16[192,1024]{1,0:T(8,128)(2,1)} collective-permute-done((bf16[192,1024]{1,0:T(8,128)(2,1)}, bf16[192,1024]{1,0:T(8,128)(2,1)}, u32[]{:S(2)}, u32[]{:S(2)}) %collective-permute-start.12) | collective-permute-done | bytes 393248 | tf_op jit(solution)/shard_map/ppermute | solution.py:33
  41.1 1.6 collective-permute-start.10
  42.8 1.6 collective-permute-done.9.refs_5_
  44.5 5.7 %collective-permute-done.13.refs_1_ = bf16[208,1024]{1,0:T(8,128)(2,1)S(1)} collective-permute-done((bf16[208,1024]{1,0:T(8,128)(2,1)}, bf16[208,1024]{1,0:T(8,128)(2,1)S(1)}, u32[]{:S(2)}, u32[]{:S(2)}) %collective-permute-start.13) | collective-permute-done | bytes 426016 | tf_op jit(solution)/shard_map/ppermute | solution.py:33
  52.7 2.3 %multiply_sine_fusion = (f32[32,3072]{1,0:T(8,128)}, f32[32,3072]{1,0:T(8,128)}) fusion(f32[3072]{0:T(1024)S(1)} %subtract_convert_fusion, f32[32]{0:T(128)S(1)} %negate_power_fusion), kind=kLoop, calls=%fused_computation.6 | loop fusion | flops 98304 | bytes 798848 | tf_op jit(solution)/shard_map/sin | solution.py:501
  58.7 8.2 %project.2 = (bf16[3072,128]{1,0:T(8,128)(2,1)}, bf16[3072,256]{1,0:T(8,128)(2,1)}, bf16[8,4,24,1024]{3,2,1,0:T(8,128)(2,1)}) custom-call(s32[5]{0:T(128)} %stack.149.meta, bf16[192,1024]{1,0:T(8,128)(2,1)} %get-tuple-element.60.refs_0_, bf16[208,1024]{1,0:T(8,128)(2,1)} %get-tuple-element.61.refs_1_, bf16[192,1024]{1,0:T(8,128)(2,1)} %copy-done.12, ...), custom_call_target="tpu_custom_call" | custom-call | flops 1207959552 | bytes 6291456 | tf_op jit(solution)/shard_map/project/pallas_call | solution.py:186
  68.6 8.4 %collective-permute-done.23.refs_6_ = bf16[192,1024]{1,0:T(8,128)(2,1)} collective-permute-done((bf16[192,1024]{1,0:T(8,128)(2,1)}, bf16[192,1024]{1,0:T(8,128)(2,1)}, u32[]{:S(2)}, u32[]{:S(2)}) %collective-permute-start.23) | collective-permute-done | bytes 393248 | tf_op jit(solution)/shard_map/ppermute | solution.py:33
  77.9 8.9 %all-to-all-start = ((bf16[32,24,1024]{2,1,0:T(8,128)(2,1)}), bf16[32,24,1024]{2,1,0:T(8,128)(2,1)S(1)}, u32[]{:S(2)}, u32[]{:S(2)}) async-start(bf16[32,24,1024]{2,1,0:T(8,128)(2,1)} %bitcast.28), calls=%async_computation | async-start | bytes 3145728 | tf_op jit(solution)/shard_map/all_to_all | solution.py:612
  86.9 8.3 %project.3 = (bf16[3072,128]{1,0:T(8,128)(2,1)}, bf16[3072,256]{1,0:T(8,128)(2,1)}, bf16[8,4,24,1024]{3,2,1,0:T(8,128)(2,1)}) custom-call(s32[5]{0:T(128)} %stack.149.meta, bf16[192,1024]{1,0:T(8,128)(2,1)} %collective-permute-done.12.refs_0_, bf16[208,1024]{1,0:T(8,128)(2,1)} %copy-done.5, ...), custom_call_target="tpu_custom_call", output_to_operand_aliasing={{0}: (15, {}), {1}: (16, {})} | custom-call | flops 1207959552 | bytes 6291456 | tf_op jit(solution)/shard_map/project/pallas_call | solution.py:186
  95.2 27.8 %all-to-all-done = bf16[32,24,1024]{2,1,0:T(8,128)(2,1)S(1)} async-done(((bf16[32,24,1024]{2,1,0:T(8,128)(2,1)}), bf16[32,24,1024]{2,1,0:T(8,128)(2,1)S(1)}, u32[]{:S(2)}, u32[]{:S(2)}) %all-to-all-start) | async-done | bytes 1572896 | tf_op jit(solution)/shard_map/all_to_all | solution.py:612
  122.9 5.3 %all-to-all-start.1 = ((bf16[32,24,1024]{2,1,0:T(8,128)(2,1)}), bf16[32,24,1024]{2,1,0:T(8,128)(2,1)S(1)}, u32[]{:S(2)}, u32[]{:S(2)}) async-start(bf16[32,24,1024]{2,1,0:T(8,128)(2,1)} %bitcast.65), calls=%async_computation.1 | async-start | bytes 3145728 | tf_op jit(solution)/shard_map/all_to_all | solution.py:612
  131.4 2.3 %fusion.4 = (bf16[1024,256]{1,0:T(8,128)(2,1)}, bf16[1024,256]{1,0:T(8,128)(2,1)}) fusion(bf16[3072,256]{1,0:T(8,128)(2,1)} %get-tuple-element.82.pairs), kind=kLoop, calls=%fused_computation.48 | loop fusion | bytes 2097152 | tf_op jit(solution)/shard_map/slice | solution.py:629
  133.6 3.1 %collective-permute-start.27 = (bf16[1024,256]{1,0:T(8,128)(2,1)}, bf16[1024,256]{1,0:T(8,128)(2,1)}, u32[]{:S(2)}, u32[]{:S(2)}) collective-permute-start(bf16[1024,256]{1,0:T(8,128)(2,1)} %get-tuple-element.105), channel_id=1, source_target_pairs={{0,8},{4,12},{8,16},{12,20},{16,24},{20,28},{1,9},{5,13},{9,17},{1... | collective-permute-start | bytes 1572872 | tf_op jit(solution)/shard_map/ppermute | solution.py:39
  136.8 2.3 %collective-permute-start.28 = (bf16[1024,256]{1,0:T(8,128)(2,1)}, bf16[1024,256]{1,0:T(8,128)(2,1)}, u32[]{:S(2)}, u32[]{:S(2)}) collective-permute-start(bf16[1024,256]{1,0:T(8,128)(2,1)} %get-tuple-element.104), channel_id=1, source_target_pairs={{8,0},{12,4},{16,8},{20,12},{24,16},{28,20},{9,1},{13,5},{17,9},{2... | collective-permute-start | bytes 1572872 | tf_op jit(solution)/shard_map/ppermute | solution.py:39
  139.1 33.8 %attend_local.1 = (f32[12,160,256]{2,1,0:T(8,128)}, f32[12,8,256]{2,1,0:T(8,128)}) custom-call(s32[24]{0:T(128)} %reshape.109.ranges, bf16[3072,128]{1,0:T(8,128)(2,1)} %get-tuple-element.80.queries, s32[1,3072]{1,0:T(1,128)} %bitcast.71, s32[1,3072]{1,0:T(1,128)} %bitcast.73, bf16[3072,256]{1,0:T(8,128)(2,1)} %get-tuple-element.82.pairs), custom_call_target="tpu_custom_call" | custom-call | flops 6442450944 | bytes 5242880 | tf_op jit(solution)/shard_map/attend_local/pallas_call | solution.py:363
  177.0 12.8 %attend_finish.1 = (bf16[384,128]{1,0:T(8,128)(2,1)}, bf16[384,128]{1,0:T(8,128)(2,1)}, bf16[384,128]{1,0:T(8,128)(2,1)}, bf16[384,128]{1,0:T(8,128)(2,1)}, bf16...) custom-call(s32[25]{0:T(128)} %pad_add_fusion.1.meta, ...), custom_call_target="tpu_custom_call" | custom-call | flops 1610612736 | bytes 5242880 | tf_op jit(solution)/shard_map/attend_finish/pallas_call | solution.py:397
  190.3 1.8 collective-permute-start.31
  193.5 1.7 select_bitcast_fusion.1
  195.2 1.6 collective-permute-start.34
  198.3 1.5 pad_maximum_fusion
  199.8 3.3 %collective-permute-done.33.refs_5_ = bf16[384,128]{1,0:T(8,128)(2,1)S(1)} collective-permute-done((bf16[384,128]{1,0:T(8,128)(2,1)}, bf16[384,128]{1,0:T(8,128)(2,1)S(1)}, u32[]{:S(2)}, u32[]{:S(2)}) %collective-permute-start.33) | collective-permute-done | bytes 98336 | tf_op jit(solution)/shard_map/ppermute | solution.py:650
  203.9 4.7 %output_projection.1 = bf16[384,1024]{1,0:T(8,128)(2,1)} custom-call(s32[1]{0:T(128)} %bitcast.meta, bf16[384,128]{1,0:T(8,128)(2,1)} %get-tuple-element.89.refs_0_, bf16[384,128]{1,0:T(8,128)(2,1)} %copy-done.14, bf16[384,128]{1,0:T(8,128)(2,1)} %copy-done.15, bf16[384,128]{1,0:T(8,128)(2,1)} %copy-done.16, bf16[384,128]{1,0:T(8,128)(2,1)} %copy-done.17, ...), custom_call_target="tpu_custom_call" | custom-call | flops 805306368 | bytes 4194304 | tf_op jit(solution)/shard_map/output_projection/pallas_call | solution.py:447
  208.6 2.5 %unpack.1 = bf16[8,24,8192]{2,1,0:T(8,128)(2,1)} custom-call(bf16[4,2,4,24,1024]{4,3,2,1,0:T(8,128)(2,1)S(1)} %bitcast.59, bf16[4,2,4,24,1024]{4,3,2,1,0:T(8,128)(2,1)S(1)} %bitcast.60), custom_call_target="tpu_custom_call" | custom-call | bytes 6291456 | tf_op jit(solution)/shard_map/unpack/pallas_call | solution.py:483
  (158 shorter events, 30.4 us)
Async XLA Ops:
  2.8 11.8 %collective-permute-start.4 = (bf16[128,128]{1,0:T(8,128)(2,1)S(1)}, bf16[128,128]{1,0:T(8,128)(2,1)S(1)}, u32[]{:S(2)}, u32[]{:S(2)}) collective-permute-start(bf16[128,128]{1,0:T(8,128)(2,1)S(1)} %get-tuple-element.113), channel_id=1, source_target_pairs={{0,5},{1,4},{2,7},{3,6},{4,1},{5,0},{6,3},{7,2},{8,13},{9,12},{10,... | collective-permute-start | bytes 98312 | tf_op jit(solution)/shard_map/ppermute | solution.py:547
  4.8 11.1 %collective-permute-start.3 = (bf16[128,128]{1,0:T(8,128)(2,1)S(1)}, bf16[128,128]{1,0:T(8,128)(2,1)S(1)}, u32[]{:S(2)}, u32[]{:S(2)}) collective-permute-start(bf16[128,128]{1,0:T(8,128)(2,1)S(1)} %get-tuple-element.114), channel_id=1, source_target_pairs={{0,4},{1,7},{2,6},{3,5},{4,0},{5,3},{6,2},{7,1},{8,12},{9,15},{10,... | collective-permute-start | bytes 98312 | tf_op jit(solution)/shard_map/ppermute | solution.py:547
  6.0 9.9 %collective-permute-start.2 = (bf16[128,128]{1,0:T(8,128)(2,1)S(1)}, bf16[128,128]{1,0:T(8,128)(2,1)S(1)}, u32[]{:S(2)}, u32[]{:S(2)}) collective-permute-start(bf16[128,128]{1,0:T(8,128)(2,1)S(1)} %get-tuple-element.117), channel_id=1, source_target_pairs={{0,2},{1,1},{2,0},{3,3},{4,6},{5,5},{6,4},{7,7},{8,10},{9,9},{10,8... | collective-permute-start | bytes 98312 | tf_op jit(solution)/shard_map/ppermute | solution.py:547
  6.7 9.3 %collective-permute-start.1 = (bf16[128,128]{1,0:T(8,128)(2,1)S(1)}, bf16[128,128]{1,0:T(8,128)(2,1)S(1)}, u32[]{:S(2)}, u32[]{:S(2)}) collective-permute-start(bf16[128,128]{1,0:T(8,128)(2,1)S(1)} %get-tuple-element.116), channel_id=1, source_target_pairs={{0,1},{1,0},{2,3},{3,2},{4,5},{5,4},{6,7},{7,6},{8,9},{9,8},{10,11... | collective-permute-start | bytes 98312 | tf_op jit(solution)/shard_map/ppermute | solution.py:547
  16.0 15.2 %collective-permute-start.16 = (bf16[256,384]{1,0:T(8,128)(2,1)S(1)}, bf16[256,384]{1,0:T(8,128)(2,1)S(1)}, u32[]{:S(2)}, u32[]{:S(2)}) collective-permute-start(bf16[256,384]{1,0:T(8,128)(2,1)S(1)} %maximum_maximum_fusion.refs_8_), channel_id=1, source_target_pairs={{0,8},{4,12},{8,0},{12,4},{16,24},{20,28},{24,16},{28,20},{1,9},{5... | collective-permute-start | bytes 589832 | tf_op jit(solution)/shard_map/ppermute | solution.py:33
  16.3 15.7 %collective-permute-start.17 = (bf16[256,384]{1,0:T(8,128)(2,1)S(1)}, bf16[256,384]{1,0:T(8,128)(2,1)S(1)}, u32[]{:S(2)}, u32[]{:S(2)}) collective-permute-start(bf16[256,384]{1,0:T(8,128)(2,1)S(1)} %maximum_maximum_fusion.refs_8_), channel_id=1, source_target_pairs={{0,16},{4,20},{8,24},{12,28},{16,0},{20,4},{24,8},{28,12},{1,17},{... | collective-permute-start | bytes 589832 | tf_op jit(solution)/shard_map/ppermute | solution.py:33
  16.3 16.3 %collective-permute-start.6 = (bf16[192,1024]{1,0:T(8,128)(2,1)}, bf16[192,1024]{1,0:T(8,128)(2,1)S(1)}, u32[]{:S(2)}, u32[]{:S(2)}) collective-permute-start(bf16[192,1024]{1,0:T(8,128)(2,1)} %get-tuple-element.60.refs_0_), channel_id=1, source_target_pairs={{0,1},{1,0},{2,3},{3,2},{4,5},{5,4},{6,7},{7,6},{8,9},{9,8},{10,11... | collective-permute-start | bytes 1179656 | tf_op jit(solution)/shard_map/ppermute | solution.py:33
  18.8 11.5 %collective-permute-start.20 = (bf16[256,256]{1,0:T(8,128)(2,1)S(1)}, bf16[256,256]{1,0:T(8,128)(2,1)S(1)}, u32[]{:S(2)}, u32[]{:S(2)}) collective-permute-start(bf16[256,256]{1,0:T(8,128)(2,1)S(1)} %bitcast.68), channel_id=1, source_target_pairs={{0,16},{4,20},{8,24},{12,28},{16,0},{20,4},{24,8},{28,12},{1,17},{... | collective-permute-start | bytes 393224 | tf_op jit(solution)/shard_map/ppermute | solution.py:33
  22.8 13.9 %collective-permute-start.8 = (bf16[192,1024]{1,0:T(8,128)(2,1)}, bf16[192,1024]{1,0:T(8,128)(2,1)}, u32[]{:S(2)}, u32[]{:S(2)}) collective-permute-start(bf16[192,1024]{1,0:T(8,128)(2,1)} %get-tuple-element.60.refs_0_), channel_id=1, source_target_pairs={{0,2},{1,3},{2,0},{3,1},{4,6},{5,7},{6,4},{7,5},{8,10},{9,11},{10,... | collective-permute-start | bytes 1179656 | tf_op jit(solution)/shard_map/ppermute | solution.py:33
  30.3 10.8 %collective-permute-start.12 = (bf16[192,1024]{1,0:T(8,128)(2,1)}, bf16[192,1024]{1,0:T(8,128)(2,1)}, u32[]{:S(2)}, u32[]{:S(2)}) collective-permute-start(bf16[192,1024]{1,0:T(8,128)(2,1)} %get-tuple-element.60.refs_0_), channel_id=1, source_target_pairs={{0,4},{4,0},{8,12},{12,8},{16,20},{20,16},{24,28},{28,24},{1,5},{5... | collective-permute-start | bytes 1179656 | tf_op jit(solution)/shard_map/ppermute | solution.py:33
  31.2 13.3 %collective-permute-start.9 = (bf16[208,1024]{1,0:T(8,128)(2,1)}, bf16[208,1024]{1,0:T(8,128)(2,1)S(1)}, u32[]{:S(2)}, u32[]{:S(2)}) collective-permute-start(bf16[208,1024]{1,0:T(8,128)(2,1)} %get-tuple-element.61.refs_1_), channel_id=1, source_target_pairs={{0,2},{1,3},{2,0},{3,1},{4,6},{5,7},{6,4},{7,5},{8,10},{9,11},{10,... | collective-permute-start | bytes 1277960 | tf_op jit(solution)/shard_map/ppermute | solution.py:33
  32.0 18.2 %collective-permute-start.13 = (bf16[208,1024]{1,0:T(8,128)(2,1)}, bf16[208,1024]{1,0:T(8,128)(2,1)S(1)}, u32[]{:S(2)}, u32[]{:S(2)}) collective-permute-start(bf16[208,1024]{1,0:T(8,128)(2,1)} %get-tuple-element.61.refs_1_), channel_id=1, source_target_pairs={{0,4},{4,0},{8,12},{12,8},{16,20},{20,16},{24,28},{28,24},{1,5},{5... | collective-permute-start | bytes 1277960 | tf_op jit(solution)/shard_map/ppermute | solution.py:33
  32.6 10.2 %collective-permute-start.18 = (bf16[256,384]{1,0:T(8,128)(2,1)S(1)}, bf16[256,384]{1,0:T(8,128)(2,1)S(1)}, u32[]{:S(2)}, u32[]{:S(2)}) collective-permute-start(bf16[256,384]{1,0:T(8,128)(2,1)S(1)} %collective-permute-done.17.refs_10_), channel_id=1, source_target_pairs={{0,8},{4,12},{8,0},{12,4},{16,24},{20,28},{24,16},{28,20},{1,9},{5... | collective-permute-start | bytes 589832 | tf_op jit(solution)/shard_map/ppermute | solution.py:33
  36.7 15.4 %collective-permute-start.7 = (bf16[208,1024]{1,0:T(8,128)(2,1)}, bf16[208,1024]{1,0:T(8,128)(2,1)S(1)}, u32[]{:S(2)}, u32[]{:S(2)}) collective-permute-start(bf16[208,1024]{1,0:T(8,128)(2,1)} %get-tuple-element.61.refs_1_), channel_id=1, source_target_pairs={{0,1},{1,0},{2,3},{3,2},{4,5},{5,4},{6,7},{7,6},{8,9},{9,8},{10,11... | collective-permute-start | bytes 1277960 | tf_op jit(solution)/shard_map/ppermute | solution.py:33
  41.1 11.0 %collective-permute-start.10 = (bf16[192,1024]{1,0:T(8,128)(2,1)}, bf16[192,1024]{1,0:T(8,128)(2,1)}, u32[]{:S(2)}, u32[]{:S(2)}) collective-permute-start(bf16[192,1024]{1,0:T(8,128)(2,1)} %collective-permute-done.8.refs_4_), channel_id=1, source_target_pairs={{0,1},{1,0},{2,3},{3,2},{4,5},{5,4},{6,7},{7,6},{8,9},{9,8},{10,11... | collective-permute-start | bytes 1179656 | tf_op jit(solution)/shard_map/ppermute | solution.py:33
  42.8 9.4 %collective-permute-start.14 = (bf16[192,1024]{1,0:T(8,128)(2,1)}, bf16[192,1024]{1,0:T(8,128)(2,1)}, u32[]{:S(2)}, u32[]{:S(2)}) collective-permute-start(bf16[192,1024]{1,0:T(8,128)(2,1)} %collective-permute-done.12.refs_0_), channel_id=1, source_target_pairs={{0,1},{1,0},{2,3},{3,2},{4,5},{5,4},{6,7},{7,6},{8,9},{9,8},{10,11... | collective-permute-start | bytes 1179656 | tf_op jit(solution)/shard_map/ppermute | solution.py:33
  44.5 7.7 %collective-permute-start.11 = (bf16[208,1024]{1,0:T(8,128)(2,1)S(1)}, bf16[208,1024]{1,0:T(8,128)(2,1)S(1)}, u32[]{:S(2)}, u32[]{:S(2)}) collective-permute-start(bf16[208,1024]{1,0:T(8,128)(2,1)S(1)} %collective-permute-done.9.refs_5_), channel_id=1, source_target_pairs={{0,1},{1,0},{2,3},{3,2},{4,5},{5,4},{6,7},{7,6},{8,9},{9,8},{10,11... | collective-permute-start | bytes 1277960 | tf_op jit(solution)/shard_map/ppermute | solution.py:33
  52.6 14.3 %collective-permute-start.25 = (bf16[4,128,256]{2,1,0:T(8,128)(2,1)S(1)}, bf16[4,128,256]{2,1,0:T(8,128)(2,1)S(1)}, u32[]{:S(2)}, u32[]{:S(2)}) collective-permute-start(bf16[4,128,256]{2,1,0:T(8,128)(2,1)S(1)} %bitcast.66), channel_id=1, source_target_pairs={{0,4},{4,0},{8,12},{12,8},{16,20},{20,16},{24,28},{28,24},{1,5},{5... | collective-permute-start | bytes 786440 | tf_op jit(solution)/shard_map/ppermute | solution.py:33
  55.6 13.0 %collective-permute-start.21 = (bf16[192,1024]{1,0:T(8,128)(2,1)}, bf16[192,1024]{1,0:T(8,128)(2,1)}, u32[]{:S(2)}, u32[]{:S(2)}) collective-permute-start(bf16[192,1024]{1,0:T(8,128)(2,1)} %collective-permute-done.8.refs_4_), channel_id=1, source_target_pairs={{0,4},{4,0},{8,12},{12,8},{16,20},{20,16},{24,28},{28,24},{1,5},{5... | collective-permute-start | bytes 1179656 | tf_op jit(solution)/shard_map/ppermute | solution.py:33
  56.9 20.1 %collective-permute-start.22 = (bf16[208,1024]{1,0:T(8,128)(2,1)S(1)}, bf16[208,1024]{1,0:T(8,128)(2,1)S(1)}, u32[]{:S(2)}, u32[]{:S(2)}) collective-permute-start(bf16[208,1024]{1,0:T(8,128)(2,1)S(1)} %collective-permute-done.13.refs_1_), channel_id=1, source_target_pairs={{0,2},{1,3},{2,0},{3,1},{4,6},{5,7},{6,4},{7,5},{8,10},{9,11},{10,... | collective-permute-start | bytes 1277960 | tf_op jit(solution)/shard_map/ppermute | solution.py:33
  57.2 19.9 %collective-permute-start.23 = (bf16[192,1024]{1,0:T(8,128)(2,1)}, bf16[192,1024]{1,0:T(8,128)(2,1)}, u32[]{:S(2)}, u32[]{:S(2)}) collective-permute-start(bf16[192,1024]{1,0:T(8,128)(2,1)} %collective-permute-done.10.refs_6_), channel_id=1, source_target_pairs={{0,4},{4,0},{8,12},{12,8},{16,20},{20,16},{24,28},{28,24},{1,5},{5... | collective-permute-start | bytes 1179656 | tf_op jit(solution)/shard_map/ppermute | solution.py:33
  58.6 18.4 %collective-permute-start.24 = (bf16[208,1024]{1,0:T(8,128)(2,1)S(1)}, bf16[208,1024]{1,0:T(8,128)(2,1)S(1)}, u32[]{:S(2)}, u32[]{:S(2)}) collective-permute-start(bf16[208,1024]{1,0:T(8,128)(2,1)S(1)} %collective-permute-done.15.refs_3_), channel_id=1, source_target_pairs={{0,2},{1,3},{2,0},{3,1},{4,6},{5,7},{6,4},{7,5},{8,10},{9,11},{10,... | collective-permute-start | bytes 1277960 | tf_op jit(solution)/shard_map/ppermute | solution.py:33
  77.9 45.1 %all-to-all-start = ((bf16[32,24,1024]{2,1,0:T(8,128)(2,1)}), bf16[32,24,1024]{2,1,0:T(8,128)(2,1)S(1)}, u32[]{:S(2)}, u32[]{:S(2)}) async-start(bf16[32,24,1024]{2,1,0:T(8,128)(2,1)} %bitcast.28), calls=%async_computation | async-start | bytes 3145728 | tf_op jit(solution)/shard_map/all_to_all | solution.py:612
  122.9 85.6 %all-to-all-start.1 = ((bf16[32,24,1024]{2,1,0:T(8,128)(2,1)}), bf16[32,24,1024]{2,1,0:T(8,128)(2,1)S(1)}, u32[]{:S(2)}, u32[]{:S(2)}) async-start(bf16[32,24,1024]{2,1,0:T(8,128)(2,1)} %bitcast.65), calls=%async_computation.1 | async-start | bytes 3145728 | tf_op jit(solution)/shard_map/all_to_all | solution.py:612
  130.2 42.7 %collective-permute-start.26 = (bf16[1,1024,256]{2,1,0:T(8,128)(2,1)}, bf16[1,1024,256]{2,1,0:T(8,128)(2,1)}, u32[]{:S(2)}, u32[]{:S(2)}) collective-permute-start(bf16[1,1024,256]{2,1,0:T(8,128)(2,1)} %bitcast.63), channel_id=1, source_target_pairs={{0,2},{1,3},{2,0},{3,1},{4,6},{5,7},{6,4},{7,5},{8,10},{9,11},{10,... | collective-permute-start | bytes 1572872 | tf_op jit(solution)/shard_map/ppermute | solution.py:33
  133.6 41.6 %collective-permute-start.27 = (bf16[1024,256]{1,0:T(8,128)(2,1)}, bf16[1024,256]{1,0:T(8,128)(2,1)}, u32[]{:S(2)}, u32[]{:S(2)}) collective-permute-start(bf16[1024,256]{1,0:T(8,128)(2,1)} %get-tuple-element.105), channel_id=1, source_target_pairs={{0,8},{4,12},{8,16},{12,20},{16,24},{20,28},{1,9},{5,13},{9,17},{1... | collective-permute-start | bytes 1572872 | tf_op jit(solution)/shard_map/ppermute | solution.py:39
  136.8 38.5 %collective-permute-start.28 = (bf16[1024,256]{1,0:T(8,128)(2,1)}, bf16[1024,256]{1,0:T(8,128)(2,1)}, u32[]{:S(2)}, u32[]{:S(2)}) collective-permute-start(bf16[1024,256]{1,0:T(8,128)(2,1)} %get-tuple-element.104), channel_id=1, source_target_pairs={{8,0},{12,4},{16,8},{20,12},{24,16},{28,20},{9,1},{13,5},{17,9},{2... | collective-permute-start | bytes 1572872 | tf_op jit(solution)/shard_map/ppermute | solution.py:39
  175.3 18.0 %collective-permute-start.36 = (bf16[2,1024,256]{2,1,0:T(8,128)(2,1)}, bf16[2,1024,256]{2,1,0:T(8,128)(2,1)}, u32[]{:S(2)}, u32[]{:S(2)}) collective-permute-start(bf16[2,1024,256]{2,1,0:T(8,128)(2,1)} %maximum_bitcast_fusion), channel_id=1, source_target_pairs={{0,1},{1,0},{2,3},{3,2},{4,5},{5,4},{6,7},{7,6},{8,9},{9,8},{10,11... | collective-permute-start | bytes 3145736 | tf_op jit(solution)/shard_map/ppermute | solution.py:33
  190.3 9.6 %collective-permute-start.31 = (bf16[384,128]{1,0:T(8,128)(2,1)}, bf16[384,128]{1,0:T(8,128)(2,1)S(1)}, u32[]{:S(2)}, u32[]{:S(2)}) collective-permute-start(bf16[384,128]{1,0:T(8,128)(2,1)} %get-tuple-element.92), channel_id=1, source_target_pairs={{0,3},{1,2},{2,1},{3,0},{4,7},{5,6},{6,5},{7,4},{8,11},{9,10},{10,... | collective-permute-start | bytes 294920 | tf_op jit(solution)/shard_map/ppermute | solution.py:650
  192.1 7.8 %collective-permute-start.32 = (bf16[384,128]{1,0:T(8,128)(2,1)}, bf16[384,128]{1,0:T(8,128)(2,1)S(1)}, u32[]{:S(2)}, u32[]{:S(2)}) collective-permute-start(bf16[384,128]{1,0:T(8,128)(2,1)} %get-tuple-element.93), channel_id=1, source_target_pairs={{0,4},{1,5},{2,6},{3,7},{4,0},{5,1},{6,2},{7,3},{8,12},{9,13},{10,... | collective-permute-start | bytes 294920 | tf_op jit(solution)/shard_map/ppermute | solution.py:650
  193.3 9.9 %collective-permute-start.33 = (bf16[384,128]{1,0:T(8,128)(2,1)}, bf16[384,128]{1,0:T(8,128)(2,1)S(1)}, u32[]{:S(2)}, u32[]{:S(2)}) collective-permute-start(bf16[384,128]{1,0:T(8,128)(2,1)} %get-tuple-element.94), channel_id=1, source_target_pairs={{0,5},{1,4},{2,7},{3,6},{4,1},{5,0},{6,3},{7,2},{8,13},{9,12},{10,... | collective-permute-start | bytes 294920 | tf_op jit(solution)/shard_map/ppermute | solution.py:650
  195.2 8.0 %collective-permute-start.34 = (bf16[384,128]{1,0:T(8,128)(2,1)S(1)}, bf16[384,128]{1,0:T(8,128)(2,1)S(1)}, u32[]{:S(2)}, u32[]{:S(2)}) collective-permute-start(bf16[384,128]{1,0:T(8,128)(2,1)S(1)} %copy-done.24), channel_id=1, source_target_pairs={{0,6},{1,7},{2,4},{3,5},{4,2},{5,3},{6,0},{7,1},{8,14},{9,15},{10,... | collective-permute-start | bytes 294920 | tf_op jit(solution)/shard_map/ppermute | solution.py:650
  (32 other events, 315.5 us)

commit v2 on v1

--- a/solution.py
+++ b/solution.py
@@ -225,9 +225,10 @@
 
 
 def mask_heads(queries, masked):
-    head_of_lane = lax.broadcasted_iota(jnp.int32, queries.shape, 1) // HEAD_DIM
+    turned = queries[...].T
+    head_of_row = lax.broadcasted_iota(jnp.int32, turned.shape, 0) // HEAD_DIM
     for head in range(masked.shape[0]):
-        masked[head] = jnp.where(head_of_lane == head, queries[...], jnp.zeros((), jnp.bfloat16))
+        masked[head] = jnp.where(head_of_row == head, turned, jnp.zeros((), jnp.bfloat16))
 
 
 def with_ones(values):
@@ -256,9 +257,7 @@
         allowed = (index >= jnp.maximum(starts, wanted * TILE)) & (index < last)
         new_peaks = []
         for head, old_peak in enumerate(peaks):
-            scores = lax.dot_general(
-                keys, masked[head], (((1,), (1,)), ((), ())), preferred_element_type=jnp.float32
-            )
+            scores = jnp.dot(keys, masked[head], preferred_element_type=jnp.float32)
             scores = jnp.where(allowed, scores * SCALE, NEG_FILL)
             peak = jnp.maximum(old_peak, jnp.max(scores, axis=0, keepdims=True))
             fade = jnp.exp2(old_peak - peak)
@@ -371,7 +370,7 @@
                 pl.BlockSpec((1, 8, TILE), lambda i, m: (i, 0, 0)),
             ],
             scratch_shapes=[
-                pltpu.VMEM((heads, TILE, width), jnp.bfloat16),
+                pltpu.VMEM((heads, width, TILE), jnp.bfloat16),
                 pltpu.VMEM((heads * HEAD_ROWS, group_rows), jnp.bfloat16),
             ],
         ),
@@ -406,7 +405,7 @@
             ],
             out_specs=[pl.BlockSpec((rows, width), lambda i, m: (0, 0))] * members,
             scratch_shapes=[
-                pltpu.VMEM((heads, TILE, width), jnp.bfloat16),
+                pltpu.VMEM((heads, width, TILE), jnp.bfloat16),
                 pltpu.VMEM(total.shape[1:], jnp.float32),
                 pltpu.VMEM((group_rows, width), jnp.bfloat16),
             ],
@@ -549,42 +548,41 @@
     plane = jnp.concatenate(halves, axis=0)
     top, bottom = layer_norm(tokens, norm_gain[None, :], owners, capacity)
     top, bottom, plane = lax.optimization_barrier((top, bottom, plane))
+    across = [flipped(top, "grp", 2), flipped(bottom, "grp", 2)]
+    along = [flipped(top, "tok", 1), flipped(bottom, "tok", 1)]
+    sibling = [flipped(top, "grp", 1), flipped(bottom, "grp", 1)]
     planes = {0: plane}
     bit = peers // 2
     while bit > 1:
         for distance in list(planes):
             planes[distance ^ bit] = flipped(planes[distance], "tok", bit)
         bit //= 2
+    last_weight = output_weight
+    bit = PAIR
+    while 2 * bit < peers:
+        last_weight = doubled(last_weight, "tok", bit, 0)
+        bit *= 2
+    across, along, sibling, last_weight = lax.optimization_barrier(
+        (across, along, sibling, last_weight)
+    )
+    corner = [flipped(across[0], "tok", 1), flipped(along[1], "grp", 2)]
+    across_sibling = [flipped(block, "grp", 1) for block in across]
+    along_sibling = [flipped(block, "grp", 1) for block in along]
+    if bit < peers:
+        last_weight = doubled(last_weight, "tok", bit, 0)
+    last_weight = last_weight.reshape((peers // PAIR,) + output_weight.shape)
     weights = [planes[distance] for distance in range(0, peers, 2)]
-
-    across_top, along_bottom = flipped(top, "grp", 2), flipped(bottom, "tok", 1)
-    across_bottom, along_top = flipped(bottom, "grp", 2), flipped(top, "tok", 1)
-    near_blocks = [top, bottom, flipped(top, "grp", 1), flipped(bottom, "grp", 1)]
-    near_blocks += [across_top, across_bottom]
-    near_blocks += [flipped(across_top, "grp", 1), flipped(across_bottom, "grp", 1)]
-    far_blocks = [along_top, along_bottom]
-    far_blocks += [flipped(along_top, "grp", 1), flipped(along_bottom, "grp", 1)]
+    across_sibling, along_sibling, corner, weights, last_weight = lax.optimization_barrier(
+        (across_sibling, along_sibling, corner, weights, last_weight)
+    )
+    corner_sibling = [flipped(block, "grp", 1) for block in corner]
+    last_weight = doubled(last_weight, "tok", 1, 1).reshape(model_width, output_weight.shape[1])
+    near_blocks = [top, bottom] + sibling + across + across_sibling
+    far_blocks = along + along_sibling + corner
     half, held = rows // 2, rows + EXTRA_ROWS
     layout = [
         [(2 * number, 0, half), (2 * number + 1, half, held - half)] for number in range(4)
     ]
-
-    last_weight = output_weight
-    bit = PAIR
-    while bit < peers:
-        last_weight = doubled(last_weight, "tok", bit, 0)
-        bit *= 2
-    last_weight = last_weight.reshape((peers // PAIR,) + output_weight.shape)
-    near_blocks, far_blocks, weights, last_weight = lax.optimization_barrier(
-        (near_blocks, far_blocks, weights, last_weight)
-    )
-    corners = [
-        flipped(near_blocks[4], "tok", 1),
-        flipped(far_blocks[1], "grp", 2),
-        flipped(near_blocks[6], "tok", 1),
-        flipped(far_blocks[3], "grp", 2),
-    ]
-    last_weight = doubled(last_weight, "tok", 1, 1).reshape(model_width, output_weight.shape[1])
 
     first_row = place // PAIR * group_rows
     padded_ids = jnp.concatenate(
@@ -619,21 +617,23 @@
         return received.reshape((peers // PAIR, PAIR, members) + send.shape[2:])
 
     queries, pairs, send = project(meta, 0, layout, near_blocks, *sizes, ())
-    send, corners, last_weight = lax.optimization_barrier((send, corners, last_weight))
+    send, corner_sibling, last_weight = lax.optimization_barrier(
+        (send, corner_sibling, last_weight)
+    )
     own_row = to_owners(send)
     queries, pairs, send = project(
-        meta, 4, layout, far_blocks + corners, *sizes, (queries, pairs)
-    )
-    other_row = to_owners(send)
+        meta, 4, layout, far_blocks + corner_sibling, *sizes, (queries, pairs)
+    )
     before = shifted(pairs[group_rows - SPAN :], "tok", PAIR)
     after = shifted(pairs[:SPAN], "tok", -PAIR)
     last_weight = doubled(last_weight[None], "grp", 2, 0)
 
     bounds = (starts[None, :], ends[None, :])
     total, peaks = attend_local(ranges, queries, *bounds, pairs)
-    last_weight, before, after, total, peaks = lax.optimization_barrier(
-        (last_weight, before, after, total, peaks)
-    )
+    last_weight, before, after, total, peaks, send = lax.optimization_barrier(
+        (last_weight, before, after, total, peaks, send)
+    )
+    other_row = to_owners(send)
     last_weight = doubled(last_weight, "grp", 1, 1).reshape(members * model_width, -1)
     own_member = member[None].astype(jnp.int32)
     mixed = attend_finish(

time: 214 us -> 186 us (0.87); the launches traced: 211 us -> 187 us
  waiting for transfers between devices: 56.4 us -> 31.6 us
  starting transfers between devices: 57.8 us -> 60.7 us
    all_to_all x2, waiting for transfers between devices: 27.8 us -> 0.01 us  [to_owners(): lax.all_to_all(send.reshape((flat,) + send.shape[2:]), ('tok', 'grp'), sp...]
    ppermute x7, starting transfers between devices: 6.7 us -> 9.3 us  [per_device(): lax.ppermute(mixed[distance], ('tok', 'grp'), [(source, source ^ distance...]
    ppermute x7, waiting for transfers between devices: 3.33 us -> 5.75 us  [per_device(): lax.ppermute(mixed[distance], ('tok', 'grp'), [(source, source ^ distance...]
  transfers between devices with their start and end apart: 39 -> 39, of which waited for: 12 -> 10; matrix products, arithmetic and copies ran while one was open for 10% -> 9% of each run, Pallas kernels for 33% -> 38%
where the time goes in v2:
time: 186 us; the launch traced here: 187 us
  Pallas kernels  73.2 us (39%)
  starting transfers between devices  60.7 us (33%)
  waiting for transfers between devices  31.6 us (17%)
  other arithmetic  14 us (8%)
  local copies, waits for them, and re-layouts  5.7 us (3%)
    pallas_call x1, Pallas kernels, attend_local(): pl.pallas_call(attend_kernel, grid_spec=pltpu.PrefetchScalarGridSpec(num_...  33.1 us
    ppermute x22, waiting for transfers between devices, flipped(): lax.ppermute(value, axis, [(source, source ^ bit) for source in range(cou...  25.8 us
    ppermute x22, starting transfers between devices, flipped(): lax.ppermute(value, axis, [(source, source ^ bit) for source in range(cou...  22 us
    pallas_call x2, Pallas kernels, project(): pl.pallas_call(functools.partial(project_kernel, first, layout, len(weigh...  16.4 us
    all_to_all x2, starting transfers between devices, to_owners(): lax.all_to_all(send.reshape((flat,) + send.shape[2:]), ('tok', 'grp'), sp...  14.8 us
    pallas_call x1, Pallas kernels, attend_finish(): pl.pallas_call(finish_kernel, grid_spec=pltpu.PrefetchScalarGridSpec(num_...  14.1 us
    ppermute x6, starting transfers between devices, per_device(): pieces.append(lax.ppermute(piece, ('tok', 'grp'), route))  9.34 us
    ppermute x7, starting transfers between devices, per_device(): lax.ppermute(mixed[distance], ('tok', 'grp'), [(source, source ^ distance...  9.3 us
  transfers between devices with their start and end apart: 39, of which 10 were waited for; matrix products, arithmetic and copies ran while one was open for 9% of the time, Pallas kernels for 38%

profile of v2, /device:TPU:17, one launch (start us, length us, event | category | flops | bytes accessed | tf_op | source)
XLA Modules:
  0.0 186.6 jit_solution(10262509407986416758)
XLA Ops:
  2.8 2.0 %collective-permute-start.4 = (bf16[128,128]{1,0:T(8,128)(2,1)S(1)}, bf16[128,128]{1,0:T(8,128)(2,1)S(1)}, u32[]{:S(2)}, u32[]{:S(2)}) collective-permute-start(bf16[128,128]{1,0:T(8,128)(2,1)S(1)} %get-tuple-element.113), channel_id=1, source_target_pairs={{0,5},{1,4},{2,7},{3,6},{4,1},{5,0},{6,3},{7,2},{8,13},{9,12},{10,... | collective-permute-start | bytes 98312 | tf_op jit(solution)/shard_map/ppermute | solution.py:546
  6.7 1.7 collective-permute-start.1
  9.2 2.4 %collective-permute-start = (bf16[128,128]{1,0:T(8,128)(2,1)S(1)}, bf16[128,128]{1,0:T(8,128)(2,1)S(1)}, u32[]{:S(2)}, u32[]{:S(2)}) collective-permute-start(bf16[128,128]{1,0:T(8,128)(2,1)S(1)} %get-tuple-element.112), channel_id=1, source_target_pairs={{0,0},{1,3},{2,2},{3,1},{4,4},{5,7},{6,6},{7,5},{8,8},{9,11},{10,1... | collective-permute-start | bytes 98312 | tf_op jit(solution)/shard_map/ppermute | solution.py:546
  11.9 2.5 %layer_norm.1 = (bf16[192,1024]{1,0:T(8,128)(2,1)}, bf16[208,1024]{1,0:T(8,128)(2,1)}) custom-call(bf16[384,1024]{1,0:T(8,128)(2,1)} %tokens.1, f32[1,1024]{1,0:T(1,128)} %bitcast.75, s32[1,96]{1,0:T(1,128)} %bitcast.76), custom_call_target="tpu_custom_call" | custom-call | tf_op jit(solution)/shard_map/layer_norm/pallas_call | solution.py:76
  17.0 3.9 %convert_reduce_fusion.1 = (s32[8,384]{1,0:T(8,128)S(1)}, s32[8,384]{1,0:T(8,128)S(1)}) fusion(s32[8,384]{1,0:T(8,128)S(1)} %lt.39, s32[8,1408]{1,0:T(8,128)S(1)} %stack.132, s32[8,1408]{1,0:T(8,128)S(1)} %stack.142), kind=kLoop, calls=%fused_computation.1 | loop fusion | flops 25946112 | bytes 126976 | tf_op jit(solution)/shard_map/reduce_sum | solution.py:511
  23.0 4.4 %collective-permute-done.6.refs_4_ = bf16[192,1024]{1,0:T(8,128)(2,1)} collective-permute-done((bf16[192,1024]{1,0:T(8,128)(2,1)}, bf16[192,1024]{1,0:T(8,128)(2,1)}, u32[]{:S(2)}, u32[]{:S(2)}) %collective-permute-start.6) | collective-permute-done | bytes 393248 | tf_op jit(solution)/shard_map/ppermute | solution.py:33
  27.4 4.9 %collective-permute-done.8.refs_0_ = bf16[192,1024]{1,0:T(8,128)(2,1)S(1)} collective-permute-done((bf16[192,1024]{1,0:T(8,128)(2,1)}, bf16[192,1024]{1,0:T(8,128)(2,1)S(1)}, u32[]{:S(2)}, u32[]{:S(2)}) %collective-permute-start.8) | collective-permute-done | bytes 393248 | tf_op jit(solution)/shard_map/ppermute | solution.py:33
  32.4 3.1 %collective-permute-done.7.refs_5_ = bf16[208,1024]{1,0:T(8,128)(2,1)S(1)} collective-permute-done((bf16[208,1024]{1,0:T(8,128)(2,1)}, bf16[208,1024]{1,0:T(8,128)(2,1)S(1)}, u32[]{:S(2)}, u32[]{:S(2)}) %collective-permute-start.7) | collective-permute-done | bytes 426016 | tf_op jit(solution)/shard_map/ppermute | solution.py:33
  35.5 4.5 %collective-permute-done.9.refs_1_ = bf16[208,1024]{1,0:T(8,128)(2,1)S(1)} collective-permute-done((bf16[208,1024]{1,0:T(8,128)(2,1)}, bf16[208,1024]{1,0:T(8,128)(2,1)S(1)}, u32[]{:S(2)}, u32[]{:S(2)}) %collective-permute-start.9) | collective-permute-done | bytes 426016 | tf_op jit(solution)/shard_map/ppermute | solution.py:33
  40.8 2.1 %collective-permute-start.21 = (bf16[256,384]{1,0:T(8,128)(2,1)S(1)}, bf16[256,384]{1,0:T(8,128)(2,1)S(1)}, u32[]{:S(2)}, u32[]{:S(2)}) collective-permute-start(bf16[256,384]{1,0:T(8,128)(2,1)S(1)} %collective-permute-done.20.refs_10_), channel_id=1, source_target_pairs={{0,8},{4,12},{8,0},{12,4},{16,24},{20,28},{24,16},{28,20},{1,9},{5... | collective-permute-start | bytes 589832 | tf_op jit(solution)/shard_map/ppermute | solution.py:33
  42.9 2.0 %collective-permute-start.17 = (bf16[192,1024]{1,0:T(8,128)(2,1)}, bf16[192,1024]{1,0:T(8,128)(2,1)}, u32[]{:S(2)}, u32[]{:S(2)}) collective-permute-start(bf16[192,1024]{1,0:T(8,128)(2,1)} %collective-permute-done.6.refs_4_), channel_id=1, source_target_pairs={{0,4},{4,0},{8,12},{12,8},{16,20},{20,16},{24,28},{28,24},{1,5},{5... | collective-permute-start | bytes 1179656 | tf_op jit(solution)/shard_map/ppermute | solution.py:33
  46.3 3.4 %collective-permute-start.16 = (bf16[208,1024]{1,0:T(8,128)(2,1)S(1)}, bf16[208,1024]{1,0:T(8,128)(2,1)S(1)}, u32[]{:S(2)}, u32[]{:S(2)}) collective-permute-start(bf16[208,1024]{1,0:T(8,128)(2,1)S(1)} %collective-permute-done.9.refs_1_), channel_id=1, source_target_pairs={{0,1},{1,0},{2,3},{3,2},{4,5},{5,4},{6,7},{7,6},{8,9},{9,8},{10,11... | collective-permute-start | bytes 1277960 | tf_op jit(solution)/shard_map/ppermute | solution.py:33
  49.6 1.9 %collective-permute-done.21.refs_11_ = bf16[256,384]{1,0:T(8,128)(2,1)S(1)} collective-permute-done((bf16[256,384]{1,0:T(8,128)(2,1)S(1)}, bf16[256,384]{1,0:T(8,128)(2,1)S(1)}, u32[]{:S(2)}, u32[]{:S(2)}) %collective-permute-start.21) | collective-permute-done | bytes 196640 | tf_op jit(solution)/shard_map/ppermute | solution.py:33
  56.4 5.1 %collective-permute-done.18.refs_5_ = bf16[208,1024]{1,0:T(8,128)(2,1)S(1)} collective-permute-done((bf16[208,1024]{1,0:T(8,128)(2,1)S(1)}, bf16[208,1024]{1,0:T(8,128)(2,1)S(1)}, u32[]{:S(2)}, u32[]{:S(2)}) %collective-permute-start.18) | collective-permute-done | bytes 426016 | tf_op jit(solution)/shard_map/ppermute | solution.py:33
  61.5 2.2 %collective-permute-start.25 = (bf16[4,128,256]{2,1,0:T(8,128)(2,1)S(1)}, bf16[4,128,256]{2,1,0:T(8,128)(2,1)S(1)}, u32[]{:S(2)}, u32[]{:S(2)}) collective-permute-start(bf16[4,128,256]{2,1,0:T(8,128)(2,1)S(1)} %bitcast.65), channel_id=1, source_target_pairs={{0,4},{4,0},{8,12},{12,8},{16,20},{20,16},{24,28},{28,24},{1,5},{5... | collective-permute-start | bytes 786440 | tf_op jit(solution)/shard_map/ppermute | solution.py:33
  63.7 2.3 %multiply_sine_fusion = (f32[32,3072]{1,0:T(8,128)}, f32[32,3072]{1,0:T(8,128)}) fusion(f32[3072]{0:T(1024)S(1)} %subtract_convert_fusion, f32[32]{0:T(128)S(1)} %negate_power_fusion), kind=kLoop, calls=%fused_computation.6 | loop fusion | flops 98304 | bytes 798848 | tf_op jit(solution)/shard_map/sin | solution.py:500
  66.6 2.2 %collective-permute-start.23 = (bf16[192,1024]{1,0:T(8,128)(2,1)}, bf16[192,1024]{1,0:T(8,128)(2,1)}, u32[]{:S(2)}, u32[]{:S(2)}) collective-permute-start(bf16[192,1024]{1,0:T(8,128)(2,1)} %collective-permute-done.17.refs_4_), channel_id=1, source_target_pairs={{0,1},{1,0},{2,3},{3,2},{4,5},{5,4},{6,7},{7,6},{8,9},{9,8},{10,11... | collective-permute-start | bytes 1179656 | tf_op jit(solution)/shard_map/ppermute | solution.py:33
  68.9 8.2 %project.2 = (bf16[3072,128]{1,0:T(8,128)(2,1)}, bf16[3072,256]{1,0:T(8,128)(2,1)}, bf16[8,4,24,1024]{3,2,1,0:T(8,128)(2,1)}) custom-call(s32[5]{0:T(128)} %stack.149.meta, bf16[192,1024]{1,0:T(8,128)(2,1)} %get-tuple-element.53.refs_0_, bf16[208,1024]{1,0:T(8,128)(2,1)} %get-tuple-element.54.refs_1_, bf16[192,1024]{1,0:T(8,128)(2,1)} %copy-done.11, ...), custom_call_target="tpu_custom_call" | custom-call | flops 1207959552 | bytes 6291456 | tf_op jit(solution)/shard_map/project/pallas_call | solution.py:186
  78.1 5.5 %all-to-all-start = ((bf16[32,24,1024]{2,1,0:T(8,128)(2,1)}), bf16[32,24,1024]{2,1,0:T(8,128)(2,1)S(1)}, u32[]{:S(2)}, u32[]{:S(2)}) async-start(bf16[32,24,1024]{2,1,0:T(8,128)(2,1)} %bitcast.64), calls=%async_computation | async-start | bytes 3145728 | tf_op jit(solution)/shard_map/all_to_all | solution.py:610
  86.9 8.2 %project.3 = (bf16[3072,128]{1,0:T(8,128)(2,1)}, bf16[3072,256]{1,0:T(8,128)(2,1)}, bf16[8,4,24,1024]{3,2,1,0:T(8,128)(2,1)}) custom-call(s32[5]{0:T(128)} %stack.149.meta, bf16[192,1024]{1,0:T(8,128)(2,1)} %copy-done.10, bf16[208,1024]{1,0:T(8,128)(2,1)} %copy-done.4, ...), custom_call_target="tpu_custom_call", output_to_operand_aliasing={{0}: (15, {}), {1}: (16, {})} | custom-call | flops 1207959552 | bytes 6291456 | tf_op jit(solution)/shard_map/project/pallas_call | solution.py:186
  96.4 3.2 %collective-permute-start.27 = (bf16[1024,256]{1,0:T(8,128)(2,1)S(1)}, bf16[1024,256]{1,0:T(8,128)(2,1)}, u32[]{:S(2)}, u32[]{:S(2)}) collective-permute-start(bf16[1024,256]{1,0:T(8,128)(2,1)S(1)} %get-tuple-element.105), channel_id=1, source_target_pairs={{0,8},{4,12},{8,16},{12,20},{16,24},{20,28},{1,9},{5,13},{9,17},{1... | collective-permute-start | bytes 1572872 | tf_op jit(solution)/shard_map/ppermute | solution.py:39
  99.5 2.1 %collective-permute-start.28 = (bf16[1024,256]{1,0:T(8,128)(2,1)S(1)}, bf16[1024,256]{1,0:T(8,128)(2,1)}, u32[]{:S(2)}, u32[]{:S(2)}) collective-permute-start(bf16[1024,256]{1,0:T(8,128)(2,1)S(1)} %get-tuple-element.104), channel_id=1, source_target_pairs={{8,0},{12,4},{16,8},{20,12},{24,16},{28,20},{9,1},{13,5},{17,9},{2... | collective-permute-start | bytes 1572872 | tf_op jit(solution)/shard_map/ppermute | solution.py:39
  101.7 33.1 %attend_local.1 = (f32[12,160,256]{2,1,0:T(8,128)}, f32[12,8,256]{2,1,0:T(8,128)}) custom-call(s32[24]{0:T(128)} %reshape.109.ranges, bf16[3072,128]{1,0:T(8,128)(2,1)} %get-tuple-element.79.queries, s32[1,3072]{1,0:T(1,128)} %bitcast.71, s32[1,3072]{1,0:T(1,128)} %bitcast.73, bf16[3072,256]{1,0:T(8,128)(2,1)} %get-tuple-element.81.pairs), custom_call_target="tpu_custom_call" | custom-call | flops 6442450944 | bytes 5242880 | tf_op jit(solution)/shard_map/attend_local/pallas_call | solution.py:362
  135.9 9.3 %all-to-all-start.1 = ((bf16[32,24,1024]{2,1,0:T(8,128)(2,1)}), bf16[32,24,1024]{2,1,0:T(8,128)(2,1)S(1)}, u32[]{:S(2)}, u32[]{:S(2)}) async-start(bf16[32,24,1024]{2,1,0:T(8,128)(2,1)} %bitcast.63), calls=%async_computation.1 | async-start | bytes 3145728 | tf_op jit(solution)/shard_map/all_to_all | solution.py:610
  146.3 14.1 %attend_finish.1 = (bf16[384,128]{1,0:T(8,128)(2,1)}, bf16[384,128]{1,0:T(8,128)(2,1)}, bf16[384,128]{1,0:T(8,128)(2,1)}, bf16[384,128]{1,0:T(8,128)(2,1)}, bf16...) custom-call(s32[25]{0:T(128)} %pad_add_fusion.1.meta, ...), custom_call_target="tpu_custom_call" | custom-call | flops 1610612736 | bytes 5242880 | tf_op jit(solution)/shard_map/attend_finish/pallas_call | solution.py:396
  164.1 1.7 select_bitcast_fusion.1
  165.9 2.2 %collective-permute-start.34 = (bf16[384,128]{1,0:T(8,128)(2,1)S(1)}, bf16[384,128]{1,0:T(8,128)(2,1)S(1)}, u32[]{:S(2)}, u32[]{:S(2)}) collective-permute-start(bf16[384,128]{1,0:T(8,128)(2,1)S(1)} %copy-done.23), channel_id=1, source_target_pairs={{0,6},{1,7},{2,4},{3,5},{4,2},{5,3},{6,0},{7,1},{8,14},{9,15},{10,... | collective-permute-start | bytes 294920 | tf_op jit(solution)/shard_map/ppermute | solution.py:650
  168.0 3.4 %collective-permute-start.35 = (bf16[384,128]{1,0:T(8,128)(2,1)S(1)}, bf16[384,128]{1,0:T(8,128)(2,1)S(1)}, u32[]{:S(2)}, u32[]{:S(2)}) collective-permute-start(bf16[384,128]{1,0:T(8,128)(2,1)S(1)} %copy-done.22), channel_id=1, source_target_pairs={{0,7},{1,6},{2,5},{3,4},{4,3},{5,2},{6,1},{7,0},{8,15},{9,14},{10,... | collective-permute-start | bytes 294920 | tf_op jit(solution)/shard_map/ppermute | solution.py:650
  171.5 1.5 pad_maximum_fusion
  173.0 4.8 %collective-permute-done.33.refs_5_ = bf16[384,128]{1,0:T(8,128)(2,1)S(1)} collective-permute-done((bf16[384,128]{1,0:T(8,128)(2,1)}, bf16[384,128]{1,0:T(8,128)(2,1)S(1)}, u32[]{:S(2)}, u32[]{:S(2)}) %collective-permute-start.33) | collective-permute-done | bytes 98336 | tf_op jit(solution)/shard_map/ppermute | solution.py:650
  179.4 4.7 %output_projection.1 = bf16[384,1024]{1,0:T(8,128)(2,1)} custom-call(s32[1]{0:T(128)} %bitcast.meta, bf16[384,128]{1,0:T(8,128)(2,1)} %get-tuple-element.89.refs_0_, bf16[384,128]{1,0:T(8,128)(2,1)} %copy-done.13, bf16[384,128]{1,0:T(8,128)(2,1)} %copy-done.14, bf16[384,128]{1,0:T(8,128)(2,1)} %copy-done.15, bf16[384,128]{1,0:T(8,128)(2,1)} %copy-done.16, ...), custom_call_target="tpu_custom_call" | custom-call | flops 805306368 | bytes 4194304 | tf_op jit(solution)/shard_map/output_projection/pallas_call | solution.py:446
  184.1 2.5 %unpack.1 = bf16[8,24,8192]{2,1,0:T(8,128)(2,1)} custom-call(bf16[4,2,4,24,1024]{4,3,2,1,0:T(8,128)(2,1)S(1)} %bitcast.57, bf16[4,2,4,24,1024]{4,3,2,1,0:T(8,128)(2,1)S(1)} %bitcast.58), custom_call_target="tpu_custom_call" | custom-call | bytes 6291456 | tf_op jit(solution)/shard_map/unpack/pallas_call | solution.py:482
  (156 shorter events, 30.1 us)
Async XLA Ops:
  2.8 11.7 %collective-permute-start.4 = (bf16[128,128]{1,0:T(8,128)(2,1)S(1)}, bf16[128,128]{1,0:T(8,128)(2,1)S(1)}, u32[]{:S(2)}, u32[]{:S(2)}) collective-permute-start(bf16[128,128]{1,0:T(8,128)(2,1)S(1)} %get-tuple-element.113), channel_id=1, source_target_pairs={{0,5},{1,4},{2,7},{3,6},{4,1},{5,0},{6,3},{7,2},{8,13},{9,12},{10,... | collective-permute-start | bytes 98312 | tf_op jit(solution)/shard_map/ppermute | solution.py:546
  4.8 11.1 %collective-permute-start.3 = (bf16[128,128]{1,0:T(8,128)(2,1)S(1)}, bf16[128,128]{1,0:T(8,128)(2,1)S(1)}, u32[]{:S(2)}, u32[]{:S(2)}) collective-permute-start(bf16[128,128]{1,0:T(8,128)(2,1)S(1)} %get-tuple-element.114), channel_id=1, source_target_pairs={{0,4},{1,7},{2,6},{3,5},{4,0},{5,3},{6,2},{7,1},{8,12},{9,15},{10,... | collective-permute-start | bytes 98312 | tf_op jit(solution)/shard_map/ppermute | solution.py:546
  6.0 9.9 %collective-permute-start.2 = (bf16[128,128]{1,0:T(8,128)(2,1)S(1)}, bf16[128,128]{1,0:T(8,128)(2,1)S(1)}, u32[]{:S(2)}, u32[]{:S(2)}) collective-permute-start(bf16[128,128]{1,0:T(8,128)(2,1)S(1)} %get-tuple-element.117), channel_id=1, source_target_pairs={{0,2},{1,1},{2,0},{3,3},{4,6},{5,5},{6,4},{7,7},{8,10},{9,9},{10,8... | collective-permute-start | bytes 98312 | tf_op jit(solution)/shard_map/ppermute | solution.py:546
  6.7 9.2 %collective-permute-start.1 = (bf16[128,128]{1,0:T(8,128)(2,1)S(1)}, bf16[128,128]{1,0:T(8,128)(2,1)S(1)}, u32[]{:S(2)}, u32[]{:S(2)}) collective-permute-start(bf16[128,128]{1,0:T(8,128)(2,1)S(1)} %get-tuple-element.116), channel_id=1, source_target_pairs={{0,1},{1,0},{2,3},{3,2},{4,5},{5,4},{6,7},{7,6},{8,9},{9,8},{10,11... | collective-permute-start | bytes 98312 | tf_op jit(solution)/shard_map/ppermute | solution.py:546
  14.6 8.4 %collective-permute-start.12 = (bf16[128,256]{1,0:T(8,128)(2,1)}, bf16[128,256]{1,0:T(8,128)(2,1)S(1)}, u32[]{:S(2)}, u32[]{:S(2)}) collective-permute-start(bf16[128,256]{1,0:T(8,128)(2,1)} %param.9), channel_id=1, source_target_pairs={{0,8},{4,12},{8,0},{12,4},{16,24},{20,28},{24,16},{28,20},{1,9},{5... | collective-permute-start | bytes 196616 | tf_op jit(solution)/shard_map/ppermute | solution.py:33
  16.0 11.4 %collective-permute-start.6 = (bf16[192,1024]{1,0:T(8,128)(2,1)}, bf16[192,1024]{1,0:T(8,128)(2,1)}, u32[]{:S(2)}, u32[]{:S(2)}) collective-permute-start(bf16[192,1024]{1,0:T(8,128)(2,1)} %get-tuple-element.53.refs_0_), channel_id=1, source_target_pairs={{0,2},{1,3},{2,0},{3,1},{4,6},{5,7},{6,4},{7,5},{8,10},{9,11},{10,... | collective-permute-start | bytes 1179656 | tf_op jit(solution)/shard_map/ppermute | solution.py:33
  20.9 11.4 %collective-permute-start.8 = (bf16[192,1024]{1,0:T(8,128)(2,1)}, bf16[192,1024]{1,0:T(8,128)(2,1)S(1)}, u32[]{:S(2)}, u32[]{:S(2)}) collective-permute-start(bf16[192,1024]{1,0:T(8,128)(2,1)} %get-tuple-element.53.refs_0_), channel_id=1, source_target_pairs={{0,4},{4,0},{8,12},{12,8},{16,20},{20,16},{24,28},{28,24},{1,5},{5... | collective-permute-start | bytes 1179656 | tf_op jit(solution)/shard_map/ppermute | solution.py:33
  21.5 14.0 %collective-permute-start.7 = (bf16[208,1024]{1,0:T(8,128)(2,1)}, bf16[208,1024]{1,0:T(8,128)(2,1)S(1)}, u32[]{:S(2)}, u32[]{:S(2)}) collective-permute-start(bf16[208,1024]{1,0:T(8,128)(2,1)} %get-tuple-element.54.refs_1_), channel_id=1, source_target_pairs={{0,2},{1,3},{2,0},{3,1},{4,6},{5,7},{6,4},{7,5},{8,10},{9,11},{10,... | collective-permute-start | bytes 1277960 | tf_op jit(solution)/shard_map/ppermute | solution.py:33
  22.8 17.3 %collective-permute-start.9 = (bf16[208,1024]{1,0:T(8,128)(2,1)}, bf16[208,1024]{1,0:T(8,128)(2,1)S(1)}, u32[]{:S(2)}, u32[]{:S(2)}) collective-permute-start(bf16[208,1024]{1,0:T(8,128)(2,1)} %get-tuple-element.54.refs_1_), channel_id=1, source_target_pairs={{0,4},{4,0},{8,12},{12,8},{16,20},{20,16},{24,28},{28,24},{1,5},{5... | collective-permute-start | bytes 1277960 | tf_op jit(solution)/shard_map/ppermute | solution.py:33
  23.0 9.4 %collective-permute-start.10 = (bf16[192,1024]{1,0:T(8,128)(2,1)}, bf16[192,1024]{1,0:T(8,128)(2,1)S(1)}, u32[]{:S(2)}, u32[]{:S(2)}) collective-permute-start(bf16[192,1024]{1,0:T(8,128)(2,1)} %get-tuple-element.53.refs_0_), channel_id=1, source_target_pairs={{0,1},{1,0},{2,3},{3,2},{4,5},{5,4},{6,7},{7,6},{8,9},{9,8},{10,11... | collective-permute-start | bytes 1179656 | tf_op jit(solution)/shard_map/ppermute | solution.py:33
  27.4 12.7 %collective-permute-start.11 = (bf16[208,1024]{1,0:T(8,128)(2,1)}, bf16[208,1024]{1,0:T(8,128)(2,1)S(1)}, u32[]{:S(2)}, u32[]{:S(2)}) collective-permute-start(bf16[208,1024]{1,0:T(8,128)(2,1)} %get-tuple-element.54.refs_1_), channel_id=1, source_target_pairs={{0,1},{1,0},{2,3},{3,2},{4,5},{5,4},{6,7},{7,6},{8,9},{9,8},{10,11... | collective-permute-start | bytes 1277960 | tf_op jit(solution)/shard_map/ppermute | solution.py:33
  32.3 8.4 %collective-permute-start.20 = (bf16[256,384]{1,0:T(8,128)(2,1)S(1)}, bf16[256,384]{1,0:T(8,128)(2,1)S(1)}, u32[]{:S(2)}, u32[]{:S(2)}) collective-permute-start(bf16[256,384]{1,0:T(8,128)(2,1)S(1)} %maximum_maximum_fusion.refs_8_), channel_id=1, source_target_pairs={{0,16},{4,20},{8,24},{12,28},{16,0},{20,4},{24,8},{28,12},{1,17},{... | collective-permute-start | bytes 589832 | tf_op jit(solution)/shard_map/ppermute | solution.py:33
  40.1 14.2 %collective-permute-start.13 = (bf16[192,1024]{1,0:T(8,128)(2,1)}, bf16[192,1024]{1,0:T(8,128)(2,1)}, u32[]{:S(2)}, u32[]{:S(2)}) collective-permute-start(bf16[192,1024]{1,0:T(8,128)(2,1)} %collective-permute-done.6.refs_4_), channel_id=1, source_target_pairs={{0,1},{1,0},{2,3},{3,2},{4,5},{5,4},{6,7},{7,6},{8,9},{9,8},{10,11... | collective-permute-start | bytes 1179656 | tf_op jit(solution)/shard_map/ppermute | solution.py:33
  40.8 10.8 %collective-permute-start.21 = (bf16[256,384]{1,0:T(8,128)(2,1)S(1)}, bf16[256,384]{1,0:T(8,128)(2,1)S(1)}, u32[]{:S(2)}, u32[]{:S(2)}) collective-permute-start(bf16[256,384]{1,0:T(8,128)(2,1)S(1)} %collective-permute-done.20.refs_10_), channel_id=1, source_target_pairs={{0,8},{4,12},{8,0},{12,4},{16,24},{20,28},{24,16},{28,20},{1,9},{5... | collective-permute-start | bytes 589832 | tf_op jit(solution)/shard_map/ppermute | solution.py:33
  42.9 10.0 %collective-permute-start.22 = (bf16[256,256]{1,0:T(8,128)(2,1)S(1)}, bf16[256,256]{1,0:T(8,128)(2,1)S(1)}, u32[]{:S(2)}, u32[]{:S(2)}) collective-permute-start(bf16[256,256]{1,0:T(8,128)(2,1)S(1)} %bitcast.67), channel_id=1, source_target_pairs={{0,16},{4,20},{8,24},{12,28},{16,0},{20,4},{24,8},{28,12},{1,17},{... | collective-permute-start | bytes 393224 | tf_op jit(solution)/shard_map/ppermute | solution.py:33
  42.9 13.5 %collective-permute-start.17 = (bf16[192,1024]{1,0:T(8,128)(2,1)}, bf16[192,1024]{1,0:T(8,128)(2,1)}, u32[]{:S(2)}, u32[]{:S(2)}) collective-permute-start(bf16[192,1024]{1,0:T(8,128)(2,1)} %collective-permute-done.6.refs_4_), channel_id=1, source_target_pairs={{0,4},{4,0},{8,12},{12,8},{16,20},{20,16},{24,28},{28,24},{1,5},{5... | collective-permute-start | bytes 1179656 | tf_op jit(solution)/shard_map/ppermute | solution.py:33
  46.3 10.2 %collective-permute-start.16 = (bf16[208,1024]{1,0:T(8,128)(2,1)S(1)}, bf16[208,1024]{1,0:T(8,128)(2,1)S(1)}, u32[]{:S(2)}, u32[]{:S(2)}) collective-permute-start(bf16[208,1024]{1,0:T(8,128)(2,1)S(1)} %collective-permute-done.9.refs_1_), channel_id=1, source_target_pairs={{0,1},{1,0},{2,3},{3,2},{4,5},{5,4},{6,7},{7,6},{8,9},{9,8},{10,11... | collective-permute-start | bytes 1277960 | tf_op jit(solution)/shard_map/ppermute | solution.py:33
  51.6 10.0 %collective-permute-start.18 = (bf16[208,1024]{1,0:T(8,128)(2,1)S(1)}, bf16[208,1024]{1,0:T(8,128)(2,1)S(1)}, u32[]{:S(2)}, u32[]{:S(2)}) collective-permute-start(bf16[208,1024]{1,0:T(8,128)(2,1)S(1)} %collective-permute-done.9.refs_1_), channel_id=1, source_target_pairs={{0,2},{1,3},{2,0},{3,1},{4,6},{5,7},{6,4},{7,5},{8,10},{9,11},{10,... | collective-permute-start | bytes 1277960 | tf_op jit(solution)/shard_map/ppermute | solution.py:33
  61.5 15.6 %collective-permute-start.25 = (bf16[4,128,256]{2,1,0:T(8,128)(2,1)S(1)}, bf16[4,128,256]{2,1,0:T(8,128)(2,1)S(1)}, u32[]{:S(2)}, u32[]{:S(2)}) collective-permute-start(bf16[4,128,256]{2,1,0:T(8,128)(2,1)S(1)} %bitcast.65), channel_id=1, source_target_pairs={{0,4},{4,0},{8,12},{12,8},{16,20},{20,16},{24,28},{28,24},{1,5},{5... | collective-permute-start | bytes 786440 | tf_op jit(solution)/shard_map/ppermute | solution.py:33
  66.6 10.6 %collective-permute-start.23 = (bf16[192,1024]{1,0:T(8,128)(2,1)}, bf16[192,1024]{1,0:T(8,128)(2,1)}, u32[]{:S(2)}, u32[]{:S(2)}) collective-permute-start(bf16[192,1024]{1,0:T(8,128)(2,1)} %collective-permute-done.17.refs_4_), channel_id=1, source_target_pairs={{0,1},{1,0},{2,3},{3,2},{4,5},{5,4},{6,7},{7,6},{8,9},{9,8},{10,11... | collective-permute-start | bytes 1179656 | tf_op jit(solution)/shard_map/ppermute | solution.py:33
  68.8 8.4 %collective-permute-start.24 = (bf16[208,1024]{1,0:T(8,128)(2,1)S(1)}, bf16[208,1024]{1,0:T(8,128)(2,1)S(1)}, u32[]{:S(2)}, u32[]{:S(2)}) collective-permute-start(bf16[208,1024]{1,0:T(8,128)(2,1)S(1)} %collective-permute-done.18.refs_5_), channel_id=1, source_target_pairs={{0,1},{1,0},{2,3},{3,2},{4,5},{5,4},{6,7},{7,6},{8,9},{9,8},{10,11... | collective-permute-start | bytes 1277960 | tf_op jit(solution)/shard_map/ppermute | solution.py:33
  78.1 57.8 %all-to-all-start = ((bf16[32,24,1024]{2,1,0:T(8,128)(2,1)}), bf16[32,24,1024]{2,1,0:T(8,128)(2,1)S(1)}, u32[]{:S(2)}, u32[]{:S(2)}) async-start(bf16[32,24,1024]{2,1,0:T(8,128)(2,1)} %bitcast.64), calls=%async_computation | async-start | bytes 3145728 | tf_op jit(solution)/shard_map/all_to_all | solution.py:610
  85.7 49.0 %collective-permute-start.26 = (bf16[1,1024,256]{2,1,0:T(8,128)(2,1)S(1)}, bf16[1,1024,256]{2,1,0:T(8,128)(2,1)S(1)}, u32[]{:S(2)}, u32[]{:S(2)}) collective-permute-start(bf16[1,1024,256]{2,1,0:T(8,128)(2,1)S(1)} %bitcast.61), channel_id=1, source_target_pairs={{0,2},{1,3},{2,0},{3,1},{4,6},{5,7},{6,4},{7,5},{8,10},{9,11},{10,... | collective-permute-start | bytes 1572872 | tf_op jit(solution)/shard_map/ppermute | solution.py:33
  96.4 39.5 %collective-permute-start.27 = (bf16[1024,256]{1,0:T(8,128)(2,1)S(1)}, bf16[1024,256]{1,0:T(8,128)(2,1)}, u32[]{:S(2)}, u32[]{:S(2)}) collective-permute-start(bf16[1024,256]{1,0:T(8,128)(2,1)S(1)} %get-tuple-element.105), channel_id=1, source_target_pairs={{0,8},{4,12},{8,16},{12,20},{16,24},{20,28},{1,9},{5,13},{9,17},{1... | collective-permute-start | bytes 1572872 | tf_op jit(solution)/shard_map/ppermute | solution.py:39
  99.5 36.4 %collective-permute-start.28 = (bf16[1024,256]{1,0:T(8,128)(2,1)S(1)}, bf16[1024,256]{1,0:T(8,128)(2,1)}, u32[]{:S(2)}, u32[]{:S(2)}) collective-permute-start(bf16[1024,256]{1,0:T(8,128)(2,1)S(1)} %get-tuple-element.104), channel_id=1, source_target_pairs={{8,0},{12,4},{16,8},{20,12},{24,16},{28,20},{9,1},{13,5},{17,9},{2... | collective-permute-start | bytes 1572872 | tf_op jit(solution)/shard_map/ppermute | solution.py:39
  135.9 48.2 %all-to-all-start.1 = ((bf16[32,24,1024]{2,1,0:T(8,128)(2,1)}), bf16[32,24,1024]{2,1,0:T(8,128)(2,1)S(1)}, u32[]{:S(2)}, u32[]{:S(2)}) async-start(bf16[32,24,1024]{2,1,0:T(8,128)(2,1)} %bitcast.63), calls=%async_computation.1 | async-start | bytes 3145728 | tf_op jit(solution)/shard_map/all_to_all | solution.py:610
  145.2 18.6 %collective-permute-start.36 = (bf16[2,1024,256]{2,1,0:T(8,128)(2,1)}, bf16[2,1024,256]{2,1,0:T(8,128)(2,1)}, u32[]{:S(2)}, u32[]{:S(2)}) collective-permute-start(bf16[2,1024,256]{2,1,0:T(8,128)(2,1)} %maximum_bitcast_fusion), channel_id=1, source_target_pairs={{0,1},{1,0},{2,3},{3,2},{4,5},{5,4},{6,7},{7,6},{8,9},{9,8},{10,11... | collective-permute-start | bytes 3145736 | tf_op jit(solution)/shard_map/ppermute | solution.py:33
  161.8 11.2 %collective-permute-start.31 = (bf16[384,128]{1,0:T(8,128)(2,1)}, bf16[384,128]{1,0:T(8,128)(2,1)S(1)}, u32[]{:S(2)}, u32[]{:S(2)}) collective-permute-start(bf16[384,128]{1,0:T(8,128)(2,1)} %get-tuple-element.92), channel_id=1, source_target_pairs={{0,3},{1,2},{2,1},{3,0},{4,7},{5,6},{6,5},{7,4},{8,11},{9,10},{10,... | collective-permute-start | bytes 294920 | tf_op jit(solution)/shard_map/ppermute | solution.py:650
  162.6 10.4 %collective-permute-start.32 = (bf16[384,128]{1,0:T(8,128)(2,1)}, bf16[384,128]{1,0:T(8,128)(2,1)S(1)}, u32[]{:S(2)}, u32[]{:S(2)}) collective-permute-start(bf16[384,128]{1,0:T(8,128)(2,1)} %get-tuple-element.93), channel_id=1, source_target_pairs={{0,4},{1,5},{2,6},{3,7},{4,0},{5,1},{6,2},{7,3},{8,12},{9,13},{10,... | collective-permute-start | bytes 294920 | tf_op jit(solution)/shard_map/ppermute | solution.py:650
  163.8 14.0 %collective-permute-start.33 = (bf16[384,128]{1,0:T(8,128)(2,1)}, bf16[384,128]{1,0:T(8,128)(2,1)S(1)}, u32[]{:S(2)}, u32[]{:S(2)}) collective-permute-start(bf16[384,128]{1,0:T(8,128)(2,1)} %get-tuple-element.94), channel_id=1, source_target_pairs={{0,5},{1,4},{2,7},{3,6},{4,1},{5,0},{6,3},{7,2},{8,13},{9,12},{10,... | collective-permute-start | bytes 294920 | tf_op jit(solution)/shard_map/ppermute | solution.py:650
  165.9 12.0 %collective-permute-start.34 = (bf16[384,128]{1,0:T(8,128)(2,1)S(1)}, bf16[384,128]{1,0:T(8,128)(2,1)S(1)}, u32[]{:S(2)}, u32[]{:S(2)}) collective-permute-start(bf16[384,128]{1,0:T(8,128)(2,1)S(1)} %copy-done.23), channel_id=1, source_target_pairs={{0,6},{1,7},{2,4},{3,5},{4,2},{5,3},{6,0},{7,1},{8,14},{9,15},{10,... | collective-permute-start | bytes 294920 | tf_op jit(solution)/shard_map/ppermute | solution.py:650
  168.0 10.7 %collective-permute-start.35 = (bf16[384,128]{1,0:T(8,128)(2,1)S(1)}, bf16[384,128]{1,0:T(8,128)(2,1)S(1)}, u32[]{:S(2)}, u32[]{:S(2)}) collective-permute-start(bf16[384,128]{1,0:T(8,128)(2,1)S(1)} %copy-done.22), channel_id=1, source_target_pairs={{0,7},{1,6},{2,5},{3,4},{4,3},{5,2},{6,1},{7,0},{8,15},{9,14},{10,... | collective-permute-start | bytes 294920 | tf_op jit(solution)/shard_map/ppermute | solution.py:650
  (31 other events, 415.0 us)

commit v3 on v2

--- a/solution.py
+++ b/solution.py
@@ -39,8 +39,7 @@
     return lax.ppermute(value, axis, [(source, source + steps) for source in range(initial, last)])
 
 
-def doubled(value, axis, bit, low):
-    other = flipped(value, axis, bit)
+def merged(value, other, axis, bit, low):
     first = (lax.axis_index(axis) & bit) == 0
     pair = jnp.stack([jnp.where(first, value, other), jnp.where(first, other, value)], axis=low)
     return pair.reshape((-1,) + value.shape[1:])
@@ -240,192 +239,243 @@
     return jnp.concatenate(rows, axis=0)
 
 
-def sweep(begin, end, base, pairs, values_of, masked, starts, ends, total, peaks):
-    width = pairs.shape[1] // 2
-    held = pairs.shape[0] // TILE
-    begin = jnp.maximum(begin, base)
-    end = jnp.minimum(end, base + held)
-    last = jnp.minimum(ends, end * TILE)
+def sweep(jobs, peaks):
+    plans = []
+    steps = 0
+    for begin, end, base, pairs, values_of, masked, starts, ends, total in jobs:
+        held = pairs.shape[0] // TILE
+        begin, end = jnp.maximum(begin, base), jnp.minimum(end, base + held)
+        last = jnp.minimum(ends, end * TILE)
+        steps = jnp.maximum(steps, (end - begin + KEYS // TILE - 1) // (KEYS // TILE))
+        plans.append((begin, base, held, pairs, values_of, masked, starts, last, total))
 
     def one(number, peaks):
-        wanted = begin + number * (KEYS // TILE)
-        block = jnp.minimum(wanted, base + held - KEYS // TILE)
-        row = pl.multiple_of((block - base) * TILE, TILE)
-        keys = pairs[pl.ds(row, KEYS), :width]
-        values = values_of(row)
-        index = block * TILE + lax.broadcasted_iota(jnp.int32, (KEYS, TILE), 0)
-        allowed = (index >= jnp.maximum(starts, wanted * TILE)) & (index < last)
         new_peaks = []
-        for head, old_peak in enumerate(peaks):
-            scores = jnp.dot(keys, masked[head], preferred_element_type=jnp.float32)
-            scores = jnp.where(allowed, scores * SCALE, NEG_FILL)
-            peak = jnp.maximum(old_peak, jnp.max(scores, axis=0, keepdims=True))
-            fade = jnp.exp2(old_peak - peak)
-            weights = jnp.exp2(scores - peak).astype(jnp.bfloat16)
-            own = slice(head * HEAD_ROWS, (head + 1) * HEAD_ROWS)
-            total[own, :] = total[own, :] * fade + jnp.dot(
-                values[own, :], weights, preferred_element_type=jnp.float32
-            )
-            new_peaks.append(peak)
+        for plan, old_peaks in zip(plans, peaks):
+            begin, base, held, pairs, values_of, masked, starts, last, total = plan
+            wanted = begin + number * (KEYS // TILE)
+            block = jnp.minimum(wanted, base + held - KEYS // TILE)
+            row = pl.multiple_of((block - base) * TILE, TILE)
+            keys = pairs[pl.ds(row, KEYS), : pairs.shape[1] // 2]
+            values = values_of(row)
+            index = block * TILE + lax.broadcasted_iota(jnp.int32, (KEYS, TILE), 0)
+            allowed = (index >= jnp.maximum(starts, wanted * TILE)) & (index < last)
+            job_peaks = []
+            for head, old_peak in enumerate(old_peaks):
+                scores = jnp.dot(keys, masked[head], preferred_element_type=jnp.float32)
+                scores = jnp.where(allowed, scores * SCALE, NEG_FILL)
+                peak = jnp.maximum(old_peak, jnp.max(scores, axis=0, keepdims=True))
+                fade = jnp.exp2(old_peak - peak)
+                weights = jnp.exp2(scores - peak).astype(jnp.bfloat16)
+                own = slice(head * HEAD_ROWS, (head + 1) * HEAD_ROWS)
+                total[own, :] = total[own, :] * fade + jnp.dot(
+                    values[own, :], weights, preferred_element_type=jnp.float32
+                )
+                job_peaks.append(peak)
+            new_peaks.append(tuple(job_peaks))
         return tuple(new_peaks)
 
-    steps = jnp.maximum(end - begin + KEYS // TILE - 1, 0) // (KEYS // TILE)
     return lax.fori_loop(0, steps, one, peaks)
 
 
-def attend_kernel(ranges, queries, starts, ends, pairs, total, peak_out, masked, values):
+def fresh_peaks(heads):
+    return tuple(jnp.full((1, TILE), NEG_FILL, jnp.float32) for _ in range(heads))
+
+
+def edge_kernel(meta, *refs):
+    rows, pairs, outs, (masked, values) = refs[:6], refs[6], refs[7:11], refs[11:]
     step = pl.program_id(0)
-    width = queries.shape[1]
+    width = rows[0].shape[1]
     heads = width // HEAD_DIM
-    per_span = SPAN // TILE
+    edge = pl.num_programs(0)
+    tiles = pairs.shape[0] // TILE
 
     @pl.when(step == 0)
     def _():
-        for number in range(pairs.shape[0] // TILE):
-            rows = slice(number * TILE, (number + 1) * TILE)
-            values[:, rows] = with_ones(pairs[rows, width:])
-
-    mask_heads(queries, masked)
-    total[...] = jnp.zeros_like(total)
-    peaks = sweep(
-        ranges[2 * step],
-        ranges[2 * step + 1],
-        per_span,
-        pairs,
-        lambda row: values[:, pl.ds(row, KEYS)],
-        masked,
-        starts[...],
-        ends[...],
-        total.at[0],
-        tuple(jnp.full((1, TILE), NEG_FILL, jnp.float32) for _ in range(heads)),
-    )
-    for head in range(heads):
-        peak_out[0, head : head + 1, :] = peaks[head]
-
-
-def finish_kernel(meta, queries, starts, ends, before, after, total, peak_in, *refs):
-    outs = refs[:-3]
-    masked, sums, mixed = refs[-3:]
-    step = pl.program_id(0)
-    width = queries.shape[1]
-    heads = width // HEAD_DIM
-    per_span = SPAN // TILE
-    own_tiles = pl.num_programs(0)
-    sums[...] = total[0]
-    begin, end = meta[1 + 2 * step], meta[2 + 2 * step]
-
-    @pl.when((begin < per_span) | (end > per_span + own_tiles))
-    def _():
-        mask_heads(queries, masked)
-        peaks = tuple(peak_in[0, head : head + 1, :] for head in range(heads))
-        for chunk, base in ((before, 0), (after, per_span + own_tiles)):
-            peaks = sweep(
-                begin,
-                end,
-                base,
-                chunk,
-                lambda row: with_ones(chunk[pl.ds(row, KEYS), width:]),
-                masked,
+        for number in range(tiles):
+            own = slice(number * TILE, (number + 1) * TILE)
+            values[:, own] = with_ones(pairs[own, width:])
+
+    jobs = []
+    for side in range(2):
+        tile = step + side * (tiles - edge)
+        queries, starts, ends = rows[3 * side : 3 * side + 3]
+        mask_heads(queries, masked.at[side])
+        total = outs[side]
+        total[...] = jnp.zeros_like(total)
+        jobs.append(
+            (
+                meta[1 + 2 * tile],
+                meta[2 + 2 * tile],
+                edge,
+                pairs,
+                lambda row: values[:, pl.ds(row, KEYS)],
+                masked.at[side],
                 starts[...],
                 ends[...],
-                sums,
-                peaks,
+                total.at[0],
             )
-
-    parts = []
-    for head in range(heads):
-        row = head * HEAD_ROWS
-        parts.append(sums[row : row + HEAD_DIM, :] / sums[row + HEAD_DIM : row + HEAD_DIM + 1, :])
-    tile_rows = pl.ds(pl.multiple_of(step * TILE, TILE), TILE)
-    mixed[tile_rows, :] = jnp.concatenate(parts, axis=0).T.astype(jnp.bfloat16)
-
-    @pl.when(step == own_tiles - 1)
+        )
+    peaks = sweep(jobs, (fresh_peaks(heads), fresh_peaks(heads)))
+    for side in range(2):
+        for head in range(heads):
+            outs[2 + side][0, head : head + 1, :] = peaks[side][head]
+
+
+def finish_kernel(edge, meta, *refs):
+    rows, pairs, halos, held, held_peaks = refs[:6], refs[6], refs[7:9], refs[9:11], refs[11:13]
+    outs, (masked, sums, mixed) = refs[13:-3], refs[-3:]
+    step = pl.program_id(0)
+    width = rows[0].shape[1]
+    heads = width // HEAD_DIM
+    tiles = pairs.shape[0] // TILE
+    places = tile_places(step, edge, tiles)
+
+    def jobs_on(keys, bases):
+        jobs = []
+        for side in range(2):
+            queries, starts, ends = rows[3 * side : 3 * side + 3]
+            mask_heads(queries, masked.at[side])
+            jobs.append(
+                (
+                    meta[1 + 2 * places[side]],
+                    meta[2 + 2 * places[side]],
+                    bases[side],
+                    keys[side],
+                    lambda row, held=keys[side]: with_ones(held[pl.ds(row, KEYS), width:]),
+                    masked.at[side],
+                    starts[...],
+                    ends[...],
+                    sums.at[side],
+                )
+            )
+        return jobs
+
+    @pl.when(step < edge)
     def _():
-        rows = outs[0].shape[0]
+        for side in range(2):
+            sums[side] = held[side][0]
+
+    reaches_back = meta[1 + 2 * places[0]] < edge
+    reaches_ahead = meta[2 + 2 * places[1]] > edge + tiles
+
+    @pl.when((step < edge) & (reaches_back | reaches_ahead))
+    def _():
+        peaks = tuple(
+            tuple(held_peaks[side][0, head : head + 1, :] for head in range(heads))
+            for side in range(2)
+        )
+        sweep(jobs_on(halos, (0, edge + tiles)), peaks)
+
+    @pl.when(step >= edge)
+    def _():
+        sums[...] = jnp.zeros_like(sums)
+        sweep(jobs_on((pairs, pairs), (edge, edge)), (fresh_peaks(heads), fresh_peaks(heads)))
+
+    for side in range(2):
+        parts = []
+        for head in range(heads):
+            row = head * HEAD_ROWS
+            parts.append(
+                sums[side, row : row + HEAD_DIM, :]
+                / sums[side, row + HEAD_DIM : row + HEAD_DIM + 1, :]
+            )
+        tile_rows = pl.ds(pl.multiple_of(places[side] * TILE, TILE), TILE)
+        mixed[tile_rows, :] = jnp.concatenate(parts, axis=0).T.astype(jnp.bfloat16)
+
+    @pl.when(step == pl.num_programs(0) - 1)
+    def _():
+        count = outs[0].shape[0]
         for distance, out in enumerate(outs):
-            out[...] = mixed[pl.ds(pl.multiple_of((meta[0] ^ distance) * rows, 128), rows), :]
-
-
-def attend_specs(width, held):
-    spec = lambda shape, index: pl.BlockSpec(shape, lambda i, m: index(i))
-    return [
-        spec((TILE, width), lambda i: (i, 0)),
-        spec((1, TILE), lambda i: (0, i)),
-        spec((1, TILE), lambda i: (0, i)),
-    ] + [spec((rows, 2 * width), lambda i: (0, 0)) for rows in held]
-
-
-def attend_local(ranges, queries, starts, ends, pairs):
+            out[...] = mixed[pl.ds(pl.multiple_of((meta[0] ^ distance) * count, 128), count), :]
+
+
+def tile_places(step, edge, tiles):
+    middle = edge + 2 * (step - edge)
+    return (
+        jnp.where(step < edge, step, middle),
+        jnp.where(step < edge, tiles - edge + step, middle + 1),
+    )
+
+
+def attend_specs(width, edge, tiles):
+    specs = []
+    for side in range(2):
+        place = lambda i, side=side: tile_places(i, edge, tiles)[side]
+        specs.append(pl.BlockSpec((TILE, width), lambda i, m, place=place: (place(i), 0)))
+        specs += [pl.BlockSpec((1, TILE), lambda i, m, place=place: (0, place(i)))] * 2
+    return specs + [pl.BlockSpec((tiles * TILE, 2 * width), lambda i, m: (0, 0))]
+
+
+def attend_edges(meta, queries, starts, ends, pairs):
     group_rows, width = queries.shape
     heads = width // HEAD_DIM
-    tiles = group_rows // TILE
+    tiles, edge = group_rows // TILE, SPAN // TILE
+    shapes = [(edge, heads * HEAD_ROWS, TILE)] * 2 + [(edge, 8, TILE)] * 2
     return pl.pallas_call(
-        attend_kernel,
+        edge_kernel,
         grid_spec=pltpu.PrefetchScalarGridSpec(
             num_scalar_prefetch=1,
-            grid=(tiles,),
-            in_specs=attend_specs(width, (group_rows,)),
-            out_specs=[
-                pl.BlockSpec((1, heads * HEAD_ROWS, TILE), lambda i, m: (i, 0, 0)),
-                pl.BlockSpec((1, 8, TILE), lambda i, m: (i, 0, 0)),
-            ],
+            grid=(edge,),
+            in_specs=attend_specs(width, edge, tiles),
+            out_specs=[pl.BlockSpec((1,) + shape[1:], lambda i, m: (i, 0, 0)) for shape in shapes],
             scratch_shapes=[
-                pltpu.VMEM((heads, width, TILE), jnp.bfloat16),
+                pltpu.VMEM((2, heads, width, TILE), jnp.bfloat16),
                 pltpu.VMEM((heads * HEAD_ROWS, group_rows), jnp.bfloat16),
             ],
         ),
-        out_shape=[
-            jax.ShapeDtypeStruct((tiles, heads * HEAD_ROWS, TILE), jnp.float32),
-            jax.ShapeDtypeStruct((tiles, 8, TILE), jnp.float32),
-        ],
+        out_shape=[jax.ShapeDtypeStruct(shape, jnp.float32) for shape in shapes],
         compiler_params=PARAMS,
         cost_estimate=pl.CostEstimate(
             flops=16 * group_rows * 1024 * width,
             bytes_accessed=5 << 20,
             transcendentals=group_rows * 1024 * heads,
         ),
-        name="attend_local",
-    )(ranges, queries, starts, ends, pairs)
-
-
-def attend_finish(meta, queries, starts, ends, before, after, total, peaks, rows):
+        name="attend_edges",
+    )(meta, queries, starts, ends, queries, starts, ends, pairs)
+
+
+def attend_finish(meta, queries, starts, ends, pairs, before, after, held, rows):
     group_rows, width = queries.shape
     heads = width // HEAD_DIM
-    tiles = group_rows // TILE
+    tiles, edge = group_rows // TILE, SPAN // TILE
     members = group_rows // rows
     return pl.pallas_call(
-        finish_kernel,
+        functools.partial(finish_kernel, edge),
         grid_spec=pltpu.PrefetchScalarGridSpec(
             num_scalar_prefetch=1,
-            grid=(tiles,),
-            in_specs=attend_specs(width, (SPAN, SPAN))
+            grid=(edge + (tiles - 2 * edge) // 2,),
+            in_specs=attend_specs(width, edge, tiles)
+            + [pl.BlockSpec((SPAN, 2 * width), lambda i, m: (0, 0))] * 2
             + [
-                pl.BlockSpec((1,) + total.shape[1:], lambda i, m: (i, 0, 0)),
-                pl.BlockSpec((1,) + peaks.shape[1:], lambda i, m: (i, 0, 0)),
+                pl.BlockSpec((1,) + part.shape[1:], lambda i, m: (jnp.minimum(i, edge - 1), 0, 0))
+                for part in held
             ],
             out_specs=[pl.BlockSpec((rows, width), lambda i, m: (0, 0))] * members,
             scratch_shapes=[
-                pltpu.VMEM((heads, width, TILE), jnp.bfloat16),
-                pltpu.VMEM(total.shape[1:], jnp.float32),
+                pltpu.VMEM((2, heads, width, TILE), jnp.bfloat16),
+                pltpu.VMEM((2, heads * HEAD_ROWS, TILE), jnp.float32),
                 pltpu.VMEM((group_rows, width), jnp.bfloat16),
             ],
         ),
         out_shape=[jax.ShapeDtypeStruct((rows, width), jnp.bfloat16)] * members,
         compiler_params=PARAMS,
         cost_estimate=pl.CostEstimate(
-            flops=4 * group_rows * 1024 * width,
+            flops=16 * group_rows * 1024 * width,
             bytes_accessed=5 << 20,
-            transcendentals=group_rows * 256 * heads,
+            transcendentals=group_rows * 1024 * heads,
         ),
         name="attend_finish",
-    )(meta, queries, starts, ends, before, after, total, peaks)
+    )(meta, queries, starts, ends, queries, starts, ends, pairs, before, after, *held)
 
 
 def output_kernel(members, meta, *refs):
-    parts, weight, result, mixed = refs[:members], refs[members], refs[-2], refs[-1]
+    parts, result, mixed = refs[:members], refs[-2], refs[-1]
+    weights = refs[members:-2]
+    step = pl.program_id(0)
     width = parts[0].shape[1]
 
-    @pl.when(pl.program_id(0) == 0)
+    @pl.when(step == 0)
     def _():
         for distance in range(members):
             source = meta[0] ^ distance
@@ -433,24 +483,27 @@
             columns = pl.ds(pl.multiple_of(head_pair * width, width), width)
             mixed[:, columns] = parts[distance][...]
 
-    result[...] = jnp.dot(
-        mixed[...], weight[...], preferred_element_type=jnp.float32
-    ).astype(jnp.bfloat16)
-
-
-def output_projection(meta, parts, weight):
+    for distance, weight in enumerate(weights):
+
+        @pl.when(step == distance)
+        def _():
+            result[...] = jnp.dot(
+                mixed[...], weight[...], preferred_element_type=jnp.float32
+            ).astype(jnp.bfloat16)
+
+
+def output_projection(meta, parts, weights):
     rows, width = parts[0].shape
-    depth = width * len(parts)
-    tile = weight.shape[1]
-    steps = weight.shape[0] // depth
+    depth, tile = weights[0].shape
+    steps = len(weights)
     return pl.pallas_call(
         functools.partial(output_kernel, len(parts)),
         grid_spec=pltpu.PrefetchScalarGridSpec(
             num_scalar_prefetch=1,
             grid=(steps,),
             in_specs=[pl.BlockSpec((rows, width), lambda i, m: (0, 0))] * len(parts)
-            + [pl.BlockSpec((depth, tile), lambda i, m: (i, 0))],
-            out_specs=pl.BlockSpec((rows, tile), lambda i, m: (0, i)),
+            + [pl.BlockSpec((depth, tile), lambda i, m: (0, 0))] * steps,
+            out_specs=pl.BlockSpec((rows, tile), lambda i, m: (0, (m[0] % steps) ^ i)),
             scratch_shapes=[pltpu.VMEM((rows, depth), jnp.bfloat16)],
         ),
         out_shape=jax.ShapeDtypeStruct((rows, steps * tile), jnp.bfloat16),
@@ -459,7 +512,7 @@
             flops=2 * rows * depth * steps * tile, bytes_accessed=4 << 20, transcendentals=0
         ),
         name="output_projection",
-    )(meta, *parts, weight)
+    )(meta, *parts, *weights)
 
 
 def unpack_kernel(own_row, other_row, pages):
@@ -554,37 +607,16 @@
     planes = {0: plane}
     bit = peers // 2
     while bit > 1:
-        for distance in list(planes):
-            planes[distance ^ bit] = flipped(planes[distance], "tok", bit)
+        planes[bit] = flipped(plane, "tok", bit)
         bit //= 2
     last_weight = output_weight
     bit = PAIR
     while 2 * bit < peers:
-        last_weight = doubled(last_weight, "tok", bit, 0)
+        last_weight = merged(last_weight, flipped(last_weight, "tok", bit), "tok", bit, 0)
         bit *= 2
-    across, along, sibling, last_weight = lax.optimization_barrier(
-        (across, along, sibling, last_weight)
-    )
-    corner = [flipped(across[0], "tok", 1), flipped(along[1], "grp", 2)]
-    across_sibling = [flipped(block, "grp", 1) for block in across]
-    along_sibling = [flipped(block, "grp", 1) for block in along]
-    if bit < peers:
-        last_weight = doubled(last_weight, "tok", bit, 0)
-    last_weight = last_weight.reshape((peers // PAIR,) + output_weight.shape)
-    weights = [planes[distance] for distance in range(0, peers, 2)]
-    across_sibling, along_sibling, corner, weights, last_weight = lax.optimization_barrier(
-        (across_sibling, along_sibling, corner, weights, last_weight)
-    )
-    corner_sibling = [flipped(block, "grp", 1) for block in corner]
-    last_weight = doubled(last_weight, "tok", 1, 1).reshape(model_width, output_weight.shape[1])
-    near_blocks = [top, bottom] + sibling + across + across_sibling
-    far_blocks = along + along_sibling + corner
-    half, held = rows // 2, rows + EXTRA_ROWS
-    layout = [
-        [(2 * number, 0, half), (2 * number + 1, half, held - half)] for number in range(4)
-    ]
 
     first_row = place // PAIR * group_rows
+    segment_ids, last_weight = lax.optimization_barrier((segment_ids, last_weight))
     padded_ids = jnp.concatenate(
         [
             jnp.full((SPAN,), -1, jnp.int32),
@@ -599,11 +631,40 @@
     ranges = jnp.stack(
         [starts[::TILE] // TILE, (ends[TILE - 1 :: TILE] + TILE - 1) // TILE], axis=1
     ).reshape(-1)
-
-    order = [
-        (number * members + column) % PARTS for number in range(PARTS)
+    own_member = member[None].astype(jnp.int32)
+    tile_meta = jnp.concatenate([own_member, ranges])
+    order = [(number * members + column) % PARTS for number in range(PARTS)]
+    meta = jnp.stack([member, place] + order).astype(jnp.int32)
+    bounds = (starts[None, :], ends[None, :])
+
+    across, along, sibling, planes, last_weight, cosine, sine, tile_meta, meta, bounds = (
+        lax.optimization_barrier(
+            (across, along, sibling, planes, last_weight, cosine, sine, tile_meta, meta, bounds)
+        )
+    )
+    corner = [flipped(across[0], "tok", 1), flipped(along[1], "grp", 2)]
+    across_sibling = [flipped(block, "grp", 1) for block in across]
+    along_sibling = [flipped(block, "grp", 1) for block in along]
+    for distance in range(PAIR, peers, PAIR):
+        if distance not in planes:
+            step_bit = distance & -distance
+            planes[distance] = flipped(planes[distance ^ step_bit], "tok", step_bit)
+    if bit < peers:
+        last_weight = merged(last_weight, flipped(last_weight, "tok", bit), "tok", bit, 0)
+    last_weight = last_weight.reshape((peers // PAIR,) + output_weight.shape)
+    weights = [planes[distance] for distance in range(0, peers, PAIR)]
+    across_sibling, along_sibling, corner, weights, last_weight = lax.optimization_barrier(
+        (across_sibling, along_sibling, corner, weights, last_weight)
+    )
+    corner_sibling = [flipped(block, "grp", 1) for block in corner]
+    other_weight = flipped(last_weight, "tok", 1)
+    near_blocks = [top, bottom] + sibling + across + across_sibling
+    far_blocks = along + along_sibling + corner
+    half, held = rows // 2, rows + EXTRA_ROWS
+    layout = [
+        [(2 * number, 0, half), (2 * number + 1, half, held - half)] for number in range(4)
     ]
-    meta = jnp.stack([member, place] + order).astype(jnp.int32)
+
     sizes = (weights, cosine, sine, rows, blocks, peers, capacity)
 
     def to_owners(send):
@@ -617,8 +678,8 @@
         return received.reshape((peers // PAIR, PAIR, members) + send.shape[2:])
 
     queries, pairs, send = project(meta, 0, layout, near_blocks, *sizes, ())
-    send, corner_sibling, last_weight = lax.optimization_barrier(
-        (send, corner_sibling, last_weight)
+    send, corner_sibling, other_weight = lax.optimization_barrier(
+        (send, corner_sibling, other_weight)
     )
     own_row = to_owners(send)
     queries, pairs, send = project(
@@ -626,26 +687,17 @@
     )
     before = shifted(pairs[group_rows - SPAN :], "tok", PAIR)
     after = shifted(pairs[:SPAN], "tok", -PAIR)
-    last_weight = doubled(last_weight[None], "grp", 2, 0)
-
-    bounds = (starts[None, :], ends[None, :])
-    total, peaks = attend_local(ranges, queries, *bounds, pairs)
-    last_weight, before, after, total, peaks, send = lax.optimization_barrier(
-        (last_weight, before, after, total, peaks, send)
+    columns = merged(last_weight, other_weight, "tok", 1, 1).reshape(model_width, -1)
+    columns_across = flipped(columns, "grp", 2)
+
+    edges = attend_edges(tile_meta, queries, *bounds, pairs)
+    columns_across, before, after, edges, send = lax.optimization_barrier(
+        (columns_across, before, after, edges, send)
     )
     other_row = to_owners(send)
-    last_weight = doubled(last_weight, "grp", 1, 1).reshape(members * model_width, -1)
-    own_member = member[None].astype(jnp.int32)
-    mixed = attend_finish(
-        jnp.concatenate([own_member, ranges]),
-        queries,
-        *bounds,
-        before,
-        after,
-        total,
-        peaks,
-        rows,
-    )
+    last_weights = [columns, flipped(columns, "grp", 1)]
+    last_weights += [columns_across, flipped(columns_across, "grp", 1)]
+    mixed = attend_finish(tile_meta, queries, *bounds, pairs, before, after, edges, rows)
     parts = [mixed[0]] + [
         lax.ppermute(
             mixed[distance],
@@ -654,7 +706,7 @@
         )
         for distance in range(1, blocks)
     ]
-    attended = output_projection(own_member, parts, last_weight)
+    attended = output_projection(own_member, parts, last_weights)
 
     cache_pages = unpack(own_row, other_row).reshape(
         peers * capacity, 2 * PAGE * model_width

time: 186 us -> 183 us (0.984); the launches traced: 187 us -> 180 us
  waiting for transfers between devices: 31.6 us -> 42 us
  starting transfers between devices: 60.7 us -> 52 us
  other arithmetic: 14 us -> 9.65 us
  Pallas kernels: 73.2 us -> 70.1 us
    ppermute x2, waiting for transfers between devices: 0.01 us -> 6 us  [shifted(): lax.ppermute(value, axis, [(source, source + steps) for source in range(i...]
    ppermute x7, waiting for transfers between devices: 5.75 us -> 10.9 us  [per_device(): lax.ppermute(mixed[distance], ('tok', 'grp'), [(source, source ^ distance...]
    another operation x9 -> x6, other arithmetic: 4.34 us -> 1.01 us  [merged(): jnp.stack([jnp.where(first, value, other), jnp.where(first, other, value)...]
    pallas_call x2, Pallas kernels: 47.2 us -> 44 us  [the longest x1 24 us: attend_edges(): pl.pallas_call(edge_kernel, grid_spec=pltpu.PrefetchScalarGridSpec(num_sc...]
    all_to_all x2, starting transfers between devices: 14.8 us -> 11.7 us  [to_owners(): lax.all_to_all(send.reshape((flat,) + send.shape[2:]), ('tok', 'grp'), sp...]
    ppermute x7, starting transfers between devices: 9.3 us -> 6.31 us  [per_device(): lax.ppermute(mixed[distance], ('tok', 'grp'), [(source, source ^ distance...]
    ppermute x6, starting transfers between devices: 9.34 us -> 7.47 us  [per_device(): pieces.append(lax.ppermute(piece, ('tok', 'grp'), route))]
    ppermute x22 -> x23, starting transfers between devices: 22 us -> 20.5 us  [flipped(): lax.ppermute(value, axis, [(source, source ^ bit) for source in range(cou...]
  transfers between devices with their start and end apart: 39 -> 40, of which waited for: 10 -> 9; matrix products, arithmetic and copies ran while one was open for 9% -> 7% of each run, Pallas kernels for 38% -> 38%
where the time goes in v3:
time: 183 us; the launch traced here: 180 us
  Pallas kernels  70.1 us (38%)
  starting transfers between devices  52 us (28%)
  waiting for transfers between devices  42 us (23%)
  other arithmetic  9.65 us (5%)
  local copies, waits for them, and re-layouts  4.7 us (3%)
    ppermute x23, waiting for transfers between devices, flipped(): lax.ppermute(value, axis, [(source, source ^ bit) for source in range(cou...  25.1 us
    pallas_call x1, Pallas kernels, attend_edges(): pl.pallas_call(edge_kernel, grid_spec=pltpu.PrefetchScalarGridSpec(num_sc...  24 us
    ppermute x23, starting transfers between devices, flipped(): lax.ppermute(value, axis, [(source, source ^ bit) for source in range(cou...  20.5 us
    pallas_call x1, Pallas kernels, attend_finish(): pl.pallas_call(functools.partial(finish_kernel, edge), grid_spec=pltpu.Pr...  19.9 us
    pallas_call x2, Pallas kernels, project(): pl.pallas_call(functools.partial(project_kernel, first, layout, len(weigh...  16.4 us
    all_to_all x2, starting transfers between devices, to_owners(): lax.all_to_all(send.reshape((flat,) + send.shape[2:]), ('tok', 'grp'), sp...  11.7 us
    ppermute x7, waiting for transfers between devices, per_device(): lax.ppermute(mixed[distance], ('tok', 'grp'), [(source, source ^ distance...  10.9 us
    ppermute x6, starting transfers between devices, per_device(): pieces.append(lax.ppermute(piece, ('tok', 'grp'), route))  7.47 us
  transfers between devices with their start and end apart: 40, of which 9 were waited for; matrix products, arithmetic and copies ran while one was open for 7% of the time, Pallas kernels for 38%

profile of v3, /device:TPU:17, one launch (start us, length us, event | category | flops | bytes accessed | tf_op | source)
XLA Modules:
  0.0 179.7 jit_solution(8438763378695529548)
XLA Ops:
  1.5 3.1 %collective-permute-start = (bf16[128,128]{1,0:T(8,128)(2,1)S(1)}, bf16[128,128]{1,0:T(8,128)(2,1)S(1)}, u32[]{:S(2)}, u32[]{:S(2)}) collective-permute-start(bf16[128,128]{1,0:T(8,128)(2,1)S(1)} %get-tuple-element.138), channel_id=1, source_target_pairs={{0,0},{1,3},{2,2},{3,1},{4,4},{5,7},{6,6},{7,5},{8,8},{9,11},{10,1... | collective-permute-start | bytes 98312 | tf_op jit(solution)/shard_map/ppermute | solution.py:599
  4.7 1.3 collective-permute-start.3
  6.4 1.9 %collective-permute-start.1 = (bf16[128,128]{1,0:T(8,128)(2,1)S(1)}, bf16[128,128]{1,0:T(8,128)(2,1)S(1)}, u32[]{:S(2)}, u32[]{:S(2)}) collective-permute-start(bf16[128,128]{1,0:T(8,128)(2,1)S(1)} %get-tuple-element.142), channel_id=1, source_target_pairs={{0,1},{1,0},{2,3},{3,2},{4,5},{5,4},{6,7},{7,6},{8,9},{9,8},{10,11... | collective-permute-start | bytes 98312 | tf_op jit(solution)/shard_map/ppermute | solution.py:599
  9.1 2.5 %layer_norm.1 = (bf16[192,1024]{1,0:T(8,128)(2,1)}, bf16[208,1024]{1,0:T(8,128)(2,1)}) custom-call(bf16[384,1024]{1,0:T(8,128)(2,1)} %tokens.1, f32[1,1024]{1,0:T(1,128)} %bitcast.61, s32[1,96]{1,0:T(1,128)} %bitcast.62), custom_call_target="tpu_custom_call" | custom-call | tf_op jit(solution)/shard_map/layer_norm/pallas_call | solution.py:75
  12.2 1.3 collective-permute-start.14
  13.9 3.6 %collective-permute-start.10 = (bf16[192,1024]{1,0:T(8,128)(2,1)}, bf16[192,1024]{1,0:T(8,128)(2,1)S(1)}, u32[]{:S(2)}, u32[]{:S(2)}) collective-permute-start(bf16[192,1024]{1,0:T(8,128)(2,1)} %get-tuple-element.68.refs_0_), channel_id=1, source_target_pairs={{0,1},{1,0},{2,3},{3,2},{4,5},{5,4},{6,7},{7,6},{8,9},{9,8},{10,11... | collective-permute-start | bytes 1179656 | tf_op jit(solution)/shard_map/ppermute | solution.py:33
  19.8 3.9 %convert_reduce_fusion = (s32[8,384]{1,0:T(8,128)S(1)}, s32[8,384]{1,0:T(8,128)S(1)}) fusion(s32[8,1408]{1,0:T(8,128)S(1)} %stack.127, s32[8,384]{1,0:T(8,128)S(1)} %lt.39, s32[8,1408]{1,0:T(8,128)S(1)} %stack.117), kind=kLoop, calls=%fused_computation | loop fusion | flops 25946112 | bytes 126976 | tf_op jit(solution)/shard_map/reduce_sum | solution.py:566
  23.9 2.3 %multiply_sine_fusion = (f32[32,3072]{1,0:T(8,128)}, f32[32,3072]{1,0:T(8,128)}) fusion(f32[3072]{0:T(1024)S(1)} %subtract_convert_fusion, f32[32]{0:T(128)S(1)} %negate_power_fusion), kind=kLoop, calls=%fused_computation.2 | loop fusion | flops 98304 | bytes 798848 | tf_op jit(solution)/shard_map/sin | solution.py:553
  27.6 3.2 %collective-permute-start.11 = (bf16[208,1024]{1,0:T(8,128)(2,1)}, bf16[208,1024]{1,0:T(8,128)(2,1)S(1)}, u32[]{:S(2)}, u32[]{:S(2)}) collective-permute-start(bf16[208,1024]{1,0:T(8,128)(2,1)} %get-tuple-element.69.refs_1_), channel_id=1, source_target_pairs={{0,1},{1,0},{2,3},{3,2},{4,5},{5,4},{6,7},{7,6},{8,9},{9,8},{10,11... | collective-permute-start | bytes 1277960 | tf_op jit(solution)/shard_map/ppermute | solution.py:33
  31.1 1.7 collective-permute-start.7
  33.7 8.8 %collective-permute-done.9.refs_1_ = bf16[208,1024]{1,0:T(8,128)(2,1)S(1)} collective-permute-done((bf16[208,1024]{1,0:T(8,128)(2,1)}, bf16[208,1024]{1,0:T(8,128)(2,1)S(1)}, u32[]{:S(2)}, u32[]{:S(2)}) %collective-permute-start.9) | collective-permute-done | bytes 426016 | tf_op jit(solution)/shard_map/ppermute | solution.py:33
  44.0 2.2 %collective-permute-start.21 = (bf16[256,384]{1,0:T(8,128)(2,1)S(1)}, bf16[256,384]{1,0:T(8,128)(2,1)S(1)}, u32[]{:S(2)}, u32[]{:S(2)}) collective-permute-start(bf16[256,384]{1,0:T(8,128)(2,1)S(1)} %collective-permute-done.13.refs_10_), channel_id=1, source_target_pairs={{0,8},{4,12},{8,0},{12,4},{16,24},{20,28},{24,16},{28,20},{1,9},{5... | collective-permute-start | bytes 589832 | tf_op jit(solution)/shard_map/ppermute | solution.py:33
  46.6 1.4 collective-permute-start.20
  48.0 5.7 %collective-permute-done.22 = bf16[256,256]{1,0:T(8,128)(2,1)S(1)} collective-permute-done((bf16[256,256]{1,0:T(8,128)(2,1)S(1)}, bf16[256,256]{1,0:T(8,128)(2,1)S(1)}, u32[]{:S(2)}, u32[]{:S(2)}) %collective-permute-start.22) | collective-permute-done | bytes 131104 | tf_op jit(solution)/shard_map/ppermute | solution.py:33
  55.7 9.9 %collective-permute-done.19.refs_4_ = bf16[192,1024]{1,0:T(8,128)(2,1)} collective-permute-done((bf16[192,1024]{1,0:T(8,128)(2,1)}, bf16[192,1024]{1,0:T(8,128)(2,1)}, u32[]{:S(2)}, u32[]{:S(2)}) %collective-permute-start.19) | collective-permute-done | bytes 393248 | tf_op jit(solution)/shard_map/ppermute | solution.py:33
  66.9 8.2 %project.2 = (bf16[3072,128]{1,0:T(8,128)(2,1)}, bf16[3072,256]{1,0:T(8,128)(2,1)}, bf16[8,4,24,1024]{3,2,1,0:T(8,128)(2,1)}) custom-call(s32[5]{0:T(128)} %stack.134.meta, bf16[192,1024]{1,0:T(8,128)(2,1)} %get-tuple-element.68.refs_0_, bf16[208,1024]{1,0:T(8,128)(2,1)} %get-tuple-element.69.refs_1_, bf16[192,1024]{1,0:T(8,128)(2,1)} %copy-done.15, ...), custom_call_target="tpu_custom_call" | custom-call | flops 1207959552 | bytes 6291456 | tf_op jit(solution)/shard_map/project/pallas_call | solution.py:185
  76.1 6.6 %all-to-all-start = ((bf16[32,24,1024]{2,1,0:T(8,128)(2,1)}), bf16[32,24,1024]{2,1,0:T(8,128)(2,1)S(1)}, u32[]{:S(2)}, u32[]{:S(2)}) async-start(bf16[32,24,1024]{2,1,0:T(8,128)(2,1)} %bitcast.46), calls=%async_computation | async-start | bytes 3145728 | tf_op jit(solution)/shard_map/all_to_all | solution.py:671
  84.1 8.2 %project.3 = (bf16[3072,128]{1,0:T(8,128)(2,1)}, bf16[3072,256]{1,0:T(8,128)(2,1)}, bf16[8,4,24,1024]{3,2,1,0:T(8,128)(2,1)}) custom-call(s32[5]{0:T(128)} %stack.134.meta, bf16[192,1024]{1,0:T(8,128)(2,1)} %copy-done.12, bf16[208,1024]{1,0:T(8,128)(2,1)} %copy-done.7, bf16[192,1024]{1,0:T(8,128)(2,1)} %copy-done.13, ...), custom_call_target="tpu_custom_call", output_to_operand_aliasing={{0}: (15, {}), {1}: (16, {})} | custom-call | flops 1207959552 | bytes 6291456 | tf_op jit(solution)/shard_map/project/pallas_call | solution.py:185
  92.3 1.3 fusion.4
  93.6 2.2 %collective-permute-start.28 = (bf16[1024,256]{1,0:T(8,128)(2,1)S(1)}, bf16[1024,256]{1,0:T(8,128)(2,1)}, u32[]{:S(2)}, u32[]{:S(2)}) collective-permute-start(bf16[1024,256]{1,0:T(8,128)(2,1)S(1)} %get-tuple-element.132), channel_id=1, source_target_pairs={{8,0},{12,4},{16,8},{20,12},{24,16},{28,20},{9,1},{13,5},{17,9},{2... | collective-permute-start | bytes 1572872 | tf_op jit(solution)/shard_map/ppermute | solution.py:39
  95.8 3.9 %collective-permute-start.27 = (bf16[1024,256]{1,0:T(8,128)(2,1)S(1)}, bf16[1024,256]{1,0:T(8,128)(2,1)}, u32[]{:S(2)}, u32[]{:S(2)}) collective-permute-start(bf16[1024,256]{1,0:T(8,128)(2,1)S(1)} %get-tuple-element.133), channel_id=1, source_target_pairs={{0,8},{4,12},{8,16},{12,20},{16,24},{20,28},{1,9},{5,13},{9,17},{1... | collective-permute-start | bytes 1572872 | tf_op jit(solution)/shard_map/ppermute | solution.py:39
  99.6 24.0 %attend_edges.1 = (f32[4,160,256]{2,1,0:T(8,128)}, f32[4,160,256]{2,1,0:T(8,128)}, f32[4,8,256]{2,1,0:T(8,128)}, f32[4,8,256]{2,1,0:T(8,128)}) custom-call(s32[25]{0:T(128)} %pad_add_fusion.1.meta, bf16[3072,128]{1,0:T(8,128)(2,1)} %get-tuple-element.103.refs_0_.refs_3_, s32[1,3072]{1,0:T(1,128)} %bitcast.53, s32[1,3072]{1,0:T(1,128)} %bitcast.57, ...), custom_call_target="tpu_custom_call" | custom-call | flops 6442450944 | bytes 5242880 | tf_op jit(solution)/shard_map/attend_edges/pallas_call | solution.py:415
  123.7 4.5 %collective-permute-done.28.refs_8_ = bf16[1024,256]{1,0:T(8,128)(2,1)} collective-permute-done((bf16[1024,256]{1,0:T(8,128)(2,1)S(1)}, bf16[1024,256]{1,0:T(8,128)(2,1)}, u32[]{:S(2)}, u32[]{:S(2)}) %collective-permute-start.28) | collective-permute-done | bytes 524320 | tf_op jit(solution)/shard_map/ppermute | solution.py:39
  128.2 1.5 collective-permute-done.27.refs_7_
  129.7 5.1 %all-to-all-start.1 = ((bf16[32,24,1024]{2,1,0:T(8,128)(2,1)}), bf16[32,24,1024]{2,1,0:T(8,128)(2,1)S(1)}, u32[]{:S(2)}, u32[]{:S(2)}) async-start(bf16[32,24,1024]{2,1,0:T(8,128)(2,1)} %bitcast.45), calls=%async_computation.1 | async-start | bytes 3145728 | tf_op jit(solution)/shard_map/all_to_all | solution.py:671
  135.4 19.9 %attend_finish.1 = (bf16[384,128]{1,0:T(8,128)(2,1)}, bf16[384,128]{1,0:T(8,128)(2,1)}, bf16[384,128]{1,0:T(8,128)(2,1)}, bf16[384,128]{1,0:T(8,128)(2,1)}, bf16...) custom-call(s32[25]{0:T(128)} %pad_add_fusion.1.meta, ...), custom_call_target="tpu_custom_call" | custom-call | flops 6442450944 | bytes 5242880 | tf_op jit(solution)/shard_map/attend_finish/pallas_call | solution.py:443
  159.3 3.2 %collective-permute-done.30.refs_2_ = bf16[384,128]{1,0:T(8,128)(2,1)S(1)} collective-permute-done((bf16[384,128]{1,0:T(8,128)(2,1)}, bf16[384,128]{1,0:T(8,128)(2,1)S(1)}, u32[]{:S(2)}, u32[]{:S(2)}) %collective-permute-start.30) | collective-permute-done | bytes 98336 | tf_op jit(solution)/shard_map/ppermute | solution.py:702
  163.5 3.2 %collective-permute-done.31.refs_3_ = bf16[384,128]{1,0:T(8,128)(2,1)S(1)} collective-permute-done((bf16[384,128]{1,0:T(8,128)(2,1)}, bf16[384,128]{1,0:T(8,128)(2,1)S(1)}, u32[]{:S(2)}, u32[]{:S(2)}) %collective-permute-start.31) | collective-permute-done | bytes 98336 | tf_op jit(solution)/shard_map/ppermute | solution.py:702
  166.7 1.3 collective-permute-start.35
  168.0 4.5 %collective-permute-done.35.refs_7_ = bf16[384,128]{1,0:T(8,128)(2,1)} collective-permute-done((bf16[384,128]{1,0:T(8,128)(2,1)}, bf16[384,128]{1,0:T(8,128)(2,1)}, u32[]{:S(2)}, u32[]{:S(2)}) %collective-permute-start.35) | collective-permute-done | bytes 98336 | tf_op jit(solution)/shard_map/ppermute | solution.py:702
  172.6 4.7 %output_projection.1 = bf16[384,1024]{1,0:T(8,128)(2,1)} custom-call(s32[1]{0:T(128)} %bitcast.meta, bf16[384,128]{1,0:T(8,128)(2,1)} %get-tuple-element.119.refs_0_, bf16[384,128]{1,0:T(8,128)(2,1)} %copy-done.17, bf16[384,128]{1,0:T(8,128)(2,1)} %copy-done.18, bf16[384,128]{1,0:T(8,128)(2,1)} %copy-done.19, bf16[384,128]{1,0:T(8,128)(2,1)} %copy-done.20, ...), custom_call_target="tpu_custom_call" | custom-call | flops 805306368 | bytes 4194304 | tf_op jit(solution)/shard_map/output_projection/pallas_call | solution.py:499
  177.2 2.5 %unpack.1 = bf16[8,24,8192]{2,1,0:T(8,128)(2,1)} custom-call(bf16[4,2,4,24,1024]{4,3,2,1,0:T(8,128)(2,1)S(1)} %bitcast.39, bf16[4,2,4,24,1024]{4,3,2,1,0:T(8,128)(2,1)S(1)} %bitcast.40), custom_call_target="tpu_custom_call" | custom-call | bytes 6291456 | tf_op jit(solution)/shard_map/unpack/pallas_call | solution.py:535
  (148 shorter events, 20.7 us)
Async XLA Ops:
  4.6 7.6 %collective-permute-start.4 = (bf16[128,128]{1,0:T(8,128)(2,1)S(1)}, bf16[128,128]{1,0:T(8,128)(2,1)S(1)}, u32[]{:S(2)}, u32[]{:S(2)}) collective-permute-start(bf16[128,128]{1,0:T(8,128)(2,1)S(1)} %get-tuple-element.139), channel_id=1, source_target_pairs={{0,5},{1,4},{2,7},{3,6},{4,1},{5,0},{6,3},{7,2},{8,13},{9,12},{10,... | collective-permute-start | bytes 98312 | tf_op jit(solution)/shard_map/ppermute | solution.py:599
  4.7 8.8 %collective-permute-start.3 = (bf16[128,128]{1,0:T(8,128)(2,1)S(1)}, bf16[128,128]{1,0:T(8,128)(2,1)S(1)}, u32[]{:S(2)}, u32[]{:S(2)}) collective-permute-start(bf16[128,128]{1,0:T(8,128)(2,1)S(1)} %get-tuple-element.140), channel_id=1, source_target_pairs={{0,4},{1,7},{2,6},{3,5},{4,0},{5,3},{6,2},{7,1},{8,12},{9,15},{10,... | collective-permute-start | bytes 98312 | tf_op jit(solution)/shard_map/ppermute | solution.py:599
  6.0 7.5 %collective-permute-start.5 = (bf16[128,128]{1,0:T(8,128)(2,1)S(1)}, bf16[128,128]{1,0:T(8,128)(2,1)S(1)}, u32[]{:S(2)}, u32[]{:S(2)}) collective-permute-start(bf16[128,128]{1,0:T(8,128)(2,1)S(1)} %get-tuple-element.141), channel_id=1, source_target_pairs={{0,6},{1,5},{2,4},{3,7},{4,2},{5,1},{6,0},{7,3},{8,14},{9,13},{10,... | collective-permute-start | bytes 98312 | tf_op jit(solution)/shard_map/ppermute | solution.py:599
  6.4 7.1 %collective-permute-start.1 = (bf16[128,128]{1,0:T(8,128)(2,1)S(1)}, bf16[128,128]{1,0:T(8,128)(2,1)S(1)}, u32[]{:S(2)}, u32[]{:S(2)}) collective-permute-start(bf16[128,128]{1,0:T(8,128)(2,1)S(1)} %get-tuple-element.142), channel_id=1, source_target_pairs={{0,1},{1,0},{2,3},{3,2},{4,5},{5,4},{6,7},{7,6},{8,9},{9,8},{10,11... | collective-permute-start | bytes 98312 | tf_op jit(solution)/shard_map/ppermute | solution.py:599
  13.6 14.0 %collective-permute-start.13 = (bf16[256,384]{1,0:T(8,128)(2,1)S(1)}, bf16[256,384]{1,0:T(8,128)(2,1)S(1)}, u32[]{:S(2)}, u32[]{:S(2)}) collective-permute-start(bf16[256,384]{1,0:T(8,128)(2,1)S(1)} %maximum_maximum_fusion.refs_8_), channel_id=1, source_target_pairs={{0,16},{4,20},{8,24},{12,28},{16,0},{20,4},{24,8},{28,12},{1,17},{... | collective-permute-start | bytes 589832 | tf_op jit(solution)/shard_map/ppermute | solution.py:33
  13.7 17.1 %collective-permute-start.12 = (bf16[256,384]{1,0:T(8,128)(2,1)S(1)}, bf16[256,384]{1,0:T(8,128)(2,1)S(1)}, u32[]{:S(2)}, u32[]{:S(2)}) collective-permute-start(bf16[256,384]{1,0:T(8,128)(2,1)S(1)} %maximum_maximum_fusion.refs_8_), channel_id=1, source_target_pairs={{0,8},{4,12},{8,0},{12,4},{16,24},{20,28},{24,16},{28,20},{1,9},{5... | collective-permute-start | bytes 589832 | tf_op jit(solution)/shard_map/ppermute | solution.py:33
  13.9 17.2 %collective-permute-start.10 = (bf16[192,1024]{1,0:T(8,128)(2,1)}, bf16[192,1024]{1,0:T(8,128)(2,1)S(1)}, u32[]{:S(2)}, u32[]{:S(2)}) collective-permute-start(bf16[192,1024]{1,0:T(8,128)(2,1)} %get-tuple-element.68.refs_0_), channel_id=1, source_target_pairs={{0,1},{1,0},{2,3},{3,2},{4,5},{5,4},{6,7},{7,6},{8,9},{9,8},{10,11... | collective-permute-start | bytes 1179656 | tf_op jit(solution)/shard_map/ppermute | solution.py:33
  17.5 16.2 %collective-permute-start.8 = (bf16[192,1024]{1,0:T(8,128)(2,1)}, bf16[192,1024]{1,0:T(8,128)(2,1)S(1)}, u32[]{:S(2)}, u32[]{:S(2)}) collective-permute-start(bf16[192,1024]{1,0:T(8,128)(2,1)} %get-tuple-element.68.refs_0_), channel_id=1, source_target_pairs={{0,4},{4,0},{8,12},{12,8},{16,20},{20,16},{24,28},{28,24},{1,5},{5... | collective-permute-start | bytes 1179656 | tf_op jit(solution)/shard_map/ppermute | solution.py:33
  17.7 16.0 %collective-permute-start.6 = (bf16[192,1024]{1,0:T(8,128)(2,1)}, bf16[192,1024]{1,0:T(8,128)(2,1)S(1)}, u32[]{:S(2)}, u32[]{:S(2)}) collective-permute-start(bf16[192,1024]{1,0:T(8,128)(2,1)} %get-tuple-element.68.refs_0_), channel_id=1, source_target_pairs={{0,2},{1,3},{2,0},{3,1},{4,6},{5,7},{6,4},{7,5},{8,10},{9,11},{10,... | collective-permute-start | bytes 1179656 | tf_op jit(solution)/shard_map/ppermute | solution.py:33
  30.8 11.7 %collective-permute-start.9 = (bf16[208,1024]{1,0:T(8,128)(2,1)}, bf16[208,1024]{1,0:T(8,128)(2,1)S(1)}, u32[]{:S(2)}, u32[]{:S(2)}) collective-permute-start(bf16[208,1024]{1,0:T(8,128)(2,1)} %get-tuple-element.69.refs_1_), channel_id=1, source_target_pairs={{0,4},{4,0},{8,12},{12,8},{16,20},{20,16},{24,28},{28,24},{1,5},{5... | collective-permute-start | bytes 1277960 | tf_op jit(solution)/shard_map/ppermute | solution.py:33
  31.1 12.0 %collective-permute-start.7 = (bf16[208,1024]{1,0:T(8,128)(2,1)}, bf16[208,1024]{1,0:T(8,128)(2,1)}, u32[]{:S(2)}, u32[]{:S(2)}) collective-permute-start(bf16[208,1024]{1,0:T(8,128)(2,1)} %get-tuple-element.69.refs_1_), channel_id=1, source_target_pairs={{0,2},{1,3},{2,0},{3,1},{4,6},{5,7},{6,4},{7,5},{8,10},{9,11},{10,... | collective-permute-start | bytes 1277960 | tf_op jit(solution)/shard_map/ppermute | solution.py:33
  43.1 11.8 %collective-permute-start.17 = (bf16[192,1024]{1,0:T(8,128)(2,1)S(1)}, bf16[192,1024]{1,0:T(8,128)(2,1)S(1)}, u32[]{:S(2)}, u32[]{:S(2)}) collective-permute-start(bf16[192,1024]{1,0:T(8,128)(2,1)S(1)} %collective-permute-done.8.refs_0_), channel_id=1, source_target_pairs={{0,1},{1,0},{2,3},{3,2},{4,5},{5,4},{6,7},{7,6},{8,9},{9,8},{10,11... | collective-permute-start | bytes 1179656 | tf_op jit(solution)/shard_map/ppermute | solution.py:33
  44.0 10.7 %collective-permute-start.21 = (bf16[256,384]{1,0:T(8,128)(2,1)S(1)}, bf16[256,384]{1,0:T(8,128)(2,1)S(1)}, u32[]{:S(2)}, u32[]{:S(2)}) collective-permute-start(bf16[256,384]{1,0:T(8,128)(2,1)S(1)} %collective-permute-done.13.refs_10_), channel_id=1, source_target_pairs={{0,8},{4,12},{8,0},{12,4},{16,24},{20,28},{24,16},{28,20},{1,9},{5... | collective-permute-start | bytes 589832 | tf_op jit(solution)/shard_map/ppermute | solution.py:33
  46.2 7.5 %collective-permute-start.22 = (bf16[256,256]{1,0:T(8,128)(2,1)S(1)}, bf16[256,256]{1,0:T(8,128)(2,1)S(1)}, u32[]{:S(2)}, u32[]{:S(2)}) collective-permute-start(bf16[256,256]{1,0:T(8,128)(2,1)S(1)} %bitcast.49), channel_id=1, source_target_pairs={{0,16},{4,20},{8,24},{12,28},{16,0},{20,4},{24,8},{28,12},{1,17},{... | collective-permute-start | bytes 393224 | tf_op jit(solution)/shard_map/ppermute | solution.py:33
  46.2 19.4 %collective-permute-start.16 = (bf16[208,1024]{1,0:T(8,128)(2,1)}, bf16[208,1024]{1,0:T(8,128)(2,1)}, u32[]{:S(2)}, u32[]{:S(2)}) collective-permute-start(bf16[208,1024]{1,0:T(8,128)(2,1)} %collective-permute-done.7.refs_5_), channel_id=1, source_target_pairs={{0,1},{1,0},{2,3},{3,2},{4,5},{5,4},{6,7},{7,6},{8,9},{9,8},{10,11... | collective-permute-start | bytes 1277960 | tf_op jit(solution)/shard_map/ppermute | solution.py:33
  46.6 19.1 %collective-permute-start.20 = (bf16[208,1024]{1,0:T(8,128)(2,1)S(1)}, bf16[208,1024]{1,0:T(8,128)(2,1)S(1)}, u32[]{:S(2)}, u32[]{:S(2)}) collective-permute-start(bf16[208,1024]{1,0:T(8,128)(2,1)S(1)} %collective-permute-done.9.refs_1_), channel_id=1, source_target_pairs={{0,2},{1,3},{2,0},{3,1},{4,6},{5,7},{6,4},{7,5},{8,10},{9,11},{10,... | collective-permute-start | bytes 1277960 | tf_op jit(solution)/shard_map/ppermute | solution.py:33
  53.7 11.9 %collective-permute-start.18 = (bf16[208,1024]{1,0:T(8,128)(2,1)S(1)}, bf16[208,1024]{1,0:T(8,128)(2,1)S(1)}, u32[]{:S(2)}, u32[]{:S(2)}) collective-permute-start(bf16[208,1024]{1,0:T(8,128)(2,1)S(1)} %collective-permute-done.9.refs_1_), channel_id=1, source_target_pairs={{0,1},{1,0},{2,3},{3,2},{4,5},{5,4},{6,7},{7,6},{8,9},{9,8},{10,11... | collective-permute-start | bytes 1277960 | tf_op jit(solution)/shard_map/ppermute | solution.py:33
  54.7 11.0 %collective-permute-start.19 = (bf16[192,1024]{1,0:T(8,128)(2,1)}, bf16[192,1024]{1,0:T(8,128)(2,1)}, u32[]{:S(2)}, u32[]{:S(2)}) collective-permute-start(bf16[192,1024]{1,0:T(8,128)(2,1)} %copy-done.16), channel_id=1, source_target_pairs={{0,4},{4,0},{8,12},{12,8},{16,20},{20,16},{24,28},{28,24},{1,5},{5... | collective-permute-start | bytes 1179656 | tf_op jit(solution)/shard_map/ppermute | solution.py:33
  54.9 10.8 %collective-permute-start.15 = (bf16[192,1024]{1,0:T(8,128)(2,1)}, bf16[192,1024]{1,0:T(8,128)(2,1)}, u32[]{:S(2)}, u32[]{:S(2)}) collective-permute-start(bf16[192,1024]{1,0:T(8,128)(2,1)} %copy-done.16), channel_id=1, source_target_pairs={{0,1},{1,0},{2,3},{3,2},{4,5},{5,4},{6,7},{7,6},{8,9},{9,8},{10,11... | collective-permute-start | bytes 1179656 | tf_op jit(solution)/shard_map/ppermute | solution.py:33
  65.7 9.5 %collective-permute-start.24 = (bf16[208,1024]{1,0:T(8,128)(2,1)S(1)}, bf16[208,1024]{1,0:T(8,128)(2,1)S(1)}, u32[]{:S(2)}, u32[]{:S(2)}) collective-permute-start(bf16[208,1024]{1,0:T(8,128)(2,1)S(1)} %collective-permute-done.20.refs_5_), channel_id=1, source_target_pairs={{0,1},{1,0},{2,3},{3,2},{4,5},{5,4},{6,7},{7,6},{8,9},{9,8},{10,11... | collective-permute-start | bytes 1277960 | tf_op jit(solution)/shard_map/ppermute | solution.py:33
  66.6 8.5 %collective-permute-start.23 = (bf16[192,1024]{1,0:T(8,128)(2,1)}, bf16[192,1024]{1,0:T(8,128)(2,1)S(1)}, u32[]{:S(2)}, u32[]{:S(2)}) collective-permute-start(bf16[192,1024]{1,0:T(8,128)(2,1)} %collective-permute-done.19.refs_4_), channel_id=1, source_target_pairs={{0,1},{1,0},{2,3},{3,2},{4,5},{5,4},{6,7},{7,6},{8,9},{9,8},{10,11... | collective-permute-start | bytes 1179656 | tf_op jit(solution)/shard_map/ppermute | solution.py:33
  66.7 8.5 %collective-permute-start.25 = (bf16[4,128,256]{2,1,0:T(8,128)(2,1)S(1)}, bf16[4,128,256]{2,1,0:T(8,128)(2,1)S(1)}, u32[]{:S(2)}, u32[]{:S(2)}) collective-permute-start(bf16[4,128,256]{2,1,0:T(8,128)(2,1)S(1)} %bitcast.47), channel_id=1, source_target_pairs={{0,4},{4,0},{8,12},{12,8},{16,20},{20,16},{24,28},{28,24},{1,5},{5... | collective-permute-start | bytes 786440 | tf_op jit(solution)/shard_map/ppermute | solution.py:33
  76.1 53.6 %all-to-all-start = ((bf16[32,24,1024]{2,1,0:T(8,128)(2,1)}), bf16[32,24,1024]{2,1,0:T(8,128)(2,1)S(1)}, u32[]{:S(2)}, u32[]{:S(2)}) async-start(bf16[32,24,1024]{2,1,0:T(8,128)(2,1)} %bitcast.46), calls=%async_computation | async-start | bytes 3145728 | tf_op jit(solution)/shard_map/all_to_all | solution.py:671
  82.8 40.9 %collective-permute-start.26 = (bf16[1024,256]{1,0:T(8,128)(2,1)S(1)}, bf16[1024,256]{1,0:T(8,128)(2,1)S(1)}, u32[]{:S(2)}, u32[]{:S(2)}) collective-permute-start(bf16[1024,256]{1,0:T(8,128)(2,1)S(1)} %bitcast.42), channel_id=1, source_target_pairs={{0,2},{1,3},{2,0},{3,1},{4,6},{5,7},{6,4},{7,5},{8,10},{9,11},{10,... | collective-permute-start | bytes 1572872 | tf_op jit(solution)/shard_map/ppermute | solution.py:33
  93.6 34.6 %collective-permute-start.28 = (bf16[1024,256]{1,0:T(8,128)(2,1)S(1)}, bf16[1024,256]{1,0:T(8,128)(2,1)}, u32[]{:S(2)}, u32[]{:S(2)}) collective-permute-start(bf16[1024,256]{1,0:T(8,128)(2,1)S(1)} %get-tuple-element.132), channel_id=1, source_target_pairs={{8,0},{12,4},{16,8},{20,12},{24,16},{28,20},{9,1},{13,5},{17,9},{2... | collective-permute-start | bytes 1572872 | tf_op jit(solution)/shard_map/ppermute | solution.py:39
  95.8 33.9 %collective-permute-start.27 = (bf16[1024,256]{1,0:T(8,128)(2,1)S(1)}, bf16[1024,256]{1,0:T(8,128)(2,1)}, u32[]{:S(2)}, u32[]{:S(2)}) collective-permute-start(bf16[1024,256]{1,0:T(8,128)(2,1)S(1)} %get-tuple-element.133), channel_id=1, source_target_pairs={{0,8},{4,12},{8,16},{12,20},{16,24},{20,28},{1,9},{5,13},{9,17},{1... | collective-permute-start | bytes 1572872 | tf_op jit(solution)/shard_map/ppermute | solution.py:39
  129.7 47.5 %all-to-all-start.1 = ((bf16[32,24,1024]{2,1,0:T(8,128)(2,1)}), bf16[32,24,1024]{2,1,0:T(8,128)(2,1)S(1)}, u32[]{:S(2)}, u32[]{:S(2)}) async-start(bf16[32,24,1024]{2,1,0:T(8,128)(2,1)} %bitcast.45), calls=%async_computation.1 | async-start | bytes 3145728 | tf_op jit(solution)/shard_map/all_to_all | solution.py:671
  134.8 22.8 %collective-permute-start.36 = (bf16[1024,256]{1,0:T(8,128)(2,1)}, bf16[1024,256]{1,0:T(8,128)(2,1)S(1)}, u32[]{:S(2)}, u32[]{:S(2)}) collective-permute-start(bf16[1024,256]{1,0:T(8,128)(2,1)} %bitcast.43), channel_id=1, source_target_pairs={{0,1},{1,0},{2,3},{3,2},{4,5},{5,4},{6,7},{7,6},{8,9},{9,8},{10,11... | collective-permute-start | bytes 1572872 | tf_op jit(solution)/shard_map/ppermute | solution.py:33
  135.2 37.3 %collective-permute-start.37 = (bf16[1024,256]{1,0:T(8,128)(2,1)}, bf16[1024,256]{1,0:T(8,128)(2,1)}, u32[]{:S(2)}, u32[]{:S(2)}) collective-permute-start(bf16[1024,256]{1,0:T(8,128)(2,1)} %copy-done.5), channel_id=1, source_target_pairs={{0,1},{1,0},{2,3},{3,2},{4,5},{5,4},{6,7},{7,6},{8,9},{9,8},{10,11... | collective-permute-start | bytes 1572872 | tf_op jit(solution)/shard_map/ppermute | solution.py:33
  156.9 9.7 %collective-permute-start.31 = (bf16[384,128]{1,0:T(8,128)(2,1)}, bf16[384,128]{1,0:T(8,128)(2,1)S(1)}, u32[]{:S(2)}, u32[]{:S(2)}) collective-permute-start(bf16[384,128]{1,0:T(8,128)(2,1)} %get-tuple-element.122), channel_id=1, source_target_pairs={{0,3},{1,2},{2,1},{3,0},{4,7},{5,6},{6,5},{7,4},{8,11},{9,10},{10,... | collective-permute-start | bytes 294920 | tf_op jit(solution)/shard_map/ppermute | solution.py:702
  157.6 10.4 %collective-permute-start.32 = (bf16[384,128]{1,0:T(8,128)(2,1)}, bf16[384,128]{1,0:T(8,128)(2,1)S(1)}, u32[]{:S(2)}, u32[]{:S(2)}) collective-permute-start(bf16[384,128]{1,0:T(8,128)(2,1)} %get-tuple-element.123), channel_id=1, source_target_pairs={{0,4},{1,5},{2,6},{3,7},{4,0},{5,1},{6,2},{7,3},{8,12},{9,13},{10,... | collective-permute-start | bytes 294920 | tf_op jit(solution)/shard_map/ppermute | solution.py:702
  158.8 9.2 %collective-permute-start.33 = (bf16[384,128]{1,0:T(8,128)(2,1)}, bf16[384,128]{1,0:T(8,128)(2,1)}, u32[]{:S(2)}, u32[]{:S(2)}) collective-permute-start(bf16[384,128]{1,0:T(8,128)(2,1)} %get-tuple-element.124), channel_id=1, source_target_pairs={{0,5},{1,4},{2,7},{3,6},{4,1},{5,0},{6,3},{7,2},{8,13},{9,12},{10,... | collective-permute-start | bytes 294920 | tf_op jit(solution)/shard_map/ppermute | solution.py:702
  (29 other events, 363.9 us)

commit v4 on v3

--- a/solution.py
+++ b/solution.py
@@ -45,15 +45,12 @@
     return pair.reshape((-1,) + value.shape[1:])
 
 
-def norm_kernel(capacity, tokens, gain, owner_row, top, bottom, owners):
-    half = top.shape[0]
-    rest = tokens.shape[0] - half
+def norm_kernel(capacity, tokens, gain, owner_row, normed, owners):
+    rows = tokens.shape[0]
     values = tokens[...].astype(jnp.float32)
     centred = values - jnp.mean(values, axis=-1, keepdims=True)
     spread = jnp.mean(jnp.square(centred), axis=-1, keepdims=True)
-    normed = (centred * lax.rsqrt(spread + EPSILON) * gain[...]).astype(jnp.bfloat16)
-    top[...] = normed[:half]
-    bottom[:rest, :] = normed[half:]
+    normed[:rows, :] = (centred * lax.rsqrt(spread + EPSILON) * gain[...]).astype(jnp.bfloat16)
     pages = owner_row.shape[1]
     owners[...] = jnp.full(owners.shape, -1.0, jnp.float32)
     owners[:1, :pages] = owner_row[...].astype(jnp.float32)
@@ -65,8 +62,8 @@
     same = (across.T == across) & earlier
     ranks = jnp.sum(jnp.where(same, 1.0, 0.0), axis=0, keepdims=True)
     slots = owners[:1, :] * capacity + ranks
-    bottom[rest:, :] = jnp.zeros((EXTRA_ROWS, bottom.shape[1]), jnp.bfloat16)
-    bottom[rest:, :lanes] = jnp.broadcast_to(slots, (EXTRA_ROWS, lanes)).astype(jnp.bfloat16)
+    normed[rows:, :] = jnp.zeros((EXTRA_ROWS, normed.shape[1]), jnp.bfloat16)
+    normed[rows:, :lanes] = jnp.broadcast_to(slots, (EXTRA_ROWS, lanes)).astype(jnp.bfloat16)
 
 
 def layer_norm(tokens, gain, owners, capacity):
@@ -74,10 +71,7 @@
     lanes = -(-owners.shape[0] // 128) * 128
     return pl.pallas_call(
         functools.partial(norm_kernel, capacity),
-        out_shape=[
-            jax.ShapeDtypeStruct((rows // 2, width), jnp.bfloat16),
-            jax.ShapeDtypeStruct((rows // 2 + EXTRA_ROWS, width), jnp.bfloat16),
-        ],
+        out_shape=jax.ShapeDtypeStruct((rows + EXTRA_ROWS, width), jnp.bfloat16),
         scratch_shapes=[pltpu.VMEM((8, lanes), jnp.float32)],
         compiler_params=PARAMS,
         name="layer_norm",
@@ -215,7 +209,7 @@
         },
         compiler_params=PARAMS,
         cost_estimate=pl.CostEstimate(
-            flops=2 * steps * rows * model_width * PARTS * width,
+            flops=16 * steps * rows * model_width * PARTS * width,
             bytes_accessed=(3 * steps) << 19,
             transcendentals=0,
         ),
@@ -553,21 +547,33 @@
     return jnp.cos(angles), jnp.sin(angles)
 
 
-def document_bounds(window_ids, rows, blocks):
-    reach = SPAN + rows
-    firsts = jnp.arange(blocks, dtype=jnp.int32)[:, None] * rows
-    own = window_ids[SPAN : SPAN + rows * blocks].reshape(blocks, rows)
-    behind = jnp.stack([window_ids[k * rows : k * rows + reach] for k in range(blocks)])
-    ahead = jnp.stack(
-        [window_ids[SPAN + k * rows : SPAN + k * rows + reach] for k in range(blocks)]
-    )
-    starts = jnp.sum((behind[:, None, :] < own[:, :, None]).astype(jnp.int32), axis=2) + firsts
-    ends = (
-        jnp.sum((ahead[:, None, :] <= own[:, :, None]).astype(jnp.int32), axis=2)
-        + firsts
-        + SPAN
-    )
-    return starts.reshape(-1), ends.reshape(-1)
+def bounds_kernel(ids, starts, ends):
+    shape = (8, ids.shape[1])
+    width = ids.shape[1]
+    own = jnp.broadcast_to(ids[...], shape)
+    index = lax.broadcasted_iota(jnp.int32, shape, 1)
+    first = jnp.where((own != pltpu.roll(own, 1, 1)) | (index == 0), index, 0)
+    after = jnp.where((own != pltpu.roll(own, width - 1, 1)) | (index == width - 1), index + 1, width)
+    shift = 1
+    while shift < SPAN:
+        first = jnp.maximum(first, jnp.where(index >= shift, pltpu.roll(first, shift, 1), 0))
+        after = jnp.minimum(
+            after, jnp.where(index < width - shift, pltpu.roll(after, width - shift, 1), width)
+        )
+        shift *= 2
+    rows = starts.shape[1]
+    starts[...] = first[:1, SPAN : SPAN + rows]
+    ends[...] = after[:1, SPAN : SPAN + rows]
+
+
+def document_bounds(window_ids, rows):
+    return pl.pallas_call(
+        bounds_kernel,
+        out_shape=[jax.ShapeDtypeStruct((1, rows), jnp.int32)] * 2,
+        compiler_params=PARAMS,
+        cost_estimate=pl.CostEstimate(flops=1 << 34, bytes_accessed=0, transcendentals=0),
+        name="document_bounds",
+    )(window_ids[None, :])
 
 
 def per_device(tokens, norm_gain, input_weight, output_weight, segment_ids, page_owner):
@@ -599,16 +605,17 @@
             pieces.append(lax.ppermute(piece, ("tok", "grp"), route))
         halves.append(jnp.concatenate(pieces, axis=1))
     plane = jnp.concatenate(halves, axis=0)
-    top, bottom = layer_norm(tokens, norm_gain[None, :], owners, capacity)
-    top, bottom, plane = lax.optimization_barrier((top, bottom, plane))
-    across = [flipped(top, "grp", 2), flipped(bottom, "grp", 2)]
-    along = [flipped(top, "tok", 1), flipped(bottom, "tok", 1)]
-    sibling = [flipped(top, "grp", 1), flipped(bottom, "grp", 1)]
+    own = layer_norm(tokens, norm_gain[None, :], owners, capacity)
+    own, plane = lax.optimization_barrier((own, plane))
+
+    across, along = flipped(own, "grp", 2), flipped(own, "tok", 1)
+    sibling = flipped(own, "grp", 1)
     planes = {0: plane}
     bit = peers // 2
     while bit > 1:
         planes[bit] = flipped(plane, "tok", bit)
         bit //= 2
+
     last_weight = output_weight
     bit = PAIR
     while 2 * bit < peers:
@@ -616,7 +623,6 @@
         bit *= 2
 
     first_row = place // PAIR * group_rows
-    segment_ids, last_weight = lax.optimization_barrier((segment_ids, last_weight))
     padded_ids = jnp.concatenate(
         [
             jnp.full((SPAN,), -1, jnp.int32),
@@ -625,45 +631,32 @@
         ]
     )
     window_ids = lax.dynamic_slice_in_dim(padded_ids, first_row, group_rows + 2 * SPAN, 0)
-    starts, ends = document_bounds(window_ids, rows, blocks)
+    window_ids, plane = lax.optimization_barrier((window_ids, plane))
+    bounds = document_bounds(window_ids, group_rows)
+    starts, ends = bounds[0][0], bounds[1][0]
     positions = SPAN + jnp.arange(group_rows, dtype=jnp.int32) - starts
-    cosine, sine = rope_tables(positions)
-    ranges = jnp.stack(
-        [starts[::TILE] // TILE, (ends[TILE - 1 :: TILE] + TILE - 1) // TILE], axis=1
-    ).reshape(-1)
-    own_member = member[None].astype(jnp.int32)
-    tile_meta = jnp.concatenate([own_member, ranges])
     order = [(number * members + column) % PARTS for number in range(PARTS)]
     meta = jnp.stack([member, place] + order).astype(jnp.int32)
-    bounds = (starts[None, :], ends[None, :])
-
-    across, along, sibling, planes, last_weight, cosine, sine, tile_meta, meta, bounds = (
-        lax.optimization_barrier(
-            (across, along, sibling, planes, last_weight, cosine, sine, tile_meta, meta, bounds)
-        )
-    )
-    corner = [flipped(across[0], "tok", 1), flipped(along[1], "grp", 2)]
-    across_sibling = [flipped(block, "grp", 1) for block in across]
-    along_sibling = [flipped(block, "grp", 1) for block in along]
+    cosine, sine = rope_tables(positions)
+    across, along, sibling, planes, last_weight, cosine, sine, meta = lax.optimization_barrier(
+        (across, along, sibling, planes, last_weight, cosine, sine, meta)
+    )
+    other_planes = flipped(last_weight, "tok", bit)
+
+    half, held = rows // 2, rows + EXTRA_ROWS
+    corner = [flipped(across[:half], "tok", 1), flipped(along[half:], "grp", 2)]
+    across_sibling = flipped(across, "grp", 1)
+    along_sibling = flipped(along, "grp", 1)
     for distance in range(PAIR, peers, PAIR):
         if distance not in planes:
             step_bit = distance & -distance
             planes[distance] = flipped(planes[distance ^ step_bit], "tok", step_bit)
-    if bit < peers:
-        last_weight = merged(last_weight, flipped(last_weight, "tok", bit), "tok", bit, 0)
-    last_weight = last_weight.reshape((peers // PAIR,) + output_weight.shape)
     weights = [planes[distance] for distance in range(0, peers, PAIR)]
-    across_sibling, along_sibling, corner, weights, last_weight = lax.optimization_barrier(
-        (across_sibling, along_sibling, corner, weights, last_weight)
-    )
-    corner_sibling = [flipped(block, "grp", 1) for block in corner]
-    other_weight = flipped(last_weight, "tok", 1)
-    near_blocks = [top, bottom] + sibling + across + across_sibling
-    far_blocks = along + along_sibling + corner
-    half, held = rows // 2, rows + EXTRA_ROWS
-    layout = [
-        [(2 * number, 0, half), (2 * number + 1, half, held - half)] for number in range(4)
-    ]
+    across_sibling, weights = lax.optimization_barrier((across_sibling, weights))
+    near_blocks = [own, sibling, across, across_sibling]
+    near_layout = [[(number, 0, held)] for number in range(4)]
+    far_layout = [[(0, 0, held)], [(1, 0, held)]]
+    far_layout += [[(number, 0, half), (number + 1, half, held - half)] for number in (2, 4)]
 
     sizes = (weights, cosine, sine, rows, blocks, peers, capacity)
 
@@ -677,27 +670,36 @@
         )
         return received.reshape((peers // PAIR, PAIR, members) + send.shape[2:])
 
-    queries, pairs, send = project(meta, 0, layout, near_blocks, *sizes, ())
-    send, corner_sibling, other_weight = lax.optimization_barrier(
-        (send, corner_sibling, other_weight)
+    queries, pairs, send = project(meta, 0, near_layout, near_blocks, *sizes, ())
+    send, corner, along_sibling, other_planes = lax.optimization_barrier(
+        (send, corner, along_sibling, other_planes)
     )
     own_row = to_owners(send)
-    queries, pairs, send = project(
-        meta, 4, layout, far_blocks + corner_sibling, *sizes, (queries, pairs)
-    )
+    corner_sibling = [flipped(block, "grp", 1) for block in corner]
+    far_blocks = [along, along_sibling] + corner + corner_sibling
+    queries, pairs, send = project(meta, 4, far_layout, far_blocks, *sizes, (queries, pairs))
     before = shifted(pairs[group_rows - SPAN :], "tok", PAIR)
     after = shifted(pairs[:SPAN], "tok", -PAIR)
+    last_weight = merged(last_weight, other_planes, "tok", bit, 0)
+    last_weight = last_weight.reshape((peers // PAIR,) + output_weight.shape)
+    other_weight = flipped(last_weight, "tok", 1)
+
+    own_member = member[None].astype(jnp.int32)
+    ranges = jnp.stack(
+        [starts[::TILE] // TILE, (ends[TILE - 1 :: TILE] + TILE - 1) // TILE], axis=1
+    ).reshape(-1)
+    tile_meta = jnp.concatenate([own_member, ranges])
+    edges = attend_edges(tile_meta, queries, *bounds, pairs)
+    other_weight, before, after, edges, send = lax.optimization_barrier(
+        (other_weight, before, after, edges, send)
+    )
+    other_row = to_owners(send)
     columns = merged(last_weight, other_weight, "tok", 1, 1).reshape(model_width, -1)
     columns_across = flipped(columns, "grp", 2)
-
-    edges = attend_edges(tile_meta, queries, *bounds, pairs)
-    columns_across, before, after, edges, send = lax.optimization_barrier(
-        (columns_across, before, after, edges, send)
-    )
-    other_row = to_owners(send)
+    mixed = attend_finish(tile_meta, queries, *bounds, pairs, before, after, edges, rows)
+    mixed, columns_across = lax.optimization_barrier((mixed, columns_across))
     last_weights = [columns, flipped(columns, "grp", 1)]
     last_weights += [columns_across, flipped(columns_across, "grp", 1)]
-    mixed = attend_finish(tile_meta, queries, *bounds, pairs, before, after, edges, rows)
     parts = [mixed[0]] + [
         lax.ppermute(
             mixed[distance],

time: 183 us -> 166 us (0.907)
  waiting for transfers between devices: 42 us -> 31.9 us
  starting transfers between devices: 52 us -> 43 us
  Pallas kernels: 70.1 us -> 74 us
  other arithmetic: 9.65 us -> 7.09 us
  local copies, waits for them, and re-layouts: 4.7 us -> 6.67 us
    ppermute x23 -> x18, starting transfers between devices: 20.5 us -> 10.4 us  [flipped(): lax.ppermute(value, axis, [(source, source ^ bit) for source in range(cou...]
    ppermute x23 -> x18, waiting for transfers between devices: 25.1 us -> 19.6 us  [flipped(): lax.ppermute(value, axis, [(source, source ^ bit) for source in range(cou...]
    pallas_call x1, Pallas kernels: 19.9 us -> 25.1 us  [attend_finish(): pl.pallas_call(functools.partial(finish_kernel, edge), grid_spec=pltpu.Pr...]
    ppermute x7, waiting for transfers between devices: 10.9 us -> 6.37 us  [per_device(): lax.ppermute(mixed[distance], ('tok', 'grp'), [(source, source ^ distance...]
    reduce_sum x1 -> x0, other arithmetic: 3.95 us -> none  [document_bounds(): jnp.sum((ahead[:, None, :] <= own[:, :, None]).astype(jnp.int32), axis=2)]
    pallas_call x1, Pallas kernels: 24 us -> 20.7 us  [attend_edges(): pl.pallas_call(edge_kernel, grid_spec=pltpu.PrefetchScalarGridSpec(num_sc...]
    pallas_call x1 -> x2, Pallas kernels: 2.51 us -> 4.74 us  [the longest x1 2.61 us: layer_norm(): pl.pallas_call(functools.partial(norm_kernel, capacity), out_shape=jax.Sh...]
  transfers between devices with their start and end apart: 40 -> 35, of which waited for: 9 -> 10; matrix products, arithmetic and copies ran while one was open for 7% -> 6% of each run, Pallas kernels for 38% -> 44%
where the time goes in v4:
time: 166 us; the launch traced here: 164 us
  Pallas kernels  74 us (45%)
  starting transfers between devices  43 us (26%)
  waiting for transfers between devices  31.9 us (19%)
  other arithmetic  7.09 us (4%)
  local copies, waits for them, and re-layouts  6.67 us (4%)
    pallas_call x1, Pallas kernels, attend_finish(): pl.pallas_call(functools.partial(finish_kernel, edge), grid_spec=pltpu.Pr...  25.1 us
    pallas_call x1, Pallas kernels, attend_edges(): pl.pallas_call(edge_kernel, grid_spec=pltpu.PrefetchScalarGridSpec(num_sc...  20.7 us
    ppermute x18, waiting for transfers between devices, flipped(): lax.ppermute(value, axis, [(source, source ^ bit) for source in range(cou...  19.6 us
    pallas_call x2, Pallas kernels, project(): pl.pallas_call(functools.partial(project_kernel, first, layout, len(weigh...  16.4 us
    ppermute x18, starting transfers between devices, flipped(): lax.ppermute(value, axis, [(source, source ^ bit) for source in range(cou...  10.4 us
    all_to_all x2, starting transfers between devices, to_owners(): lax.all_to_all(send.reshape((flat,) + send.shape[2:]), ('tok', 'grp'), sp...  10.3 us
    ppermute x6, starting transfers between devices, per_device(): pieces.append(lax.ppermute(piece, ('tok', 'grp'), route))  9.05 us
    ppermute x7, starting transfers between devices, per_device(): lax.ppermute(mixed[distance], ('tok', 'grp'), [(source, source ^ distance...  7.95 us
  transfers between devices with their start and end apart: 35, of which 10 were waited for; matrix products, arithmetic and copies ran while one was open for 6% of the time, Pallas kernels for 44%

profile of v4, /device:TPU:17, one launch (start us, length us, event | category | flops | bytes accessed | tf_op | source)
XLA Modules:
  0.0 163.7 jit_solution(5352909979750027725)
XLA Ops:
  1.5 3.1 %collective-permute-start = (bf16[128,128]{1,0:T(8,128)(2,1)S(1)}, bf16[128,128]{1,0:T(8,128)(2,1)S(1)}, u32[]{:S(2)}, u32[]{:S(2)}) collective-permute-start(bf16[128,128]{1,0:T(8,128)(2,1)S(1)} %get-tuple-element.128), channel_id=1, source_target_pairs={{0,0},{1,3},{2,2},{3,1},{4,4},{5,7},{6,6},{7,5},{8,8},{9,11},{10,1... | collective-permute-start | bytes 98312 | tf_op jit(solution)/shard_map/ppermute | solution.py:605
  5.4 1.3 collective-permute-start.3
  6.7 2.7 %collective-permute-start.4 = (bf16[128,128]{1,0:T(8,128)(2,1)S(1)}, bf16[128,128]{1,0:T(8,128)(2,1)S(1)}, u32[]{:S(2)}, u32[]{:S(2)}) collective-permute-start(bf16[128,128]{1,0:T(8,128)(2,1)S(1)} %get-tuple-element.129), channel_id=1, source_target_pairs={{0,5},{1,4},{2,7},{3,6},{4,1},{5,0},{6,3},{7,2},{8,13},{9,12},{10,... | collective-permute-start | bytes 98312 | tf_op jit(solution)/shard_map/ppermute | solution.py:605
  9.4 1.3 fusion.1
  12.0 2.6 %layer_norm.1.refs_0_ = bf16[400,1024]{1,0:T(8,128)(2,1)} custom-call(bf16[384,1024]{1,0:T(8,128)(2,1)} %tokens.1, f32[1,1024]{1,0:T(1,128)} %bitcast.52, s32[1,96]{1,0:T(1,128)} %bitcast.53), custom_call_target="tpu_custom_call" | custom-call | tf_op jit(solution)/shard_map/layer_norm/pallas_call | solution.py:72
  15.2 1.3 collective-permute-start.11
  19.1 2.1 %document_bounds.1 = (s32[1,3072]{1,0:T(1,128)}, s32[1,3072]{1,0:T(1,128)}) custom-call(s32[1,5120]{1,0:T(1,128)} %bitcast.50), custom_call_target="tpu_custom_call" | custom-call | flops 17179869184 | tf_op jit(solution)/shard_map/document_bounds/pallas_call | solution.py:570
  22.0 2.3 %multiply_sine_fusion = (f32[32,3072]{1,0:T(8,128)}, f32[32,3072]{1,0:T(8,128)}) fusion(f32[3072]{0:T(1024)S(1)} %bitcast.49, f32[32]{0:T(128)S(1)} %negate_power_fusion), kind=kLoop, calls=%fused_computation | loop fusion | flops 98304 | bytes 798848 | tf_op jit(solution)/shard_map/sin | solution.py:547
  24.5 3.3 %collective-permute-done.10.refs_6_.refs_8_ = bf16[256,384]{1,0:T(8,128)(2,1)S(1)} collective-permute-done((bf16[256,384]{1,0:T(8,128)(2,1)S(1)}, bf16[256,384]{1,0:T(8,128)(2,1)S(1)}, u32[]{:S(2)}, u32[]{:S(2)}) %collective-permute-start.10) | collective-permute-done | bytes 196640 | tf_op jit(solution)/shard_map/ppermute | solution.py:33
  27.9 3.7 %collective-permute-done.9.refs_5_.refs_7_ = bf16[256,384]{1,0:T(8,128)(2,1)S(1)} collective-permute-done((bf16[256,384]{1,0:T(8,128)(2,1)S(1)}, bf16[256,384]{1,0:T(8,128)(2,1)S(1)}, u32[]{:S(2)}, u32[]{:S(2)}) %collective-permute-start.9) | collective-permute-done | bytes 196640 | tf_op jit(solution)/shard_map/ppermute | solution.py:33
  31.6 4.7 %collective-permute-done.6.refs_2_ = bf16[400,1024]{1,0:T(8,128)(2,1)S(1)} collective-permute-done((bf16[400,1024]{1,0:T(8,128)(2,1)}, bf16[400,1024]{1,0:T(8,128)(2,1)S(1)}, u32[]{:S(2)}, u32[]{:S(2)}) %collective-permute-start.6) | collective-permute-done | bytes 819232 | tf_op jit(solution)/shard_map/ppermute | solution.py:33
  36.3 1.8 %collective-permute-done.7.refs_0_ = bf16[400,1024]{1,0:T(8,128)(2,1)S(1)} collective-permute-done((bf16[400,1024]{1,0:T(8,128)(2,1)}, bf16[400,1024]{1,0:T(8,128)(2,1)S(1)}, u32[]{:S(2)}, u32[]{:S(2)}) %collective-permute-start.7) | collective-permute-done | bytes 819232 | tf_op jit(solution)/shard_map/ppermute | solution.py:33
  39.9 5.4 %collective-permute-done.13.refs_7_.refs_9_ = bf16[256,384]{1,0:T(8,128)(2,1)S(1)} collective-permute-done((bf16[256,384]{1,0:T(8,128)(2,1)S(1)}, bf16[256,384]{1,0:T(8,128)(2,1)S(1)}, u32[]{:S(2)}, u32[]{:S(2)}) %collective-permute-start.13) | collective-permute-done | bytes 196640 | tf_op jit(solution)/shard_map/ppermute | solution.py:33
  45.9 8.2 %project.2 = (bf16[3072,128]{1,0:T(8,128)(2,1)}, bf16[3072,256]{1,0:T(8,128)(2,1)}, bf16[8,4,24,1024]{3,2,1,0:T(8,128)(2,1)}) custom-call(s32[5]{0:T(128)} %stack.62.meta, bf16[400,1024]{1,0:T(8,128)(2,1)} %layer_norm.1.refs_0_, bf16[400,1024]{1,0:T(8,128)(2,1)} %collective-permute-done.8.refs_1_, bf16[400,1024]{1,0:T(8,128)(2,1)} %copy-done.4, ...), custom_call_target="tpu_custom_call" | custom-call | flops 9663676416 | bytes 6291456 | tf_op jit(solution)/shard_map/project/pallas_call | solution.py:179
  54.2 5.1 %all-to-all-start = ((bf16[32,24,1024]{2,1,0:T(8,128)(2,1)}), bf16[32,24,1024]{2,1,0:T(8,128)(2,1)S(1)}, u32[]{:S(2)}, u32[]{:S(2)}) async-start(bf16[32,24,1024]{2,1,0:T(8,128)(2,1)} %bitcast.44), calls=%async_computation | async-start | bytes 3145728 | tf_op jit(solution)/shard_map/all_to_all | solution.py:664
  62.4 1.3 collective-permute-start.20
  64.7 8.2 %project.3 = (bf16[3072,128]{1,0:T(8,128)(2,1)}, bf16[3072,256]{1,0:T(8,128)(2,1)}, bf16[8,4,24,1024]{3,2,1,0:T(8,128)(2,1)}) custom-call(s32[5]{0:T(128)} %stack.62.meta, bf16[400,1024]{1,0:T(8,128)(2,1)} %copy-done.2, bf16[400,1024]{1,0:T(8,128)(2,1)} %collective-permute-done.16.refs_1_, ...), custom_call_target="tpu_custom_call", output_to_operand_aliasing={{0}: (13, {}), {1}: (14, {})} | custom-call | flops 9663676416 | bytes 6291456 | tf_op jit(solution)/shard_map/project/pallas_call | solution.py:179
  72.9 1.3 fusion.4
  74.1 3.2 %collective-permute-start.21 = (bf16[1024,256]{1,0:T(8,128)(2,1)S(1)}, bf16[1024,256]{1,0:T(8,128)(2,1)S(1)}, u32[]{:S(2)}, u32[]{:S(2)}) collective-permute-start(bf16[1024,256]{1,0:T(8,128)(2,1)S(1)} %get-tuple-element.123), channel_id=1, source_target_pairs={{0,8},{4,12},{8,16},{12,20},{16,24},{20,28},{1,9},{5,13},{9,17},{1... | collective-permute-start | bytes 1572872 | tf_op jit(solution)/shard_map/ppermute | solution.py:39
  77.3 2.1 %collective-permute-start.22 = (bf16[1024,256]{1,0:T(8,128)(2,1)S(1)}, bf16[1024,256]{1,0:T(8,128)(2,1)}, u32[]{:S(2)}, u32[]{:S(2)}) collective-permute-start(bf16[1024,256]{1,0:T(8,128)(2,1)S(1)} %get-tuple-element.122), channel_id=1, source_target_pairs={{8,0},{12,4},{16,8},{20,12},{24,16},{28,20},{9,1},{13,5},{17,9},{2... | collective-permute-start | bytes 1572872 | tf_op jit(solution)/shard_map/ppermute | solution.py:39
  79.4 20.7 %attend_edges.1 = (f32[4,160,256]{2,1,0:T(8,128)}, f32[4,160,256]{2,1,0:T(8,128)}, f32[4,8,256]{2,1,0:T(8,128)}, f32[4,8,256]{2,1,0:T(8,128)}) custom-call(s32[25]{0:T(128)} %pad_add_fusion.1.meta, bf16[3072,128]{1,0:T(8,128)(2,1)} %get-tuple-element.88.refs_0_.refs_3_, s32[1,3072]{1,0:T(1,128)} %get-tuple-element.64.refs_1_.refs_4_, ...), custom_call_target="tpu_custom_call" | custom-call | flops 6442450944 | bytes 5242880 | tf_op jit(solution)/shard_map/attend_edges/pallas_call | solution.py:409
  100.1 5.9 %collective-permute-done.21.refs_7_ = bf16[1024,256]{1,0:T(8,128)(2,1)S(1)} collective-permute-done((bf16[1024,256]{1,0:T(8,128)(2,1)S(1)}, bf16[1024,256]{1,0:T(8,128)(2,1)S(1)}, u32[]{:S(2)}, u32[]{:S(2)}) %collective-permute-start.21) | collective-permute-done | bytes 524320 | tf_op jit(solution)/shard_map/ppermute | solution.py:39
  106.8 5.2 %all-to-all-start.1 = ((bf16[32,24,1024]{2,1,0:T(8,128)(2,1)}), bf16[32,24,1024]{2,1,0:T(8,128)(2,1)S(1)}, u32[]{:S(2)}, u32[]{:S(2)}) async-start(bf16[32,24,1024]{2,1,0:T(8,128)(2,1)} %bitcast.43), calls=%async_computation.1 | async-start | bytes 3145728 | tf_op jit(solution)/shard_map/all_to_all | solution.py:664
  115.0 25.1 %attend_finish.1 = (bf16[384,128]{1,0:T(8,128)(2,1)}, bf16[384,128]{1,0:T(8,128)(2,1)}, bf16[384,128]{1,0:T(8,128)(2,1)}, bf16[384,128]{1,0:T(8,128)(2,1)}, bf16...) custom-call(s32[25]{0:T(128)} %pad_add_fusion.1.meta, ...), custom_call_target="tpu_custom_call" | custom-call | flops 6442450944 | bytes 5242880 | tf_op jit(solution)/shard_map/attend_finish/pallas_call | solution.py:437
  141.6 2.1 %collective-permute-start.26 = (bf16[384,128]{1,0:T(8,128)(2,1)}, bf16[384,128]{1,0:T(8,128)(2,1)S(1)}, u32[]{:S(2)}, u32[]{:S(2)}) collective-permute-start(bf16[384,128]{1,0:T(8,128)(2,1)} %get-tuple-element.114), channel_id=1, source_target_pairs={{0,3},{1,2},{2,1},{3,0},{4,7},{5,6},{6,5},{7,4},{8,11},{9,10},{10,... | collective-permute-start | bytes 294920 | tf_op jit(solution)/shard_map/ppermute | solution.py:704
  143.7 1.7 %collective-permute-start.27 = (bf16[384,128]{1,0:T(8,128)(2,1)}, bf16[384,128]{1,0:T(8,128)(2,1)S(1)}, u32[]{:S(2)}, u32[]{:S(2)}) collective-permute-start(bf16[384,128]{1,0:T(8,128)(2,1)} %get-tuple-element.115), channel_id=1, source_target_pairs={{0,4},{1,5},{2,6},{3,7},{4,0},{5,1},{6,2},{7,3},{8,12},{9,13},{10,... | collective-permute-start | bytes 294920 | tf_op jit(solution)/shard_map/ppermute | solution.py:704
  145.6 1.5 collective-permute-start.29
  147.1 1.6 collective-permute-done.26.refs_3_
  148.7 2.6 %collective-permute-start.30 = (bf16[384,128]{1,0:T(8,128)(2,1)}, bf16[384,128]{1,0:T(8,128)(2,1)S(1)}, u32[]{:S(2)}, u32[]{:S(2)}) collective-permute-start(bf16[384,128]{1,0:T(8,128)(2,1)} %get-tuple-element.118), channel_id=1, source_target_pairs={{0,7},{1,6},{2,5},{3,4},{4,3},{5,2},{6,1},{7,0},{8,15},{9,14},{10,... | collective-permute-start | bytes 294920 | tf_op jit(solution)/shard_map/ppermute | solution.py:704
  151.3 4.6 %collective-permute-done.28.refs_5_ = bf16[384,128]{1,0:T(8,128)(2,1)S(1)} collective-permute-done((bf16[384,128]{1,0:T(8,128)(2,1)}, bf16[384,128]{1,0:T(8,128)(2,1)S(1)}, u32[]{:S(2)}, u32[]{:S(2)}) %collective-permute-start.28) | collective-permute-done | bytes 98336 | tf_op jit(solution)/shard_map/ppermute | solution.py:704
  156.6 4.6 %output_projection.1 = bf16[384,1024]{1,0:T(8,128)(2,1)} custom-call(s32[1]{0:T(128)} %bitcast.meta, bf16[384,128]{1,0:T(8,128)(2,1)} %get-tuple-element.111.refs_0_, bf16[384,128]{1,0:T(8,128)(2,1)} %copy-done.5, bf16[384,128]{1,0:T(8,128)(2,1)} %copy-done.6, bf16[384,128]{1,0:T(8,128)(2,1)} %copy-done.7, bf16[384,128]{1,0:T(8,128)(2,1)} %copy-done.8, ...), custom_call_target="tpu_custom_call" | custom-call | flops 805306368 | bytes 4194304 | tf_op jit(solution)/shard_map/output_projection/pallas_call | solution.py:493
  161.2 2.5 %unpack.1 = bf16[8,24,8192]{2,1,0:T(8,128)(2,1)} custom-call(bf16[4,2,4,24,1024]{4,3,2,1,0:T(8,128)(2,1)S(1)} %bitcast.37, bf16[4,2,4,24,1024]{4,3,2,1,0:T(8,128)(2,1)S(1)} %bitcast.38), custom_call_target="tpu_custom_call" | custom-call | bytes 6291456 | tf_op jit(solution)/shard_map/unpack/pallas_call | solution.py:529
  (109 shorter events, 19.6 us)
Async XLA Ops:
  1.5 9.2 %collective-permute-start = (bf16[128,128]{1,0:T(8,128)(2,1)S(1)}, bf16[128,128]{1,0:T(8,128)(2,1)S(1)}, u32[]{:S(2)}, u32[]{:S(2)}) collective-permute-start(bf16[128,128]{1,0:T(8,128)(2,1)S(1)} %get-tuple-element.128), channel_id=1, source_target_pairs={{0,0},{1,3},{2,2},{3,1},{4,4},{5,7},{6,6},{7,5},{8,8},{9,11},{10,1... | collective-permute-start | bytes 98312 | tf_op jit(solution)/shard_map/ppermute | solution.py:605
  4.7 10.5 %collective-permute-start.1 = (bf16[128,128]{1,0:T(8,128)(2,1)S(1)}, bf16[128,128]{1,0:T(8,128)(2,1)S(1)}, u32[]{:S(2)}, u32[]{:S(2)}) collective-permute-start(bf16[128,128]{1,0:T(8,128)(2,1)S(1)} %get-tuple-element.132), channel_id=1, source_target_pairs={{0,1},{1,0},{2,3},{3,2},{4,5},{5,4},{6,7},{7,6},{8,9},{9,8},{10,11... | collective-permute-start | bytes 98312 | tf_op jit(solution)/shard_map/ppermute | solution.py:605
  4.7 11.8 %collective-permute-start.2 = (bf16[128,128]{1,0:T(8,128)(2,1)S(1)}, bf16[128,128]{1,0:T(8,128)(2,1)S(1)}, u32[]{:S(2)}, u32[]{:S(2)}) collective-permute-start(bf16[128,128]{1,0:T(8,128)(2,1)S(1)} %get-tuple-element.133), channel_id=1, source_target_pairs={{0,2},{1,1},{2,0},{3,3},{4,6},{5,5},{6,4},{7,7},{8,10},{9,9},{10,8... | collective-permute-start | bytes 98312 | tf_op jit(solution)/shard_map/ppermute | solution.py:605
  5.4 11.1 %collective-permute-start.3 = (bf16[128,128]{1,0:T(8,128)(2,1)S(1)}, bf16[128,128]{1,0:T(8,128)(2,1)S(1)}, u32[]{:S(2)}, u32[]{:S(2)}) collective-permute-start(bf16[128,128]{1,0:T(8,128)(2,1)S(1)} %get-tuple-element.130), channel_id=1, source_target_pairs={{0,4},{1,7},{2,6},{3,5},{4,0},{5,3},{6,2},{7,1},{8,12},{9,15},{10,... | collective-permute-start | bytes 98312 | tf_op jit(solution)/shard_map/ppermute | solution.py:605
  6.7 9.8 %collective-permute-start.4 = (bf16[128,128]{1,0:T(8,128)(2,1)S(1)}, bf16[128,128]{1,0:T(8,128)(2,1)S(1)}, u32[]{:S(2)}, u32[]{:S(2)}) collective-permute-start(bf16[128,128]{1,0:T(8,128)(2,1)S(1)} %get-tuple-element.129), channel_id=1, source_target_pairs={{0,5},{1,4},{2,7},{3,6},{4,1},{5,0},{6,3},{7,2},{8,13},{9,12},{10,... | collective-permute-start | bytes 98312 | tf_op jit(solution)/shard_map/ppermute | solution.py:605
  10.7 5.8 %collective-permute-start.5 = (bf16[128,128]{1,0:T(8,128)(2,1)S(1)}, bf16[128,128]{1,0:T(8,128)(2,1)S(1)}, u32[]{:S(2)}, u32[]{:S(2)}) collective-permute-start(bf16[128,128]{1,0:T(8,128)(2,1)S(1)} %get-tuple-element.131), channel_id=1, source_target_pairs={{0,6},{1,5},{2,4},{3,7},{4,2},{5,1},{6,0},{7,3},{8,14},{9,13},{10,... | collective-permute-start | bytes 98312 | tf_op jit(solution)/shard_map/ppermute | solution.py:605
  15.2 9.1 %collective-permute-start.11 = (bf16[128,256]{1,0:T(8,128)(2,1)S(1)}, bf16[128,256]{1,0:T(8,128)(2,1)S(1)}, u32[]{:S(2)}, u32[]{:S(2)}) collective-permute-start(bf16[128,256]{1,0:T(8,128)(2,1)S(1)} %copy-done.12), channel_id=1, source_target_pairs={{0,8},{4,12},{8,0},{12,4},{16,24},{20,28},{24,16},{28,20},{1,9},{5... | collective-permute-start | bytes 196616 | tf_op jit(solution)/shard_map/ppermute | solution.py:33
  16.6 19.8 %collective-permute-start.6 = (bf16[400,1024]{1,0:T(8,128)(2,1)}, bf16[400,1024]{1,0:T(8,128)(2,1)S(1)}, u32[]{:S(2)}, u32[]{:S(2)}) collective-permute-start(bf16[400,1024]{1,0:T(8,128)(2,1)} %layer_norm.1.refs_0_), channel_id=1, source_target_pairs={{0,2},{1,3},{2,0},{3,1},{4,6},{5,7},{6,4},{7,5},{8,10},{9,11},{10,... | collective-permute-start | bytes 2457608 | tf_op jit(solution)/shard_map/ppermute | solution.py:33
  17.8 20.3 %collective-permute-start.7 = (bf16[400,1024]{1,0:T(8,128)(2,1)}, bf16[400,1024]{1,0:T(8,128)(2,1)S(1)}, u32[]{:S(2)}, u32[]{:S(2)}) collective-permute-start(bf16[400,1024]{1,0:T(8,128)(2,1)} %layer_norm.1.refs_0_), channel_id=1, source_target_pairs={{0,4},{4,0},{8,12},{12,8},{16,20},{20,16},{24,28},{28,24},{1,5},{5... | collective-permute-start | bytes 2457608 | tf_op jit(solution)/shard_map/ppermute | solution.py:33
  18.0 20.1 %collective-permute-start.8 = (bf16[400,1024]{1,0:T(8,128)(2,1)}, bf16[400,1024]{1,0:T(8,128)(2,1)}, u32[]{:S(2)}, u32[]{:S(2)}) collective-permute-start(bf16[400,1024]{1,0:T(8,128)(2,1)} %layer_norm.1.refs_0_), channel_id=1, source_target_pairs={{0,1},{1,0},{2,3},{3,2},{4,5},{5,4},{6,7},{7,6},{8,9},{9,8},{10,11... | collective-permute-start | bytes 2457608 | tf_op jit(solution)/shard_map/ppermute | solution.py:33
  19.0 8.8 %collective-permute-start.10 = (bf16[256,384]{1,0:T(8,128)(2,1)S(1)}, bf16[256,384]{1,0:T(8,128)(2,1)S(1)}, u32[]{:S(2)}, u32[]{:S(2)}) collective-permute-start(bf16[256,384]{1,0:T(8,128)(2,1)S(1)} %maximum_maximum_fusion.refs_4_.refs_6_), channel_id=1, source_target_pairs={{0,16},{4,20},{8,24},{12,28},{16,0},{20,4},{24,8},{28,12},{1,17},{... | collective-permute-start | bytes 589832 | tf_op jit(solution)/shard_map/ppermute | solution.py:33
  24.3 7.3 %collective-permute-start.9 = (bf16[256,384]{1,0:T(8,128)(2,1)S(1)}, bf16[256,384]{1,0:T(8,128)(2,1)S(1)}, u32[]{:S(2)}, u32[]{:S(2)}) collective-permute-start(bf16[256,384]{1,0:T(8,128)(2,1)S(1)} %maximum_maximum_fusion.refs_4_.refs_6_), channel_id=1, source_target_pairs={{0,8},{4,12},{8,0},{12,4},{16,24},{20,28},{24,16},{28,20},{1,9},{5... | collective-permute-start | bytes 589832 | tf_op jit(solution)/shard_map/ppermute | solution.py:33
  38.1 7.2 %collective-permute-start.12 = (bf16[400,1024]{1,0:T(8,128)(2,1)S(1)}, bf16[400,1024]{1,0:T(8,128)(2,1)}, u32[]{:S(2)}, u32[]{:S(2)}) collective-permute-start(bf16[400,1024]{1,0:T(8,128)(2,1)S(1)} %collective-permute-done.6.refs_2_), channel_id=1, source_target_pairs={{0,1},{1,0},{2,3},{3,2},{4,5},{5,4},{6,7},{7,6},{8,9},{9,8},{10,11... | collective-permute-start | bytes 2457608 | tf_op jit(solution)/shard_map/ppermute | solution.py:33
  38.7 6.6 %collective-permute-start.13 = (bf16[256,384]{1,0:T(8,128)(2,1)S(1)}, bf16[256,384]{1,0:T(8,128)(2,1)S(1)}, u32[]{:S(2)}, u32[]{:S(2)}) collective-permute-start(bf16[256,384]{1,0:T(8,128)(2,1)S(1)} %collective-permute-done.10.refs_6_.refs_8_), channel_id=1, source_target_pairs={{0,8},{4,12},{8,0},{12,4},{16,24},{20,28},{24,16},{28,20},{1,9},{5... | collective-permute-start | bytes 589832 | tf_op jit(solution)/shard_map/ppermute | solution.py:33
  38.9 15.3 %collective-permute-start.16 = (bf16[400,1024]{1,0:T(8,128)(2,1)S(1)}, bf16[400,1024]{1,0:T(8,128)(2,1)}, u32[]{:S(2)}, u32[]{:S(2)}) collective-permute-start(bf16[400,1024]{1,0:T(8,128)(2,1)S(1)} %collective-permute-done.7.refs_0_), channel_id=1, source_target_pairs={{0,1},{1,0},{2,3},{3,2},{4,5},{5,4},{6,7},{7,6},{8,9},{9,8},{10,11... | collective-permute-start | bytes 2457608 | tf_op jit(solution)/shard_map/ppermute | solution.py:33
  39.3 14.9 %collective-permute-start.15 = (bf16[208,1024]{1,0:T(8,128)(2,1)S(1)}, bf16[208,1024]{1,0:T(8,128)(2,1)}, u32[]{:S(2)}, u32[]{:S(2)}) collective-permute-start(bf16[208,1024]{1,0:T(8,128)(2,1)S(1)} %slice.51), channel_id=1, source_target_pairs={{0,2},{1,3},{2,0},{3,1},{4,6},{5,7},{6,4},{7,5},{8,10},{9,11},{10,... | collective-permute-start | bytes 1277960 | tf_op jit(solution)/shard_map/ppermute | solution.py:33
  39.7 14.5 %collective-permute-start.14 = (bf16[192,1024]{1,0:T(8,128)(2,1)S(1)}, bf16[192,1024]{1,0:T(8,128)(2,1)}, u32[]{:S(2)}, u32[]{:S(2)}) collective-permute-start(bf16[192,1024]{1,0:T(8,128)(2,1)S(1)} %slice.50), channel_id=1, source_target_pairs={{0,4},{4,0},{8,12},{12,8},{16,20},{20,16},{24,28},{28,24},{1,5},{5... | collective-permute-start | bytes 1179656 | tf_op jit(solution)/shard_map/ppermute | solution.py:33
  45.3 8.9 %collective-permute-start.17 = (bf16[256,256]{1,0:T(8,128)(2,1)S(1)}, bf16[256,256]{1,0:T(8,128)(2,1)S(1)}, u32[]{:S(2)}, u32[]{:S(2)}) collective-permute-start(bf16[256,256]{1,0:T(8,128)(2,1)S(1)} %bitcast.47), channel_id=1, source_target_pairs={{0,16},{4,20},{8,24},{12,28},{16,0},{20,4},{24,8},{28,12},{1,17},{... | collective-permute-start | bytes 393224 | tf_op jit(solution)/shard_map/ppermute | solution.py:33
  54.2 51.8 %all-to-all-start = ((bf16[32,24,1024]{2,1,0:T(8,128)(2,1)}), bf16[32,24,1024]{2,1,0:T(8,128)(2,1)S(1)}, u32[]{:S(2)}, u32[]{:S(2)}) async-start(bf16[32,24,1024]{2,1,0:T(8,128)(2,1)} %bitcast.44), calls=%async_computation | async-start | bytes 3145728 | tf_op jit(solution)/shard_map/all_to_all | solution.py:664
  62.4 37.7 %collective-permute-start.20 = (bf16[4,128,256]{2,1,0:T(8,128)(2,1)S(1)}, bf16[4,128,256]{2,1,0:T(8,128)(2,1)S(1)}, u32[]{:S(2)}, u32[]{:S(2)}) collective-permute-start(bf16[4,128,256]{2,1,0:T(8,128)(2,1)S(1)} %bitcast.45), channel_id=1, source_target_pairs={{0,4},{4,0},{8,12},{12,8},{16,20},{20,16},{24,28},{28,24},{1,5},{5... | collective-permute-start | bytes 786440 | tf_op jit(solution)/shard_map/ppermute | solution.py:33
  74.1 31.8 %collective-permute-start.21 = (bf16[1024,256]{1,0:T(8,128)(2,1)S(1)}, bf16[1024,256]{1,0:T(8,128)(2,1)S(1)}, u32[]{:S(2)}, u32[]{:S(2)}) collective-permute-start(bf16[1024,256]{1,0:T(8,128)(2,1)S(1)} %get-tuple-element.123), channel_id=1, source_target_pairs={{0,8},{4,12},{8,16},{12,20},{16,24},{20,28},{1,9},{5,13},{9,17},{1... | collective-permute-start | bytes 1572872 | tf_op jit(solution)/shard_map/ppermute | solution.py:39
  77.3 28.7 %collective-permute-start.22 = (bf16[1024,256]{1,0:T(8,128)(2,1)S(1)}, bf16[1024,256]{1,0:T(8,128)(2,1)}, u32[]{:S(2)}, u32[]{:S(2)}) collective-permute-start(bf16[1024,256]{1,0:T(8,128)(2,1)S(1)} %get-tuple-element.122), channel_id=1, source_target_pairs={{8,0},{12,4},{16,8},{20,12},{24,16},{28,20},{9,1},{13,5},{17,9},{2... | collective-permute-start | bytes 1572872 | tf_op jit(solution)/shard_map/ppermute | solution.py:39
  106.8 54.4 %all-to-all-start.1 = ((bf16[32,24,1024]{2,1,0:T(8,128)(2,1)}), bf16[32,24,1024]{2,1,0:T(8,128)(2,1)S(1)}, u32[]{:S(2)}, u32[]{:S(2)}) async-start(bf16[32,24,1024]{2,1,0:T(8,128)(2,1)} %bitcast.43), calls=%async_computation.1 | async-start | bytes 3145728 | tf_op jit(solution)/shard_map/all_to_all | solution.py:664
  113.1 27.6 %collective-permute-start.23 = (bf16[1024,256]{1,0:T(8,128)(2,1)S(1)}, bf16[1024,256]{1,0:T(8,128)(2,1)}, u32[]{:S(2)}, u32[]{:S(2)}) collective-permute-start(bf16[1024,256]{1,0:T(8,128)(2,1)S(1)} %bitcast.40), channel_id=1, source_target_pairs={{0,2},{1,3},{2,0},{3,1},{4,6},{5,7},{6,4},{7,5},{8,10},{9,11},{10,... | collective-permute-start | bytes 1572872 | tf_op jit(solution)/shard_map/ppermute | solution.py:33
  114.3 29.4 %collective-permute-start.31 = (bf16[1024,256]{1,0:T(8,128)(2,1)S(1)}, bf16[1024,256]{1,0:T(8,128)(2,1)}, u32[]{:S(2)}, u32[]{:S(2)}) collective-permute-start(bf16[1024,256]{1,0:T(8,128)(2,1)S(1)} %bitcast.41), channel_id=1, source_target_pairs={{0,1},{1,0},{2,3},{3,2},{4,5},{5,4},{6,7},{7,6},{8,9},{9,8},{10,11... | collective-permute-start | bytes 1572872 | tf_op jit(solution)/shard_map/ppermute | solution.py:33
  140.7 15.2 %collective-permute-start.32 = (bf16[1024,256]{1,0:T(8,128)(2,1)}, bf16[1024,256]{1,0:T(8,128)(2,1)}, u32[]{:S(2)}, u32[]{:S(2)}) collective-permute-start(bf16[1024,256]{1,0:T(8,128)(2,1)} %collective-permute-done.23.refs_10_), channel_id=1, source_target_pairs={{0,1},{1,0},{2,3},{3,2},{4,5},{5,4},{6,7},{7,6},{8,9},{9,8},{10,11... | collective-permute-start | bytes 1572872 | tf_op jit(solution)/shard_map/ppermute | solution.py:33
  141.6 4.1 %collective-permute-start.25 = (bf16[384,128]{1,0:T(8,128)(2,1)}, bf16[384,128]{1,0:T(8,128)(2,1)S(1)}, u32[]{:S(2)}, u32[]{:S(2)}) collective-permute-start(bf16[384,128]{1,0:T(8,128)(2,1)} %get-tuple-element.113), channel_id=1, source_target_pairs={{0,2},{1,3},{2,0},{3,1},{4,6},{5,7},{6,4},{7,5},{8,10},{9,11},{10,... | collective-permute-start | bytes 294920 | tf_op jit(solution)/shard_map/ppermute | solution.py:704
  141.6 7.1 %collective-permute-start.26 = (bf16[384,128]{1,0:T(8,128)(2,1)}, bf16[384,128]{1,0:T(8,128)(2,1)S(1)}, u32[]{:S(2)}, u32[]{:S(2)}) collective-permute-start(bf16[384,128]{1,0:T(8,128)(2,1)} %get-tuple-element.114), channel_id=1, source_target_pairs={{0,3},{1,2},{2,1},{3,0},{4,7},{5,6},{6,5},{7,4},{8,11},{9,10},{10,... | collective-permute-start | bytes 294920 | tf_op jit(solution)/shard_map/ppermute | solution.py:704
  143.7 7.6 %collective-permute-start.27 = (bf16[384,128]{1,0:T(8,128)(2,1)}, bf16[384,128]{1,0:T(8,128)(2,1)S(1)}, u32[]{:S(2)}, u32[]{:S(2)}) collective-permute-start(bf16[384,128]{1,0:T(8,128)(2,1)} %get-tuple-element.115), channel_id=1, source_target_pairs={{0,4},{1,5},{2,6},{3,7},{4,0},{5,1},{6,2},{7,3},{8,12},{9,13},{10,... | collective-permute-start | bytes 294920 | tf_op jit(solution)/shard_map/ppermute | solution.py:704
  145.4 10.4 %collective-permute-start.28 = (bf16[384,128]{1,0:T(8,128)(2,1)}, bf16[384,128]{1,0:T(8,128)(2,1)S(1)}, u32[]{:S(2)}, u32[]{:S(2)}) collective-permute-start(bf16[384,128]{1,0:T(8,128)(2,1)} %get-tuple-element.116), channel_id=1, source_target_pairs={{0,5},{1,4},{2,7},{3,6},{4,1},{5,0},{6,3},{7,2},{8,13},{9,12},{10,... | collective-permute-start | bytes 294920 | tf_op jit(solution)/shard_map/ppermute | solution.py:704
  145.6 10.3 %collective-permute-start.29 = (bf16[384,128]{1,0:T(8,128)(2,1)}, bf16[384,128]{1,0:T(8,128)(2,1)S(1)}, u32[]{:S(2)}, u32[]{:S(2)}) collective-permute-start(bf16[384,128]{1,0:T(8,128)(2,1)} %get-tuple-element.117), channel_id=1, source_target_pairs={{0,6},{1,7},{2,4},{3,5},{4,2},{5,3},{6,0},{7,1},{8,14},{9,15},{10,... | collective-permute-start | bytes 294920 | tf_op jit(solution)/shard_map/ppermute | solution.py:704
  148.7 7.2 %collective-permute-start.30 = (bf16[384,128]{1,0:T(8,128)(2,1)}, bf16[384,128]{1,0:T(8,128)(2,1)S(1)}, u32[]{:S(2)}, u32[]{:S(2)}) collective-permute-start(bf16[384,128]{1,0:T(8,128)(2,1)} %get-tuple-element.118), channel_id=1, source_target_pairs={{0,7},{1,6},{2,5},{3,4},{4,3},{5,2},{6,1},{7,0},{8,15},{9,14},{10,... | collective-permute-start | bytes 294920 | tf_op jit(solution)/shard_map/ppermute | solution.py:704
  (22 other events, 158.0 us)

commit v5 on v4

--- a/solution.py
+++ b/solution.py
@@ -37,12 +37,6 @@
     count = lax.axis_size(axis)
     initial, last = (max(0, -steps), min(count, count - steps))
     return lax.ppermute(value, axis, [(source, source + steps) for source in range(initial, last)])
-
-
-def merged(value, other, axis, bit, low):
-    first = (lax.axis_index(axis) & bit) == 0
-    pair = jnp.stack([jnp.where(first, value, other), jnp.where(first, other, value)], axis=low)
-    return pair.reshape((-1,) + value.shape[1:])
 
 
 def norm_kernel(capacity, tokens, gain, owner_row, normed, owners):
@@ -170,7 +164,7 @@
     steps = len(layout)
     model_width = operands[0].shape[1]
     group_rows = rows * blocks
-    width = weights[0].shape[1] // PARTS
+    width = model_width // blocks
     members = blocks // PAIR
     whole = lambda shape: pl.BlockSpec(shape, lambda i, m: (0,) * len(shape))
     place = lambda i, m: m[0] ^ (first + i)
@@ -276,7 +270,7 @@
     return tuple(jnp.full((1, TILE), NEG_FILL, jnp.float32) for _ in range(heads))
 
 
-def edge_kernel(meta, *refs):
+def edge_kernel(meta, ranges, *refs):
     rows, pairs, outs, (masked, values) = refs[:6], refs[6], refs[7:11], refs[11:]
     step = pl.program_id(0)
     width = rows[0].shape[1]
@@ -299,8 +293,8 @@
         total[...] = jnp.zeros_like(total)
         jobs.append(
             (
-                meta[1 + 2 * tile],
-                meta[2 + 2 * tile],
+                ranges[0, 2 * tile],
+                ranges[0, 2 * tile + 1],
                 edge,
                 pairs,
                 lambda row: values[:, pl.ds(row, KEYS)],
@@ -316,7 +310,7 @@
             outs[2 + side][0, head : head + 1, :] = peaks[side][head]
 
 
-def finish_kernel(edge, meta, *refs):
+def finish_kernel(edge, meta, ranges, *refs):
     rows, pairs, halos, held, held_peaks = refs[:6], refs[6], refs[7:9], refs[9:11], refs[11:13]
     outs, (masked, sums, mixed) = refs[13:-3], refs[-3:]
     step = pl.program_id(0)
@@ -332,8 +326,8 @@
             mask_heads(queries, masked.at[side])
             jobs.append(
                 (
-                    meta[1 + 2 * places[side]],
-                    meta[2 + 2 * places[side]],
+                    ranges[0, 2 * places[side]],
+                    ranges[0, 2 * places[side] + 1],
                     bases[side],
                     keys[side],
                     lambda row, held=keys[side]: with_ones(held[pl.ds(row, KEYS), width:]),
@@ -350,8 +344,8 @@
         for side in range(2):
             sums[side] = held[side][0]
 
-    reaches_back = meta[1 + 2 * places[0]] < edge
-    reaches_ahead = meta[2 + 2 * places[1]] > edge + tiles
+    reaches_back = ranges[0, 2 * places[0]] < edge
+    reaches_ahead = ranges[0, 2 * places[1] + 1] > edge + tiles
 
     @pl.when((step < edge) & (reaches_back | reaches_ahead))
     def _():
@@ -396,12 +390,12 @@
     specs = []
     for side in range(2):
         place = lambda i, side=side: tile_places(i, edge, tiles)[side]
-        specs.append(pl.BlockSpec((TILE, width), lambda i, m, place=place: (place(i), 0)))
-        specs += [pl.BlockSpec((1, TILE), lambda i, m, place=place: (0, place(i)))] * 2
-    return specs + [pl.BlockSpec((tiles * TILE, 2 * width), lambda i, m: (0, 0))]
-
-
-def attend_edges(meta, queries, starts, ends, pairs):
+        specs.append(pl.BlockSpec((TILE, width), lambda i, m, r, place=place: (place(i), 0)))
+        specs += [pl.BlockSpec((1, TILE), lambda i, m, r, place=place: (0, place(i)))] * 2
+    return specs + [pl.BlockSpec((tiles * TILE, 2 * width), lambda i, m, r: (0, 0))]
+
+
+def attend_edges(meta, ranges, queries, starts, ends, pairs):
     group_rows, width = queries.shape
     heads = width // HEAD_DIM
     tiles, edge = group_rows // TILE, SPAN // TILE
@@ -409,10 +403,10 @@
     return pl.pallas_call(
         edge_kernel,
         grid_spec=pltpu.PrefetchScalarGridSpec(
-            num_scalar_prefetch=1,
+            num_scalar_prefetch=2,
             grid=(edge,),
             in_specs=attend_specs(width, edge, tiles),
-            out_specs=[pl.BlockSpec((1,) + shape[1:], lambda i, m: (i, 0, 0)) for shape in shapes],
+            out_specs=[pl.BlockSpec((1,) + shape[1:], lambda i, m, r: (i, 0, 0)) for shape in shapes],
             scratch_shapes=[
                 pltpu.VMEM((2, heads, width, TILE), jnp.bfloat16),
                 pltpu.VMEM((heads * HEAD_ROWS, group_rows), jnp.bfloat16),
@@ -426,10 +420,10 @@
             transcendentals=group_rows * 1024 * heads,
         ),
         name="attend_edges",
-    )(meta, queries, starts, ends, queries, starts, ends, pairs)
-
-
-def attend_finish(meta, queries, starts, ends, pairs, before, after, held, rows):
+    )(meta, ranges, queries, starts, ends, queries, starts, ends, pairs)
+
+
+def attend_finish(meta, ranges, queries, starts, ends, pairs, before, after, held, rows):
     group_rows, width = queries.shape
     heads = width // HEAD_DIM
     tiles, edge = group_rows // TILE, SPAN // TILE
@@ -437,15 +431,15 @@
     return pl.pallas_call(
         functools.partial(finish_kernel, edge),
         grid_spec=pltpu.PrefetchScalarGridSpec(
-            num_scalar_prefetch=1,
+            num_scalar_prefetch=2,
             grid=(edge + (tiles - 2 * edge) // 2,),
             in_specs=attend_specs(width, edge, tiles)
-            + [pl.BlockSpec((SPAN, 2 * width), lambda i, m: (0, 0))] * 2
+            + [pl.BlockSpec((SPAN, 2 * width), lambda i, m, r: (0, 0))] * 2
             + [
-                pl.BlockSpec((1,) + part.shape[1:], lambda i, m: (jnp.minimum(i, edge - 1), 0, 0))
+                pl.BlockSpec((1,) + part.shape[1:], lambda i, m, r: (jnp.minimum(i, edge - 1), 0, 0))
                 for part in held
             ],
-            out_specs=[pl.BlockSpec((rows, width), lambda i, m: (0, 0))] * members,
+            out_specs=[pl.BlockSpec((rows, width), lambda i, m, r: (0, 0))] * members,
             scratch_shapes=[
                 pltpu.VMEM((2, heads, width, TILE), jnp.bfloat16),
                 pltpu.VMEM((2, heads * HEAD_ROWS, TILE), jnp.float32),
@@ -460,50 +454,44 @@
             transcendentals=group_rows * 1024 * heads,
         ),
         name="attend_finish",
-    )(meta, queries, starts, ends, queries, starts, ends, pairs, before, after, *held)
+    )(meta, ranges, queries, starts, ends, queries, starts, ends, pairs, before, after, *held)
 
 
 def output_kernel(members, meta, *refs):
-    parts, result, mixed = refs[:members], refs[-2], refs[-1]
-    weights = refs[members:-2]
-    step = pl.program_id(0)
+    parts, weights, result, mixed = refs[:members], refs[members:-2], refs[-2], refs[-1]
     width = parts[0].shape[1]
-
-    @pl.when(step == 0)
-    def _():
-        for distance in range(members):
-            source = meta[0] ^ distance
-            head_pair = PAIR * (source % (members // PAIR)) + source // (members // PAIR)
-            columns = pl.ds(pl.multiple_of(head_pair * width, width), width)
-            mixed[:, columns] = parts[distance][...]
-
+    tile = weights[0].shape[1]
+    for distance in range(members):
+        source = meta[0] ^ distance
+        head_pair = PAIR * (source % (members // PAIR)) + source // (members // PAIR)
+        columns = pl.ds(pl.multiple_of((head_pair ^ meta[1]) * width, width), width)
+        mixed[:, columns] = parts[distance][...]
     for distance, weight in enumerate(weights):
-
-        @pl.when(step == distance)
-        def _():
-            result[...] = jnp.dot(
-                mixed[...], weight[...], preferred_element_type=jnp.float32
-            ).astype(jnp.bfloat16)
+        columns = pl.ds(pl.multiple_of((meta[0] % len(weights) ^ distance) * tile, tile), tile)
+        result[:, columns] = jnp.dot(
+            mixed[...], weight[...], preferred_element_type=jnp.float32
+        ).astype(jnp.bfloat16)
 
 
 def output_projection(meta, parts, weights):
     rows, width = parts[0].shape
     depth, tile = weights[0].shape
-    steps = len(weights)
+    whole = lambda shape: pl.BlockSpec(shape, lambda i, m: (0, 0))
     return pl.pallas_call(
         functools.partial(output_kernel, len(parts)),
         grid_spec=pltpu.PrefetchScalarGridSpec(
             num_scalar_prefetch=1,
-            grid=(steps,),
-            in_specs=[pl.BlockSpec((rows, width), lambda i, m: (0, 0))] * len(parts)
-            + [pl.BlockSpec((depth, tile), lambda i, m: (0, 0))] * steps,
-            out_specs=pl.BlockSpec((rows, tile), lambda i, m: (0, (m[0] % steps) ^ i)),
+            grid=(1,),
+            in_specs=[whole(parts[0].shape)] * len(parts) + [whole((depth, tile))] * len(weights),
+            out_specs=whole((rows, len(weights) * tile)),
             scratch_shapes=[pltpu.VMEM((rows, depth), jnp.bfloat16)],
         ),
-        out_shape=jax.ShapeDtypeStruct((rows, steps * tile), jnp.bfloat16),
+        out_shape=jax.ShapeDtypeStruct((rows, len(weights) * tile), jnp.bfloat16),
         compiler_params=PARAMS,
         cost_estimate=pl.CostEstimate(
-            flops=2 * rows * depth * steps * tile, bytes_accessed=4 << 20, transcendentals=0
+            flops=2 * rows * depth * len(weights) * tile,
+            bytes_accessed=4 << 20,
+            transcendentals=0,
         ),
         name="output_projection",
     )(meta, *parts, *weights)
@@ -547,7 +535,7 @@
     return jnp.cos(angles), jnp.sin(angles)
 
 
-def bounds_kernel(ids, starts, ends):
+def bounds_kernel(ids, starts, ends, ranges):
     shape = (8, ids.shape[1])
     width = ids.shape[1]
     own = jnp.broadcast_to(ids[...], shape)
@@ -564,12 +552,26 @@
     rows = starts.shape[1]
     starts[...] = first[:1, SPAN : SPAN + rows]
     ends[...] = after[:1, SPAN : SPAN + rows]
+    lane = lax.broadcasted_iota(jnp.int32, (rows, ranges.shape[1]), 0)
+    entry = lax.broadcasted_iota(jnp.int32, (rows, ranges.shape[1]), 1)
+    own_lane = entry // 2 * TILE + lax.rem(entry, 2) * (TILE - 1)
+    chosen = jnp.where(lane == own_lane, 1.0, 0.0)
+    odd = lax.rem(entry, 2) == 1
+    begin = (first[:, SPAN : SPAN + rows] // TILE).astype(jnp.bfloat16)
+    end = ((after[:, SPAN : SPAN + rows] + TILE - 1) // TILE).astype(jnp.bfloat16)
+    from_begin = jnp.where(odd, 0.0, chosen).astype(jnp.bfloat16)
+    from_end = jnp.where(odd, chosen, 0.0).astype(jnp.bfloat16)
+    found = jnp.dot(begin, from_begin, preferred_element_type=jnp.float32) + jnp.dot(
+        end, from_end, preferred_element_type=jnp.float32
+    )
+    ranges[...] = found[:1].astype(jnp.int32)
 
 
 def document_bounds(window_ids, rows):
     return pl.pallas_call(
         bounds_kernel,
-        out_shape=[jax.ShapeDtypeStruct((1, rows), jnp.int32)] * 2,
+        out_shape=[jax.ShapeDtypeStruct((1, rows), jnp.int32)] * 2
+        + [jax.ShapeDtypeStruct((1, 128), jnp.int32)],
         compiler_params=PARAMS,
         cost_estimate=pl.CostEstimate(flops=1 << 34, bytes_accessed=0, transcendentals=0),
         name="document_bounds",
@@ -603,6 +605,7 @@
                 target = (row ^ parity) * members + (PARTS * column_from + number) % members
                 route.append((source, target))
             pieces.append(lax.ppermute(piece, ("tok", "grp"), route))
+        pieces.append(flipped(output_weight, "tok", 1) if parity else output_weight)
         halves.append(jnp.concatenate(pieces, axis=1))
     plane = jnp.concatenate(halves, axis=0)
     own = layer_norm(tokens, norm_gain[None, :], owners, capacity)
@@ -615,12 +618,11 @@
     while bit > 1:
         planes[bit] = flipped(plane, "tok", bit)
         bit //= 2
-
-    last_weight = output_weight
-    bit = PAIR
-    while 2 * bit < peers:
-        last_weight = merged(last_weight, flipped(last_weight, "tok", bit), "tok", bit, 0)
-        bit *= 2
+    for distance in range(PAIR, peers, PAIR):
+        if distance not in planes:
+            step_bit = distance & -distance
+            planes[distance] = flipped(planes[distance ^ step_bit], "tok", step_bit)
+    weights = [planes[distance] for distance in range(0, peers, PAIR)]
 
     first_row = place // PAIR * group_rows
     padded_ids = jnp.concatenate(
@@ -632,27 +634,19 @@
     )
     window_ids = lax.dynamic_slice_in_dim(padded_ids, first_row, group_rows + 2 * SPAN, 0)
     window_ids, plane = lax.optimization_barrier((window_ids, plane))
-    bounds = document_bounds(window_ids, group_rows)
-    starts, ends = bounds[0][0], bounds[1][0]
-    positions = SPAN + jnp.arange(group_rows, dtype=jnp.int32) - starts
+    *bounds, ranges = document_bounds(window_ids, group_rows)
+    positions = SPAN + jnp.arange(group_rows, dtype=jnp.int32) - bounds[0][0]
     order = [(number * members + column) % PARTS for number in range(PARTS)]
     meta = jnp.stack([member, place] + order).astype(jnp.int32)
     cosine, sine = rope_tables(positions)
-    across, along, sibling, planes, last_weight, cosine, sine, meta = lax.optimization_barrier(
-        (across, along, sibling, planes, last_weight, cosine, sine, meta)
-    )
-    other_planes = flipped(last_weight, "tok", bit)
+    across, along, sibling, weights, cosine, sine, meta = lax.optimization_barrier(
+        (across, along, sibling, weights, cosine, sine, meta)
+    )
 
     half, held = rows // 2, rows + EXTRA_ROWS
     corner = [flipped(across[:half], "tok", 1), flipped(along[half:], "grp", 2)]
     across_sibling = flipped(across, "grp", 1)
     along_sibling = flipped(along, "grp", 1)
-    for distance in range(PAIR, peers, PAIR):
-        if distance not in planes:
-            step_bit = distance & -distance
-            planes[distance] = flipped(planes[distance ^ step_bit], "tok", step_bit)
-    weights = [planes[distance] for distance in range(0, peers, PAIR)]
-    across_sibling, weights = lax.optimization_barrier((across_sibling, weights))
     near_blocks = [own, sibling, across, across_sibling]
     near_layout = [[(number, 0, held)] for number in range(4)]
     far_layout = [[(0, 0, held)], [(1, 0, held)]]
@@ -671,33 +665,28 @@
         return received.reshape((peers // PAIR, PAIR, members) + send.shape[2:])
 
     queries, pairs, send = project(meta, 0, near_layout, near_blocks, *sizes, ())
-    send, corner, along_sibling, other_planes = lax.optimization_barrier(
-        (send, corner, along_sibling, other_planes)
-    )
+    send, corner, along_sibling = lax.optimization_barrier((send, corner, along_sibling))
     own_row = to_owners(send)
     corner_sibling = [flipped(block, "grp", 1) for block in corner]
     far_blocks = [along, along_sibling] + corner + corner_sibling
+    columns = jnp.concatenate([held_rows[:, PARTS * width :] for held_rows in weights], axis=0)
+    row_order = place
+    if output_weight.shape[0] != width:
+        shards = columns.reshape((peers,) + output_weight.shape)
+        columns = shards[jnp.arange(peers) ^ place].reshape(columns.shape)
+        row_order = jnp.zeros_like(place)
     queries, pairs, send = project(meta, 4, far_layout, far_blocks, *sizes, (queries, pairs))
     before = shifted(pairs[group_rows - SPAN :], "tok", PAIR)
     after = shifted(pairs[:SPAN], "tok", -PAIR)
-    last_weight = merged(last_weight, other_planes, "tok", bit, 0)
-    last_weight = last_weight.reshape((peers // PAIR,) + output_weight.shape)
-    other_weight = flipped(last_weight, "tok", 1)
-
-    own_member = member[None].astype(jnp.int32)
-    ranges = jnp.stack(
-        [starts[::TILE] // TILE, (ends[TILE - 1 :: TILE] + TILE - 1) // TILE], axis=1
-    ).reshape(-1)
-    tile_meta = jnp.concatenate([own_member, ranges])
-    edges = attend_edges(tile_meta, queries, *bounds, pairs)
-    other_weight, before, after, edges, send = lax.optimization_barrier(
-        (other_weight, before, after, edges, send)
-    )
+    columns_across = flipped(columns, "grp", 2)
+
+    edges = attend_edges(meta, ranges, queries, *bounds, pairs)
+    send, edges = lax.optimization_barrier((send, edges))
     other_row = to_owners(send)
-    columns = merged(last_weight, other_weight, "tok", 1, 1).reshape(model_width, -1)
-    columns_across = flipped(columns, "grp", 2)
-    mixed = attend_finish(tile_meta, queries, *bounds, pairs, before, after, edges, rows)
-    mixed, columns_across = lax.optimization_barrier((mixed, columns_across))
+    before, after, edges, columns_across = lax.optimization_barrier(
+        (before, after, edges, columns_across)
+    )
+    mixed = attend_finish(meta, ranges, queries, *bounds, pairs, before, after, edges, rows)
     last_weights = [columns, flipped(columns, "grp", 1)]
     last_weights += [columns_across, flipped(columns_across, "grp", 1)]
     parts = [mixed[0]] + [
@@ -708,11 +697,12 @@
         )
         for distance in range(1, blocks)
     ]
-    attended = output_projection(own_member, parts, last_weights)
-
     cache_pages = unpack(own_row, other_row).reshape(
         peers * capacity, 2 * PAGE * model_width
     )
+    parts, cache_pages = lax.optimization_barrier((parts, cache_pages))
+    output_meta = jnp.stack([member, row_order]).astype(jnp.int32)
+    attended = output_projection(output_meta, parts, last_weights)
     return attended, cache_pages
 
 

time: 166 us -> 199 us (1.20)
  waiting for transfers between devices: 31.9 us -> 59.3 us
  Pallas kernels: 74 us -> 77.1 us
  starting transfers between devices: 43 us -> 45.8 us
    ppermute x18 -> x16, waiting for transfers between devices: 19.6 us -> 36.9 us  [flipped(): lax.ppermute(value, axis, [(source, source ^ bit) for source in range(cou...]
    ppermute x2, waiting for transfers between devices: 5.86 us -> 18.3 us  [shifted(): lax.ppermute(value, axis, [(source, source + steps) for source in range(i...]
    pallas_call x1, Pallas kernels: 20.7 us -> 25.7 us  [attend_edges(): pl.pallas_call(edge_kernel, grid_spec=pltpu.PrefetchScalarGridSpec(num_sc...]
    pallas_call x1, Pallas kernels: 25.1 us -> 22.7 us  [attend_finish(): pl.pallas_call(functools.partial(finish_kernel, edge), grid_spec=pltpu.Pr...]
    ppermute x7, waiting for transfers between devices: 6.37 us -> 4.14 us  [per_device(): lax.ppermute(mixed[distance], ('tok', 'grp'), [(source, source ^ distance...]
    ppermute x18 -> x16, starting transfers between devices: 10.4 us -> 12.4 us  [flipped(): lax.ppermute(value, axis, [(source, source ^ bit) for source in range(cou...]
  transfers between devices with their start and end apart: 35 -> 33, of which waited for: 10 -> 10; matrix products, arithmetic and copies ran while one was open for 6% -> 5% of each run, Pallas kernels for 44% -> 37%
where the time goes in v5:
time: 199 us; the launch traced here: 196 us
  Pallas kernels  77.1 us (39%)
  waiting for transfers between devices  59.3 us (30%)
  starting transfers between devices  45.8 us (23%)
  other arithmetic  6.83 us (3%)
  local copies, waits for them, and re-layouts  5.46 us (3%)
    ppermute x16, waiting for transfers between devices, flipped(): lax.ppermute(value, axis, [(source, source ^ bit) for source in range(cou...  36.9 us
    pallas_call x1, Pallas kernels, attend_edges(): pl.pallas_call(edge_kernel, grid_spec=pltpu.PrefetchScalarGridSpec(num_sc...  25.7 us
    pallas_call x1, Pallas kernels, attend_finish(): pl.pallas_call(functools.partial(finish_kernel, edge), grid_spec=pltpu.Pr...  22.7 us
    ppermute x2, waiting for transfers between devices, shifted(): lax.ppermute(value, axis, [(source, source + steps) for source in range(i...  18.3 us
    pallas_call x2, Pallas kernels, project(): pl.pallas_call(functools.partial(project_kernel, first, layout, len(weigh...  16.6 us
    ppermute x16, starting transfers between devices, flipped(): lax.ppermute(value, axis, [(source, source ^ bit) for source in range(cou...  12.4 us
    all_to_all x2, starting transfers between devices, to_owners(): lax.all_to_all(send.reshape((flat,) + send.shape[2:]), ('tok', 'grp'), sp...  10.6 us
    ppermute x6, starting transfers between devices, per_device(): pieces.append(lax.ppermute(piece, ('tok', 'grp'), route))  9.55 us
  transfers between devices with their start and end apart: 33, of which 10 were waited for; matrix products, arithmetic and copies ran while one was open for 5% of the time, Pallas kernels for 37%

profile of v5, /device:TPU:17, one launch (start us, length us, event | category | flops | bytes accessed | tf_op | source)
XLA Modules:
  0.0 195.5 jit_solution(13756814453847864504)
XLA Ops:
  0.6 1.3 collective-permute-start.6
  3.1 3.3 %collective-permute-start.4 = (bf16[128,128]{1,0:T(8,128)(2,1)S(1)}, bf16[128,128]{1,0:T(8,128)(2,1)S(1)}, u32[]{:S(2)}, u32[]{:S(2)}) collective-permute-start(bf16[128,128]{1,0:T(8,128)(2,1)S(1)} %get-tuple-element.123), channel_id=1, source_target_pairs={{0,5},{1,4},{2,7},{3,6},{4,1},{5,0},{6,3},{7,2},{8,13},{9,12},{10,... | collective-permute-start | bytes 98312 | tf_op jit(solution)/shard_map/ppermute | solution.py:607
  7.3 1.4 fusion.1
  8.6 2.0 %collective-permute-start.1 = (bf16[128,128]{1,0:T(8,128)(2,1)S(1)}, bf16[128,128]{1,0:T(8,128)(2,1)S(1)}, u32[]{:S(2)}, u32[]{:S(2)}) collective-permute-start(bf16[128,128]{1,0:T(8,128)(2,1)S(1)} %get-tuple-element.126), channel_id=1, source_target_pairs={{0,1},{1,0},{2,3},{3,2},{4,5},{5,4},{6,7},{7,6},{8,9},{9,8},{10,11... | collective-permute-start | bytes 98312 | tf_op jit(solution)/shard_map/ppermute | solution.py:607
  10.7 3.1 %collective-permute-start = (bf16[128,128]{1,0:T(8,128)(2,1)S(1)}, bf16[128,128]{1,0:T(8,128)(2,1)S(1)}, u32[]{:S(2)}, u32[]{:S(2)}) collective-permute-start(bf16[128,128]{1,0:T(8,128)(2,1)S(1)} %get-tuple-element.122), channel_id=1, source_target_pairs={{0,0},{1,3},{2,2},{3,1},{4,4},{5,7},{6,6},{7,5},{8,8},{9,11},{10,1... | collective-permute-start | bytes 98312 | tf_op jit(solution)/shard_map/ppermute | solution.py:607
  13.8 2.6 %layer_norm.1.refs_0_ = bf16[400,1024]{1,0:T(8,128)(2,1)} custom-call(bf16[384,1024]{1,0:T(8,128)(2,1)} %tokens.1, f32[1,1024]{1,0:T(1,128)} %bitcast.21, s32[1,96]{1,0:T(1,128)} %bitcast.22), custom_call_target="tpu_custom_call" | custom-call | tf_op jit(solution)/shard_map/layer_norm/pallas_call | solution.py:66
  18.1 1.3 collective-permute-start.10
  19.5 2.4 %document_bounds.1 = (s32[1,3072]{1,0:T(1,128)}, s32[1,3072]{1,0:T(1,128)}, s32[1,128]{1,0:T(1,128)}) custom-call(s32[1,5120]{1,0:T(1,128)} %bitcast.20), custom_call_target="tpu_custom_call" | custom-call | flops 17179869184 | tf_op jit(solution)/shard_map/document_bounds/pallas_call | solution.py:571
  22.6 11.2 %collective-permute-done.11.refs_6_.refs_8_ = bf16[256,640]{1,0:T(8,128)(2,1)S(1)} collective-permute-done((bf16[256,640]{1,0:T(8,128)(2,1)S(1)}, bf16[256,640]{1,0:T(8,128)(2,1)S(1)}, u32[]{:S(2)}, u32[]{:S(2)}) %collective-permute-start.11) | collective-permute-done | bytes 327712 | tf_op jit(solution)/shard_map/ppermute | solution.py:33
  33.9 2.3 %multiply_sine_fusion = (f32[32,3072]{1,0:T(8,128)}, f32[32,3072]{1,0:T(8,128)}) fusion(f32[3072]{0:T(1024)S(1)} %bitcast.19, f32[32]{0:T(128)S(1)} %negate_power_fusion), kind=kLoop, calls=%fused_computation | loop fusion | flops 98304 | bytes 798848 | tf_op jit(solution)/shard_map/sin | solution.py:535
  36.2 4.7 %collective-permute-done.12.refs_7_.refs_9_ = bf16[256,640]{1,0:T(8,128)(2,1)S(1)} collective-permute-done((bf16[256,640]{1,0:T(8,128)(2,1)S(1)}, bf16[256,640]{1,0:T(8,128)(2,1)S(1)}, u32[]{:S(2)}, u32[]{:S(2)}) %collective-permute-start.12) | collective-permute-done | bytes 327712 | tf_op jit(solution)/shard_map/ppermute | solution.py:33
  41.9 3.1 %collective-permute-start.13 = (bf16[400,1024]{1,0:T(8,128)(2,1)S(1)}, bf16[400,1024]{1,0:T(8,128)(2,1)}, u32[]{:S(2)}, u32[]{:S(2)}) collective-permute-start(bf16[400,1024]{1,0:T(8,128)(2,1)S(1)} %collective-permute-done.7.refs_2_), channel_id=1, source_target_pairs={{0,1},{1,0},{2,3},{3,2},{4,5},{5,4},{6,7},{7,6},{8,9},{9,8},{10,11... | collective-permute-start | bytes 2457608 | tf_op jit(solution)/shard_map/ppermute | solution.py:33
  46.0 1.2 collective-permute-start.15
  47.3 8.3 %project.2 = (bf16[3072,128]{1,0:T(8,128)(2,1)}, bf16[3072,256]{1,0:T(8,128)(2,1)}, bf16[8,4,24,1024]{3,2,1,0:T(8,128)(2,1)}) custom-call(s32[5]{0:T(128)} %stack.29.meta, bf16[400,1024]{1,0:T(8,128)(2,1)} %layer_norm.1.refs_0_, bf16[400,1024]{1,0:T(8,128)(2,1)} %copy-done.12, bf16[400,1024]{1,0:T(8,128)(2,1)} %copy-done.5, ...), custom_call_target="tpu_custom_call" | custom-call | flops 9663676416 | bytes 6291456 | tf_op jit(solution)/shard_map/project/pallas_call | solution.py:173
  56.7 5.8 %all-to-all-start = ((bf16[32,24,1024]{2,1,0:T(8,128)(2,1)}), bf16[32,24,1024]{2,1,0:T(8,128)(2,1)S(1)}, u32[]{:S(2)}, u32[]{:S(2)}) async-start(bf16[32,24,1024]{2,1,0:T(8,128)(2,1)} %bitcast.18), calls=%async_computation | async-start | bytes 3145728 | tf_op jit(solution)/shard_map/all_to_all | solution.py:658
  63.1 2.0 %collective-permute-done.17.refs_4_ = bf16[192,1024]{1,0:T(8,128)(2,1)S(1)} collective-permute-done((bf16[192,1024]{1,0:T(8,128)(2,1)}, bf16[192,1024]{1,0:T(8,128)(2,1)S(1)}, u32[]{:S(2)}, u32[]{:S(2)}) %collective-permute-start.17) | collective-permute-done | bytes 393248 | tf_op jit(solution)/shard_map/ppermute | solution.py:33
  66.0 8.3 %project.3 = (bf16[3072,128]{1,0:T(8,128)(2,1)}, bf16[3072,256]{1,0:T(8,128)(2,1)}, bf16[8,4,24,1024]{3,2,1,0:T(8,128)(2,1)}) custom-call(s32[5]{0:T(128)} %stack.29.meta, bf16[400,1024]{1,0:T(8,128)(2,1)} %copy-done.4, bf16[400,1024]{1,0:T(8,128)(2,1)} %collective-permute-done.16.refs_1_, ...), custom_call_target="tpu_custom_call", output_to_operand_aliasing={{0}: (13, {}), {1}: (14, {})} | custom-call | flops 9663676416 | bytes 6291456 | tf_op jit(solution)/shard_map/project/pallas_call | solution.py:173
  74.3 25.7 %attend_edges.1 = (f32[4,160,256]{2,1,0:T(8,128)}, f32[4,160,256]{2,1,0:T(8,128)}, f32[4,8,256]{2,1,0:T(8,128)}, f32[4,8,256]{2,1,0:T(8,128)}) custom-call(s32[5]{0:T(128)} %stack.29.meta, s32[1,128]{1,0:T(1,128)} %get-tuple-element.66.ranges, bf16[3072,128]{1,0:T(8,128)(2,1)} %get-tuple-element.82.refs_0_.refs_3_, ...), custom_call_target="tpu_custom_call" | custom-call | flops 6442450944 | bytes 5242880 | tf_op jit(solution)/shard_map/attend_edges/pallas_call | solution.py:403
  100.1 4.8 %all-to-all-start.1 = ((bf16[32,24,1024]{2,1,0:T(8,128)(2,1)}), bf16[32,24,1024]{2,1,0:T(8,128)(2,1)S(1)}, u32[]{:S(2)}, u32[]{:S(2)}) async-start(bf16[32,24,1024]{2,1,0:T(8,128)(2,1)} %bitcast.17), calls=%async_computation.1 | async-start | bytes 3145728 | tf_op jit(solution)/shard_map/all_to_all | solution.py:658
  107.7 1.2 collective-permute-start.21
  109.0 3.2 %collective-permute-start.19 = (bf16[1024,256]{1,0:T(8,128)(2,1)S(1)}, bf16[1024,256]{1,0:T(8,128)(2,1)S(1)}, u32[]{:S(2)}, u32[]{:S(2)}) collective-permute-start(bf16[1024,256]{1,0:T(8,128)(2,1)S(1)} %get-tuple-element.121), channel_id=1, source_target_pairs={{0,8},{4,12},{8,16},{12,20},{16,24},{20,28},{1,9},{5,13},{9,17},{1... | collective-permute-start | bytes 1572872 | tf_op jit(solution)/shard_map/ppermute | solution.py:39
  112.2 2.3 %collective-permute-start.20 = (bf16[1024,256]{1,0:T(8,128)(2,1)S(1)}, bf16[1024,256]{1,0:T(8,128)(2,1)S(1)}, u32[]{:S(2)}, u32[]{:S(2)}) collective-permute-start(bf16[1024,256]{1,0:T(8,128)(2,1)S(1)} %get-tuple-element.120), channel_id=1, source_target_pairs={{8,0},{12,4},{16,8},{20,12},{24,16},{28,20},{9,1},{13,5},{17,9},{2... | collective-permute-start | bytes 1572872 | tf_op jit(solution)/shard_map/ppermute | solution.py:39
  114.5 1.3 collective-permute-start.29
  115.7 17.8 %collective-permute-done.21.refs_10_ = bf16[1024,256]{1,0:T(8,128)(2,1)} collective-permute-done((bf16[1024,256]{1,0:T(8,128)(2,1)}, bf16[1024,256]{1,0:T(8,128)(2,1)}, u32[]{:S(2)}, u32[]{:S(2)}) %collective-permute-start.21) | collective-permute-done | bytes 524320 | tf_op jit(solution)/shard_map/ppermute | solution.py:33
  133.6 18.3 %collective-permute-done.19.refs_7_ = bf16[1024,256]{1,0:T(8,128)(2,1)S(1)} collective-permute-done((bf16[1024,256]{1,0:T(8,128)(2,1)S(1)}, bf16[1024,256]{1,0:T(8,128)(2,1)S(1)}, u32[]{:S(2)}, u32[]{:S(2)}) %collective-permute-start.19) | collective-permute-done | bytes 524320 | tf_op jit(solution)/shard_map/ppermute | solution.py:39
  153.1 22.7 %attend_finish.1 = (bf16[384,128]{1,0:T(8,128)(2,1)}, bf16[384,128]{1,0:T(8,128)(2,1)}, bf16[384,128]{1,0:T(8,128)(2,1)}, bf16[384,128]{1,0:T(8,128)(2,1)}, bf16...) custom-call(s32[5]{0:T(128)} %stack.29.meta, ...), custom_call_target="tpu_custom_call" | custom-call | flops 6442450944 | bytes 5242880 | tf_op jit(solution)/shard_map/attend_finish/pallas_call | solution.py:431
  178.9 1.4 collective-permute-done.23.refs_2_
  180.3 2.2 %collective-permute-start.26 = (bf16[384,128]{1,0:T(8,128)(2,1)}, bf16[384,128]{1,0:T(8,128)(2,1)}, u32[]{:S(2)}, u32[]{:S(2)}) collective-permute-start(bf16[384,128]{1,0:T(8,128)(2,1)} %get-tuple-element.105), channel_id=1, source_target_pairs={{0,5},{1,4},{2,7},{3,6},{4,1},{5,0},{6,3},{7,2},{8,13},{9,12},{10,... | collective-permute-start | bytes 294920 | tf_op jit(solution)/shard_map/ppermute | solution.py:693
  183.0 2.2 %collective-permute-start.27 = (bf16[384,128]{1,0:T(8,128)(2,1)}, bf16[384,128]{1,0:T(8,128)(2,1)}, u32[]{:S(2)}, u32[]{:S(2)}) collective-permute-start(bf16[384,128]{1,0:T(8,128)(2,1)} %get-tuple-element.106), channel_id=1, source_target_pairs={{0,6},{1,7},{2,4},{3,5},{4,2},{5,3},{6,0},{7,1},{8,14},{9,15},{10,... | collective-permute-start | bytes 294920 | tf_op jit(solution)/shard_map/ppermute | solution.py:693
  186.2 2.4 %unpack.1 = bf16[8,24,8192]{2,1,0:T(8,128)(2,1)} custom-call(bf16[4,2,4,24,1024]{4,3,2,1,0:T(8,128)(2,1)S(1)} %bitcast.14, bf16[4,2,4,24,1024]{4,3,2,1,0:T(8,128)(2,1)S(1)} %bitcast.15), custom_call_target="tpu_custom_call" | custom-call | bytes 6291456 | tf_op jit(solution)/shard_map/unpack/pallas_call | solution.py:517
  188.8 2.0 %collective-permute-done.28.refs_7_ = bf16[384,128]{1,0:T(8,128)(2,1)} collective-permute-done((bf16[384,128]{1,0:T(8,128)(2,1)}, bf16[384,128]{1,0:T(8,128)(2,1)}, u32[]{:S(2)}, u32[]{:S(2)}) %collective-permute-start.28) | collective-permute-done | bytes 98336 | tf_op jit(solution)/shard_map/ppermute | solution.py:693
  190.9 4.7 %output_projection.1 = bf16[384,1024]{1,0:T(8,128)(2,1)} custom-call(s32[2]{0:T(128)} %pad_add_fusion.meta, bf16[384,128]{1,0:T(8,128)(2,1)} %get-tuple-element.110.refs_0_, bf16[384,128]{1,0:T(8,128)(2,1)} %copy-done.6, bf16[384,128]{1,0:T(8,128)(2,1)} %copy-done.7, bf16[384,128]{1,0:T(8,128)(2,1)} %copy-done.8, bf16[384,128]{1,0:T(8,128)(2,1)} %copy-done.9, ...), custom_call_target="tpu_custom_call" | custom-call | flops 805306368 | bytes 4194304 | tf_op jit(solution)/shard_map/output_projection/pallas_call | solution.py:480
  (98 shorter events, 18.0 us)
Async XLA Ops:
  0.6 16.5 %collective-permute-start.6 = (bf16[128,256]{1,0:T(8,128)(2,1)}, bf16[128,256]{1,0:T(8,128)(2,1)S(1)}, u32[]{:S(2)}, u32[]{:S(2)}) collective-permute-start(bf16[128,256]{1,0:T(8,128)(2,1)} %param.9), channel_id=1, source_target_pairs={{0,4},{4,0},{8,12},{12,8},{16,20},{20,16},{24,28},{28,24},{1,5},{5... | collective-permute-start | bytes 196616 | tf_op jit(solution)/shard_map/ppermute | solution.py:33
  2.8 5.8 %collective-permute-start.5 = (bf16[128,128]{1,0:T(8,128)(2,1)S(1)}, bf16[128,128]{1,0:T(8,128)(2,1)S(1)}, u32[]{:S(2)}, u32[]{:S(2)}) collective-permute-start(bf16[128,128]{1,0:T(8,128)(2,1)S(1)} %get-tuple-element.125), channel_id=1, source_target_pairs={{0,6},{1,5},{2,4},{3,7},{4,2},{5,1},{6,0},{7,3},{8,14},{9,13},{10,... | collective-permute-start | bytes 98312 | tf_op jit(solution)/shard_map/ppermute | solution.py:607
  3.1 7.6 %collective-permute-start.4 = (bf16[128,128]{1,0:T(8,128)(2,1)S(1)}, bf16[128,128]{1,0:T(8,128)(2,1)S(1)}, u32[]{:S(2)}, u32[]{:S(2)}) collective-permute-start(bf16[128,128]{1,0:T(8,128)(2,1)S(1)} %get-tuple-element.123), channel_id=1, source_target_pairs={{0,5},{1,4},{2,7},{3,6},{4,1},{5,0},{6,3},{7,2},{8,13},{9,12},{10,... | collective-permute-start | bytes 98312 | tf_op jit(solution)/shard_map/ppermute | solution.py:607
  6.4 10.7 %collective-permute-start.3 = (bf16[128,128]{1,0:T(8,128)(2,1)S(1)}, bf16[128,128]{1,0:T(8,128)(2,1)S(1)}, u32[]{:S(2)}, u32[]{:S(2)}) collective-permute-start(bf16[128,128]{1,0:T(8,128)(2,1)S(1)} %get-tuple-element.124), channel_id=1, source_target_pairs={{0,4},{1,7},{2,6},{3,5},{4,0},{5,3},{6,2},{7,1},{8,12},{9,15},{10,... | collective-permute-start | bytes 98312 | tf_op jit(solution)/shard_map/ppermute | solution.py:607
  6.6 10.5 %collective-permute-start.2 = (bf16[128,128]{1,0:T(8,128)(2,1)S(1)}, bf16[128,128]{1,0:T(8,128)(2,1)S(1)}, u32[]{:S(2)}, u32[]{:S(2)}) collective-permute-start(bf16[128,128]{1,0:T(8,128)(2,1)S(1)} %get-tuple-element.127), channel_id=1, source_target_pairs={{0,2},{1,1},{2,0},{3,3},{4,6},{5,5},{6,4},{7,7},{8,10},{9,9},{10,8... | collective-permute-start | bytes 98312 | tf_op jit(solution)/shard_map/ppermute | solution.py:607
  8.6 8.5 %collective-permute-start.1 = (bf16[128,128]{1,0:T(8,128)(2,1)S(1)}, bf16[128,128]{1,0:T(8,128)(2,1)S(1)}, u32[]{:S(2)}, u32[]{:S(2)}) collective-permute-start(bf16[128,128]{1,0:T(8,128)(2,1)S(1)} %get-tuple-element.126), channel_id=1, source_target_pairs={{0,1},{1,0},{2,3},{3,2},{4,5},{5,4},{6,7},{7,6},{8,9},{9,8},{10,11... | collective-permute-start | bytes 98312 | tf_op jit(solution)/shard_map/ppermute | solution.py:607
  10.7 6.5 %collective-permute-start = (bf16[128,128]{1,0:T(8,128)(2,1)S(1)}, bf16[128,128]{1,0:T(8,128)(2,1)S(1)}, u32[]{:S(2)}, u32[]{:S(2)}) collective-permute-start(bf16[128,128]{1,0:T(8,128)(2,1)S(1)} %get-tuple-element.122), channel_id=1, source_target_pairs={{0,0},{1,3},{2,2},{3,1},{4,4},{5,7},{6,6},{7,5},{8,8},{9,11},{10,1... | collective-permute-start | bytes 98312 | tf_op jit(solution)/shard_map/ppermute | solution.py:607
  17.2 23.7 %collective-permute-start.7 = (bf16[400,1024]{1,0:T(8,128)(2,1)}, bf16[400,1024]{1,0:T(8,128)(2,1)S(1)}, u32[]{:S(2)}, u32[]{:S(2)}) collective-permute-start(bf16[400,1024]{1,0:T(8,128)(2,1)} %layer_norm.1.refs_0_), channel_id=1, source_target_pairs={{0,2},{1,3},{2,0},{3,1},{4,6},{5,7},{6,4},{7,5},{8,10},{9,11},{10,... | collective-permute-start | bytes 2457608 | tf_op jit(solution)/shard_map/ppermute | solution.py:33
  17.5 23.4 %collective-permute-start.8 = (bf16[400,1024]{1,0:T(8,128)(2,1)}, bf16[400,1024]{1,0:T(8,128)(2,1)S(1)}, u32[]{:S(2)}, u32[]{:S(2)}) collective-permute-start(bf16[400,1024]{1,0:T(8,128)(2,1)} %layer_norm.1.refs_0_), channel_id=1, source_target_pairs={{0,4},{4,0},{8,12},{12,8},{16,20},{20,16},{24,28},{28,24},{1,5},{5... | collective-permute-start | bytes 2457608 | tf_op jit(solution)/shard_map/ppermute | solution.py:33
  18.1 22.8 %collective-permute-start.9 = (bf16[400,1024]{1,0:T(8,128)(2,1)}, bf16[400,1024]{1,0:T(8,128)(2,1)S(1)}, u32[]{:S(2)}, u32[]{:S(2)}) collective-permute-start(bf16[400,1024]{1,0:T(8,128)(2,1)} %layer_norm.1.refs_0_), channel_id=1, source_target_pairs={{0,1},{1,0},{2,3},{3,2},{4,5},{5,4},{6,7},{7,6},{8,9},{9,8},{10,11... | collective-permute-start | bytes 2457608 | tf_op jit(solution)/shard_map/ppermute | solution.py:33
  18.1 18.1 %collective-permute-start.10 = (bf16[256,640]{1,0:T(8,128)(2,1)S(1)}, bf16[256,640]{1,0:T(8,128)(2,1)S(1)}, u32[]{:S(2)}, u32[]{:S(2)}) collective-permute-start(bf16[256,640]{1,0:T(8,128)(2,1)S(1)} %maximum_maximum_fusion.refs_4_.refs_6_), channel_id=1, source_target_pairs={{0,8},{4,12},{8,0},{12,4},{16,24},{20,28},{24,16},{28,20},{1,9},{5... | collective-permute-start | bytes 983048 | tf_op jit(solution)/shard_map/ppermute | solution.py:33
  19.4 14.4 %collective-permute-start.11 = (bf16[256,640]{1,0:T(8,128)(2,1)S(1)}, bf16[256,640]{1,0:T(8,128)(2,1)S(1)}, u32[]{:S(2)}, u32[]{:S(2)}) collective-permute-start(bf16[256,640]{1,0:T(8,128)(2,1)S(1)} %maximum_maximum_fusion.refs_4_.refs_6_), channel_id=1, source_target_pairs={{0,16},{4,20},{8,24},{12,28},{16,0},{20,4},{24,8},{28,12},{1,17},{... | collective-permute-start | bytes 983048 | tf_op jit(solution)/shard_map/ppermute | solution.py:33
  33.9 7.0 %collective-permute-start.12 = (bf16[256,640]{1,0:T(8,128)(2,1)S(1)}, bf16[256,640]{1,0:T(8,128)(2,1)S(1)}, u32[]{:S(2)}, u32[]{:S(2)}) collective-permute-start(bf16[256,640]{1,0:T(8,128)(2,1)S(1)} %collective-permute-done.11.refs_6_.refs_8_), channel_id=1, source_target_pairs={{0,8},{4,12},{8,0},{12,4},{16,24},{20,28},{24,16},{28,20},{1,9},{5... | collective-permute-start | bytes 983048 | tf_op jit(solution)/shard_map/ppermute | solution.py:33
  41.9 5.4 %collective-permute-start.13 = (bf16[400,1024]{1,0:T(8,128)(2,1)S(1)}, bf16[400,1024]{1,0:T(8,128)(2,1)}, u32[]{:S(2)}, u32[]{:S(2)}) collective-permute-start(bf16[400,1024]{1,0:T(8,128)(2,1)S(1)} %collective-permute-done.7.refs_2_), channel_id=1, source_target_pairs={{0,1},{1,0},{2,3},{3,2},{4,5},{5,4},{6,7},{7,6},{8,9},{9,8},{10,11... | collective-permute-start | bytes 2457608 | tf_op jit(solution)/shard_map/ppermute | solution.py:33
  45.1 11.6 %collective-permute-start.16 = (bf16[400,1024]{1,0:T(8,128)(2,1)S(1)}, bf16[400,1024]{1,0:T(8,128)(2,1)}, u32[]{:S(2)}, u32[]{:S(2)}) collective-permute-start(bf16[400,1024]{1,0:T(8,128)(2,1)S(1)} %collective-permute-done.8.refs_0_), channel_id=1, source_target_pairs={{0,1},{1,0},{2,3},{3,2},{4,5},{5,4},{6,7},{7,6},{8,9},{9,8},{10,11... | collective-permute-start | bytes 2457608 | tf_op jit(solution)/shard_map/ppermute | solution.py:33
  45.1 10.4 %collective-permute-start.14 = (bf16[192,1024]{1,0:T(8,128)(2,1)S(1)}, bf16[192,1024]{1,0:T(8,128)(2,1)}, u32[]{:S(2)}, u32[]{:S(2)}) collective-permute-start(bf16[192,1024]{1,0:T(8,128)(2,1)S(1)} %slice.54), channel_id=1, source_target_pairs={{0,4},{4,0},{8,12},{12,8},{16,20},{20,16},{24,28},{28,24},{1,5},{5... | collective-permute-start | bytes 1179656 | tf_op jit(solution)/shard_map/ppermute | solution.py:33
  46.0 10.6 %collective-permute-start.15 = (bf16[208,1024]{1,0:T(8,128)(2,1)S(1)}, bf16[208,1024]{1,0:T(8,128)(2,1)S(1)}, u32[]{:S(2)}, u32[]{:S(2)}) collective-permute-start(bf16[208,1024]{1,0:T(8,128)(2,1)S(1)} %slice.55), channel_id=1, source_target_pairs={{0,2},{1,3},{2,0},{3,1},{4,6},{5,7},{6,4},{7,5},{8,10},{9,11},{10,... | collective-permute-start | bytes 1277960 | tf_op jit(solution)/shard_map/ppermute | solution.py:33
  56.7 43.3 %all-to-all-start = ((bf16[32,24,1024]{2,1,0:T(8,128)(2,1)}), bf16[32,24,1024]{2,1,0:T(8,128)(2,1)S(1)}, u32[]{:S(2)}, u32[]{:S(2)}) async-start(bf16[32,24,1024]{2,1,0:T(8,128)(2,1)} %bitcast.18), calls=%async_computation | async-start | bytes 3145728 | tf_op jit(solution)/shard_map/all_to_all | solution.py:658
  62.5 2.6 %collective-permute-start.18 = (bf16[208,1024]{1,0:T(8,128)(2,1)S(1)}, bf16[208,1024]{1,0:T(8,128)(2,1)S(1)}, u32[]{:S(2)}, u32[]{:S(2)}) collective-permute-start(bf16[208,1024]{1,0:T(8,128)(2,1)S(1)} %collective-permute-done.15.refs_3_), channel_id=1, source_target_pairs={{0,1},{1,0},{2,3},{3,2},{4,5},{5,4},{6,7},{7,6},{8,9},{9,8},{10,11... | collective-permute-start | bytes 1277960 | tf_op jit(solution)/shard_map/ppermute | solution.py:33
  100.1 86.1 %all-to-all-start.1 = ((bf16[32,24,1024]{2,1,0:T(8,128)(2,1)}), bf16[32,24,1024]{2,1,0:T(8,128)(2,1)S(1)}, u32[]{:S(2)}, u32[]{:S(2)}) async-start(bf16[32,24,1024]{2,1,0:T(8,128)(2,1)} %bitcast.17), calls=%async_computation.1 | async-start | bytes 3145728 | tf_op jit(solution)/shard_map/all_to_all | solution.py:658
  107.7 25.8 %collective-permute-start.21 = (bf16[1024,256]{1,0:T(8,128)(2,1)}, bf16[1024,256]{1,0:T(8,128)(2,1)}, u32[]{:S(2)}, u32[]{:S(2)}) collective-permute-start(bf16[1024,256]{1,0:T(8,128)(2,1)} %pad_maximum_fusion.refs_8_), channel_id=1, source_target_pairs={{0,2},{1,3},{2,0},{3,1},{4,6},{5,7},{6,4},{7,5},{8,10},{9,11},{10,... | collective-permute-start | bytes 1572872 | tf_op jit(solution)/shard_map/ppermute | solution.py:33
  109.0 42.8 %collective-permute-start.19 = (bf16[1024,256]{1,0:T(8,128)(2,1)S(1)}, bf16[1024,256]{1,0:T(8,128)(2,1)S(1)}, u32[]{:S(2)}, u32[]{:S(2)}) collective-permute-start(bf16[1024,256]{1,0:T(8,128)(2,1)S(1)} %get-tuple-element.121), channel_id=1, source_target_pairs={{0,8},{4,12},{8,16},{12,20},{16,24},{20,28},{1,9},{5,13},{9,17},{1... | collective-permute-start | bytes 1572872 | tf_op jit(solution)/shard_map/ppermute | solution.py:39
  112.2 39.7 %collective-permute-start.20 = (bf16[1024,256]{1,0:T(8,128)(2,1)S(1)}, bf16[1024,256]{1,0:T(8,128)(2,1)S(1)}, u32[]{:S(2)}, u32[]{:S(2)}) collective-permute-start(bf16[1024,256]{1,0:T(8,128)(2,1)S(1)} %get-tuple-element.120), channel_id=1, source_target_pairs={{8,0},{12,4},{16,8},{20,12},{24,16},{28,20},{9,1},{13,5},{17,9},{2... | collective-permute-start | bytes 1572872 | tf_op jit(solution)/shard_map/ppermute | solution.py:39
  114.5 76.4 %collective-permute-start.29 = (bf16[1024,256]{1,0:T(8,128)(2,1)}, bf16[1024,256]{1,0:T(8,128)(2,1)}, u32[]{:S(2)}, u32[]{:S(2)}) collective-permute-start(bf16[1024,256]{1,0:T(8,128)(2,1)} %pad_maximum_fusion.refs_8_), channel_id=1, source_target_pairs={{0,1},{1,0},{2,3},{3,2},{4,5},{5,4},{6,7},{7,6},{8,9},{9,8},{10,11... | collective-permute-start | bytes 1572872 | tf_op jit(solution)/shard_map/ppermute | solution.py:33
  152.7 38.2 %collective-permute-start.30 = (bf16[1024,256]{1,0:T(8,128)(2,1)}, bf16[1024,256]{1,0:T(8,128)(2,1)}, u32[]{:S(2)}, u32[]{:S(2)}) collective-permute-start(bf16[1024,256]{1,0:T(8,128)(2,1)} %collective-permute-done.21.refs_10_), channel_id=1, source_target_pairs={{0,1},{1,0},{2,3},{3,2},{4,5},{5,4},{6,7},{7,6},{8,9},{9,8},{10,11... | collective-permute-start | bytes 1572872 | tf_op jit(solution)/shard_map/ppermute | solution.py:33
  175.8 2.2 %collective-permute-start.22 = (bf16[384,128]{1,0:T(8,128)(2,1)}, bf16[384,128]{1,0:T(8,128)(2,1)S(1)}, u32[]{:S(2)}, u32[]{:S(2)}) collective-permute-start(bf16[384,128]{1,0:T(8,128)(2,1)} %get-tuple-element.101), channel_id=1, source_target_pairs={{0,1},{1,0},{2,3},{3,2},{4,5},{5,4},{6,7},{7,6},{8,9},{9,8},{10,11... | collective-permute-start | bytes 294920 | tf_op jit(solution)/shard_map/ppermute | solution.py:693
  176.0 4.2 %collective-permute-start.23 = (bf16[384,128]{1,0:T(8,128)(2,1)}, bf16[384,128]{1,0:T(8,128)(2,1)S(1)}, u32[]{:S(2)}, u32[]{:S(2)}) collective-permute-start(bf16[384,128]{1,0:T(8,128)(2,1)} %get-tuple-element.102), channel_id=1, source_target_pairs={{0,2},{1,3},{2,0},{3,1},{4,6},{5,7},{6,4},{7,5},{8,10},{9,11},{10,... | collective-permute-start | bytes 294920 | tf_op jit(solution)/shard_map/ppermute | solution.py:693
  176.9 6.1 %collective-permute-start.24 = (bf16[384,128]{1,0:T(8,128)(2,1)}, bf16[384,128]{1,0:T(8,128)(2,1)S(1)}, u32[]{:S(2)}, u32[]{:S(2)}) collective-permute-start(bf16[384,128]{1,0:T(8,128)(2,1)} %get-tuple-element.103), channel_id=1, source_target_pairs={{0,3},{1,2},{2,1},{3,0},{4,7},{5,6},{6,5},{7,4},{8,11},{9,10},{10,... | collective-permute-start | bytes 294920 | tf_op jit(solution)/shard_map/ppermute | solution.py:693
  178.0 7.2 %collective-permute-start.25 = (bf16[384,128]{1,0:T(8,128)(2,1)}, bf16[384,128]{1,0:T(8,128)(2,1)S(1)}, u32[]{:S(2)}, u32[]{:S(2)}) collective-permute-start(bf16[384,128]{1,0:T(8,128)(2,1)} %get-tuple-element.104), channel_id=1, source_target_pairs={{0,4},{1,5},{2,6},{3,7},{4,0},{5,1},{6,2},{7,3},{8,12},{9,13},{10,... | collective-permute-start | bytes 294920 | tf_op jit(solution)/shard_map/ppermute | solution.py:693
  180.3 8.4 %collective-permute-start.26 = (bf16[384,128]{1,0:T(8,128)(2,1)}, bf16[384,128]{1,0:T(8,128)(2,1)}, u32[]{:S(2)}, u32[]{:S(2)}) collective-permute-start(bf16[384,128]{1,0:T(8,128)(2,1)} %get-tuple-element.105), channel_id=1, source_target_pairs={{0,5},{1,4},{2,7},{3,6},{4,1},{5,0},{6,3},{7,2},{8,13},{9,12},{10,... | collective-permute-start | bytes 294920 | tf_op jit(solution)/shard_map/ppermute | solution.py:693
  183.0 5.8 %collective-permute-start.27 = (bf16[384,128]{1,0:T(8,128)(2,1)}, bf16[384,128]{1,0:T(8,128)(2,1)}, u32[]{:S(2)}, u32[]{:S(2)}) collective-permute-start(bf16[384,128]{1,0:T(8,128)(2,1)} %get-tuple-element.106), channel_id=1, source_target_pairs={{0,6},{1,7},{2,4},{3,5},{4,2},{5,3},{6,0},{7,1},{8,14},{9,15},{10,... | collective-permute-start | bytes 294920 | tf_op jit(solution)/shard_map/ppermute | solution.py:693
  185.2 5.6 %collective-permute-start.28 = (bf16[384,128]{1,0:T(8,128)(2,1)}, bf16[384,128]{1,0:T(8,128)(2,1)}, u32[]{:S(2)}, u32[]{:S(2)}) collective-permute-start(bf16[384,128]{1,0:T(8,128)(2,1)} %get-tuple-element.107), channel_id=1, source_target_pairs={{0,7},{1,6},{2,5},{3,4},{4,3},{5,2},{6,1},{7,0},{8,15},{9,14},{10,... | collective-permute-start | bytes 294920 | tf_op jit(solution)/shard_map/ppermute | solution.py:693
  (21 other events, 131.4 us)

commit v6 on v5

--- a/solution.py
+++ b/solution.py
@@ -681,11 +681,10 @@
     columns_across = flipped(columns, "grp", 2)
 
     edges = attend_edges(meta, ranges, queries, *bounds, pairs)
-    send, edges = lax.optimization_barrier((send, edges))
+    before, after, edges, columns_across, send = lax.optimization_barrier(
+        (before, after, edges, columns_across, send)
+    )
     other_row = to_owners(send)
-    before, after, edges, columns_across = lax.optimization_barrier(
-        (before, after, edges, columns_across)
-    )
     mixed = attend_finish(meta, ranges, queries, *bounds, pairs, before, after, edges, rows)
     last_weights = [columns, flipped(columns, "grp", 1)]
     last_weights += [columns_across, flipped(columns_across, "grp", 1)]
@@ -697,12 +696,11 @@
         )
         for distance in range(1, blocks)
     ]
+    output_meta = jnp.stack([member, row_order]).astype(jnp.int32)
+    attended = output_projection(output_meta, parts, last_weights)
     cache_pages = unpack(own_row, other_row).reshape(
         peers * capacity, 2 * PAGE * model_width
     )
-    parts, cache_pages = lax.optimization_barrier((parts, cache_pages))
-    output_meta = jnp.stack([member, row_order]).astype(jnp.int32)
-    attended = output_projection(output_meta, parts, last_weights)
     return attended, cache_pages
 
 

time: 199 us -> 163 us (0.82)
  waiting for transfers between devices: 59.3 us -> 29.3 us
  Pallas kernels: 77.1 us -> 72.1 us
    ppermute x16, waiting for transfers between devices: 36.9 us -> 17 us  [flipped(): lax.ppermute(value, axis, [(source, source ^ bit) for source in range(cou...]
    ppermute x2, waiting for transfers between devices: 18.3 us -> 6.22 us  [shifted(): lax.ppermute(value, axis, [(source, source + steps) for source in range(i...]
    pallas_call x1, Pallas kernels: 25.7 us -> 20.7 us  [attend_edges(): pl.pallas_call(edge_kernel, grid_spec=pltpu.PrefetchScalarGridSpec(num_sc...]
  transfers between devices with their start and end apart: 33 -> 33, of which waited for: 10 -> 8; matrix products, arithmetic and copies ran while one was open for 5% -> 6% of each run, Pallas kernels for 37% -> 43%
where the time goes in v6:
time: 163 us; the launch traced here: 160 us
  Pallas kernels  72.1 us (44%)
  starting transfers between devices  46.4 us (28%)
  waiting for transfers between devices  29.3 us (18%)
  other arithmetic  6.03 us (4%)
  local copies, waits for them, and re-layouts  5.4 us (3%)
    pallas_call x1, Pallas kernels, attend_finish(): pl.pallas_call(functools.partial(finish_kernel, edge), grid_spec=pltpu.Pr...  22.7 us
    pallas_call x1, Pallas kernels, attend_edges(): pl.pallas_call(edge_kernel, grid_spec=pltpu.PrefetchScalarGridSpec(num_sc...  20.7 us
    ppermute x16, waiting for transfers between devices, flipped(): lax.ppermute(value, axis, [(source, source ^ bit) for source in range(cou...  17 us
    pallas_call x2, Pallas kernels, project(): pl.pallas_call(functools.partial(project_kernel, first, layout, len(weigh...  16.5 us
    ppermute x16, starting transfers between devices, flipped(): lax.ppermute(value, axis, [(source, source ^ bit) for source in range(cou...  11.4 us
    all_to_all x2, starting transfers between devices, to_owners(): lax.all_to_all(send.reshape((flat,) + send.shape[2:]), ('tok', 'grp'), sp...  10.9 us
    ppermute x6, starting transfers between devices, per_device(): pieces.append(lax.ppermute(piece, ('tok', 'grp'), route))  9.55 us
    ppermute x7, starting transfers between devices, per_device(): lax.ppermute(mixed[distance], ('tok', 'grp'), [(source, source ^ distance...  9.32 us
  transfers between devices with their start and end apart: 33, of which 8 were waited for; matrix products, arithmetic and copies ran while one was open for 6% of the time, Pallas kernels for 43%

profile of v6, /device:TPU:17, one launch (start us, length us, event | category | flops | bytes accessed | tf_op | source)
XLA Modules:
  0.0 160.2 jit_solution(8593843836267046505)
XLA Ops:
  0.6 1.3 collective-permute-start.6
  3.1 3.3 %collective-permute-start.4 = (bf16[128,128]{1,0:T(8,128)(2,1)S(1)}, bf16[128,128]{1,0:T(8,128)(2,1)S(1)}, u32[]{:S(2)}, u32[]{:S(2)}) collective-permute-start(bf16[128,128]{1,0:T(8,128)(2,1)S(1)} %get-tuple-element.97), channel_id=1, source_target_pairs={{0,5},{1,4},{2,7},{3,6},{4,1},{5,0},{6,3},{7,2},{8,13},{9,12},{10,... | collective-permute-start | bytes 98312 | tf_op jit(solution)/shard_map/ppermute | solution.py:607
  7.3 1.4 fusion.1
  8.6 2.0 %collective-permute-start.1 = (bf16[128,128]{1,0:T(8,128)(2,1)S(1)}, bf16[128,128]{1,0:T(8,128)(2,1)S(1)}, u32[]{:S(2)}, u32[]{:S(2)}) collective-permute-start(bf16[128,128]{1,0:T(8,128)(2,1)S(1)} %get-tuple-element.100), channel_id=1, source_target_pairs={{0,1},{1,0},{2,3},{3,2},{4,5},{5,4},{6,7},{7,6},{8,9},{9,8},{10,11... | collective-permute-start | bytes 98312 | tf_op jit(solution)/shard_map/ppermute | solution.py:607
  10.7 3.1 %collective-permute-start = (bf16[128,128]{1,0:T(8,128)(2,1)S(1)}, bf16[128,128]{1,0:T(8,128)(2,1)S(1)}, u32[]{:S(2)}, u32[]{:S(2)}) collective-permute-start(bf16[128,128]{1,0:T(8,128)(2,1)S(1)} %get-tuple-element.96), channel_id=1, source_target_pairs={{0,0},{1,3},{2,2},{3,1},{4,4},{5,7},{6,6},{7,5},{8,8},{9,11},{10,1... | collective-permute-start | bytes 98312 | tf_op jit(solution)/shard_map/ppermute | solution.py:607
  13.8 2.6 %layer_norm.1.refs_0_ = bf16[400,1024]{1,0:T(8,128)(2,1)} custom-call(bf16[384,1024]{1,0:T(8,128)(2,1)} %tokens.1, f32[1,1024]{1,0:T(1,128)} %bitcast.21, s32[1,96]{1,0:T(1,128)} %bitcast.22), custom_call_target="tpu_custom_call" | custom-call | tf_op jit(solution)/shard_map/layer_norm/pallas_call | solution.py:66
  18.2 1.3 collective-permute-start.10
  19.5 2.5 %document_bounds.1 = (s32[1,3072]{1,0:T(1,128)}, s32[1,3072]{1,0:T(1,128)}, s32[1,128]{1,0:T(1,128)}) custom-call(s32[1,5120]{1,0:T(1,128)} %bitcast.20), custom_call_target="tpu_custom_call" | custom-call | flops 17179869184 | tf_op jit(solution)/shard_map/document_bounds/pallas_call | solution.py:571
  22.7 11.2 %collective-permute-done.11.refs_6_.refs_8_ = bf16[256,640]{1,0:T(8,128)(2,1)S(1)} collective-permute-done((bf16[256,640]{1,0:T(8,128)(2,1)S(1)}, bf16[256,640]{1,0:T(8,128)(2,1)S(1)}, u32[]{:S(2)}, u32[]{:S(2)}) %collective-permute-start.11) | collective-permute-done | bytes 327712 | tf_op jit(solution)/shard_map/ppermute | solution.py:33
  33.9 2.3 %multiply_sine_fusion = (f32[32,3072]{1,0:T(8,128)}, f32[32,3072]{1,0:T(8,128)}) fusion(f32[3072]{0:T(1024)S(1)} %bitcast.19, f32[32]{0:T(128)S(1)} %negate_power_fusion), kind=kLoop, calls=%fused_computation | loop fusion | flops 98304 | bytes 798848 | tf_op jit(solution)/shard_map/sin | solution.py:535
  36.2 4.7 %collective-permute-done.12.refs_7_.refs_9_ = bf16[256,640]{1,0:T(8,128)(2,1)S(1)} collective-permute-done((bf16[256,640]{1,0:T(8,128)(2,1)S(1)}, bf16[256,640]{1,0:T(8,128)(2,1)S(1)}, u32[]{:S(2)}, u32[]{:S(2)}) %collective-permute-start.12) | collective-permute-done | bytes 327712 | tf_op jit(solution)/shard_map/ppermute | solution.py:33
  41.0 3.2 %collective-permute-start.13 = (bf16[400,1024]{1,0:T(8,128)(2,1)S(1)}, bf16[400,1024]{1,0:T(8,128)(2,1)}, u32[]{:S(2)}, u32[]{:S(2)}) collective-permute-start(bf16[400,1024]{1,0:T(8,128)(2,1)S(1)} %collective-permute-done.7.refs_2_), channel_id=1, source_target_pairs={{0,1},{1,0},{2,3},{3,2},{4,5},{5,4},{6,7},{7,6},{8,9},{9,8},{10,11... | collective-permute-start | bytes 2457608 | tf_op jit(solution)/shard_map/ppermute | solution.py:33
  45.2 1.2 collective-permute-start.15
  46.4 8.3 %project.2 = (bf16[3072,128]{1,0:T(8,128)(2,1)}, bf16[3072,256]{1,0:T(8,128)(2,1)}, bf16[8,4,24,1024]{3,2,1,0:T(8,128)(2,1)}) custom-call(s32[5]{0:T(128)} %stack.29.meta, bf16[400,1024]{1,0:T(8,128)(2,1)} %layer_norm.1.refs_0_, bf16[400,1024]{1,0:T(8,128)(2,1)} %collective-permute-done.9.refs_1_, bf16[400,1024]{1,0:T(8,128)(2,1)} %copy-done.7, ...), custom_call_target="tpu_custom_call" | custom-call | flops 9663676416 | bytes 6291456 | tf_op jit(solution)/shard_map/project/pallas_call | solution.py:173
  55.8 5.8 %all-to-all-start = ((bf16[32,24,1024]{2,1,0:T(8,128)(2,1)}), bf16[32,24,1024]{2,1,0:T(8,128)(2,1)S(1)}, u32[]{:S(2)}, u32[]{:S(2)}) async-start(bf16[32,24,1024]{2,1,0:T(8,128)(2,1)} %bitcast.18), calls=%async_computation | async-start | bytes 3145728 | tf_op jit(solution)/shard_map/all_to_all | solution.py:658
  64.1 1.2 collective-permute-start.21
  66.9 8.3 %project.3 = (bf16[3072,128]{1,0:T(8,128)(2,1)}, bf16[3072,256]{1,0:T(8,128)(2,1)}, bf16[8,4,24,1024]{3,2,1,0:T(8,128)(2,1)}) custom-call(s32[5]{0:T(128)} %stack.29.meta, bf16[400,1024]{1,0:T(8,128)(2,1)} %copy-done.6, bf16[400,1024]{1,0:T(8,128)(2,1)} %collective-permute-done.16.refs_1_, ...), custom_call_target="tpu_custom_call", output_to_operand_aliasing={{0}: (13, {}), {1}: (14, {})} | custom-call | flops 9663676416 | bytes 6291456 | tf_op jit(solution)/shard_map/project/pallas_call | solution.py:173
  75.2 1.3 fusion.2
  76.4 3.2 %collective-permute-start.19 = (bf16[1024,256]{1,0:T(8,128)(2,1)S(1)}, bf16[1024,256]{1,0:T(8,128)(2,1)}, u32[]{:S(2)}, u32[]{:S(2)}) collective-permute-start(bf16[1024,256]{1,0:T(8,128)(2,1)S(1)} %get-tuple-element.95), channel_id=1, source_target_pairs={{0,8},{4,12},{8,16},{12,20},{16,24},{20,28},{1,9},{5,13},{9,17},{1... | collective-permute-start | bytes 1572872 | tf_op jit(solution)/shard_map/ppermute | solution.py:39
  79.6 2.1 %collective-permute-start.20 = (bf16[1024,256]{1,0:T(8,128)(2,1)S(1)}, bf16[1024,256]{1,0:T(8,128)(2,1)}, u32[]{:S(2)}, u32[]{:S(2)}) collective-permute-start(bf16[1024,256]{1,0:T(8,128)(2,1)S(1)} %get-tuple-element.94), channel_id=1, source_target_pairs={{8,0},{12,4},{16,8},{20,12},{24,16},{28,20},{9,1},{13,5},{17,9},{2... | collective-permute-start | bytes 1572872 | tf_op jit(solution)/shard_map/ppermute | solution.py:39
  81.7 20.7 %attend_edges.1 = (f32[4,160,256]{2,1,0:T(8,128)}, f32[4,160,256]{2,1,0:T(8,128)}, f32[4,8,256]{2,1,0:T(8,128)}, f32[4,8,256]{2,1,0:T(8,128)}) custom-call(s32[5]{0:T(128)} %stack.29.meta, s32[1,128]{1,0:T(1,128)} %get-tuple-element.53.ranges, bf16[3072,128]{1,0:T(8,128)(2,1)} %get-tuple-element.69.refs_0_.refs_3_, ...), custom_call_target="tpu_custom_call" | custom-call | flops 6442450944 | bytes 5242880 | tf_op jit(solution)/shard_map/attend_edges/pallas_call | solution.py:403
  102.4 6.2 %collective-permute-done.19.refs_7_ = bf16[1024,256]{1,0:T(8,128)(2,1)} collective-permute-done((bf16[1024,256]{1,0:T(8,128)(2,1)S(1)}, bf16[1024,256]{1,0:T(8,128)(2,1)}, u32[]{:S(2)}, u32[]{:S(2)}) %collective-permute-start.19) | collective-permute-done | bytes 524320 | tf_op jit(solution)/shard_map/ppermute | solution.py:39
  108.6 5.1 %all-to-all-start.1 = ((bf16[32,24,1024]{2,1,0:T(8,128)(2,1)}), bf16[32,24,1024]{2,1,0:T(8,128)(2,1)S(1)}, u32[]{:S(2)}, u32[]{:S(2)}) async-start(bf16[32,24,1024]{2,1,0:T(8,128)(2,1)} %bitcast.17), calls=%async_computation.1 | async-start | bytes 3145728 | tf_op jit(solution)/shard_map/all_to_all | solution.py:658
  114.3 22.7 %attend_finish.1 = (bf16[384,128]{1,0:T(8,128)(2,1)}, bf16[384,128]{1,0:T(8,128)(2,1)}, bf16[384,128]{1,0:T(8,128)(2,1)}, bf16[384,128]{1,0:T(8,128)(2,1)}, bf16...) custom-call(s32[5]{0:T(128)} %stack.29.meta, ...), custom_call_target="tpu_custom_call" | custom-call | flops 6442450944 | bytes 5242880 | tf_op jit(solution)/shard_map/attend_finish/pallas_call | solution.py:431
  139.2 1.2 collective-permute-start.25
  140.9 1.7 %collective-permute-done.23.refs_2_ = bf16[384,128]{1,0:T(8,128)(2,1)S(1)} collective-permute-done((bf16[384,128]{1,0:T(8,128)(2,1)}, bf16[384,128]{1,0:T(8,128)(2,1)S(1)}, u32[]{:S(2)}, u32[]{:S(2)}) %collective-permute-start.23) | collective-permute-done | bytes 98336 | tf_op jit(solution)/shard_map/ppermute | solution.py:692
  142.7 3.6 %collective-permute-start.27 = (bf16[384,128]{1,0:T(8,128)(2,1)}, bf16[384,128]{1,0:T(8,128)(2,1)}, u32[]{:S(2)}, u32[]{:S(2)}) collective-permute-start(bf16[384,128]{1,0:T(8,128)(2,1)} %get-tuple-element.89), channel_id=1, source_target_pairs={{0,6},{1,7},{2,4},{3,5},{4,2},{5,3},{6,0},{7,1},{8,14},{9,15},{10,... | collective-permute-start | bytes 294920 | tf_op jit(solution)/shard_map/ppermute | solution.py:692
  146.8 1.8 %collective-permute-start.28 = (bf16[384,128]{1,0:T(8,128)(2,1)}, bf16[384,128]{1,0:T(8,128)(2,1)}, u32[]{:S(2)}, u32[]{:S(2)}) collective-permute-start(bf16[384,128]{1,0:T(8,128)(2,1)} %get-tuple-element.90), channel_id=1, source_target_pairs={{0,7},{1,6},{2,5},{3,4},{4,3},{5,2},{6,1},{7,0},{8,15},{9,14},{10,... | collective-permute-start | bytes 294920 | tf_op jit(solution)/shard_map/ppermute | solution.py:692
  149.2 1.8 %collective-permute-done.26.refs_5_ = bf16[384,128]{1,0:T(8,128)(2,1)} collective-permute-done((bf16[384,128]{1,0:T(8,128)(2,1)}, bf16[384,128]{1,0:T(8,128)(2,1)}, u32[]{:S(2)}, u32[]{:S(2)}) %collective-permute-start.26) | collective-permute-done | bytes 98336 | tf_op jit(solution)/shard_map/ppermute | solution.py:692
  151.0 2.0 %collective-permute-done.28.refs_7_ = bf16[384,128]{1,0:T(8,128)(2,1)} collective-permute-done((bf16[384,128]{1,0:T(8,128)(2,1)}, bf16[384,128]{1,0:T(8,128)(2,1)}, u32[]{:S(2)}, u32[]{:S(2)}) %collective-permute-start.28) | collective-permute-done | bytes 98336 | tf_op jit(solution)/shard_map/ppermute | solution.py:692
  153.1 4.7 %output_projection.1 = bf16[384,1024]{1,0:T(8,128)(2,1)} custom-call(s32[2]{0:T(128)} %pad_add_fusion.meta, bf16[384,128]{1,0:T(8,128)(2,1)} %get-tuple-element.83.refs_0_, bf16[384,128]{1,0:T(8,128)(2,1)} %copy-done.8, bf16[384,128]{1,0:T(8,128)(2,1)} %copy-done.9, bf16[384,128]{1,0:T(8,128)(2,1)} %copy-done.10, bf16[384,128]{1,0:T(8,128)(2,1)} %copy-done.11, ...), custom_call_target="tpu_custom_call" | custom-call | flops 805306368 | bytes 4194304 | tf_op jit(solution)/shard_map/output_projection/pallas_call | solution.py:480
  157.8 2.5 %unpack.1 = bf16[8,24,8192]{2,1,0:T(8,128)(2,1)} custom-call(bf16[4,2,4,24,1024]{4,3,2,1,0:T(8,128)(2,1)S(1)} %bitcast.14, bf16[4,2,4,24,1024]{4,3,2,1,0:T(8,128)(2,1)S(1)} %bitcast.15), custom_call_target="tpu_custom_call" | custom-call | bytes 6291456 | tf_op jit(solution)/shard_map/unpack/pallas_call | solution.py:517
  (96 shorter events, 15.1 us)
Async XLA Ops:
  0.6 16.5 %collective-permute-start.6 = (bf16[128,256]{1,0:T(8,128)(2,1)}, bf16[128,256]{1,0:T(8,128)(2,1)S(1)}, u32[]{:S(2)}, u32[]{:S(2)}) collective-permute-start(bf16[128,256]{1,0:T(8,128)(2,1)} %param.9), channel_id=1, source_target_pairs={{0,4},{4,0},{8,12},{12,8},{16,20},{20,16},{24,28},{28,24},{1,5},{5... | collective-permute-start | bytes 196616 | tf_op jit(solution)/shard_map/ppermute | solution.py:33
  2.8 5.8 %collective-permute-start.5 = (bf16[128,128]{1,0:T(8,128)(2,1)S(1)}, bf16[128,128]{1,0:T(8,128)(2,1)S(1)}, u32[]{:S(2)}, u32[]{:S(2)}) collective-permute-start(bf16[128,128]{1,0:T(8,128)(2,1)S(1)} %get-tuple-element.99), channel_id=1, source_target_pairs={{0,6},{1,5},{2,4},{3,7},{4,2},{5,1},{6,0},{7,3},{8,14},{9,13},{10,... | collective-permute-start | bytes 98312 | tf_op jit(solution)/shard_map/ppermute | solution.py:607
  3.1 7.6 %collective-permute-start.4 = (bf16[128,128]{1,0:T(8,128)(2,1)S(1)}, bf16[128,128]{1,0:T(8,128)(2,1)S(1)}, u32[]{:S(2)}, u32[]{:S(2)}) collective-permute-start(bf16[128,128]{1,0:T(8,128)(2,1)S(1)} %get-tuple-element.97), channel_id=1, source_target_pairs={{0,5},{1,4},{2,7},{3,6},{4,1},{5,0},{6,3},{7,2},{8,13},{9,12},{10,... | collective-permute-start | bytes 98312 | tf_op jit(solution)/shard_map/ppermute | solution.py:607
  6.4 10.7 %collective-permute-start.3 = (bf16[128,128]{1,0:T(8,128)(2,1)S(1)}, bf16[128,128]{1,0:T(8,128)(2,1)S(1)}, u32[]{:S(2)}, u32[]{:S(2)}) collective-permute-start(bf16[128,128]{1,0:T(8,128)(2,1)S(1)} %get-tuple-element.98), channel_id=1, source_target_pairs={{0,4},{1,7},{2,6},{3,5},{4,0},{5,3},{6,2},{7,1},{8,12},{9,15},{10,... | collective-permute-start | bytes 98312 | tf_op jit(solution)/shard_map/ppermute | solution.py:607
  6.6 10.5 %collective-permute-start.2 = (bf16[128,128]{1,0:T(8,128)(2,1)S(1)}, bf16[128,128]{1,0:T(8,128)(2,1)S(1)}, u32[]{:S(2)}, u32[]{:S(2)}) collective-permute-start(bf16[128,128]{1,0:T(8,128)(2,1)S(1)} %get-tuple-element.101), channel_id=1, source_target_pairs={{0,2},{1,1},{2,0},{3,3},{4,6},{5,5},{6,4},{7,7},{8,10},{9,9},{10,8... | collective-permute-start | bytes 98312 | tf_op jit(solution)/shard_map/ppermute | solution.py:607
  8.6 8.5 %collective-permute-start.1 = (bf16[128,128]{1,0:T(8,128)(2,1)S(1)}, bf16[128,128]{1,0:T(8,128)(2,1)S(1)}, u32[]{:S(2)}, u32[]{:S(2)}) collective-permute-start(bf16[128,128]{1,0:T(8,128)(2,1)S(1)} %get-tuple-element.100), channel_id=1, source_target_pairs={{0,1},{1,0},{2,3},{3,2},{4,5},{5,4},{6,7},{7,6},{8,9},{9,8},{10,11... | collective-permute-start | bytes 98312 | tf_op jit(solution)/shard_map/ppermute | solution.py:607
  10.7 6.5 %collective-permute-start = (bf16[128,128]{1,0:T(8,128)(2,1)S(1)}, bf16[128,128]{1,0:T(8,128)(2,1)S(1)}, u32[]{:S(2)}, u32[]{:S(2)}) collective-permute-start(bf16[128,128]{1,0:T(8,128)(2,1)S(1)} %get-tuple-element.96), channel_id=1, source_target_pairs={{0,0},{1,3},{2,2},{3,1},{4,4},{5,7},{6,6},{7,5},{8,8},{9,11},{10,1... | collective-permute-start | bytes 98312 | tf_op jit(solution)/shard_map/ppermute | solution.py:607
  17.2 23.7 %collective-permute-start.7 = (bf16[400,1024]{1,0:T(8,128)(2,1)}, bf16[400,1024]{1,0:T(8,128)(2,1)S(1)}, u32[]{:S(2)}, u32[]{:S(2)}) collective-permute-start(bf16[400,1024]{1,0:T(8,128)(2,1)} %layer_norm.1.refs_0_), channel_id=1, source_target_pairs={{0,2},{1,3},{2,0},{3,1},{4,6},{5,7},{6,4},{7,5},{8,10},{9,11},{10,... | collective-permute-start | bytes 2457608 | tf_op jit(solution)/shard_map/ppermute | solution.py:33
  17.5 23.4 %collective-permute-start.8 = (bf16[400,1024]{1,0:T(8,128)(2,1)}, bf16[400,1024]{1,0:T(8,128)(2,1)S(1)}, u32[]{:S(2)}, u32[]{:S(2)}) collective-permute-start(bf16[400,1024]{1,0:T(8,128)(2,1)} %layer_norm.1.refs_0_), channel_id=1, source_target_pairs={{0,4},{4,0},{8,12},{12,8},{16,20},{20,16},{24,28},{28,24},{1,5},{5... | collective-permute-start | bytes 2457608 | tf_op jit(solution)/shard_map/ppermute | solution.py:33
  18.2 22.8 %collective-permute-start.9 = (bf16[400,1024]{1,0:T(8,128)(2,1)}, bf16[400,1024]{1,0:T(8,128)(2,1)}, u32[]{:S(2)}, u32[]{:S(2)}) collective-permute-start(bf16[400,1024]{1,0:T(8,128)(2,1)} %layer_norm.1.refs_0_), channel_id=1, source_target_pairs={{0,1},{1,0},{2,3},{3,2},{4,5},{5,4},{6,7},{7,6},{8,9},{9,8},{10,11... | collective-permute-start | bytes 2457608 | tf_op jit(solution)/shard_map/ppermute | solution.py:33
  18.2 18.1 %collective-permute-start.10 = (bf16[256,640]{1,0:T(8,128)(2,1)S(1)}, bf16[256,640]{1,0:T(8,128)(2,1)S(1)}, u32[]{:S(2)}, u32[]{:S(2)}) collective-permute-start(bf16[256,640]{1,0:T(8,128)(2,1)S(1)} %maximum_maximum_fusion.refs_4_.refs_6_), channel_id=1, source_target_pairs={{0,8},{4,12},{8,0},{12,4},{16,24},{20,28},{24,16},{28,20},{1,9},{5... | collective-permute-start | bytes 983048 | tf_op jit(solution)/shard_map/ppermute | solution.py:33
  19.5 14.4 %collective-permute-start.11 = (bf16[256,640]{1,0:T(8,128)(2,1)S(1)}, bf16[256,640]{1,0:T(8,128)(2,1)S(1)}, u32[]{:S(2)}, u32[]{:S(2)}) collective-permute-start(bf16[256,640]{1,0:T(8,128)(2,1)S(1)} %maximum_maximum_fusion.refs_4_.refs_6_), channel_id=1, source_target_pairs={{0,16},{4,20},{8,24},{12,28},{16,0},{20,4},{24,8},{28,12},{1,17},{... | collective-permute-start | bytes 983048 | tf_op jit(solution)/shard_map/ppermute | solution.py:33
  33.9 7.0 %collective-permute-start.12 = (bf16[256,640]{1,0:T(8,128)(2,1)S(1)}, bf16[256,640]{1,0:T(8,128)(2,1)S(1)}, u32[]{:S(2)}, u32[]{:S(2)}) collective-permute-start(bf16[256,640]{1,0:T(8,128)(2,1)S(1)} %collective-permute-done.11.refs_6_.refs_8_), channel_id=1, source_target_pairs={{0,8},{4,12},{8,0},{12,4},{16,24},{20,28},{24,16},{28,20},{1,9},{5... | collective-permute-start | bytes 983048 | tf_op jit(solution)/shard_map/ppermute | solution.py:33
  41.0 5.4 %collective-permute-start.13 = (bf16[400,1024]{1,0:T(8,128)(2,1)S(1)}, bf16[400,1024]{1,0:T(8,128)(2,1)}, u32[]{:S(2)}, u32[]{:S(2)}) collective-permute-start(bf16[400,1024]{1,0:T(8,128)(2,1)S(1)} %collective-permute-done.7.refs_2_), channel_id=1, source_target_pairs={{0,1},{1,0},{2,3},{3,2},{4,5},{5,4},{6,7},{7,6},{8,9},{9,8},{10,11... | collective-permute-start | bytes 2457608 | tf_op jit(solution)/shard_map/ppermute | solution.py:33
  44.2 11.6 %collective-permute-start.16 = (bf16[400,1024]{1,0:T(8,128)(2,1)S(1)}, bf16[400,1024]{1,0:T(8,128)(2,1)}, u32[]{:S(2)}, u32[]{:S(2)}) collective-permute-start(bf16[400,1024]{1,0:T(8,128)(2,1)S(1)} %collective-permute-done.8.refs_0_), channel_id=1, source_target_pairs={{0,1},{1,0},{2,3},{3,2},{4,5},{5,4},{6,7},{7,6},{8,9},{9,8},{10,11... | collective-permute-start | bytes 2457608 | tf_op jit(solution)/shard_map/ppermute | solution.py:33
  44.3 10.4 %collective-permute-start.14 = (bf16[192,1024]{1,0:T(8,128)(2,1)S(1)}, bf16[192,1024]{1,0:T(8,128)(2,1)}, u32[]{:S(2)}, u32[]{:S(2)}) collective-permute-start(bf16[192,1024]{1,0:T(8,128)(2,1)S(1)} %slice.54), channel_id=1, source_target_pairs={{0,4},{4,0},{8,12},{12,8},{16,20},{20,16},{24,28},{28,24},{1,5},{5... | collective-permute-start | bytes 1179656 | tf_op jit(solution)/shard_map/ppermute | solution.py:33
  45.2 10.6 %collective-permute-start.15 = (bf16[208,1024]{1,0:T(8,128)(2,1)S(1)}, bf16[208,1024]{1,0:T(8,128)(2,1)S(1)}, u32[]{:S(2)}, u32[]{:S(2)}) collective-permute-start(bf16[208,1024]{1,0:T(8,128)(2,1)S(1)} %slice.55), channel_id=1, source_target_pairs={{0,2},{1,3},{2,0},{3,1},{4,6},{5,7},{6,4},{7,5},{8,10},{9,11},{10,... | collective-permute-start | bytes 1277960 | tf_op jit(solution)/shard_map/ppermute | solution.py:33
  55.8 52.8 %all-to-all-start = ((bf16[32,24,1024]{2,1,0:T(8,128)(2,1)}), bf16[32,24,1024]{2,1,0:T(8,128)(2,1)S(1)}, u32[]{:S(2)}, u32[]{:S(2)}) async-start(bf16[32,24,1024]{2,1,0:T(8,128)(2,1)} %bitcast.18), calls=%async_computation | async-start | bytes 3145728 | tf_op jit(solution)/shard_map/all_to_all | solution.py:658
  61.6 3.7 %collective-permute-start.18 = (bf16[208,1024]{1,0:T(8,128)(2,1)S(1)}, bf16[208,1024]{1,0:T(8,128)(2,1)S(1)}, u32[]{:S(2)}, u32[]{:S(2)}) collective-permute-start(bf16[208,1024]{1,0:T(8,128)(2,1)S(1)} %collective-permute-done.15.refs_3_), channel_id=1, source_target_pairs={{0,1},{1,0},{2,3},{3,2},{4,5},{5,4},{6,7},{7,6},{8,9},{9,8},{10,11... | collective-permute-start | bytes 1277960 | tf_op jit(solution)/shard_map/ppermute | solution.py:33
  64.1 38.3 %collective-permute-start.21 = (bf16[1024,256]{1,0:T(8,128)(2,1)S(1)}, bf16[1024,256]{1,0:T(8,128)(2,1)S(1)}, u32[]{:S(2)}, u32[]{:S(2)}) collective-permute-start(bf16[1024,256]{1,0:T(8,128)(2,1)S(1)} %pad_maximum_fusion.refs_8_), channel_id=1, source_target_pairs={{0,2},{1,3},{2,0},{3,1},{4,6},{5,7},{6,4},{7,5},{8,10},{9,11},{10,... | collective-permute-start | bytes 1572872 | tf_op jit(solution)/shard_map/ppermute | solution.py:33
  76.4 32.2 %collective-permute-start.19 = (bf16[1024,256]{1,0:T(8,128)(2,1)S(1)}, bf16[1024,256]{1,0:T(8,128)(2,1)}, u32[]{:S(2)}, u32[]{:S(2)}) collective-permute-start(bf16[1024,256]{1,0:T(8,128)(2,1)S(1)} %get-tuple-element.95), channel_id=1, source_target_pairs={{0,8},{4,12},{8,16},{12,20},{16,24},{20,28},{1,9},{5,13},{9,17},{1... | collective-permute-start | bytes 1572872 | tf_op jit(solution)/shard_map/ppermute | solution.py:39
  79.6 29.0 %collective-permute-start.20 = (bf16[1024,256]{1,0:T(8,128)(2,1)S(1)}, bf16[1024,256]{1,0:T(8,128)(2,1)}, u32[]{:S(2)}, u32[]{:S(2)}) collective-permute-start(bf16[1024,256]{1,0:T(8,128)(2,1)S(1)} %get-tuple-element.94), channel_id=1, source_target_pairs={{8,0},{12,4},{16,8},{20,12},{24,16},{28,20},{9,1},{13,5},{17,9},{2... | collective-permute-start | bytes 1572872 | tf_op jit(solution)/shard_map/ppermute | solution.py:39
  108.6 49.1 %all-to-all-start.1 = ((bf16[32,24,1024]{2,1,0:T(8,128)(2,1)}), bf16[32,24,1024]{2,1,0:T(8,128)(2,1)S(1)}, u32[]{:S(2)}, u32[]{:S(2)}) async-start(bf16[32,24,1024]{2,1,0:T(8,128)(2,1)} %bitcast.17), calls=%async_computation.1 | async-start | bytes 3145728 | tf_op jit(solution)/shard_map/all_to_all | solution.py:658
  113.7 25.5 %collective-permute-start.29 = (bf16[1024,256]{1,0:T(8,128)(2,1)}, bf16[1024,256]{1,0:T(8,128)(2,1)S(1)}, u32[]{:S(2)}, u32[]{:S(2)}) collective-permute-start(bf16[1024,256]{1,0:T(8,128)(2,1)} %copy-done), channel_id=1, source_target_pairs={{0,1},{1,0},{2,3},{3,2},{4,5},{5,4},{6,7},{7,6},{8,9},{9,8},{10,11... | collective-permute-start | bytes 1572872 | tf_op jit(solution)/shard_map/ppermute | solution.py:33
  114.2 38.9 %collective-permute-start.30 = (bf16[1024,256]{1,0:T(8,128)(2,1)}, bf16[1024,256]{1,0:T(8,128)(2,1)}, u32[]{:S(2)}, u32[]{:S(2)}) collective-permute-start(bf16[1024,256]{1,0:T(8,128)(2,1)} %copy-done.2), channel_id=1, source_target_pairs={{0,1},{1,0},{2,3},{3,2},{4,5},{5,4},{6,7},{7,6},{8,9},{9,8},{10,11... | collective-permute-start | bytes 1572872 | tf_op jit(solution)/shard_map/ppermute | solution.py:33
  137.0 3.4 %collective-permute-start.22 = (bf16[384,128]{1,0:T(8,128)(2,1)}, bf16[384,128]{1,0:T(8,128)(2,1)S(1)}, u32[]{:S(2)}, u32[]{:S(2)}) collective-permute-start(bf16[384,128]{1,0:T(8,128)(2,1)} %get-tuple-element.84), channel_id=1, source_target_pairs={{0,1},{1,0},{2,3},{3,2},{4,5},{5,4},{6,7},{7,6},{8,9},{9,8},{10,11... | collective-permute-start | bytes 294920 | tf_op jit(solution)/shard_map/ppermute | solution.py:692
  137.4 5.2 %collective-permute-start.23 = (bf16[384,128]{1,0:T(8,128)(2,1)}, bf16[384,128]{1,0:T(8,128)(2,1)S(1)}, u32[]{:S(2)}, u32[]{:S(2)}) collective-permute-start(bf16[384,128]{1,0:T(8,128)(2,1)} %get-tuple-element.85), channel_id=1, source_target_pairs={{0,2},{1,3},{2,0},{3,1},{4,6},{5,7},{6,4},{7,5},{8,10},{9,11},{10,... | collective-permute-start | bytes 294920 | tf_op jit(solution)/shard_map/ppermute | solution.py:692
  138.6 8.2 %collective-permute-start.24 = (bf16[384,128]{1,0:T(8,128)(2,1)}, bf16[384,128]{1,0:T(8,128)(2,1)S(1)}, u32[]{:S(2)}, u32[]{:S(2)}) collective-permute-start(bf16[384,128]{1,0:T(8,128)(2,1)} %get-tuple-element.86), channel_id=1, source_target_pairs={{0,3},{1,2},{2,1},{3,0},{4,7},{5,6},{6,5},{7,4},{8,11},{9,10},{10,... | collective-permute-start | bytes 294920 | tf_op jit(solution)/shard_map/ppermute | solution.py:692
  139.2 10.0 %collective-permute-start.25 = (bf16[384,128]{1,0:T(8,128)(2,1)}, bf16[384,128]{1,0:T(8,128)(2,1)S(1)}, u32[]{:S(2)}, u32[]{:S(2)}) collective-permute-start(bf16[384,128]{1,0:T(8,128)(2,1)} %get-tuple-element.87), channel_id=1, source_target_pairs={{0,4},{1,5},{2,6},{3,7},{4,0},{5,1},{6,2},{7,3},{8,12},{9,13},{10,... | collective-permute-start | bytes 294920 | tf_op jit(solution)/shard_map/ppermute | solution.py:692
  140.4 10.6 %collective-permute-start.26 = (bf16[384,128]{1,0:T(8,128)(2,1)}, bf16[384,128]{1,0:T(8,128)(2,1)}, u32[]{:S(2)}, u32[]{:S(2)}) collective-permute-start(bf16[384,128]{1,0:T(8,128)(2,1)} %get-tuple-element.88), channel_id=1, source_target_pairs={{0,5},{1,4},{2,7},{3,6},{4,1},{5,0},{6,3},{7,2},{8,13},{9,12},{10,... | collective-permute-start | bytes 294920 | tf_op jit(solution)/shard_map/ppermute | solution.py:692
  142.7 8.4 %collective-permute-start.27 = (bf16[384,128]{1,0:T(8,128)(2,1)}, bf16[384,128]{1,0:T(8,128)(2,1)}, u32[]{:S(2)}, u32[]{:S(2)}) collective-permute-start(bf16[384,128]{1,0:T(8,128)(2,1)} %get-tuple-element.89), channel_id=1, source_target_pairs={{0,6},{1,7},{2,4},{3,5},{4,2},{5,3},{6,0},{7,1},{8,14},{9,15},{10,... | collective-permute-start | bytes 294920 | tf_op jit(solution)/shard_map/ppermute | solution.py:692
  146.8 6.3 %collective-permute-start.28 = (bf16[384,128]{1,0:T(8,128)(2,1)}, bf16[384,128]{1,0:T(8,128)(2,1)}, u32[]{:S(2)}, u32[]{:S(2)}) collective-permute-start(bf16[384,128]{1,0:T(8,128)(2,1)} %get-tuple-element.90), channel_id=1, source_target_pairs={{0,7},{1,6},{2,5},{3,4},{4,3},{5,2},{6,1},{7,0},{8,15},{9,14},{10,... | collective-permute-start | bytes 294920 | tf_op jit(solution)/shard_map/ppermute | solution.py:692
  (20 other events, 160.1 us)

commit v7 on v6

--- a/solution.py
+++ b/solution.py
@@ -270,12 +270,11 @@
     return tuple(jnp.full((1, TILE), NEG_FILL, jnp.float32) for _ in range(heads))
 
 
-def edge_kernel(meta, ranges, *refs):
+def edge_kernel(edge, meta, ranges, *refs):
     rows, pairs, outs, (masked, values) = refs[:6], refs[6], refs[7:11], refs[11:]
     step = pl.program_id(0)
     width = rows[0].shape[1]
     heads = width // HEAD_DIM
-    edge = pl.num_programs(0)
     tiles = pairs.shape[0] // TILE
 
     @pl.when(step == 0)
@@ -312,7 +311,8 @@
 
 def finish_kernel(edge, meta, ranges, *refs):
     rows, pairs, halos, held, held_peaks = refs[:6], refs[6], refs[7:9], refs[9:11], refs[11:13]
-    outs, (masked, sums, mixed) = refs[13:-3], refs[-3:]
+    outs, (masked, sums, peaks_held, mixed) = refs[13:-4], refs[-4:]
+    held_steps = edge // 2
     step = pl.program_id(0)
     width = rows[0].shape[1]
     heads = width // HEAD_DIM
@@ -339,10 +339,19 @@
             )
         return jobs
 
-    @pl.when(step < edge)
+    @pl.when(step < held_steps)
     def _():
         for side in range(2):
             sums[side] = held[side][0]
+            peaks_held[side] = held_peaks[side][0]
+
+    @pl.when(step >= held_steps)
+    def _():
+        sums[...] = jnp.zeros_like(sums)
+        peaks = sweep(jobs_on((pairs, pairs), (edge, edge)), (fresh_peaks(heads),) * 2)
+        for side in range(2):
+            for head in range(heads):
+                peaks_held[side, head : head + 1, :] = peaks[side][head]
 
     reaches_back = ranges[0, 2 * places[0]] < edge
     reaches_ahead = ranges[0, 2 * places[1] + 1] > edge + tiles
@@ -350,15 +359,10 @@
     @pl.when((step < edge) & (reaches_back | reaches_ahead))
     def _():
         peaks = tuple(
-            tuple(held_peaks[side][0, head : head + 1, :] for head in range(heads))
+            tuple(peaks_held[side, head : head + 1, :] for head in range(heads))
             for side in range(2)
         )
         sweep(jobs_on(halos, (0, edge + tiles)), peaks)
-
-    @pl.when(step >= edge)
-    def _():
-        sums[...] = jnp.zeros_like(sums)
-        sweep(jobs_on((pairs, pairs), (edge, edge)), (fresh_peaks(heads), fresh_peaks(heads)))
 
     for side in range(2):
         parts = []
@@ -399,12 +403,13 @@
     group_rows, width = queries.shape
     heads = width // HEAD_DIM
     tiles, edge = group_rows // TILE, SPAN // TILE
-    shapes = [(edge, heads * HEAD_ROWS, TILE)] * 2 + [(edge, 8, TILE)] * 2
+    steps = edge // 2
+    shapes = [(steps, heads * HEAD_ROWS, TILE)] * 2 + [(steps, 8, TILE)] * 2
     return pl.pallas_call(
-        edge_kernel,
+        functools.partial(edge_kernel, edge),
         grid_spec=pltpu.PrefetchScalarGridSpec(
             num_scalar_prefetch=2,
-            grid=(edge,),
+            grid=(steps,),
             in_specs=attend_specs(width, edge, tiles),
             out_specs=[pl.BlockSpec((1,) + shape[1:], lambda i, m, r: (i, 0, 0)) for shape in shapes],
             scratch_shapes=[
@@ -436,13 +441,16 @@
             in_specs=attend_specs(width, edge, tiles)
             + [pl.BlockSpec((SPAN, 2 * width), lambda i, m, r: (0, 0))] * 2
             + [
-                pl.BlockSpec((1,) + part.shape[1:], lambda i, m, r: (jnp.minimum(i, edge - 1), 0, 0))
+                pl.BlockSpec(
+                    (1,) + part.shape[1:], lambda i, m, r: (jnp.minimum(i, edge // 2 - 1), 0, 0)
+                )
                 for part in held
             ],
             out_specs=[pl.BlockSpec((rows, width), lambda i, m, r: (0, 0))] * members,
             scratch_shapes=[
                 pltpu.VMEM((2, heads, width, TILE), jnp.bfloat16),
                 pltpu.VMEM((2, heads * HEAD_ROWS, TILE), jnp.float32),
+                pltpu.VMEM((2, 8, TILE), jnp.float32),
                 pltpu.VMEM((group_rows, width), jnp.bfloat16),
             ],
         ),
@@ -464,7 +472,9 @@
     for distance in range(members):
         source = meta[0] ^ distance
         head_pair = PAIR * (source % (members // PAIR)) + source // (members // PAIR)
-        columns = pl.ds(pl.multiple_of((head_pair ^ meta[1]) * width, width), width)
+        shard = head_pair ^ meta[1]
+        shard = jnp.where(meta[1] < 0, head_pair, shard // PAIR + shard % PAIR * (members // PAIR))
+        columns = pl.ds(pl.multiple_of(shard * width, width), width)
         mixed[:, columns] = parts[distance][...]
     for distance, weight in enumerate(weights):
         columns = pl.ds(pl.multiple_of((meta[0] % len(weights) ^ distance) * tile, tile), tile)
@@ -605,7 +615,6 @@
                 target = (row ^ parity) * members + (PARTS * column_from + number) % members
                 route.append((source, target))
             pieces.append(lax.ppermute(piece, ("tok", "grp"), route))
-        pieces.append(flipped(output_weight, "tok", 1) if parity else output_weight)
         halves.append(jnp.concatenate(pieces, axis=1))
     plane = jnp.concatenate(halves, axis=0)
     own = layer_norm(tokens, norm_gain[None, :], owners, capacity)
@@ -639,14 +648,24 @@
     order = [(number * members + column) % PARTS for number in range(PARTS)]
     meta = jnp.stack([member, place] + order).astype(jnp.int32)
     cosine, sine = rope_tables(positions)
-    across, along, sibling, weights, cosine, sine, meta = lax.optimization_barrier(
-        (across, along, sibling, weights, cosine, sine, meta)
-    )
+    last_rows = output_weight
+    bit = PAIR
+    while 4 * bit < peers:
+        last_rows = jnp.concatenate([last_rows, flipped(last_rows, "tok", bit)], axis=0)
+        bit *= 2
+    other_rows = flipped(last_rows, "tok", bit)
+    across, along, sibling, weights, last_rows, other_rows, cosine, sine, meta = (
+        lax.optimization_barrier(
+            (across, along, sibling, weights, last_rows, other_rows, cosine, sine, meta)
+        )
+    )
+    last_rows = jnp.concatenate([last_rows, other_rows], axis=0)
 
     half, held = rows // 2, rows + EXTRA_ROWS
     corner = [flipped(across[:half], "tok", 1), flipped(along[half:], "grp", 2)]
     across_sibling = flipped(across, "grp", 1)
     along_sibling = flipped(along, "grp", 1)
+    other_rows = flipped(last_rows, "tok", peers // 2)
     near_blocks = [own, sibling, across, across_sibling]
     near_layout = [[(number, 0, held)] for number in range(4)]
     far_layout = [[(0, 0, held)], [(1, 0, held)]]
@@ -665,26 +684,31 @@
         return received.reshape((peers // PAIR, PAIR, members) + send.shape[2:])
 
     queries, pairs, send = project(meta, 0, near_layout, near_blocks, *sizes, ())
-    send, corner, along_sibling = lax.optimization_barrier((send, corner, along_sibling))
+    send, corner, along_sibling, last_rows, other_rows = lax.optimization_barrier(
+        (send, corner, along_sibling, last_rows, other_rows)
+    )
     own_row = to_owners(send)
     corner_sibling = [flipped(block, "grp", 1) for block in corner]
     far_blocks = [along, along_sibling] + corner + corner_sibling
-    columns = jnp.concatenate([held_rows[:, PARTS * width :] for held_rows in weights], axis=0)
-    row_order = place
-    if output_weight.shape[0] != width:
-        shards = columns.reshape((peers,) + output_weight.shape)
-        columns = shards[jnp.arange(peers) ^ place].reshape(columns.shape)
-        row_order = jnp.zeros_like(place)
+    last_rows = jnp.concatenate([last_rows, other_rows], axis=0)
     queries, pairs, send = project(meta, 4, far_layout, far_blocks, *sizes, (queries, pairs))
     before = shifted(pairs[group_rows - SPAN :], "tok", PAIR)
     after = shifted(pairs[:SPAN], "tok", -PAIR)
+    other_rows = flipped(last_rows, "tok", 1)
+
+    edges = attend_edges(meta, ranges, queries, *bounds, pairs)
+    before, after, edges, last_rows, other_rows, send = lax.optimization_barrier(
+        (before, after, edges, last_rows, other_rows, send)
+    )
+    other_row = to_owners(send)
+    columns = jnp.concatenate([last_rows, other_rows], axis=0)
+    row_order = place
+    if output_weight.shape[0] != width:
+        wanted = jnp.arange(peers) ^ place
+        shards = columns.reshape((peers,) + output_weight.shape)
+        columns = shards[wanted // PAIR + wanted % PAIR * (peers // PAIR)].reshape(columns.shape)
+        row_order = jnp.full_like(place, -1)
     columns_across = flipped(columns, "grp", 2)
-
-    edges = attend_edges(meta, ranges, queries, *bounds, pairs)
-    before, after, edges, columns_across, send = lax.optimization_barrier(
-        (before, after, edges, columns_across, send)
-    )
-    other_row = to_owners(send)
     mixed = attend_finish(meta, ranges, queries, *bounds, pairs, before, after, edges, rows)
     last_weights = [columns, flipped(columns, "grp", 1)]
     last_weights += [columns_across, flipped(columns_across, "grp", 1)]

time: 163 us -> 201 us (1.23); the launches traced: 160 us -> 202 us
  waiting for transfers between devices: 29.3 us -> 57.8 us
  Pallas kernels: 72.1 us -> 82.3 us
    ppermute x16 -> x18, waiting for transfers between devices: 17 us -> 37.3 us  [flipped(): lax.ppermute(value, axis, [(source, source ^ bit) for source in range(cou...]
    pallas_call x1, Pallas kernels: 22.7 us -> 40.2 us  [attend_finish(): pl.pallas_call(functools.partial(finish_kernel, edge), grid_spec=pltpu.Pr...]
    ppermute x2, waiting for transfers between devices: 6.22 us -> 14.7 us  [shifted(): lax.ppermute(value, axis, [(source, source + steps) for source in range(i...]
    pallas_call x1, Pallas kernels: 20.7 us -> 13.6 us  [attend_edges(): pl.pallas_call(functools.partial(edge_kernel, edge), grid_spec=pltpu.Pref...]
    ppermute x16 -> x18, starting transfers between devices: 11.4 us -> 14.2 us  [flipped(): lax.ppermute(value, axis, [(source, source ^ bit) for source in range(cou...]
    unnamed x34 -> x45, local copies, waits for them, and re-layouts: 1.55 us -> 4.19 us
  transfers between devices with their start and end apart: 33 -> 35, of which waited for: 8 -> 10; matrix products, arithmetic and copies ran while one was open for 6% -> 4% of each run, Pallas kernels for 43% -> 39%
where the time goes in v7:
time: 201 us; the launch traced here: 202 us
  Pallas kernels  82.3 us (41%)
  waiting for transfers between devices  57.8 us (29%)
  starting transfers between devices  48.3 us (24%)
  local copies, waits for them, and re-layouts  7.08 us (4%)
  other arithmetic  5.87 us (3%)
    pallas_call x1, Pallas kernels, attend_finish(): pl.pallas_call(functools.partial(finish_kernel, edge), grid_spec=pltpu.Pr...  40.2 us
    ppermute x18, waiting for transfers between devices, flipped(): lax.ppermute(value, axis, [(source, source ^ bit) for source in range(cou...  37.3 us
    pallas_call x2, Pallas kernels, project(): pl.pallas_call(functools.partial(project_kernel, first, layout, len(weigh...  16.4 us
    ppermute x2, waiting for transfers between devices, shifted(): lax.ppermute(value, axis, [(source, source + steps) for source in range(i...  14.7 us
    ppermute x18, starting transfers between devices, flipped(): lax.ppermute(value, axis, [(source, source ^ bit) for source in range(cou...  14.2 us
    pallas_call x1, Pallas kernels, attend_edges(): pl.pallas_call(functools.partial(edge_kernel, edge), grid_spec=pltpu.Pref...  13.6 us
    all_to_all x2, starting transfers between devices, to_owners(): lax.all_to_all(send.reshape((flat,) + send.shape[2:]), ('tok', 'grp'), sp...  10.5 us
    ppermute x6, starting transfers between devices, per_device(): pieces.append(lax.ppermute(piece, ('tok', 'grp'), route))  9.33 us
  transfers between devices with their start and end apart: 35, of which 10 were waited for; matrix products, arithmetic and copies ran while one was open for 4% of the time, Pallas kernels for 39%

profile of v7, /device:TPU:17, one launch (start us, length us, event | category | flops | bytes accessed | tf_op | source)
XLA Modules:
  0.0 202.4 jit_solution(909595429982446848)
XLA Ops:
  1.5 1.3 collective-permute-start.5
  2.8 2.0 collective-permute-start.4
  6.7 1.7 collective-permute-start.1
  8.4 1.3 fusion.1
  9.8 2.4 %collective-permute-start = (bf16[128,128]{1,0:T(8,128)(2,1)S(1)}, bf16[128,128]{1,0:T(8,128)(2,1)S(1)}, u32[]{:S(2)}, u32[]{:S(2)}) collective-permute-start(bf16[128,128]{1,0:T(8,128)(2,1)S(1)} %get-tuple-element.106), channel_id=1, source_target_pairs={{0,0},{1,3},{2,2},{3,1},{4,4},{5,7},{6,6},{7,5},{8,8},{9,11},{10,1... | collective-permute-start | bytes 98312 | tf_op jit(solution)/shard_map/ppermute | solution.py:617
  12.3 2.6 %layer_norm.1.refs_0_ = bf16[400,1024]{1,0:T(8,128)(2,1)} custom-call(bf16[384,1024]{1,0:T(8,128)(2,1)} %tokens.1, f32[1,1024]{1,0:T(1,128)} %bitcast.21, s32[1,96]{1,0:T(1,128)} %bitcast.22), custom_call_target="tpu_custom_call" | custom-call | tf_op jit(solution)/shard_map/layer_norm/pallas_call | solution.py:66
  15.5 1.3 collective-permute-start.12
  18.5 2.4 %document_bounds.1 = (s32[1,3072]{1,0:T(1,128)}, s32[1,3072]{1,0:T(1,128)}, s32[1,128]{1,0:T(1,128)}) custom-call(s32[1,5120]{1,0:T(1,128)} %bitcast.20), custom_call_target="tpu_custom_call" | custom-call | flops 17179869184 | tf_op jit(solution)/shard_map/document_bounds/pallas_call | solution.py:581
  21.8 5.4 %collective-permute-done.10.refs_6_.refs_8_ = bf16[256,384]{1,0:T(8,128)(2,1)S(1)} collective-permute-done((bf16[256,384]{1,0:T(8,128)(2,1)S(1)}, bf16[256,384]{1,0:T(8,128)(2,1)S(1)}, u32[]{:S(2)}, u32[]{:S(2)}) %collective-permute-start.10) | collective-permute-done | bytes 196640 | tf_op jit(solution)/shard_map/ppermute | solution.py:33
  27.2 2.5 %collective-permute-start.11 = (bf16[256,384]{1,0:T(8,128)(2,1)S(1)}, bf16[256,384]{1,0:T(8,128)(2,1)S(1)}, u32[]{:S(2)}, u32[]{:S(2)}) collective-permute-start(bf16[256,384]{1,0:T(8,128)(2,1)S(1)} %collective-permute-done.10.refs_6_.refs_8_), channel_id=1, source_target_pairs={{0,8},{4,12},{8,0},{12,4},{16,24},{20,28},{24,16},{28,20},{1,9},{5... | collective-permute-start | bytes 589832 | tf_op jit(solution)/shard_map/ppermute | solution.py:33
  29.7 2.3 %multiply_sine_fusion = (f32[32,3072]{1,0:T(8,128)}, f32[32,3072]{1,0:T(8,128)}) fusion(f32[3072]{0:T(1024)S(1)} %bitcast.19, f32[32]{0:T(128)S(1)} %negate_power_fusion), kind=kLoop, calls=%fused_computation | loop fusion | flops 98304 | bytes 798848 | tf_op jit(solution)/shard_map/sin | solution.py:545
  32.0 1.5 collective-permute-done.11.refs_7_.refs_9_
  33.5 2.6 %collective-permute-done.6.refs_2_ = bf16[400,1024]{1,0:T(8,128)(2,1)S(1)} collective-permute-done((bf16[400,1024]{1,0:T(8,128)(2,1)}, bf16[400,1024]{1,0:T(8,128)(2,1)S(1)}, u32[]{:S(2)}, u32[]{:S(2)}) %collective-permute-start.6) | collective-permute-done | bytes 819232 | tf_op jit(solution)/shard_map/ppermute | solution.py:33
  38.0 1.6 collective-permute-start.14
  39.6 2.2 %collective-permute-start.17 = (bf16[256,256]{1,0:T(8,128)(2,1)S(1)}, bf16[256,256]{1,0:T(8,128)(2,1)S(1)}, u32[]{:S(2)}, u32[]{:S(2)}) collective-permute-start(bf16[256,256]{1,0:T(8,128)(2,1)S(1)} %constant_dynamic-update-slice_fusion), channel_id=1, source_target_pairs={{0,16},{4,20},{8,24},{12,28},{16,0},{20,4},{24,8},{28,12},{1,17},{... | collective-permute-start | bytes 393224 | tf_op jit(solution)/shard_map/ppermute | solution.py:33
  41.8 8.2 %project.2 = (bf16[3072,128]{1,0:T(8,128)(2,1)}, bf16[3072,256]{1,0:T(8,128)(2,1)}, bf16[8,4,24,1024]{3,2,1,0:T(8,128)(2,1)}) custom-call(s32[5]{0:T(128)} %stack.29.meta, bf16[400,1024]{1,0:T(8,128)(2,1)} %layer_norm.1.refs_0_, bf16[400,1024]{1,0:T(8,128)(2,1)} %copy-done.14, bf16[400,1024]{1,0:T(8,128)(2,1)} %copy-done.4, ...), custom_call_target="tpu_custom_call" | custom-call | flops 9663676416 | bytes 6291456 | tf_op jit(solution)/shard_map/project/pallas_call | solution.py:173
  51.5 5.3 %all-to-all-start = ((bf16[32,24,1024]{2,1,0:T(8,128)(2,1)}), bf16[32,24,1024]{2,1,0:T(8,128)(2,1)S(1)}, u32[]{:S(2)}, u32[]{:S(2)}) async-start(bf16[32,24,1024]{2,1,0:T(8,128)(2,1)} %bitcast.18), calls=%async_computation | async-start | bytes 3145728 | tf_op jit(solution)/shard_map/all_to_all | solution.py:677
  57.4 1.3 collective-permute-start.22
  60.3 8.2 %project.3 = (bf16[3072,128]{1,0:T(8,128)(2,1)}, bf16[3072,256]{1,0:T(8,128)(2,1)}, bf16[8,4,24,1024]{3,2,1,0:T(8,128)(2,1)}) custom-call(s32[5]{0:T(128)} %stack.29.meta, bf16[400,1024]{1,0:T(8,128)(2,1)} %copy-done.2, bf16[400,1024]{1,0:T(8,128)(2,1)} %copy-done.13, ...), custom_call_target="tpu_custom_call", output_to_operand_aliasing={{0}: (13, {}), {1}: (14, {})} | custom-call | flops 9663676416 | bytes 6291456 | tf_op jit(solution)/shard_map/project/pallas_call | solution.py:173
  69.8 3.2 %collective-permute-start.20 = (bf16[1024,256]{1,0:T(8,128)(2,1)S(1)}, bf16[1024,256]{1,0:T(8,128)(2,1)S(1)}, u32[]{:S(2)}, u32[]{:S(2)}) collective-permute-start(bf16[1024,256]{1,0:T(8,128)(2,1)S(1)} %get-tuple-element.105), channel_id=1, source_target_pairs={{0,8},{4,12},{8,16},{12,20},{16,24},{20,28},{1,9},{5,13},{9,17},{1... | collective-permute-start | bytes 1572872 | tf_op jit(solution)/shard_map/ppermute | solution.py:39
  73.0 2.1 %collective-permute-start.21 = (bf16[1024,256]{1,0:T(8,128)(2,1)S(1)}, bf16[1024,256]{1,0:T(8,128)(2,1)}, u32[]{:S(2)}, u32[]{:S(2)}) collective-permute-start(bf16[1024,256]{1,0:T(8,128)(2,1)S(1)} %get-tuple-element.104), channel_id=1, source_target_pairs={{8,0},{12,4},{16,8},{20,12},{24,16},{28,20},{9,1},{13,5},{17,9},{2... | collective-permute-start | bytes 1572872 | tf_op jit(solution)/shard_map/ppermute | solution.py:39
  75.1 13.6 %attend_edges.1 = (f32[2,160,256]{2,1,0:T(8,128)}, f32[2,160,256]{2,1,0:T(8,128)}, f32[2,8,256]{2,1,0:T(8,128)}, f32[2,8,256]{2,1,0:T(8,128)}) custom-call(s32[5]{0:T(128)} %stack.29.meta, s32[1,128]{1,0:T(1,128)} %get-tuple-element.58.ranges, bf16[3072,128]{1,0:T(8,128)(2,1)} %get-tuple-element.76.refs_0_.refs_3_, ...), custom_call_target="tpu_custom_call" | custom-call | flops 6442450944 | bytes 5242880 | tf_op jit(solution)/shard_map/attend_edges/pallas_call | solution.py:408
  88.7 14.7 %collective-permute-done.20.refs_7_ = bf16[1024,256]{1,0:T(8,128)(2,1)S(1)} collective-permute-done((bf16[1024,256]{1,0:T(8,128)(2,1)S(1)}, bf16[1024,256]{1,0:T(8,128)(2,1)S(1)}, u32[]{:S(2)}, u32[]{:S(2)}) %collective-permute-start.20) | collective-permute-done | bytes 524320 | tf_op jit(solution)/shard_map/ppermute | solution.py:39
  104.2 5.2 %all-to-all-start.1 = ((bf16[32,24,1024]{2,1,0:T(8,128)(2,1)}), bf16[32,24,1024]{2,1,0:T(8,128)(2,1)S(1)}, u32[]{:S(2)}, u32[]{:S(2)}) async-start(bf16[32,24,1024]{2,1,0:T(8,128)(2,1)} %bitcast.17), calls=%async_computation.1 | async-start | bytes 3145728 | tf_op jit(solution)/shard_map/all_to_all | solution.py:677
  112.4 25.8 %collective-permute-done.31.refs_10_ = bf16[1024,256]{1,0:T(8,128)(2,1)} collective-permute-done((bf16[1024,256]{1,0:T(8,128)(2,1)S(1)}, bf16[1024,256]{1,0:T(8,128)(2,1)}, u32[]{:S(2)}, u32[]{:S(2)}) %collective-permute-start.31) | collective-permute-done | bytes 524320 | tf_op jit(solution)/shard_map/ppermute | solution.py:33
  139.0 40.2 %attend_finish.1 = (bf16[384,128]{1,0:T(8,128)(2,1)}, bf16[384,128]{1,0:T(8,128)(2,1)}, bf16[384,128]{1,0:T(8,128)(2,1)}, bf16[384,128]{1,0:T(8,128)(2,1)}, bf16...) custom-call(s32[5]{0:T(128)} %stack.29.meta, ...), custom_call_target="tpu_custom_call" | custom-call | flops 6442450944 | bytes 5242880 | tf_op jit(solution)/shard_map/attend_finish/pallas_call | solution.py:436
  179.4 2.0 collective-permute-start.25
  181.4 1.7 collective-permute-start.26
  183.5 3.8 %collective-permute-start.27 = (bf16[384,128]{1,0:T(8,128)(2,1)}, bf16[384,128]{1,0:T(8,128)(2,1)S(1)}, u32[]{:S(2)}, u32[]{:S(2)}) collective-permute-start(bf16[384,128]{1,0:T(8,128)(2,1)} %get-tuple-element.97), channel_id=1, source_target_pairs={{0,5},{1,4},{2,7},{3,6},{4,1},{5,0},{6,3},{7,2},{8,13},{9,12},{10,... | collective-permute-start | bytes 294920 | tf_op jit(solution)/shard_map/ppermute | solution.py:716
  189.1 5.4 %collective-permute-done.27.refs_5_ = bf16[384,128]{1,0:T(8,128)(2,1)S(1)} collective-permute-done((bf16[384,128]{1,0:T(8,128)(2,1)}, bf16[384,128]{1,0:T(8,128)(2,1)S(1)}, u32[]{:S(2)}, u32[]{:S(2)}) %collective-permute-start.27) | collective-permute-done | bytes 98336 | tf_op jit(solution)/shard_map/ppermute | solution.py:716
  195.2 4.7 %output_projection.1 = bf16[384,1024]{1,0:T(8,128)(2,1)} custom-call(s32[2]{0:T(128)} %pad_add_fusion.meta, bf16[384,128]{1,0:T(8,128)(2,1)} %get-tuple-element.92.refs_0_, bf16[384,128]{1,0:T(8,128)(2,1)} %copy-done.5, bf16[384,128]{1,0:T(8,128)(2,1)} %copy-done.6, bf16[384,128]{1,0:T(8,128)(2,1)} %copy-done.7, bf16[384,128]{1,0:T(8,128)(2,1)} %copy-done.8, ...), custom_call_target="tpu_custom_call" | custom-call | flops 805306368 | bytes 4194304 | tf_op jit(solution)/shard_map/output_projection/pallas_call | solution.py:490
  199.9 2.5 %unpack.1 = bf16[8,24,8192]{2,1,0:T(8,128)(2,1)} custom-call(bf16[4,2,4,24,1024]{4,3,2,1,0:T(8,128)(2,1)S(1)} %bitcast.14, bf16[4,2,4,24,1024]{4,3,2,1,0:T(8,128)(2,1)S(1)} %bitcast.15), custom_call_target="tpu_custom_call" | custom-call | bytes 6291456 | tf_op jit(solution)/shard_map/unpack/pallas_call | solution.py:527
  (107 shorter events, 20.4 us)
Async XLA Ops:
  1.5 8.3 %collective-permute-start.5 = (bf16[128,128]{1,0:T(8,128)(2,1)S(1)}, bf16[128,128]{1,0:T(8,128)(2,1)S(1)}, u32[]{:S(2)}, u32[]{:S(2)}) collective-permute-start(bf16[128,128]{1,0:T(8,128)(2,1)S(1)} %get-tuple-element.109), channel_id=1, source_target_pairs={{0,6},{1,5},{2,4},{3,7},{4,2},{5,1},{6,0},{7,3},{8,14},{9,13},{10,... | collective-permute-start | bytes 98312 | tf_op jit(solution)/shard_map/ppermute | solution.py:617
  2.8 12.6 %collective-permute-start.4 = (bf16[128,128]{1,0:T(8,128)(2,1)S(1)}, bf16[128,128]{1,0:T(8,128)(2,1)S(1)}, u32[]{:S(2)}, u32[]{:S(2)}) collective-permute-start(bf16[128,128]{1,0:T(8,128)(2,1)S(1)} %get-tuple-element.107), channel_id=1, source_target_pairs={{0,5},{1,4},{2,7},{3,6},{4,1},{5,0},{6,3},{7,2},{8,13},{9,12},{10,... | collective-permute-start | bytes 98312 | tf_op jit(solution)/shard_map/ppermute | solution.py:617
  4.8 11.9 %collective-permute-start.3 = (bf16[128,128]{1,0:T(8,128)(2,1)S(1)}, bf16[128,128]{1,0:T(8,128)(2,1)S(1)}, u32[]{:S(2)}, u32[]{:S(2)}) collective-permute-start(bf16[128,128]{1,0:T(8,128)(2,1)S(1)} %get-tuple-element.108), channel_id=1, source_target_pairs={{0,4},{1,7},{2,6},{3,5},{4,0},{5,3},{6,2},{7,1},{8,12},{9,15},{10,... | collective-permute-start | bytes 98312 | tf_op jit(solution)/shard_map/ppermute | solution.py:617
  6.0 10.7 %collective-permute-start.2 = (bf16[128,128]{1,0:T(8,128)(2,1)S(1)}, bf16[128,128]{1,0:T(8,128)(2,1)S(1)}, u32[]{:S(2)}, u32[]{:S(2)}) collective-permute-start(bf16[128,128]{1,0:T(8,128)(2,1)S(1)} %get-tuple-element.111), channel_id=1, source_target_pairs={{0,2},{1,1},{2,0},{3,3},{4,6},{5,5},{6,4},{7,7},{8,10},{9,9},{10,8... | collective-permute-start | bytes 98312 | tf_op jit(solution)/shard_map/ppermute | solution.py:617
  6.7 10.1 %collective-permute-start.1 = (bf16[128,128]{1,0:T(8,128)(2,1)S(1)}, bf16[128,128]{1,0:T(8,128)(2,1)S(1)}, u32[]{:S(2)}, u32[]{:S(2)}) collective-permute-start(bf16[128,128]{1,0:T(8,128)(2,1)S(1)} %get-tuple-element.110), channel_id=1, source_target_pairs={{0,1},{1,0},{2,3},{3,2},{4,5},{5,4},{6,7},{7,6},{8,9},{9,8},{10,11... | collective-permute-start | bytes 98312 | tf_op jit(solution)/shard_map/ppermute | solution.py:617
  9.8 7.0 %collective-permute-start = (bf16[128,128]{1,0:T(8,128)(2,1)S(1)}, bf16[128,128]{1,0:T(8,128)(2,1)S(1)}, u32[]{:S(2)}, u32[]{:S(2)}) collective-permute-start(bf16[128,128]{1,0:T(8,128)(2,1)S(1)} %get-tuple-element.106), channel_id=1, source_target_pairs={{0,0},{1,3},{2,2},{3,1},{4,4},{5,7},{6,6},{7,5},{8,8},{9,11},{10,1... | collective-permute-start | bytes 98312 | tf_op jit(solution)/shard_map/ppermute | solution.py:617
  15.5 6.1 %collective-permute-start.12 = (bf16[128,256]{1,0:T(8,128)(2,1)S(1)}, bf16[128,256]{1,0:T(8,128)(2,1)S(1)}, u32[]{:S(2)}, u32[]{:S(2)}) collective-permute-start(bf16[128,256]{1,0:T(8,128)(2,1)S(1)} %copy-done.12), channel_id=1, source_target_pairs={{0,8},{4,12},{8,0},{12,4},{16,24},{20,28},{24,16},{28,20},{1,9},{5... | collective-permute-start | bytes 196616 | tf_op jit(solution)/shard_map/ppermute | solution.py:33
  16.8 19.3 %collective-permute-start.6 = (bf16[400,1024]{1,0:T(8,128)(2,1)}, bf16[400,1024]{1,0:T(8,128)(2,1)S(1)}, u32[]{:S(2)}, u32[]{:S(2)}) collective-permute-start(bf16[400,1024]{1,0:T(8,128)(2,1)} %layer_norm.1.refs_0_), channel_id=1, source_target_pairs={{0,2},{1,3},{2,0},{3,1},{4,6},{5,7},{6,4},{7,5},{8,10},{9,11},{10,... | collective-permute-start | bytes 2457608 | tf_op jit(solution)/shard_map/ppermute | solution.py:33
  17.8 19.1 %collective-permute-start.7 = (bf16[400,1024]{1,0:T(8,128)(2,1)}, bf16[400,1024]{1,0:T(8,128)(2,1)S(1)}, u32[]{:S(2)}, u32[]{:S(2)}) collective-permute-start(bf16[400,1024]{1,0:T(8,128)(2,1)} %layer_norm.1.refs_0_), channel_id=1, source_target_pairs={{0,4},{4,0},{8,12},{12,8},{16,20},{20,16},{24,28},{28,24},{1,5},{5... | collective-permute-start | bytes 2457608 | tf_op jit(solution)/shard_map/ppermute | solution.py:33
  18.4 18.5 %collective-permute-start.8 = (bf16[400,1024]{1,0:T(8,128)(2,1)}, bf16[400,1024]{1,0:T(8,128)(2,1)S(1)}, u32[]{:S(2)}, u32[]{:S(2)}) collective-permute-start(bf16[400,1024]{1,0:T(8,128)(2,1)} %layer_norm.1.refs_0_), channel_id=1, source_target_pairs={{0,1},{1,0},{2,3},{3,2},{4,5},{5,4},{6,7},{7,6},{8,9},{9,8},{10,11... | collective-permute-start | bytes 2457608 | tf_op jit(solution)/shard_map/ppermute | solution.py:33
  18.4 8.8 %collective-permute-start.10 = (bf16[256,384]{1,0:T(8,128)(2,1)S(1)}, bf16[256,384]{1,0:T(8,128)(2,1)S(1)}, u32[]{:S(2)}, u32[]{:S(2)}) collective-permute-start(bf16[256,384]{1,0:T(8,128)(2,1)S(1)} %maximum_maximum_fusion.refs_4_.refs_6_), channel_id=1, source_target_pairs={{0,16},{4,20},{8,24},{12,28},{16,0},{20,4},{24,8},{28,12},{1,17},{... | collective-permute-start | bytes 589832 | tf_op jit(solution)/shard_map/ppermute | solution.py:33
  21.6 10.4 %collective-permute-start.9 = (bf16[256,384]{1,0:T(8,128)(2,1)S(1)}, bf16[256,384]{1,0:T(8,128)(2,1)S(1)}, u32[]{:S(2)}, u32[]{:S(2)}) collective-permute-start(bf16[256,384]{1,0:T(8,128)(2,1)S(1)} %maximum_maximum_fusion.refs_4_.refs_6_), channel_id=1, source_target_pairs={{0,8},{4,12},{8,0},{12,4},{16,24},{20,28},{24,16},{28,20},{1,9},{5... | collective-permute-start | bytes 589832 | tf_op jit(solution)/shard_map/ppermute | solution.py:33
  27.2 6.3 %collective-permute-start.11 = (bf16[256,384]{1,0:T(8,128)(2,1)S(1)}, bf16[256,384]{1,0:T(8,128)(2,1)S(1)}, u32[]{:S(2)}, u32[]{:S(2)}) collective-permute-start(bf16[256,384]{1,0:T(8,128)(2,1)S(1)} %collective-permute-done.10.refs_6_.refs_8_), channel_id=1, source_target_pairs={{0,8},{4,12},{8,0},{12,4},{16,24},{20,28},{24,16},{28,20},{1,9},{5... | collective-permute-start | bytes 589832 | tf_op jit(solution)/shard_map/ppermute | solution.py:33
  36.9 4.9 %collective-permute-start.13 = (bf16[400,1024]{1,0:T(8,128)(2,1)S(1)}, bf16[400,1024]{1,0:T(8,128)(2,1)}, u32[]{:S(2)}, u32[]{:S(2)}) collective-permute-start(bf16[400,1024]{1,0:T(8,128)(2,1)S(1)} %collective-permute-done.6.refs_2_), channel_id=1, source_target_pairs={{0,1},{1,0},{2,3},{3,2},{4,5},{5,4},{6,7},{7,6},{8,9},{9,8},{10,11... | collective-permute-start | bytes 2457608 | tf_op jit(solution)/shard_map/ppermute | solution.py:33
  37.9 12.7 %collective-permute-start.16 = (bf16[400,1024]{1,0:T(8,128)(2,1)S(1)}, bf16[400,1024]{1,0:T(8,128)(2,1)S(1)}, u32[]{:S(2)}, u32[]{:S(2)}) collective-permute-start(bf16[400,1024]{1,0:T(8,128)(2,1)S(1)} %collective-permute-done.7.refs_0_), channel_id=1, source_target_pairs={{0,1},{1,0},{2,3},{3,2},{4,5},{5,4},{6,7},{7,6},{8,9},{9,8},{10,11... | collective-permute-start | bytes 2457608 | tf_op jit(solution)/shard_map/ppermute | solution.py:33
  38.0 12.1 %collective-permute-start.14 = (bf16[192,1024]{1,0:T(8,128)(2,1)S(1)}, bf16[192,1024]{1,0:T(8,128)(2,1)}, u32[]{:S(2)}, u32[]{:S(2)}) collective-permute-start(bf16[192,1024]{1,0:T(8,128)(2,1)S(1)} %slice.42), channel_id=1, source_target_pairs={{0,4},{4,0},{8,12},{12,8},{16,20},{20,16},{24,28},{28,24},{1,5},{5... | collective-permute-start | bytes 1179656 | tf_op jit(solution)/shard_map/ppermute | solution.py:33
  39.5 11.1 %collective-permute-start.15 = (bf16[208,1024]{1,0:T(8,128)(2,1)S(1)}, bf16[208,1024]{1,0:T(8,128)(2,1)}, u32[]{:S(2)}, u32[]{:S(2)}) collective-permute-start(bf16[208,1024]{1,0:T(8,128)(2,1)S(1)} %slice.43), channel_id=1, source_target_pairs={{0,2},{1,3},{2,0},{3,1},{4,6},{5,7},{6,4},{7,5},{8,10},{9,11},{10,... | collective-permute-start | bytes 1277960 | tf_op jit(solution)/shard_map/ppermute | solution.py:33
  39.6 10.5 %collective-permute-start.17 = (bf16[256,256]{1,0:T(8,128)(2,1)S(1)}, bf16[256,256]{1,0:T(8,128)(2,1)S(1)}, u32[]{:S(2)}, u32[]{:S(2)}) collective-permute-start(bf16[256,256]{1,0:T(8,128)(2,1)S(1)} %constant_dynamic-update-slice_fusion), channel_id=1, source_target_pairs={{0,16},{4,20},{8,24},{12,28},{16,0},{20,4},{24,8},{28,12},{1,17},{... | collective-permute-start | bytes 393224 | tf_op jit(solution)/shard_map/ppermute | solution.py:33
  51.5 51.9 %all-to-all-start = ((bf16[32,24,1024]{2,1,0:T(8,128)(2,1)}), bf16[32,24,1024]{2,1,0:T(8,128)(2,1)S(1)}, u32[]{:S(2)}, u32[]{:S(2)}) async-start(bf16[32,24,1024]{2,1,0:T(8,128)(2,1)} %bitcast.18), calls=%async_computation | async-start | bytes 3145728 | tf_op jit(solution)/shard_map/all_to_all | solution.py:677
  57.4 31.3 %collective-permute-start.22 = (bf16[512,256]{1,0:T(8,128)(2,1)S(1)}, bf16[512,256]{1,0:T(8,128)(2,1)S(1)}, u32[]{:S(2)}, u32[]{:S(2)}) collective-permute-start(bf16[512,256]{1,0:T(8,128)(2,1)S(1)} %constant_dynamic-update-slice_fusion.2), channel_id=1, source_target_pairs={{0,4},{4,0},{8,12},{12,8},{16,20},{20,16},{24,28},{28,24},{1,5},{5... | collective-permute-start | bytes 786440 | tf_op jit(solution)/shard_map/ppermute | solution.py:33
  69.8 33.6 %collective-permute-start.20 = (bf16[1024,256]{1,0:T(8,128)(2,1)S(1)}, bf16[1024,256]{1,0:T(8,128)(2,1)S(1)}, u32[]{:S(2)}, u32[]{:S(2)}) collective-permute-start(bf16[1024,256]{1,0:T(8,128)(2,1)S(1)} %get-tuple-element.105), channel_id=1, source_target_pairs={{0,8},{4,12},{8,16},{12,20},{16,24},{20,28},{1,9},{5,13},{9,17},{1... | collective-permute-start | bytes 1572872 | tf_op jit(solution)/shard_map/ppermute | solution.py:39
  73.0 30.5 %collective-permute-start.21 = (bf16[1024,256]{1,0:T(8,128)(2,1)S(1)}, bf16[1024,256]{1,0:T(8,128)(2,1)}, u32[]{:S(2)}, u32[]{:S(2)}) collective-permute-start(bf16[1024,256]{1,0:T(8,128)(2,1)S(1)} %get-tuple-element.104), channel_id=1, source_target_pairs={{8,0},{12,4},{16,8},{20,12},{24,16},{28,20},{9,1},{13,5},{17,9},{2... | collective-permute-start | bytes 1572872 | tf_op jit(solution)/shard_map/ppermute | solution.py:39
  104.2 95.7 %all-to-all-start.1 = ((bf16[32,24,1024]{2,1,0:T(8,128)(2,1)}), bf16[32,24,1024]{2,1,0:T(8,128)(2,1)S(1)}, u32[]{:S(2)}, u32[]{:S(2)}) async-start(bf16[32,24,1024]{2,1,0:T(8,128)(2,1)} %bitcast.17), calls=%async_computation.1 | async-start | bytes 3145728 | tf_op jit(solution)/shard_map/all_to_all | solution.py:677
  110.5 27.6 %collective-permute-start.31 = (bf16[1024,256]{1,0:T(8,128)(2,1)S(1)}, bf16[1024,256]{1,0:T(8,128)(2,1)}, u32[]{:S(2)}, u32[]{:S(2)}) collective-permute-start(bf16[1024,256]{1,0:T(8,128)(2,1)S(1)} %constant_dynamic-update-slice_fusion.4.refs_8_), channel_id=1, source_target_pairs={{0,2},{1,3},{2,0},{3,1},{4,6},{5,7},{6,4},{7,5},{8,10},{9,11},{10,... | collective-permute-start | bytes 1572872 | tf_op jit(solution)/shard_map/ppermute | solution.py:33
  111.7 82.8 %collective-permute-start.30 = (bf16[1024,256]{1,0:T(8,128)(2,1)S(1)}, bf16[1024,256]{1,0:T(8,128)(2,1)}, u32[]{:S(2)}, u32[]{:S(2)}) collective-permute-start(bf16[1024,256]{1,0:T(8,128)(2,1)S(1)} %constant_dynamic-update-slice_fusion.4.refs_8_), channel_id=1, source_target_pairs={{0,1},{1,0},{2,3},{3,2},{4,5},{5,4},{6,7},{7,6},{8,9},{9,8},{10,11... | collective-permute-start | bytes 1572872 | tf_op jit(solution)/shard_map/ppermute | solution.py:33
  138.1 57.0 %collective-permute-start.32 = (bf16[1024,256]{1,0:T(8,128)(2,1)}, bf16[1024,256]{1,0:T(8,128)(2,1)}, u32[]{:S(2)}, u32[]{:S(2)}) collective-permute-start(bf16[1024,256]{1,0:T(8,128)(2,1)} %collective-permute-done.31.refs_10_), channel_id=1, source_target_pairs={{0,1},{1,0},{2,3},{3,2},{4,5},{5,4},{6,7},{7,6},{8,9},{9,8},{10,11... | collective-permute-start | bytes 1572872 | tf_op jit(solution)/shard_map/ppermute | solution.py:33
  179.2 4.2 %collective-permute-start.24 = (bf16[384,128]{1,0:T(8,128)(2,1)}, bf16[384,128]{1,0:T(8,128)(2,1)S(1)}, u32[]{:S(2)}, u32[]{:S(2)}) collective-permute-start(bf16[384,128]{1,0:T(8,128)(2,1)} %get-tuple-element.94), channel_id=1, source_target_pairs={{0,2},{1,3},{2,0},{3,1},{4,6},{5,7},{6,4},{7,5},{8,10},{9,11},{10,... | collective-permute-start | bytes 294920 | tf_op jit(solution)/shard_map/ppermute | solution.py:716
  179.4 7.9 %collective-permute-start.25 = (bf16[384,128]{1,0:T(8,128)(2,1)}, bf16[384,128]{1,0:T(8,128)(2,1)S(1)}, u32[]{:S(2)}, u32[]{:S(2)}) collective-permute-start(bf16[384,128]{1,0:T(8,128)(2,1)} %get-tuple-element.95), channel_id=1, source_target_pairs={{0,3},{1,2},{2,1},{3,0},{4,7},{5,6},{6,5},{7,4},{8,11},{9,10},{10,... | collective-permute-start | bytes 294920 | tf_op jit(solution)/shard_map/ppermute | solution.py:716
  181.4 6.5 %collective-permute-start.26 = (bf16[384,128]{1,0:T(8,128)(2,1)}, bf16[384,128]{1,0:T(8,128)(2,1)S(1)}, u32[]{:S(2)}, u32[]{:S(2)}) collective-permute-start(bf16[384,128]{1,0:T(8,128)(2,1)} %get-tuple-element.96), channel_id=1, source_target_pairs={{0,4},{1,5},{2,6},{3,7},{4,0},{5,1},{6,2},{7,3},{8,12},{9,13},{10,... | collective-permute-start | bytes 294920 | tf_op jit(solution)/shard_map/ppermute | solution.py:716
  183.5 11.0 %collective-permute-start.27 = (bf16[384,128]{1,0:T(8,128)(2,1)}, bf16[384,128]{1,0:T(8,128)(2,1)S(1)}, u32[]{:S(2)}, u32[]{:S(2)}) collective-permute-start(bf16[384,128]{1,0:T(8,128)(2,1)} %get-tuple-element.97), channel_id=1, source_target_pairs={{0,5},{1,4},{2,7},{3,6},{4,1},{5,0},{6,3},{7,2},{8,13},{9,12},{10,... | collective-permute-start | bytes 294920 | tf_op jit(solution)/shard_map/ppermute | solution.py:716
  187.2 7.3 %collective-permute-start.28 = (bf16[384,128]{1,0:T(8,128)(2,1)}, bf16[384,128]{1,0:T(8,128)(2,1)S(1)}, u32[]{:S(2)}, u32[]{:S(2)}) collective-permute-start(bf16[384,128]{1,0:T(8,128)(2,1)} %get-tuple-element.98), channel_id=1, source_target_pairs={{0,6},{1,7},{2,4},{3,5},{4,2},{5,3},{6,0},{7,1},{8,14},{9,15},{10,... | collective-permute-start | bytes 294920 | tf_op jit(solution)/shard_map/ppermute | solution.py:716
  187.9 6.6 %collective-permute-start.29 = (bf16[384,128]{1,0:T(8,128)(2,1)}, bf16[384,128]{1,0:T(8,128)(2,1)S(1)}, u32[]{:S(2)}, u32[]{:S(2)}) collective-permute-start(bf16[384,128]{1,0:T(8,128)(2,1)} %get-tuple-element.99), channel_id=1, source_target_pairs={{0,7},{1,6},{2,5},{3,4},{4,3},{5,2},{6,1},{7,0},{8,15},{9,14},{10,... | collective-permute-start | bytes 294920 | tf_op jit(solution)/shard_map/ppermute | solution.py:716
  (24 other events, 201.8 us)

commit v8 on v7

--- a/solution.py
+++ b/solution.py
@@ -312,7 +312,7 @@
 def finish_kernel(edge, meta, ranges, *refs):
     rows, pairs, halos, held, held_peaks = refs[:6], refs[6], refs[7:9], refs[9:11], refs[11:13]
     outs, (masked, sums, peaks_held, mixed) = refs[13:-4], refs[-4:]
-    held_steps = edge // 2
+    held_steps = edge
     step = pl.program_id(0)
     width = rows[0].shape[1]
     heads = width // HEAD_DIM
@@ -403,7 +403,7 @@
     group_rows, width = queries.shape
     heads = width // HEAD_DIM
     tiles, edge = group_rows // TILE, SPAN // TILE
-    steps = edge // 2
+    steps = edge
     shapes = [(steps, heads * HEAD_ROWS, TILE)] * 2 + [(steps, 8, TILE)] * 2
     return pl.pallas_call(
         functools.partial(edge_kernel, edge),
@@ -442,7 +442,7 @@
             + [pl.BlockSpec((SPAN, 2 * width), lambda i, m, r: (0, 0))] * 2
             + [
                 pl.BlockSpec(
-                    (1,) + part.shape[1:], lambda i, m, r: (jnp.minimum(i, edge // 2 - 1), 0, 0)
+                    (1,) + part.shape[1:], lambda i, m, r: (jnp.minimum(i, edge - 1), 0, 0)
                 )
                 for part in held
             ],
@@ -695,23 +695,34 @@
     before = shifted(pairs[group_rows - SPAN :], "tok", PAIR)
     after = shifted(pairs[:SPAN], "tok", -PAIR)
     other_rows = flipped(last_rows, "tok", 1)
+    across_rows = flipped(last_rows, "grp", 2)
+    corner_rows = lax.ppermute(
+        last_rows,
+        ("tok", "grp"),
+        [(source, source ^ (members + 2)) for source in range(flat)],
+    )
 
     edges = attend_edges(meta, ranges, queries, *bounds, pairs)
-    before, after, edges, last_rows, other_rows, send = lax.optimization_barrier(
-        (before, after, edges, last_rows, other_rows, send)
+    before, after, edges, last_rows, other_rows, across_rows, corner_rows, send = (
+        lax.optimization_barrier(
+            (before, after, edges, last_rows, other_rows, across_rows, corner_rows, send)
+        )
     )
     other_row = to_owners(send)
-    columns = jnp.concatenate([last_rows, other_rows], axis=0)
+    columns = [
+        jnp.concatenate([last_rows, other_rows], axis=0),
+        jnp.concatenate([across_rows, corner_rows], axis=0),
+    ]
     row_order = place
     if output_weight.shape[0] != width:
         wanted = jnp.arange(peers) ^ place
-        shards = columns.reshape((peers,) + output_weight.shape)
-        columns = shards[wanted // PAIR + wanted % PAIR * (peers // PAIR)].reshape(columns.shape)
+        wanted = wanted // PAIR + wanted % PAIR * (peers // PAIR)
+        shards = (peers,) + output_weight.shape
+        columns = [part.reshape(shards)[wanted].reshape(part.shape) for part in columns]
         row_order = jnp.full_like(place, -1)
-    columns_across = flipped(columns, "grp", 2)
     mixed = attend_finish(meta, ranges, queries, *bounds, pairs, before, after, edges, rows)
-    last_weights = [columns, flipped(columns, "grp", 1)]
-    last_weights += [columns_across, flipped(columns_across, "grp", 1)]
+    siblings = [flipped(part, "grp", 1) for part in columns]
+    last_weights = [columns[0], siblings[0], columns[1], siblings[1]]
     parts = [mixed[0]] + [
         lax.ppermute(
             mixed[distance],

time: 201 us -> 164 us (0.82)
  the two profiles are of different devices: /device:TPU:17 before, /device:TPU:9 now
where the time goes in v8:
time: 164 us; the launch traced here: 163 us
  Pallas kernels  77.7 us (47%)
  starting transfers between devices  49.8 us (30%)
  waiting for transfers between devices  20.1 us (12%)
  local copies, waits for them, and re-layouts  8.96 us (5%)
  other arithmetic  5.83 us (4%)
    pallas_call x1, Pallas kernels, attend_finish(): pl.pallas_call(functools.partial(finish_kernel, edge), grid_spec=pltpu.Pr...  25.1 us
    pallas_call x1, Pallas kernels, attend_edges(): pl.pallas_call(functools.partial(edge_kernel, edge), grid_spec=pltpu.Pref...  24 us
    pallas_call x2, Pallas kernels, project(): pl.pallas_call(functools.partial(project_kernel, first, layout, len(weigh...  16.4 us
    ppermute x18, starting transfers between devices, flipped(): lax.ppermute(value, axis, [(source, source ^ bit) for source in range(cou...  15.5 us
    all_to_all x2, starting transfers between devices, to_owners(): lax.all_to_all(send.reshape((flat,) + send.shape[2:]), ('tok', 'grp'), sp...  10.4 us
    ppermute x6, starting transfers between devices, per_device(): pieces.append(lax.ppermute(piece, ('tok', 'grp'), route))  9.33 us
    ppermute x7, waiting for transfers between devices, per_device(): lax.ppermute(mixed[distance], ('tok', 'grp'), [(source, source ^ distance...  8.55 us
    ppermute x7, starting transfers between devices, per_device(): lax.ppermute(mixed[distance], ('tok', 'grp'), [(source, source ^ distance...  8.22 us
  transfers between devices with their start and end apart: 36, of which 9 were waited for; matrix products, arithmetic and copies ran while one was open for 6% of the time, Pallas kernels for 46%

profile of v8, /device:TPU:9, one launch (start us, length us, event | category | flops | bytes accessed | tf_op | source)
XLA Modules:
  0.0 163.4 jit_solution(4136872893785104465)
XLA Ops:
  1.5 1.3 collective-permute-start.5
  2.8 2.0 %collective-permute-start.4 = (bf16[128,128]{1,0:T(8,128)(2,1)S(1)}, bf16[128,128]{1,0:T(8,128)(2,1)S(1)}, u32[]{:S(2)}, u32[]{:S(2)}) collective-permute-start(bf16[128,128]{1,0:T(8,128)(2,1)S(1)} %get-tuple-element.111), channel_id=1, source_target_pairs={{0,5},{1,4},{2,7},{3,6},{4,1},{5,0},{6,3},{7,2},{8,13},{9,12},{10,... | collective-permute-start | bytes 98312 | tf_op jit(solution)/shard_map/ppermute | solution.py:617
  6.7 1.7 %collective-permute-start.1 = (bf16[128,128]{1,0:T(8,128)(2,1)S(1)}, bf16[128,128]{1,0:T(8,128)(2,1)S(1)}, u32[]{:S(2)}, u32[]{:S(2)}) collective-permute-start(bf16[128,128]{1,0:T(8,128)(2,1)S(1)} %get-tuple-element.114), channel_id=1, source_target_pairs={{0,1},{1,0},{2,3},{3,2},{4,5},{5,4},{6,7},{7,6},{8,9},{9,8},{10,11... | collective-permute-start | bytes 98312 | tf_op jit(solution)/shard_map/ppermute | solution.py:617
  8.4 1.3 fusion.1
  9.8 2.4 %collective-permute-start = (bf16[128,128]{1,0:T(8,128)(2,1)S(1)}, bf16[128,128]{1,0:T(8,128)(2,1)S(1)}, u32[]{:S(2)}, u32[]{:S(2)}) collective-permute-start(bf16[128,128]{1,0:T(8,128)(2,1)S(1)} %get-tuple-element.110), channel_id=1, source_target_pairs={{0,0},{1,3},{2,2},{3,1},{4,4},{5,7},{6,6},{7,5},{8,8},{9,11},{10,1... | collective-permute-start | bytes 98312 | tf_op jit(solution)/shard_map/ppermute | solution.py:617
  12.3 2.6 %layer_norm.1.refs_0_ = bf16[400,1024]{1,0:T(8,128)(2,1)} custom-call(bf16[384,1024]{1,0:T(8,128)(2,1)} %tokens.1, f32[1,1024]{1,0:T(1,128)} %bitcast.21, s32[1,96]{1,0:T(1,128)} %bitcast.22), custom_call_target="tpu_custom_call" | custom-call | tf_op jit(solution)/shard_map/layer_norm/pallas_call | solution.py:66
  17.3 2.3 %collective-permute-start.10 = (bf16[256,384]{1,0:T(8,128)(2,1)S(1)}, bf16[256,384]{1,0:T(8,128)(2,1)S(1)}, u32[]{:S(2)}, u32[]{:S(2)}) collective-permute-start(bf16[256,384]{1,0:T(8,128)(2,1)S(1)} %maximum_maximum_fusion.refs_4_.refs_6_), channel_id=1, source_target_pairs={{0,16},{4,20},{8,24},{12,28},{16,0},{20,4},{24,8},{28,12},{1,17},{... | collective-permute-start | bytes 589832 | tf_op jit(solution)/shard_map/ppermute | solution.py:33
  19.6 2.4 %document_bounds.1 = (s32[1,3072]{1,0:T(1,128)}, s32[1,3072]{1,0:T(1,128)}, s32[1,128]{1,0:T(1,128)}) custom-call(s32[1,5120]{1,0:T(1,128)} %bitcast.20), custom_call_target="tpu_custom_call" | custom-call | flops 17179869184 | tf_op jit(solution)/shard_map/document_bounds/pallas_call | solution.py:581
  22.8 1.4 collective-permute-start.9
  24.1 3.5 %collective-permute-done.10.refs_6_.refs_8_ = bf16[256,384]{1,0:T(8,128)(2,1)S(1)} collective-permute-done((bf16[256,384]{1,0:T(8,128)(2,1)S(1)}, bf16[256,384]{1,0:T(8,128)(2,1)S(1)}, u32[]{:S(2)}, u32[]{:S(2)}) %collective-permute-start.10) | collective-permute-done | bytes 196640 | tf_op jit(solution)/shard_map/ppermute | solution.py:33
  27.7 2.8 %collective-permute-start.11 = (bf16[256,384]{1,0:T(8,128)(2,1)S(1)}, bf16[256,384]{1,0:T(8,128)(2,1)S(1)}, u32[]{:S(2)}, u32[]{:S(2)}) collective-permute-start(bf16[256,384]{1,0:T(8,128)(2,1)S(1)} %collective-permute-done.10.refs_6_.refs_8_), channel_id=1, source_target_pairs={{0,8},{4,12},{8,0},{12,4},{16,24},{20,28},{24,16},{28,20},{1,9},{5... | collective-permute-start | bytes 589832 | tf_op jit(solution)/shard_map/ppermute | solution.py:33
  30.5 2.3 %multiply_sine_fusion = (f32[32,3072]{1,0:T(8,128)}, f32[32,3072]{1,0:T(8,128)}) fusion(f32[3072]{0:T(1024)S(1)} %bitcast.19, f32[32]{0:T(128)S(1)} %negate_power_fusion), kind=kLoop, calls=%fused_computation | loop fusion | flops 98304 | bytes 798848 | tf_op jit(solution)/shard_map/sin | solution.py:545
  32.8 3.9 %collective-permute-done.11.refs_7_.refs_9_ = bf16[256,384]{1,0:T(8,128)(2,1)S(1)} collective-permute-done((bf16[256,384]{1,0:T(8,128)(2,1)S(1)}, bf16[256,384]{1,0:T(8,128)(2,1)S(1)}, u32[]{:S(2)}, u32[]{:S(2)}) %collective-permute-start.11) | collective-permute-done | bytes 196640 | tf_op jit(solution)/shard_map/ppermute | solution.py:33
  39.8 1.5 collective-permute-start.17
  41.4 8.2 %project.2 = (bf16[3072,128]{1,0:T(8,128)(2,1)}, bf16[3072,256]{1,0:T(8,128)(2,1)}, bf16[8,4,24,1024]{3,2,1,0:T(8,128)(2,1)}) custom-call(s32[5]{0:T(128)} %stack.29.meta, bf16[400,1024]{1,0:T(8,128)(2,1)} %layer_norm.1.refs_0_, bf16[400,1024]{1,0:T(8,128)(2,1)} %copy-done.17, bf16[400,1024]{1,0:T(8,128)(2,1)} %copy-done.7, ...), custom_call_target="tpu_custom_call" | custom-call | flops 9663676416 | bytes 6291456 | tf_op jit(solution)/shard_map/project/pallas_call | solution.py:173
  50.9 6.1 %all-to-all-start = ((bf16[32,24,1024]{2,1,0:T(8,128)(2,1)}), bf16[32,24,1024]{2,1,0:T(8,128)(2,1)S(1)}, u32[]{:S(2)}, u32[]{:S(2)}) async-start(bf16[32,24,1024]{2,1,0:T(8,128)(2,1)} %bitcast.18), calls=%async_computation | async-start | bytes 3145728 | tf_op jit(solution)/shard_map/all_to_all | solution.py:677
  61.3 8.2 %project.3 = (bf16[3072,128]{1,0:T(8,128)(2,1)}, bf16[3072,256]{1,0:T(8,128)(2,1)}, bf16[8,4,24,1024]{3,2,1,0:T(8,128)(2,1)}) custom-call(s32[5]{0:T(128)} %stack.29.meta, bf16[400,1024]{1,0:T(8,128)(2,1)} %copy-done.5, bf16[400,1024]{1,0:T(8,128)(2,1)} %copy-done.16, ...), custom_call_target="tpu_custom_call", output_to_operand_aliasing={{0}: (13, {}), {1}: (14, {})} | custom-call | flops 9663676416 | bytes 6291456 | tf_op jit(solution)/shard_map/project/pallas_call | solution.py:173
  70.8 3.2 %collective-permute-start.20 = (bf16[1024,256]{1,0:T(8,128)(2,1)S(1)}, bf16[1024,256]{1,0:T(8,128)(2,1)}, u32[]{:S(2)}, u32[]{:S(2)}) collective-permute-start(bf16[1024,256]{1,0:T(8,128)(2,1)S(1)} %get-tuple-element.109), channel_id=1, source_target_pairs={{0,8},{4,12},{8,16},{12,20},{16,24},{20,28},{1,9},{5,13},{9,17},{1... | collective-permute-start | bytes 1572872 | tf_op jit(solution)/shard_map/ppermute | solution.py:39
  73.9 2.9 %collective-permute-start.21 = (bf16[1024,256]{1,0:T(8,128)(2,1)S(1)}, bf16[1024,256]{1,0:T(8,128)(2,1)}, u32[]{:S(2)}, u32[]{:S(2)}) collective-permute-start(bf16[1024,256]{1,0:T(8,128)(2,1)S(1)} %get-tuple-element.108), channel_id=1, source_target_pairs={{8,0},{12,4},{16,8},{20,12},{24,16},{28,20},{9,1},{13,5},{17,9},{2... | collective-permute-start | bytes 1572872 | tf_op jit(solution)/shard_map/ppermute | solution.py:39
  76.9 24.0 %attend_edges.1 = (f32[4,160,256]{2,1,0:T(8,128)}, f32[4,160,256]{2,1,0:T(8,128)}, f32[4,8,256]{2,1,0:T(8,128)}, f32[4,8,256]{2,1,0:T(8,128)}) custom-call(s32[5]{0:T(128)} %stack.29.meta, s32[1,128]{1,0:T(1,128)} %get-tuple-element.60.ranges, bf16[3072,128]{1,0:T(8,128)(2,1)} %get-tuple-element.78.refs_0_.refs_3_, ...), custom_call_target="tpu_custom_call" | custom-call | flops 6442450944 | bytes 5242880 | tf_op jit(solution)/shard_map/attend_edges/pallas_call | solution.py:408
  100.9 1.9 %collective-permute-done.20.refs_7_ = bf16[1024,256]{1,0:T(8,128)(2,1)} collective-permute-done((bf16[1024,256]{1,0:T(8,128)(2,1)S(1)}, bf16[1024,256]{1,0:T(8,128)(2,1)}, u32[]{:S(2)}, u32[]{:S(2)}) %collective-permute-start.20) | collective-permute-done | bytes 524320 | tf_op jit(solution)/shard_map/ppermute | solution.py:39
  102.9 1.9 %collective-permute-done.21.refs_8_ = bf16[1024,256]{1,0:T(8,128)(2,1)} collective-permute-done((bf16[1024,256]{1,0:T(8,128)(2,1)S(1)}, bf16[1024,256]{1,0:T(8,128)(2,1)}, u32[]{:S(2)}, u32[]{:S(2)}) %collective-permute-start.21) | collective-permute-done | bytes 524320 | tf_op jit(solution)/shard_map/ppermute | solution.py:39
  104.8 4.3 %all-to-all-start.1 = ((bf16[32,24,1024]{2,1,0:T(8,128)(2,1)}), bf16[32,24,1024]{2,1,0:T(8,128)(2,1)S(1)}, u32[]{:S(2)}, u32[]{:S(2)}) async-start(bf16[32,24,1024]{2,1,0:T(8,128)(2,1)} %bitcast.17), calls=%async_computation.1 | async-start | bytes 3145728 | tf_op jit(solution)/shard_map/all_to_all | solution.py:677
  110.6 1.7 %constant_dynamic-update-slice_fusion.7 = bf16[1024,256]{1,0:T(8,128)(2,1)} fusion(bf16[512,256]{1,0:T(8,128)(2,1)} %copy-done.1), kind=kLoop, calls=%fused_computation.21 | loop fusion | bytes 524288
  113.2 25.1 %attend_finish.1 = (bf16[384,128]{1,0:T(8,128)(2,1)}, bf16[384,128]{1,0:T(8,128)(2,1)}, bf16[384,128]{1,0:T(8,128)(2,1)}, bf16[384,128]{1,0:T(8,128)(2,1)}, bf16...) custom-call(s32[5]{0:T(128)} %stack.29.meta, ...), custom_call_target="tpu_custom_call" | custom-call | flops 6442450944 | bytes 5242880 | tf_op jit(solution)/shard_map/attend_finish/pallas_call | solution.py:436
  141.7 3.7 %collective-permute-done.26.refs_2_ = bf16[384,128]{1,0:T(8,128)(2,1)S(1)} collective-permute-done((bf16[384,128]{1,0:T(8,128)(2,1)}, bf16[384,128]{1,0:T(8,128)(2,1)S(1)}, u32[]{:S(2)}, u32[]{:S(2)}) %collective-permute-start.26) | collective-permute-done | bytes 98336 | tf_op jit(solution)/shard_map/ppermute | solution.py:727
  145.5 1.9 %collective-permute-start.29 = (bf16[384,128]{1,0:T(8,128)(2,1)}, bf16[384,128]{1,0:T(8,128)(2,1)S(1)}, u32[]{:S(2)}, u32[]{:S(2)}) collective-permute-start(bf16[384,128]{1,0:T(8,128)(2,1)} %get-tuple-element.99), channel_id=1, source_target_pairs={{0,5},{1,4},{2,7},{3,6},{4,1},{5,0},{6,3},{7,2},{8,13},{9,12},{10,... | collective-permute-start | bytes 294920 | tf_op jit(solution)/shard_map/ppermute | solution.py:727
  147.6 1.6 %collective-permute-start.30 = (bf16[384,128]{1,0:T(8,128)(2,1)}, bf16[384,128]{1,0:T(8,128)(2,1)S(1)}, u32[]{:S(2)}, u32[]{:S(2)}) collective-permute-start(bf16[384,128]{1,0:T(8,128)(2,1)} %get-tuple-element.100), channel_id=1, source_target_pairs={{0,6},{1,7},{2,4},{3,5},{4,2},{5,3},{6,0},{7,1},{8,14},{9,15},{10,... | collective-permute-start | bytes 294920 | tf_op jit(solution)/shard_map/ppermute | solution.py:727
  151.1 1.6 collective-permute-done.30.refs_6_
  152.7 2.9 %collective-permute-done.31.refs_7_ = bf16[384,128]{1,0:T(8,128)(2,1)S(1)} collective-permute-done((bf16[384,128]{1,0:T(8,128)(2,1)}, bf16[384,128]{1,0:T(8,128)(2,1)S(1)}, u32[]{:S(2)}, u32[]{:S(2)}) %collective-permute-start.31) | collective-permute-done | bytes 98336 | tf_op jit(solution)/shard_map/ppermute | solution.py:727
  156.3 4.7 %output_projection.1 = bf16[384,1024]{1,0:T(8,128)(2,1)} custom-call(s32[2]{0:T(128)} %pad_add_fusion.meta, bf16[384,128]{1,0:T(8,128)(2,1)} %get-tuple-element.94.refs_0_, bf16[384,128]{1,0:T(8,128)(2,1)} %copy-done.8, bf16[384,128]{1,0:T(8,128)(2,1)} %copy-done.9, bf16[384,128]{1,0:T(8,128)(2,1)} %copy-done.10, bf16[384,128]{1,0:T(8,128)(2,1)} %copy-done.11, ...), custom_call_target="tpu_custom_call" | custom-call | flops 805306368 | bytes 4194304 | tf_op jit(solution)/shard_map/output_projection/pallas_call | solution.py:490
  161.0 2.5 %unpack.1 = bf16[8,24,8192]{2,1,0:T(8,128)(2,1)} custom-call(bf16[4,2,4,24,1024]{4,3,2,1,0:T(8,128)(2,1)S(1)} %bitcast.14, bf16[4,2,4,24,1024]{4,3,2,1,0:T(8,128)(2,1)S(1)} %bitcast.15), custom_call_target="tpu_custom_call" | custom-call | bytes 6291456 | tf_op jit(solution)/shard_map/unpack/pallas_call | solution.py:527
  (117 shorter events, 24.2 us)
Async XLA Ops:
  1.5 8.3 %collective-permute-start.5 = (bf16[128,128]{1,0:T(8,128)(2,1)S(1)}, bf16[128,128]{1,0:T(8,128)(2,1)S(1)}, u32[]{:S(2)}, u32[]{:S(2)}) collective-permute-start(bf16[128,128]{1,0:T(8,128)(2,1)S(1)} %get-tuple-element.113), channel_id=1, source_target_pairs={{0,6},{1,5},{2,4},{3,7},{4,2},{5,1},{6,0},{7,3},{8,14},{9,13},{10,... | collective-permute-start | bytes 98312 | tf_op jit(solution)/shard_map/ppermute | solution.py:617
  2.8 12.7 %collective-permute-start.4 = (bf16[128,128]{1,0:T(8,128)(2,1)S(1)}, bf16[128,128]{1,0:T(8,128)(2,1)S(1)}, u32[]{:S(2)}, u32[]{:S(2)}) collective-permute-start(bf16[128,128]{1,0:T(8,128)(2,1)S(1)} %get-tuple-element.111), channel_id=1, source_target_pairs={{0,5},{1,4},{2,7},{3,6},{4,1},{5,0},{6,3},{7,2},{8,13},{9,12},{10,... | collective-permute-start | bytes 98312 | tf_op jit(solution)/shard_map/ppermute | solution.py:617
  4.8 10.9 %collective-permute-start.3 = (bf16[128,128]{1,0:T(8,128)(2,1)S(1)}, bf16[128,128]{1,0:T(8,128)(2,1)S(1)}, u32[]{:S(2)}, u32[]{:S(2)}) collective-permute-start(bf16[128,128]{1,0:T(8,128)(2,1)S(1)} %get-tuple-element.112), channel_id=1, source_target_pairs={{0,4},{1,7},{2,6},{3,5},{4,0},{5,3},{6,2},{7,1},{8,12},{9,15},{10,... | collective-permute-start | bytes 98312 | tf_op jit(solution)/shard_map/ppermute | solution.py:617
  6.0 9.7 %collective-permute-start.2 = (bf16[128,128]{1,0:T(8,128)(2,1)S(1)}, bf16[128,128]{1,0:T(8,128)(2,1)S(1)}, u32[]{:S(2)}, u32[]{:S(2)}) collective-permute-start(bf16[128,128]{1,0:T(8,128)(2,1)S(1)} %get-tuple-element.115), channel_id=1, source_target_pairs={{0,2},{1,1},{2,0},{3,3},{4,6},{5,5},{6,4},{7,7},{8,10},{9,9},{10,8... | collective-permute-start | bytes 98312 | tf_op jit(solution)/shard_map/ppermute | solution.py:617
  6.7 9.0 %collective-permute-start.1 = (bf16[128,128]{1,0:T(8,128)(2,1)S(1)}, bf16[128,128]{1,0:T(8,128)(2,1)S(1)}, u32[]{:S(2)}, u32[]{:S(2)}) collective-permute-start(bf16[128,128]{1,0:T(8,128)(2,1)S(1)} %get-tuple-element.114), channel_id=1, source_target_pairs={{0,1},{1,0},{2,3},{3,2},{4,5},{5,4},{6,7},{7,6},{8,9},{9,8},{10,11... | collective-permute-start | bytes 98312 | tf_op jit(solution)/shard_map/ppermute | solution.py:617
  9.8 5.9 %collective-permute-start = (bf16[128,128]{1,0:T(8,128)(2,1)S(1)}, bf16[128,128]{1,0:T(8,128)(2,1)S(1)}, u32[]{:S(2)}, u32[]{:S(2)}) collective-permute-start(bf16[128,128]{1,0:T(8,128)(2,1)S(1)} %get-tuple-element.110), channel_id=1, source_target_pairs={{0,0},{1,3},{2,2},{3,1},{4,4},{5,7},{6,6},{7,5},{8,8},{9,11},{10,1... | collective-permute-start | bytes 98312 | tf_op jit(solution)/shard_map/ppermute | solution.py:617
  15.5 7.2 %collective-permute-start.12 = (bf16[128,256]{1,0:T(8,128)(2,1)S(1)}, bf16[128,256]{1,0:T(8,128)(2,1)S(1)}, u32[]{:S(2)}, u32[]{:S(2)}) collective-permute-start(bf16[128,256]{1,0:T(8,128)(2,1)S(1)} %copy-done.15), channel_id=1, source_target_pairs={{0,8},{4,12},{8,0},{12,4},{16,24},{20,28},{24,16},{28,20},{1,9},{5... | collective-permute-start | bytes 196616 | tf_op jit(solution)/shard_map/ppermute | solution.py:33
  15.8 20.9 %collective-permute-start.6 = (bf16[400,1024]{1,0:T(8,128)(2,1)}, bf16[400,1024]{1,0:T(8,128)(2,1)S(1)}, u32[]{:S(2)}, u32[]{:S(2)}) collective-permute-start(bf16[400,1024]{1,0:T(8,128)(2,1)} %layer_norm.1.refs_0_), channel_id=1, source_target_pairs={{0,2},{1,3},{2,0},{3,1},{4,6},{5,7},{6,4},{7,5},{8,10},{9,11},{10,... | collective-permute-start | bytes 2457608 | tf_op jit(solution)/shard_map/ppermute | solution.py:33
  16.8 19.9 %collective-permute-start.7 = (bf16[400,1024]{1,0:T(8,128)(2,1)}, bf16[400,1024]{1,0:T(8,128)(2,1)S(1)}, u32[]{:S(2)}, u32[]{:S(2)}) collective-permute-start(bf16[400,1024]{1,0:T(8,128)(2,1)} %layer_norm.1.refs_0_), channel_id=1, source_target_pairs={{0,4},{4,0},{8,12},{12,8},{16,20},{20,16},{24,28},{28,24},{1,5},{5... | collective-permute-start | bytes 2457608 | tf_op jit(solution)/shard_map/ppermute | solution.py:33
  17.3 19.4 %collective-permute-start.8 = (bf16[400,1024]{1,0:T(8,128)(2,1)}, bf16[400,1024]{1,0:T(8,128)(2,1)S(1)}, u32[]{:S(2)}, u32[]{:S(2)}) collective-permute-start(bf16[400,1024]{1,0:T(8,128)(2,1)} %layer_norm.1.refs_0_), channel_id=1, source_target_pairs={{0,1},{1,0},{2,3},{3,2},{4,5},{5,4},{6,7},{7,6},{8,9},{9,8},{10,11... | collective-permute-start | bytes 2457608 | tf_op jit(solution)/shard_map/ppermute | solution.py:33
  17.3 10.3 %collective-permute-start.10 = (bf16[256,384]{1,0:T(8,128)(2,1)S(1)}, bf16[256,384]{1,0:T(8,128)(2,1)S(1)}, u32[]{:S(2)}, u32[]{:S(2)}) collective-permute-start(bf16[256,384]{1,0:T(8,128)(2,1)S(1)} %maximum_maximum_fusion.refs_4_.refs_6_), channel_id=1, source_target_pairs={{0,16},{4,20},{8,24},{12,28},{16,0},{20,4},{24,8},{28,12},{1,17},{... | collective-permute-start | bytes 589832 | tf_op jit(solution)/shard_map/ppermute | solution.py:33
  22.8 10.0 %collective-permute-start.9 = (bf16[256,384]{1,0:T(8,128)(2,1)S(1)}, bf16[256,384]{1,0:T(8,128)(2,1)S(1)}, u32[]{:S(2)}, u32[]{:S(2)}) collective-permute-start(bf16[256,384]{1,0:T(8,128)(2,1)S(1)} %maximum_maximum_fusion.refs_4_.refs_6_), channel_id=1, source_target_pairs={{0,8},{4,12},{8,0},{12,4},{16,24},{20,28},{24,16},{28,20},{1,9},{5... | collective-permute-start | bytes 589832 | tf_op jit(solution)/shard_map/ppermute | solution.py:33
  27.7 9.0 %collective-permute-start.11 = (bf16[256,384]{1,0:T(8,128)(2,1)S(1)}, bf16[256,384]{1,0:T(8,128)(2,1)S(1)}, u32[]{:S(2)}, u32[]{:S(2)}) collective-permute-start(bf16[256,384]{1,0:T(8,128)(2,1)S(1)} %collective-permute-done.10.refs_6_.refs_8_), channel_id=1, source_target_pairs={{0,8},{4,12},{8,0},{12,4},{16,24},{20,28},{24,16},{28,20},{1,9},{5... | collective-permute-start | bytes 589832 | tf_op jit(solution)/shard_map/ppermute | solution.py:33
  38.2 11.7 %collective-permute-start.16 = (bf16[400,1024]{1,0:T(8,128)(2,1)S(1)}, bf16[400,1024]{1,0:T(8,128)(2,1)S(1)}, u32[]{:S(2)}, u32[]{:S(2)}) collective-permute-start(bf16[400,1024]{1,0:T(8,128)(2,1)S(1)} %collective-permute-done.7.refs_0_), channel_id=1, source_target_pairs={{0,1},{1,0},{2,3},{3,2},{4,5},{5,4},{6,7},{7,6},{8,9},{9,8},{10,11... | collective-permute-start | bytes 2457608 | tf_op jit(solution)/shard_map/ppermute | solution.py:33
  38.3 11.3 %collective-permute-start.14 = (bf16[192,1024]{1,0:T(8,128)(2,1)S(1)}, bf16[192,1024]{1,0:T(8,128)(2,1)}, u32[]{:S(2)}, u32[]{:S(2)}) collective-permute-start(bf16[192,1024]{1,0:T(8,128)(2,1)S(1)} %slice.42), channel_id=1, source_target_pairs={{0,4},{4,0},{8,12},{12,8},{16,20},{20,16},{24,28},{28,24},{1,5},{5... | collective-permute-start | bytes 1179656 | tf_op jit(solution)/shard_map/ppermute | solution.py:33
  39.3 10.6 %collective-permute-start.15 = (bf16[208,1024]{1,0:T(8,128)(2,1)S(1)}, bf16[208,1024]{1,0:T(8,128)(2,1)S(1)}, u32[]{:S(2)}, u32[]{:S(2)}) collective-permute-start(bf16[208,1024]{1,0:T(8,128)(2,1)S(1)} %slice.43), channel_id=1, source_target_pairs={{0,2},{1,3},{2,0},{3,1},{4,6},{5,7},{6,4},{7,5},{8,10},{9,11},{10,... | collective-permute-start | bytes 1277960 | tf_op jit(solution)/shard_map/ppermute | solution.py:33
  39.8 9.8 %collective-permute-start.17 = (bf16[256,256]{1,0:T(8,128)(2,1)S(1)}, bf16[256,256]{1,0:T(8,128)(2,1)S(1)}, u32[]{:S(2)}, u32[]{:S(2)}) collective-permute-start(bf16[256,256]{1,0:T(8,128)(2,1)S(1)} %constant_dynamic-update-slice_fusion), channel_id=1, source_target_pairs={{0,16},{4,20},{8,24},{12,28},{16,0},{20,4},{24,8},{28,12},{1,17},{... | collective-permute-start | bytes 393224 | tf_op jit(solution)/shard_map/ppermute | solution.py:33
  50.9 53.8 %all-to-all-start = ((bf16[32,24,1024]{2,1,0:T(8,128)(2,1)}), bf16[32,24,1024]{2,1,0:T(8,128)(2,1)S(1)}, u32[]{:S(2)}, u32[]{:S(2)}) async-start(bf16[32,24,1024]{2,1,0:T(8,128)(2,1)} %bitcast.18), calls=%async_computation | async-start | bytes 3145728 | tf_op jit(solution)/shard_map/all_to_all | solution.py:677
  57.7 43.2 %collective-permute-start.22 = (bf16[512,256]{1,0:T(8,128)(2,1)S(1)}, bf16[512,256]{1,0:T(8,128)(2,1)S(1)}, u32[]{:S(2)}, u32[]{:S(2)}) collective-permute-start(bf16[512,256]{1,0:T(8,128)(2,1)S(1)} %constant_dynamic-update-slice_fusion.2), channel_id=1, source_target_pairs={{0,4},{4,0},{8,12},{12,8},{16,20},{20,16},{24,28},{28,24},{1,5},{5... | collective-permute-start | bytes 786440 | tf_op jit(solution)/shard_map/ppermute | solution.py:33
  58.9 41.9 %collective-permute-start.23 = (bf16[512,256]{1,0:T(8,128)(2,1)S(1)}, bf16[512,256]{1,0:T(8,128)(2,1)S(1)}, u32[]{:S(2)}, u32[]{:S(2)}) collective-permute-start(bf16[512,256]{1,0:T(8,128)(2,1)S(1)} %constant_dynamic-update-slice_fusion.2), channel_id=1, source_target_pairs={{0,2},{1,3},{2,0},{3,1},{4,6},{5,7},{6,4},{7,5},{8,10},{9,11},{10,... | collective-permute-start | bytes 786440 | tf_op jit(solution)/shard_map/ppermute | solution.py:33
  60.1 40.8 %collective-permute-start.24 = (bf16[512,256]{1,0:T(8,128)(2,1)S(1)}, bf16[512,256]{1,0:T(8,128)(2,1)S(1)}, u32[]{:S(2)}, u32[]{:S(2)}) collective-permute-start(bf16[512,256]{1,0:T(8,128)(2,1)S(1)} %constant_dynamic-update-slice_fusion.2), channel_id=1, source_target_pairs={{0,6},{1,7},{2,4},{3,5},{4,2},{5,3},{6,0},{7,1},{8,14},{9,15},{10,... | collective-permute-start | bytes 786440 | tf_op jit(solution)/shard_map/ppermute | solution.py:699
  70.8 32.1 %collective-permute-start.20 = (bf16[1024,256]{1,0:T(8,128)(2,1)S(1)}, bf16[1024,256]{1,0:T(8,128)(2,1)}, u32[]{:S(2)}, u32[]{:S(2)}) collective-permute-start(bf16[1024,256]{1,0:T(8,128)(2,1)S(1)} %get-tuple-element.109), channel_id=1, source_target_pairs={{0,8},{4,12},{8,16},{12,20},{16,24},{20,28},{1,9},{5,13},{9,17},{1... | collective-permute-start | bytes 1572872 | tf_op jit(solution)/shard_map/ppermute | solution.py:39
  73.9 30.9 %collective-permute-start.21 = (bf16[1024,256]{1,0:T(8,128)(2,1)S(1)}, bf16[1024,256]{1,0:T(8,128)(2,1)}, u32[]{:S(2)}, u32[]{:S(2)}) collective-permute-start(bf16[1024,256]{1,0:T(8,128)(2,1)S(1)} %get-tuple-element.108), channel_id=1, source_target_pairs={{8,0},{12,4},{16,8},{20,12},{24,16},{28,20},{9,1},{13,5},{17,9},{2... | collective-permute-start | bytes 1572872 | tf_op jit(solution)/shard_map/ppermute | solution.py:39
  104.8 56.2 %all-to-all-start.1 = ((bf16[32,24,1024]{2,1,0:T(8,128)(2,1)}), bf16[32,24,1024]{2,1,0:T(8,128)(2,1)S(1)}, u32[]{:S(2)}, u32[]{:S(2)}) async-start(bf16[32,24,1024]{2,1,0:T(8,128)(2,1)} %bitcast.17), calls=%async_computation.1 | async-start | bytes 3145728 | tf_op jit(solution)/shard_map/all_to_all | solution.py:677
  110.2 45.5 %collective-permute-start.32 = (bf16[1024,256]{1,0:T(8,128)(2,1)S(1)}, bf16[1024,256]{1,0:T(8,128)(2,1)}, u32[]{:S(2)}, u32[]{:S(2)}) collective-permute-start(bf16[1024,256]{1,0:T(8,128)(2,1)S(1)} %constant_dynamic-update-slice_fusion.4.refs_8_), channel_id=1, source_target_pairs={{0,1},{1,0},{2,3},{3,2},{4,5},{5,4},{6,7},{7,6},{8,9},{9,8},{10,11... | collective-permute-start | bytes 1572872 | tf_op jit(solution)/shard_map/ppermute | solution.py:33
  113.0 42.6 %collective-permute-start.33 = (bf16[1024,256]{1,0:T(8,128)(2,1)}, bf16[1024,256]{1,0:T(8,128)(2,1)}, u32[]{:S(2)}, u32[]{:S(2)}) collective-permute-start(bf16[1024,256]{1,0:T(8,128)(2,1)} %constant_dynamic-update-slice_fusion.6.refs_10_), channel_id=1, source_target_pairs={{0,1},{1,0},{2,3},{3,2},{4,5},{5,4},{6,7},{7,6},{8,9},{9,8},{10,11... | collective-permute-start | bytes 1572872 | tf_op jit(solution)/shard_map/ppermute | solution.py:33
  138.7 6.7 %collective-permute-start.26 = (bf16[384,128]{1,0:T(8,128)(2,1)}, bf16[384,128]{1,0:T(8,128)(2,1)S(1)}, u32[]{:S(2)}, u32[]{:S(2)}) collective-permute-start(bf16[384,128]{1,0:T(8,128)(2,1)} %get-tuple-element.96), channel_id=1, source_target_pairs={{0,2},{1,3},{2,0},{3,1},{4,6},{5,7},{6,4},{7,5},{8,10},{9,11},{10,... | collective-permute-start | bytes 294920 | tf_op jit(solution)/shard_map/ppermute | solution.py:727
  139.9 7.7 %collective-permute-start.27 = (bf16[384,128]{1,0:T(8,128)(2,1)}, bf16[384,128]{1,0:T(8,128)(2,1)S(1)}, u32[]{:S(2)}, u32[]{:S(2)}) collective-permute-start(bf16[384,128]{1,0:T(8,128)(2,1)} %get-tuple-element.97), channel_id=1, source_target_pairs={{0,3},{1,2},{2,1},{3,0},{4,7},{5,6},{6,5},{7,4},{8,11},{9,10},{10,... | collective-permute-start | bytes 294920 | tf_op jit(solution)/shard_map/ppermute | solution.py:727
  140.5 8.7 %collective-permute-start.28 = (bf16[384,128]{1,0:T(8,128)(2,1)}, bf16[384,128]{1,0:T(8,128)(2,1)S(1)}, u32[]{:S(2)}, u32[]{:S(2)}) collective-permute-start(bf16[384,128]{1,0:T(8,128)(2,1)} %get-tuple-element.98), channel_id=1, source_target_pairs={{0,4},{1,5},{2,6},{3,7},{4,0},{5,1},{6,2},{7,3},{8,12},{9,13},{10,... | collective-permute-start | bytes 294920 | tf_op jit(solution)/shard_map/ppermute | solution.py:727
  145.5 5.6 %collective-permute-start.29 = (bf16[384,128]{1,0:T(8,128)(2,1)}, bf16[384,128]{1,0:T(8,128)(2,1)S(1)}, u32[]{:S(2)}, u32[]{:S(2)}) collective-permute-start(bf16[384,128]{1,0:T(8,128)(2,1)} %get-tuple-element.99), channel_id=1, source_target_pairs={{0,5},{1,4},{2,7},{3,6},{4,1},{5,0},{6,3},{7,2},{8,13},{9,12},{10,... | collective-permute-start | bytes 294920 | tf_op jit(solution)/shard_map/ppermute | solution.py:727
  147.6 5.1 %collective-permute-start.30 = (bf16[384,128]{1,0:T(8,128)(2,1)}, bf16[384,128]{1,0:T(8,128)(2,1)S(1)}, u32[]{:S(2)}, u32[]{:S(2)}) collective-permute-start(bf16[384,128]{1,0:T(8,128)(2,1)} %get-tuple-element.100), channel_id=1, source_target_pairs={{0,6},{1,7},{2,4},{3,5},{4,2},{5,3},{6,0},{7,1},{8,14},{9,15},{10,... | collective-permute-start | bytes 294920 | tf_op jit(solution)/shard_map/ppermute | solution.py:727
  149.2 6.4 %collective-permute-start.31 = (bf16[384,128]{1,0:T(8,128)(2,1)}, bf16[384,128]{1,0:T(8,128)(2,1)S(1)}, u32[]{:S(2)}, u32[]{:S(2)}) collective-permute-start(bf16[384,128]{1,0:T(8,128)(2,1)} %get-tuple-element.101), channel_id=1, source_target_pairs={{0,7},{1,6},{2,5},{3,4},{4,3},{5,2},{6,1},{7,0},{8,15},{9,14},{10,... | collective-permute-start | bytes 294920 | tf_op jit(solution)/shard_map/ppermute | solution.py:727
  (28 other events, 167.5 us)

commit v9 on v8

--- a/solution.py
+++ b/solution.py
@@ -1,5 +1,4 @@
 import functools
-import math
 
 import jax
 import jax.numpy as jnp
@@ -23,7 +22,7 @@
 HEAD_ROWS = HEAD_DIM + ONES_ROWS
 EXTRA_ROWS = 16
 KEYS = 512
-SCALE = HEAD_DIM ** (-0.5) * math.log2(math.e)
+SCALE = HEAD_DIM ** (-0.5)
 VMEM_LIMIT = 60 * 1024 * 1024
 PARAMS = pltpu.CompilerParams(vmem_limit_bytes=VMEM_LIMIT)
 
@@ -130,7 +129,7 @@
         )
         return (values * cosines + partner * sines).astype(jnp.bfloat16)
 
-    query_out[...] = rotate(joined[:, :width])
+    query_out[...] = rotate(joined[:, :width]) * jnp.asarray(SCALE, jnp.bfloat16)
     keys = rotate(joined[:, width : 2 * width])
     values = joined[:, 2 * width :].astype(jnp.bfloat16)
     pair_out[:, :width] = keys
@@ -237,31 +236,48 @@
         steps = jnp.maximum(steps, (end - begin + KEYS // TILE - 1) // (KEYS // TILE))
         plans.append((begin, base, held, pairs, values_of, masked, starts, last, total))
 
+    key_rows = lax.broadcasted_iota(jnp.int32, (KEYS, TILE), 0)
+
     def one(number, peaks):
-        new_peaks = []
-        for plan, old_peaks in zip(plans, peaks):
+        units = []
+        for place, plan in enumerate(plans):
             begin, base, held, pairs, values_of, masked, starts, last, total = plan
             wanted = begin + number * (KEYS // TILE)
             block = jnp.minimum(wanted, base + held - KEYS // TILE)
             row = pl.multiple_of((block - base) * TILE, TILE)
             keys = pairs[pl.ds(row, KEYS), : pairs.shape[1] // 2]
             values = values_of(row)
-            index = block * TILE + lax.broadcasted_iota(jnp.int32, (KEYS, TILE), 0)
-            allowed = (index >= jnp.maximum(starts, wanted * TILE)) & (index < last)
-            job_peaks = []
-            for head, old_peak in enumerate(old_peaks):
-                scores = jnp.dot(keys, masked[head], preferred_element_type=jnp.float32)
-                scores = jnp.where(allowed, scores * SCALE, NEG_FILL)
-                peak = jnp.maximum(old_peak, jnp.max(scores, axis=0, keepdims=True))
-                fade = jnp.exp2(old_peak - peak)
-                weights = jnp.exp2(scores - peak).astype(jnp.bfloat16)
-                own = slice(head * HEAD_ROWS, (head + 1) * HEAD_ROWS)
-                total[own, :] = total[own, :] * fade + jnp.dot(
-                    values[own, :], weights, preferred_element_type=jnp.float32
-                )
-                job_peaks.append(peak)
-            new_peaks.append(tuple(job_peaks))
-        return tuple(new_peaks)
+            first_key = block * TILE
+            allowed = (key_rows >= jnp.maximum(starts, wanted * TILE) - first_key) & (
+                key_rows < last - first_key
+            )
+            units += [
+                (place, head, keys, values, masked, allowed, total)
+                for head in range(len(peaks[place]))
+            ]
+
+        def products(unit):
+            place, head, keys, values, masked, allowed, total = unit
+            return jnp.dot(keys, masked[head], preferred_element_type=jnp.float32)
+
+        new_peaks = [[] for _ in plans]
+        ahead = products(units[0])
+        for number, unit in enumerate(units):
+            place, head, keys, values, masked, allowed, total = unit
+            scores = ahead
+            if number + 1 < len(units):
+                ahead = products(units[number + 1])
+            scores = jnp.where(allowed, scores, NEG_FILL)
+            old_peak = peaks[place][head]
+            peak = jnp.maximum(old_peak, jnp.max(scores, axis=0, keepdims=True))
+            fade = jnp.exp(old_peak - peak)
+            weights = jnp.exp(scores - peak).astype(jnp.bfloat16)
+            own = slice(head * HEAD_ROWS, (head + 1) * HEAD_ROWS)
+            total[own, :] = total[own, :] * fade + jnp.dot(
+                values[own, :], weights, preferred_element_type=jnp.float32
+            )
+            new_peaks[place].append(peak)
+        return tuple(tuple(job_peaks) for job_peaks in new_peaks)
 
     return lax.fori_loop(0, steps, one, peaks)
 

time: 164 us -> 160 us (0.976)
  the two profiles are of different devices: /device:TPU:9 before, /device:TPU:17 now
where the time goes in v9:
time: 160 us; the launch traced here: 159 us
  Pallas kernels  69.3 us (43%)
  starting transfers between devices  46.9 us (29%)
  waiting for transfers between devices  27.1 us (17%)
  local copies, waits for them, and re-layouts  8.94 us (6%)
  other arithmetic  5.83 us (4%)
    pallas_call x1, Pallas kernels, attend_finish(): pl.pallas_call(functools.partial(finish_kernel, edge), grid_spec=pltpu.Pr...  21 us
    pallas_call x1, Pallas kernels, attend_edges(): pl.pallas_call(functools.partial(edge_kernel, edge), grid_spec=pltpu.Pref...  19.7 us
    pallas_call x2, Pallas kernels, project(): pl.pallas_call(functools.partial(project_kernel, first, layout, len(weigh...  16.4 us
    ppermute x18, starting transfers between devices, flipped(): lax.ppermute(value, axis, [(source, source ^ bit) for source in range(cou...  13.2 us
    ppermute x18, waiting for transfers between devices, flipped(): lax.ppermute(value, axis, [(source, source ^ bit) for source in range(cou...  10.7 us
    all_to_all x2, starting transfers between devices, to_owners(): lax.all_to_all(send.reshape((flat,) + send.shape[2:]), ('tok', 'grp'), sp...  10.5 us
    ppermute x6, starting transfers between devices, per_device(): pieces.append(lax.ppermute(piece, ('tok', 'grp'), route))  9.33 us
    ppermute x7, starting transfers between devices, per_device(): lax.ppermute(mixed[distance], ('tok', 'grp'), [(source, source ^ distance...  8.31 us
  transfers between devices with their start and end apart: 36, of which 10 were waited for; matrix products, arithmetic and copies ran while one was open for 7% of the time, Pallas kernels for 42%

profile of v9, /device:TPU:17, one launch (start us, length us, event | category | flops | bytes accessed | tf_op | source)
XLA Modules:
  0.0 159.1 jit_solution(5846280792922622453)
XLA Ops:
  1.5 1.3 collective-permute-start.5
  2.8 2.0 %collective-permute-start.4 = (bf16[128,128]{1,0:T(8,128)(2,1)S(1)}, bf16[128,128]{1,0:T(8,128)(2,1)S(1)}, u32[]{:S(2)}, u32[]{:S(2)}) collective-permute-start(bf16[128,128]{1,0:T(8,128)(2,1)S(1)} %get-tuple-element.111), channel_id=1, source_target_pairs={{0,5},{1,4},{2,7},{3,6},{4,1},{5,0},{6,3},{7,2},{8,13},{9,12},{10,... | collective-permute-start | bytes 98312 | tf_op jit(solution)/shard_map/ppermute | solution.py:633
  6.7 1.7 %collective-permute-start.1 = (bf16[128,128]{1,0:T(8,128)(2,1)S(1)}, bf16[128,128]{1,0:T(8,128)(2,1)S(1)}, u32[]{:S(2)}, u32[]{:S(2)}) collective-permute-start(bf16[128,128]{1,0:T(8,128)(2,1)S(1)} %get-tuple-element.114), channel_id=1, source_target_pairs={{0,1},{1,0},{2,3},{3,2},{4,5},{5,4},{6,7},{7,6},{8,9},{9,8},{10,11... | collective-permute-start | bytes 98312 | tf_op jit(solution)/shard_map/ppermute | solution.py:633
  8.4 1.3 fusion.1
  9.8 2.4 %collective-permute-start = (bf16[128,128]{1,0:T(8,128)(2,1)S(1)}, bf16[128,128]{1,0:T(8,128)(2,1)S(1)}, u32[]{:S(2)}, u32[]{:S(2)}) collective-permute-start(bf16[128,128]{1,0:T(8,128)(2,1)S(1)} %get-tuple-element.110), channel_id=1, source_target_pairs={{0,0},{1,3},{2,2},{3,1},{4,4},{5,7},{6,6},{7,5},{8,8},{9,11},{10,1... | collective-permute-start | bytes 98312 | tf_op jit(solution)/shard_map/ppermute | solution.py:633
  12.3 2.6 %layer_norm.1.refs_0_ = bf16[400,1024]{1,0:T(8,128)(2,1)} custom-call(bf16[384,1024]{1,0:T(8,128)(2,1)} %tokens.1, f32[1,1024]{1,0:T(1,128)} %bitcast.21, s32[1,96]{1,0:T(1,128)} %bitcast.22), custom_call_target="tpu_custom_call" | custom-call | tf_op jit(solution)/shard_map/layer_norm/pallas_call | solution.py:65
  15.5 1.3 collective-permute-start.12
  18.5 2.4 %document_bounds.1 = (s32[1,3072]{1,0:T(1,128)}, s32[1,3072]{1,0:T(1,128)}, s32[1,128]{1,0:T(1,128)}) custom-call(s32[1,5120]{1,0:T(1,128)} %bitcast.20), custom_call_target="tpu_custom_call" | custom-call | flops 17179869184 | tf_op jit(solution)/shard_map/document_bounds/pallas_call | solution.py:597
  21.9 5.4 %collective-permute-done.10.refs_6_.refs_8_ = bf16[256,384]{1,0:T(8,128)(2,1)S(1)} collective-permute-done((bf16[256,384]{1,0:T(8,128)(2,1)S(1)}, bf16[256,384]{1,0:T(8,128)(2,1)S(1)}, u32[]{:S(2)}, u32[]{:S(2)}) %collective-permute-start.10) | collective-permute-done | bytes 196640 | tf_op jit(solution)/shard_map/ppermute | solution.py:32
  27.3 2.5 %collective-permute-start.11 = (bf16[256,384]{1,0:T(8,128)(2,1)S(1)}, bf16[256,384]{1,0:T(8,128)(2,1)S(1)}, u32[]{:S(2)}, u32[]{:S(2)}) collective-permute-start(bf16[256,384]{1,0:T(8,128)(2,1)S(1)} %collective-permute-done.10.refs_6_.refs_8_), channel_id=1, source_target_pairs={{0,8},{4,12},{8,0},{12,4},{16,24},{20,28},{24,16},{28,20},{1,9},{5... | collective-permute-start | bytes 589832 | tf_op jit(solution)/shard_map/ppermute | solution.py:32
  29.7 2.3 %multiply_sine_fusion = (f32[32,3072]{1,0:T(8,128)}, f32[32,3072]{1,0:T(8,128)}) fusion(f32[3072]{0:T(1024)S(1)} %bitcast.19, f32[32]{0:T(128)S(1)} %negate_power_fusion), kind=kLoop, calls=%fused_computation | loop fusion | flops 98304 | bytes 798848 | tf_op jit(solution)/shard_map/sin | solution.py:561
  32.1 1.5 collective-permute-done.11.refs_7_.refs_9_
  33.5 2.6 %collective-permute-done.6.refs_2_ = bf16[400,1024]{1,0:T(8,128)(2,1)S(1)} collective-permute-done((bf16[400,1024]{1,0:T(8,128)(2,1)}, bf16[400,1024]{1,0:T(8,128)(2,1)S(1)}, u32[]{:S(2)}, u32[]{:S(2)}) %collective-permute-start.6) | collective-permute-done | bytes 819232 | tf_op jit(solution)/shard_map/ppermute | solution.py:32
  38.6 1.3 collective-permute-start.14
  40.1 1.9 %collective-permute-start.17 = (bf16[256,256]{1,0:T(8,128)(2,1)S(1)}, bf16[256,256]{1,0:T(8,128)(2,1)S(1)}, u32[]{:S(2)}, u32[]{:S(2)}) collective-permute-start(bf16[256,256]{1,0:T(8,128)(2,1)S(1)} %constant_dynamic-update-slice_fusion), channel_id=1, source_target_pairs={{0,16},{4,20},{8,24},{12,28},{16,0},{20,4},{24,8},{28,12},{1,17},{... | collective-permute-start | bytes 393224 | tf_op jit(solution)/shard_map/ppermute | solution.py:32
  42.0 8.2 %project.2 = (bf16[3072,128]{1,0:T(8,128)(2,1)}, bf16[3072,256]{1,0:T(8,128)(2,1)}, bf16[8,4,24,1024]{3,2,1,0:T(8,128)(2,1)}) custom-call(s32[5]{0:T(128)} %stack.29.meta, bf16[400,1024]{1,0:T(8,128)(2,1)} %layer_norm.1.refs_0_, bf16[400,1024]{1,0:T(8,128)(2,1)} %copy-done.17, bf16[400,1024]{1,0:T(8,128)(2,1)} %copy-done.7, ...), custom_call_target="tpu_custom_call" | custom-call | flops 9663676416 | bytes 6291456 | tf_op jit(solution)/shard_map/project/pallas_call | solution.py:172
  51.6 5.4 %all-to-all-start = ((bf16[32,24,1024]{2,1,0:T(8,128)(2,1)}), bf16[32,24,1024]{2,1,0:T(8,128)(2,1)S(1)}, u32[]{:S(2)}, u32[]{:S(2)}) async-start(bf16[32,24,1024]{2,1,0:T(8,128)(2,1)} %bitcast.18), calls=%async_computation | async-start | bytes 3145728 | tf_op jit(solution)/shard_map/all_to_all | solution.py:693
  61.2 8.2 %project.3 = (bf16[3072,128]{1,0:T(8,128)(2,1)}, bf16[3072,256]{1,0:T(8,128)(2,1)}, bf16[8,4,24,1024]{3,2,1,0:T(8,128)(2,1)}) custom-call(s32[5]{0:T(128)} %stack.29.meta, bf16[400,1024]{1,0:T(8,128)(2,1)} %copy-done.5, bf16[400,1024]{1,0:T(8,128)(2,1)} %copy-done.16, ...), custom_call_target="tpu_custom_call", output_to_operand_aliasing={{0}: (13, {}), {1}: (14, {})} | custom-call | flops 9663676416 | bytes 6291456 | tf_op jit(solution)/shard_map/project/pallas_call | solution.py:172
  70.7 3.2 %collective-permute-start.20 = (bf16[1024,256]{1,0:T(8,128)(2,1)S(1)}, bf16[1024,256]{1,0:T(8,128)(2,1)}, u32[]{:S(2)}, u32[]{:S(2)}) collective-permute-start(bf16[1024,256]{1,0:T(8,128)(2,1)S(1)} %get-tuple-element.109), channel_id=1, source_target_pairs={{0,8},{4,12},{8,16},{12,20},{16,24},{20,28},{1,9},{5,13},{9,17},{1... | collective-permute-start | bytes 1572872 | tf_op jit(solution)/shard_map/ppermute | solution.py:38
  73.9 2.1 %collective-permute-start.21 = (bf16[1024,256]{1,0:T(8,128)(2,1)S(1)}, bf16[1024,256]{1,0:T(8,128)(2,1)}, u32[]{:S(2)}, u32[]{:S(2)}) collective-permute-start(bf16[1024,256]{1,0:T(8,128)(2,1)S(1)} %get-tuple-element.108), channel_id=1, source_target_pairs={{8,0},{12,4},{16,8},{20,12},{24,16},{28,20},{9,1},{13,5},{17,9},{2... | collective-permute-start | bytes 1572872 | tf_op jit(solution)/shard_map/ppermute | solution.py:38
  76.0 19.7 %attend_edges.1 = (f32[4,160,256]{2,1,0:T(8,128)}, f32[4,160,256]{2,1,0:T(8,128)}, f32[4,8,256]{2,1,0:T(8,128)}, f32[4,8,256]{2,1,0:T(8,128)}) custom-call(s32[5]{0:T(128)} %stack.29.meta, s32[1,128]{1,0:T(1,128)} %get-tuple-element.60.ranges, bf16[3072,128]{1,0:T(8,128)(2,1)} %get-tuple-element.78.refs_0_.refs_3_, ...), custom_call_target="tpu_custom_call" | custom-call | flops 6442450944 | bytes 5242880 | tf_op jit(solution)/shard_map/attend_edges/pallas_call | solution.py:424
  95.8 8.1 %collective-permute-done.20.refs_7_ = bf16[1024,256]{1,0:T(8,128)(2,1)} collective-permute-done((bf16[1024,256]{1,0:T(8,128)(2,1)S(1)}, bf16[1024,256]{1,0:T(8,128)(2,1)}, u32[]{:S(2)}, u32[]{:S(2)}) %collective-permute-start.20) | collective-permute-done | bytes 524320 | tf_op jit(solution)/shard_map/ppermute | solution.py:38
  103.9 5.1 %all-to-all-start.1 = ((bf16[32,24,1024]{2,1,0:T(8,128)(2,1)}), bf16[32,24,1024]{2,1,0:T(8,128)(2,1)S(1)}, u32[]{:S(2)}, u32[]{:S(2)}) async-start(bf16[32,24,1024]{2,1,0:T(8,128)(2,1)} %bitcast.17), calls=%async_computation.1 | async-start | bytes 3145728 | tf_op jit(solution)/shard_map/all_to_all | solution.py:693
  110.5 1.7 %constant_dynamic-update-slice_fusion.7 = bf16[1024,256]{1,0:T(8,128)(2,1)} fusion(bf16[512,256]{1,0:T(8,128)(2,1)} %copy-done.1), kind=kLoop, calls=%fused_computation.21 | loop fusion | bytes 524288
  113.1 21.0 %attend_finish.1 = (bf16[384,128]{1,0:T(8,128)(2,1)}, bf16[384,128]{1,0:T(8,128)(2,1)}, bf16[384,128]{1,0:T(8,128)(2,1)}, bf16[384,128]{1,0:T(8,128)(2,1)}, bf16...) custom-call(s32[5]{0:T(128)} %stack.29.meta, ...), custom_call_target="tpu_custom_call" | custom-call | flops 6442450944 | bytes 5242880 | tf_op jit(solution)/shard_map/attend_finish/pallas_call | solution.py:452
  137.5 1.9 %collective-permute-done.26.refs_2_ = bf16[384,128]{1,0:T(8,128)(2,1)S(1)} collective-permute-done((bf16[384,128]{1,0:T(8,128)(2,1)}, bf16[384,128]{1,0:T(8,128)(2,1)S(1)}, u32[]{:S(2)}, u32[]{:S(2)}) %collective-permute-start.26) | collective-permute-done | bytes 98336 | tf_op jit(solution)/shard_map/ppermute | solution.py:743
  139.5 2.6 %collective-permute-start.29 = (bf16[384,128]{1,0:T(8,128)(2,1)}, bf16[384,128]{1,0:T(8,128)(2,1)S(1)}, u32[]{:S(2)}, u32[]{:S(2)}) collective-permute-start(bf16[384,128]{1,0:T(8,128)(2,1)} %get-tuple-element.99), channel_id=1, source_target_pairs={{0,5},{1,4},{2,7},{3,6},{4,1},{5,0},{6,3},{7,2},{8,13},{9,12},{10,... | collective-permute-start | bytes 294920 | tf_op jit(solution)/shard_map/ppermute | solution.py:743
  143.3 1.5 collective-permute-start.30
  146.2 2.7 %collective-permute-done.30.refs_6_ = bf16[384,128]{1,0:T(8,128)(2,1)S(1)} collective-permute-done((bf16[384,128]{1,0:T(8,128)(2,1)}, bf16[384,128]{1,0:T(8,128)(2,1)S(1)}, u32[]{:S(2)}, u32[]{:S(2)}) %collective-permute-start.30) | collective-permute-done | bytes 98336 | tf_op jit(solution)/shard_map/ppermute | solution.py:743
  148.9 2.4 %collective-permute-done.31.refs_7_ = bf16[384,128]{1,0:T(8,128)(2,1)S(1)} collective-permute-done((bf16[384,128]{1,0:T(8,128)(2,1)}, bf16[384,128]{1,0:T(8,128)(2,1)S(1)}, u32[]{:S(2)}, u32[]{:S(2)}) %collective-permute-start.31) | collective-permute-done | bytes 98336 | tf_op jit(solution)/shard_map/ppermute | solution.py:743
  151.9 4.7 %output_projection.1 = bf16[384,1024]{1,0:T(8,128)(2,1)} custom-call(s32[2]{0:T(128)} %pad_add_fusion.meta, bf16[384,128]{1,0:T(8,128)(2,1)} %get-tuple-element.94.refs_0_, bf16[384,128]{1,0:T(8,128)(2,1)} %copy-done.8, bf16[384,128]{1,0:T(8,128)(2,1)} %copy-done.9, bf16[384,128]{1,0:T(8,128)(2,1)} %copy-done.10, bf16[384,128]{1,0:T(8,128)(2,1)} %copy-done.11, ...), custom_call_target="tpu_custom_call" | custom-call | flops 805306368 | bytes 4194304 | tf_op jit(solution)/shard_map/output_projection/pallas_call | solution.py:506
  156.6 2.5 %unpack.1 = bf16[8,24,8192]{2,1,0:T(8,128)(2,1)} custom-call(bf16[4,2,4,24,1024]{4,3,2,1,0:T(8,128)(2,1)S(1)} %bitcast.14, bf16[4,2,4,24,1024]{4,3,2,1,0:T(8,128)(2,1)S(1)} %bitcast.15), custom_call_target="tpu_custom_call" | custom-call | bytes 6291456 | tf_op jit(solution)/shard_map/unpack/pallas_call | solution.py:543
  (117 shorter events, 24.5 us)
Async XLA Ops:
  1.5 8.3 %collective-permute-start.5 = (bf16[128,128]{1,0:T(8,128)(2,1)S(1)}, bf16[128,128]{1,0:T(8,128)(2,1)S(1)}, u32[]{:S(2)}, u32[]{:S(2)}) collective-permute-start(bf16[128,128]{1,0:T(8,128)(2,1)S(1)} %get-tuple-element.113), channel_id=1, source_target_pairs={{0,6},{1,5},{2,4},{3,7},{4,2},{5,1},{6,0},{7,3},{8,14},{9,13},{10,... | collective-permute-start | bytes 98312 | tf_op jit(solution)/shard_map/ppermute | solution.py:633
  2.8 12.7 %collective-permute-start.4 = (bf16[128,128]{1,0:T(8,128)(2,1)S(1)}, bf16[128,128]{1,0:T(8,128)(2,1)S(1)}, u32[]{:S(2)}, u32[]{:S(2)}) collective-permute-start(bf16[128,128]{1,0:T(8,128)(2,1)S(1)} %get-tuple-element.111), channel_id=1, source_target_pairs={{0,5},{1,4},{2,7},{3,6},{4,1},{5,0},{6,3},{7,2},{8,13},{9,12},{10,... | collective-permute-start | bytes 98312 | tf_op jit(solution)/shard_map/ppermute | solution.py:633
  4.8 12.0 %collective-permute-start.3 = (bf16[128,128]{1,0:T(8,128)(2,1)S(1)}, bf16[128,128]{1,0:T(8,128)(2,1)S(1)}, u32[]{:S(2)}, u32[]{:S(2)}) collective-permute-start(bf16[128,128]{1,0:T(8,128)(2,1)S(1)} %get-tuple-element.112), channel_id=1, source_target_pairs={{0,4},{1,7},{2,6},{3,5},{4,0},{5,3},{6,2},{7,1},{8,12},{9,15},{10,... | collective-permute-start | bytes 98312 | tf_op jit(solution)/shard_map/ppermute | solution.py:633
  6.0 10.8 %collective-permute-start.2 = (bf16[128,128]{1,0:T(8,128)(2,1)S(1)}, bf16[128,128]{1,0:T(8,128)(2,1)S(1)}, u32[]{:S(2)}, u32[]{:S(2)}) collective-permute-start(bf16[128,128]{1,0:T(8,128)(2,1)S(1)} %get-tuple-element.115), channel_id=1, source_target_pairs={{0,2},{1,1},{2,0},{3,3},{4,6},{5,5},{6,4},{7,7},{8,10},{9,9},{10,8... | collective-permute-start | bytes 98312 | tf_op jit(solution)/shard_map/ppermute | solution.py:633
  6.7 10.1 %collective-permute-start.1 = (bf16[128,128]{1,0:T(8,128)(2,1)S(1)}, bf16[128,128]{1,0:T(8,128)(2,1)S(1)}, u32[]{:S(2)}, u32[]{:S(2)}) collective-permute-start(bf16[128,128]{1,0:T(8,128)(2,1)S(1)} %get-tuple-element.114), channel_id=1, source_target_pairs={{0,1},{1,0},{2,3},{3,2},{4,5},{5,4},{6,7},{7,6},{8,9},{9,8},{10,11... | collective-permute-start | bytes 98312 | tf_op jit(solution)/shard_map/ppermute | solution.py:633
  9.8 7.0 %collective-permute-start = (bf16[128,128]{1,0:T(8,128)(2,1)S(1)}, bf16[128,128]{1,0:T(8,128)(2,1)S(1)}, u32[]{:S(2)}, u32[]{:S(2)}) collective-permute-start(bf16[128,128]{1,0:T(8,128)(2,1)S(1)} %get-tuple-element.110), channel_id=1, source_target_pairs={{0,0},{1,3},{2,2},{3,1},{4,4},{5,7},{6,6},{7,5},{8,8},{9,11},{10,1... | collective-permute-start | bytes 98312 | tf_op jit(solution)/shard_map/ppermute | solution.py:633
  15.5 6.1 %collective-permute-start.12 = (bf16[128,256]{1,0:T(8,128)(2,1)S(1)}, bf16[128,256]{1,0:T(8,128)(2,1)S(1)}, u32[]{:S(2)}, u32[]{:S(2)}) collective-permute-start(bf16[128,256]{1,0:T(8,128)(2,1)S(1)} %copy-done.15), channel_id=1, source_target_pairs={{0,8},{4,12},{8,0},{12,4},{16,24},{20,28},{24,16},{28,20},{1,9},{5... | collective-permute-start | bytes 196616 | tf_op jit(solution)/shard_map/ppermute | solution.py:32
  16.9 19.3 %collective-permute-start.6 = (bf16[400,1024]{1,0:T(8,128)(2,1)}, bf16[400,1024]{1,0:T(8,128)(2,1)S(1)}, u32[]{:S(2)}, u32[]{:S(2)}) collective-permute-start(bf16[400,1024]{1,0:T(8,128)(2,1)} %layer_norm.1.refs_0_), channel_id=1, source_target_pairs={{0,2},{1,3},{2,0},{3,1},{4,6},{5,7},{6,4},{7,5},{8,10},{9,11},{10,... | collective-permute-start | bytes 2457608 | tf_op jit(solution)/shard_map/ppermute | solution.py:32
  17.9 19.1 %collective-permute-start.7 = (bf16[400,1024]{1,0:T(8,128)(2,1)}, bf16[400,1024]{1,0:T(8,128)(2,1)S(1)}, u32[]{:S(2)}, u32[]{:S(2)}) collective-permute-start(bf16[400,1024]{1,0:T(8,128)(2,1)} %layer_norm.1.refs_0_), channel_id=1, source_target_pairs={{0,4},{4,0},{8,12},{12,8},{16,20},{20,16},{24,28},{28,24},{1,5},{5... | collective-permute-start | bytes 2457608 | tf_op jit(solution)/shard_map/ppermute | solution.py:32
  18.4 18.5 %collective-permute-start.8 = (bf16[400,1024]{1,0:T(8,128)(2,1)}, bf16[400,1024]{1,0:T(8,128)(2,1)S(1)}, u32[]{:S(2)}, u32[]{:S(2)}) collective-permute-start(bf16[400,1024]{1,0:T(8,128)(2,1)} %layer_norm.1.refs_0_), channel_id=1, source_target_pairs={{0,1},{1,0},{2,3},{3,2},{4,5},{5,4},{6,7},{7,6},{8,9},{9,8},{10,11... | collective-permute-start | bytes 2457608 | tf_op jit(solution)/shard_map/ppermute | solution.py:32
  18.4 8.8 %collective-permute-start.10 = (bf16[256,384]{1,0:T(8,128)(2,1)S(1)}, bf16[256,384]{1,0:T(8,128)(2,1)S(1)}, u32[]{:S(2)}, u32[]{:S(2)}) collective-permute-start(bf16[256,384]{1,0:T(8,128)(2,1)S(1)} %maximum_maximum_fusion.refs_4_.refs_6_), channel_id=1, source_target_pairs={{0,16},{4,20},{8,24},{12,28},{16,0},{20,4},{24,8},{28,12},{1,17},{... | collective-permute-start | bytes 589832 | tf_op jit(solution)/shard_map/ppermute | solution.py:32
  21.7 10.4 %collective-permute-start.9 = (bf16[256,384]{1,0:T(8,128)(2,1)S(1)}, bf16[256,384]{1,0:T(8,128)(2,1)S(1)}, u32[]{:S(2)}, u32[]{:S(2)}) collective-permute-start(bf16[256,384]{1,0:T(8,128)(2,1)S(1)} %maximum_maximum_fusion.refs_4_.refs_6_), channel_id=1, source_target_pairs={{0,8},{4,12},{8,0},{12,4},{16,24},{20,28},{24,16},{28,20},{1,9},{5... | collective-permute-start | bytes 589832 | tf_op jit(solution)/shard_map/ppermute | solution.py:32
  27.3 6.3 %collective-permute-start.11 = (bf16[256,384]{1,0:T(8,128)(2,1)S(1)}, bf16[256,384]{1,0:T(8,128)(2,1)S(1)}, u32[]{:S(2)}, u32[]{:S(2)}) collective-permute-start(bf16[256,384]{1,0:T(8,128)(2,1)S(1)} %collective-permute-done.10.refs_6_.refs_8_), channel_id=1, source_target_pairs={{0,8},{4,12},{8,0},{12,4},{16,24},{20,28},{24,16},{28,20},{1,9},{5... | collective-permute-start | bytes 589832 | tf_op jit(solution)/shard_map/ppermute | solution.py:32
  38.0 12.6 %collective-permute-start.16 = (bf16[400,1024]{1,0:T(8,128)(2,1)S(1)}, bf16[400,1024]{1,0:T(8,128)(2,1)S(1)}, u32[]{:S(2)}, u32[]{:S(2)}) collective-permute-start(bf16[400,1024]{1,0:T(8,128)(2,1)S(1)} %collective-permute-done.7.refs_0_), channel_id=1, source_target_pairs={{0,1},{1,0},{2,3},{3,2},{4,5},{5,4},{6,7},{7,6},{8,9},{9,8},{10,11... | collective-permute-start | bytes 2457608 | tf_op jit(solution)/shard_map/ppermute | solution.py:32
  38.6 11.7 %collective-permute-start.14 = (bf16[192,1024]{1,0:T(8,128)(2,1)S(1)}, bf16[192,1024]{1,0:T(8,128)(2,1)}, u32[]{:S(2)}, u32[]{:S(2)}) collective-permute-start(bf16[192,1024]{1,0:T(8,128)(2,1)S(1)} %slice.42), channel_id=1, source_target_pairs={{0,4},{4,0},{8,12},{12,8},{16,20},{20,16},{24,28},{28,24},{1,5},{5... | collective-permute-start | bytes 1179656 | tf_op jit(solution)/shard_map/ppermute | solution.py:32
  39.9 10.7 %collective-permute-start.15 = (bf16[208,1024]{1,0:T(8,128)(2,1)S(1)}, bf16[208,1024]{1,0:T(8,128)(2,1)S(1)}, u32[]{:S(2)}, u32[]{:S(2)}) collective-permute-start(bf16[208,1024]{1,0:T(8,128)(2,1)S(1)} %slice.43), channel_id=1, source_target_pairs={{0,2},{1,3},{2,0},{3,1},{4,6},{5,7},{6,4},{7,5},{8,10},{9,11},{10,... | collective-permute-start | bytes 1277960 | tf_op jit(solution)/shard_map/ppermute | solution.py:32
  40.1 10.1 %collective-permute-start.17 = (bf16[256,256]{1,0:T(8,128)(2,1)S(1)}, bf16[256,256]{1,0:T(8,128)(2,1)S(1)}, u32[]{:S(2)}, u32[]{:S(2)}) collective-permute-start(bf16[256,256]{1,0:T(8,128)(2,1)S(1)} %constant_dynamic-update-slice_fusion), channel_id=1, source_target_pairs={{0,16},{4,20},{8,24},{12,28},{16,0},{20,4},{24,8},{28,12},{1,17},{... | collective-permute-start | bytes 393224 | tf_op jit(solution)/shard_map/ppermute | solution.py:32
  51.6 52.2 %all-to-all-start = ((bf16[32,24,1024]{2,1,0:T(8,128)(2,1)}), bf16[32,24,1024]{2,1,0:T(8,128)(2,1)S(1)}, u32[]{:S(2)}, u32[]{:S(2)}) async-start(bf16[32,24,1024]{2,1,0:T(8,128)(2,1)} %bitcast.18), calls=%async_computation | async-start | bytes 3145728 | tf_op jit(solution)/shard_map/all_to_all | solution.py:693
  57.6 38.1 %collective-permute-start.22 = (bf16[512,256]{1,0:T(8,128)(2,1)S(1)}, bf16[512,256]{1,0:T(8,128)(2,1)S(1)}, u32[]{:S(2)}, u32[]{:S(2)}) collective-permute-start(bf16[512,256]{1,0:T(8,128)(2,1)S(1)} %constant_dynamic-update-slice_fusion.2), channel_id=1, source_target_pairs={{0,4},{4,0},{8,12},{12,8},{16,20},{20,16},{24,28},{28,24},{1,5},{5... | collective-permute-start | bytes 786440 | tf_op jit(solution)/shard_map/ppermute | solution.py:32
  58.9 36.8 %collective-permute-start.23 = (bf16[512,256]{1,0:T(8,128)(2,1)S(1)}, bf16[512,256]{1,0:T(8,128)(2,1)S(1)}, u32[]{:S(2)}, u32[]{:S(2)}) collective-permute-start(bf16[512,256]{1,0:T(8,128)(2,1)S(1)} %constant_dynamic-update-slice_fusion.2), channel_id=1, source_target_pairs={{0,2},{1,3},{2,0},{3,1},{4,6},{5,7},{6,4},{7,5},{8,10},{9,11},{10,... | collective-permute-start | bytes 786440 | tf_op jit(solution)/shard_map/ppermute | solution.py:32
  60.1 35.6 %collective-permute-start.24 = (bf16[512,256]{1,0:T(8,128)(2,1)S(1)}, bf16[512,256]{1,0:T(8,128)(2,1)S(1)}, u32[]{:S(2)}, u32[]{:S(2)}) collective-permute-start(bf16[512,256]{1,0:T(8,128)(2,1)S(1)} %constant_dynamic-update-slice_fusion.2), channel_id=1, source_target_pairs={{0,6},{1,7},{2,4},{3,5},{4,2},{5,3},{6,0},{7,1},{8,14},{9,15},{10,... | collective-permute-start | bytes 786440 | tf_op jit(solution)/shard_map/ppermute | solution.py:715
  70.7 33.2 %collective-permute-start.20 = (bf16[1024,256]{1,0:T(8,128)(2,1)S(1)}, bf16[1024,256]{1,0:T(8,128)(2,1)}, u32[]{:S(2)}, u32[]{:S(2)}) collective-permute-start(bf16[1024,256]{1,0:T(8,128)(2,1)S(1)} %get-tuple-element.109), channel_id=1, source_target_pairs={{0,8},{4,12},{8,16},{12,20},{16,24},{20,28},{1,9},{5,13},{9,17},{1... | collective-permute-start | bytes 1572872 | tf_op jit(solution)/shard_map/ppermute | solution.py:38
  73.9 30.0 %collective-permute-start.21 = (bf16[1024,256]{1,0:T(8,128)(2,1)S(1)}, bf16[1024,256]{1,0:T(8,128)(2,1)}, u32[]{:S(2)}, u32[]{:S(2)}) collective-permute-start(bf16[1024,256]{1,0:T(8,128)(2,1)S(1)} %get-tuple-element.108), channel_id=1, source_target_pairs={{8,0},{12,4},{16,8},{20,12},{24,16},{28,20},{9,1},{13,5},{17,9},{2... | collective-permute-start | bytes 1572872 | tf_op jit(solution)/shard_map/ppermute | solution.py:38
  103.9 52.7 %all-to-all-start.1 = ((bf16[32,24,1024]{2,1,0:T(8,128)(2,1)}), bf16[32,24,1024]{2,1,0:T(8,128)(2,1)S(1)}, u32[]{:S(2)}, u32[]{:S(2)}) async-start(bf16[32,24,1024]{2,1,0:T(8,128)(2,1)} %bitcast.17), calls=%async_computation.1 | async-start | bytes 3145728 | tf_op jit(solution)/shard_map/all_to_all | solution.py:693
  110.1 41.2 %collective-permute-start.32 = (bf16[1024,256]{1,0:T(8,128)(2,1)S(1)}, bf16[1024,256]{1,0:T(8,128)(2,1)}, u32[]{:S(2)}, u32[]{:S(2)}) collective-permute-start(bf16[1024,256]{1,0:T(8,128)(2,1)S(1)} %constant_dynamic-update-slice_fusion.4.refs_8_), channel_id=1, source_target_pairs={{0,1},{1,0},{2,3},{3,2},{4,5},{5,4},{6,7},{7,6},{8,9},{9,8},{10,11... | collective-permute-start | bytes 1572872 | tf_op jit(solution)/shard_map/ppermute | solution.py:32
  112.9 38.4 %collective-permute-start.33 = (bf16[1024,256]{1,0:T(8,128)(2,1)}, bf16[1024,256]{1,0:T(8,128)(2,1)}, u32[]{:S(2)}, u32[]{:S(2)}) collective-permute-start(bf16[1024,256]{1,0:T(8,128)(2,1)} %constant_dynamic-update-slice_fusion.6.refs_10_), channel_id=1, source_target_pairs={{0,1},{1,0},{2,3},{3,2},{4,5},{5,4},{6,7},{7,6},{8,9},{9,8},{10,11... | collective-permute-start | bytes 1572872 | tf_op jit(solution)/shard_map/ppermute | solution.py:32
  134.6 4.9 %collective-permute-start.26 = (bf16[384,128]{1,0:T(8,128)(2,1)}, bf16[384,128]{1,0:T(8,128)(2,1)S(1)}, u32[]{:S(2)}, u32[]{:S(2)}) collective-permute-start(bf16[384,128]{1,0:T(8,128)(2,1)} %get-tuple-element.96), channel_id=1, source_target_pairs={{0,2},{1,3},{2,0},{3,1},{4,6},{5,7},{6,4},{7,5},{8,10},{9,11},{10,... | collective-permute-start | bytes 294920 | tf_op jit(solution)/shard_map/ppermute | solution.py:743
  135.7 7.5 %collective-permute-start.27 = (bf16[384,128]{1,0:T(8,128)(2,1)}, bf16[384,128]{1,0:T(8,128)(2,1)S(1)}, u32[]{:S(2)}, u32[]{:S(2)}) collective-permute-start(bf16[384,128]{1,0:T(8,128)(2,1)} %get-tuple-element.97), channel_id=1, source_target_pairs={{0,3},{1,2},{2,1},{3,0},{4,7},{5,6},{6,5},{7,4},{8,11},{9,10},{10,... | collective-permute-start | bytes 294920 | tf_op jit(solution)/shard_map/ppermute | solution.py:743
  136.3 8.5 %collective-permute-start.28 = (bf16[384,128]{1,0:T(8,128)(2,1)}, bf16[384,128]{1,0:T(8,128)(2,1)S(1)}, u32[]{:S(2)}, u32[]{:S(2)}) collective-permute-start(bf16[384,128]{1,0:T(8,128)(2,1)} %get-tuple-element.98), channel_id=1, source_target_pairs={{0,4},{1,5},{2,6},{3,7},{4,0},{5,1},{6,2},{7,3},{8,12},{9,13},{10,... | collective-permute-start | bytes 294920 | tf_op jit(solution)/shard_map/ppermute | solution.py:743
  139.5 6.7 %collective-permute-start.29 = (bf16[384,128]{1,0:T(8,128)(2,1)}, bf16[384,128]{1,0:T(8,128)(2,1)S(1)}, u32[]{:S(2)}, u32[]{:S(2)}) collective-permute-start(bf16[384,128]{1,0:T(8,128)(2,1)} %get-tuple-element.99), channel_id=1, source_target_pairs={{0,5},{1,4},{2,7},{3,6},{4,1},{5,0},{6,3},{7,2},{8,13},{9,12},{10,... | collective-permute-start | bytes 294920 | tf_op jit(solution)/shard_map/ppermute | solution.py:743
  143.3 5.6 %collective-permute-start.30 = (bf16[384,128]{1,0:T(8,128)(2,1)}, bf16[384,128]{1,0:T(8,128)(2,1)S(1)}, u32[]{:S(2)}, u32[]{:S(2)}) collective-permute-start(bf16[384,128]{1,0:T(8,128)(2,1)} %get-tuple-element.100), channel_id=1, source_target_pairs={{0,6},{1,7},{2,4},{3,5},{4,2},{5,3},{6,0},{7,1},{8,14},{9,15},{10,... | collective-permute-start | bytes 294920 | tf_op jit(solution)/shard_map/ppermute | solution.py:743
  144.8 6.5 %collective-permute-start.31 = (bf16[384,128]{1,0:T(8,128)(2,1)}, bf16[384,128]{1,0:T(8,128)(2,1)S(1)}, u32[]{:S(2)}, u32[]{:S(2)}) collective-permute-start(bf16[384,128]{1,0:T(8,128)(2,1)} %get-tuple-element.101), channel_id=1, source_target_pairs={{0,7},{1,6},{2,5},{3,4},{4,3},{5,2},{6,1},{7,0},{8,15},{9,14},{10,... | collective-permute-start | bytes 294920 | tf_op jit(solution)/shard_map/ppermute | solution.py:743
  (28 other events, 182.1 us)

commit v10 on v9

--- a/solution.py
+++ b/solution.py
@@ -300,8 +300,9 @@
             values[:, own] = with_ones(pairs[own, width:])
 
     jobs = []
+    places = tile_places(step, edge, tiles)
     for side in range(2):
-        tile = step + side * (tiles - edge)
+        tile = places[side]
         queries, starts, ends = rows[3 * side : 3 * side + 3]
         mask_heads(queries, masked.at[side])
         total = outs[side]
@@ -328,7 +329,7 @@
 def finish_kernel(edge, meta, ranges, *refs):
     rows, pairs, halos, held, held_peaks = refs[:6], refs[6], refs[7:9], refs[9:11], refs[11:13]
     outs, (masked, sums, peaks_held, mixed) = refs[13:-4], refs[-4:]
-    held_steps = edge
+    held_steps = edge + 1
     step = pl.program_id(0)
     width = rows[0].shape[1]
     heads = width // HEAD_DIM
@@ -419,7 +420,7 @@
     group_rows, width = queries.shape
     heads = width // HEAD_DIM
     tiles, edge = group_rows // TILE, SPAN // TILE
-    steps = edge
+    steps = edge + 1
     shapes = [(steps, heads * HEAD_ROWS, TILE)] * 2 + [(steps, 8, TILE)] * 2
     return pl.pallas_call(
         functools.partial(edge_kernel, edge),
@@ -458,7 +459,7 @@
             + [pl.BlockSpec((SPAN, 2 * width), lambda i, m, r: (0, 0))] * 2
             + [
                 pl.BlockSpec(
-                    (1,) + part.shape[1:], lambda i, m, r: (jnp.minimum(i, edge - 1), 0, 0)
+                    (1,) + part.shape[1:], lambda i, m, r: (jnp.minimum(i, edge), 0, 0)
                 )
                 for part in held
             ],
@@ -492,30 +493,37 @@
         shard = jnp.where(meta[1] < 0, head_pair, shard // PAIR + shard % PAIR * (members // PAIR))
         columns = pl.ds(pl.multiple_of(shard * width, width), width)
         mixed[:, columns] = parts[distance][...]
-    for distance, weight in enumerate(weights):
-        columns = pl.ds(pl.multiple_of((meta[0] % len(weights) ^ distance) * tile, tile), tile)
+    depth = mixed.shape[1]
+    groups = len(weights) * (weights[0].shape[0] // depth)
+    for distance in range(groups):
+        columns = pl.ds(pl.multiple_of((meta[0] % groups ^ distance) * tile, tile), tile)
+        start = distance // len(weights) * depth
         result[:, columns] = jnp.dot(
-            mixed[...], weight[...], preferred_element_type=jnp.float32
+            mixed[...],
+            weights[distance % len(weights)][start : start + depth, :],
+            preferred_element_type=jnp.float32,
         ).astype(jnp.bfloat16)
 
 
 def output_projection(meta, parts, weights):
     rows, width = parts[0].shape
-    depth, tile = weights[0].shape
+    depth, tile = width * len(parts), weights[0].shape[1]
+    columns = sum(weight.shape[0] for weight in weights) // depth * tile
     whole = lambda shape: pl.BlockSpec(shape, lambda i, m: (0, 0))
     return pl.pallas_call(
         functools.partial(output_kernel, len(parts)),
         grid_spec=pltpu.PrefetchScalarGridSpec(
             num_scalar_prefetch=1,
             grid=(1,),
-            in_specs=[whole(parts[0].shape)] * len(parts) + [whole((depth, tile))] * len(weights),
-            out_specs=whole((rows, len(weights) * tile)),
+            in_specs=[whole(parts[0].shape)] * len(parts)
+            + [whole(weight.shape) for weight in weights],
+            out_specs=whole((rows, columns)),
             scratch_shapes=[pltpu.VMEM((rows, depth), jnp.bfloat16)],
         ),
-        out_shape=jax.ShapeDtypeStruct((rows, len(weights) * tile), jnp.bfloat16),
+        out_shape=jax.ShapeDtypeStruct((rows, columns), jnp.bfloat16),
         compiler_params=PARAMS,
         cost_estimate=pl.CostEstimate(
-            flops=2 * rows * depth * len(weights) * tile,
+            flops=2 * rows * depth * columns,
             bytes_accessed=4 << 20,
             transcendentals=0,
         ),
@@ -725,20 +733,16 @@
         )
     )
     other_row = to_owners(send)
-    columns = [
-        jnp.concatenate([last_rows, other_rows], axis=0),
-        jnp.concatenate([across_rows, corner_rows], axis=0),
-    ]
+    columns = jnp.concatenate([last_rows, other_rows, across_rows, corner_rows], axis=0)
     row_order = place
     if output_weight.shape[0] != width:
         wanted = jnp.arange(peers) ^ place
         wanted = wanted // PAIR + wanted % PAIR * (peers // PAIR)
-        shards = (peers,) + output_weight.shape
-        columns = [part.reshape(shards)[wanted].reshape(part.shape) for part in columns]
+        shards = columns.reshape((PAIR, peers) + output_weight.shape)
+        columns = shards[:, wanted].reshape(columns.shape)
         row_order = jnp.full_like(place, -1)
     mixed = attend_finish(meta, ranges, queries, *bounds, pairs, before, after, edges, rows)
-    siblings = [flipped(part, "grp", 1) for part in columns]
-    last_weights = [columns[0], siblings[0], columns[1], siblings[1]]
+    last_weights = [columns, flipped(columns, "grp", 1)]
     parts = [mixed[0]] + [
         lax.ppermute(
             mixed[distance],

time: 160 us -> 156 us (0.975)
  waiting for transfers between devices: 27.1 us -> 24.1 us
  starting transfers between devices: 46.9 us -> 44.8 us
    pallas_call x1, Pallas kernels: 21 us -> 16.4 us  [attend_finish(): pl.pallas_call(functools.partial(finish_kernel, edge), grid_spec=pltpu.Pr...]
    pallas_call x1, Pallas kernels: 19.7 us -> 23.8 us  [attend_edges(): pl.pallas_call(functools.partial(edge_kernel, edge), grid_spec=pltpu.Pref...]
    ppermute x2, waiting for transfers between devices: 8.11 us -> 3.99 us  [shifted(): lax.ppermute(value, axis, [(source, source + steps) for source in range(i...]
    unnamed x52 -> x51, local copies, waits for them, and re-layouts: 5.26 us -> 7.54 us
    ppermute x7, starting transfers between devices: 8.31 us -> 6.46 us  [per_device(): lax.ppermute(mixed[distance], ('tok', 'grp'), [(source, source ^ distance...]
    ppermute x18 -> x17, starting transfers between devices: 13.2 us -> 13 us  [flipped(): lax.ppermute(value, axis, [(source, source ^ bit) for source in range(cou...]
    ppermute x18 -> x17, waiting for transfers between devices: 10.7 us -> 10.6 us  [flipped(): lax.ppermute(value, axis, [(source, source ^ bit) for source in range(cou...]
  transfers between devices with their start and end apart: 36 -> 35, of which waited for: 10 -> 10; matrix products, arithmetic and copies ran while one was open for 7% -> 8% of each run, Pallas kernels for 42% -> 43%
where the time goes in v10:
time: 156 us; the launch traced here: 155 us
  Pallas kernels  68.9 us (44%)
  starting transfers between devices  44.8 us (29%)
  waiting for transfers between devices  24.1 us (15%)
  local copies, waits for them, and re-layouts  10.3 us (7%)
  other arithmetic  5.94 us (4%)
    pallas_call x1, Pallas kernels, attend_edges(): pl.pallas_call(functools.partial(edge_kernel, edge), grid_spec=pltpu.Pref...  23.8 us
    pallas_call x1, Pallas kernels, attend_finish(): pl.pallas_call(functools.partial(finish_kernel, edge), grid_spec=pltpu.Pr...  16.4 us
    pallas_call x2, Pallas kernels, project(): pl.pallas_call(functools.partial(project_kernel, first, layout, len(weigh...  16.4 us
    ppermute x17, starting transfers between devices, flipped(): lax.ppermute(value, axis, [(source, source ^ bit) for source in range(cou...  13 us
    ppermute x17, waiting for transfers between devices, flipped(): lax.ppermute(value, axis, [(source, source ^ bit) for source in range(cou...  10.6 us
    all_to_all x2, starting transfers between devices, to_owners(): lax.all_to_all(send.reshape((flat,) + send.shape[2:]), ('tok', 'grp'), sp...  10.5 us
    ppermute x7, waiting for transfers between devices, per_device(): lax.ppermute(mixed[distance], ('tok', 'grp'), [(source, source ^ distance...  9.47 us
    ppermute x6, starting transfers between devices, per_device(): pieces.append(lax.ppermute(piece, ('tok', 'grp'), route))  9.33 us
  transfers between devices with their start and end apart: 35, of which 10 were waited for; matrix products, arithmetic and copies ran while one was open for 8% of the time, Pallas kernels for 43%

profile of v10, /device:TPU:17, one launch (start us, length us, event | category | flops | bytes accessed | tf_op | source)
XLA Modules:
  0.0 155.1 jit_solution(14487972945584730225)
XLA Ops:
  1.5 1.3 collective-permute-start.5
  2.8 2.0 %collective-permute-start.4 = (bf16[128,128]{1,0:T(8,128)(2,1)S(1)}, bf16[128,128]{1,0:T(8,128)(2,1)S(1)}, u32[]{:S(2)}, u32[]{:S(2)}) collective-permute-start(bf16[128,128]{1,0:T(8,128)(2,1)S(1)} %get-tuple-element.111), channel_id=1, source_target_pairs={{0,5},{1,4},{2,7},{3,6},{4,1},{5,0},{6,3},{7,2},{8,13},{9,12},{10,... | collective-permute-start | bytes 98312 | tf_op jit(solution)/shard_map/ppermute | solution.py:641
  6.7 1.7 %collective-permute-start.1 = (bf16[128,128]{1,0:T(8,128)(2,1)S(1)}, bf16[128,128]{1,0:T(8,128)(2,1)S(1)}, u32[]{:S(2)}, u32[]{:S(2)}) collective-permute-start(bf16[128,128]{1,0:T(8,128)(2,1)S(1)} %get-tuple-element.114), channel_id=1, source_target_pairs={{0,1},{1,0},{2,3},{3,2},{4,5},{5,4},{6,7},{7,6},{8,9},{9,8},{10,11... | collective-permute-start | bytes 98312 | tf_op jit(solution)/shard_map/ppermute | solution.py:641
  8.4 1.3 fusion.1
  9.8 2.4 %collective-permute-start = (bf16[128,128]{1,0:T(8,128)(2,1)S(1)}, bf16[128,128]{1,0:T(8,128)(2,1)S(1)}, u32[]{:S(2)}, u32[]{:S(2)}) collective-permute-start(bf16[128,128]{1,0:T(8,128)(2,1)S(1)} %get-tuple-element.110), channel_id=1, source_target_pairs={{0,0},{1,3},{2,2},{3,1},{4,4},{5,7},{6,6},{7,5},{8,8},{9,11},{10,1... | collective-permute-start | bytes 98312 | tf_op jit(solution)/shard_map/ppermute | solution.py:641
  12.3 2.6 %layer_norm.1.refs_0_ = bf16[400,1024]{1,0:T(8,128)(2,1)} custom-call(bf16[384,1024]{1,0:T(8,128)(2,1)} %tokens.1, f32[1,1024]{1,0:T(1,128)} %bitcast.21, s32[1,96]{1,0:T(1,128)} %bitcast.22), custom_call_target="tpu_custom_call" | custom-call | tf_op jit(solution)/shard_map/layer_norm/pallas_call | solution.py:65
  18.6 2.5 %document_bounds.1 = (s32[1,3072]{1,0:T(1,128)}, s32[1,3072]{1,0:T(1,128)}, s32[1,128]{1,0:T(1,128)}) custom-call(s32[1,5120]{1,0:T(1,128)} %bitcast.20), custom_call_target="tpu_custom_call" | custom-call | flops 17179869184 | tf_op jit(solution)/shard_map/document_bounds/pallas_call | solution.py:605
  22.0 5.3 %collective-permute-done.10.refs_6_.refs_8_ = bf16[256,384]{1,0:T(8,128)(2,1)S(1)} collective-permute-done((bf16[256,384]{1,0:T(8,128)(2,1)S(1)}, bf16[256,384]{1,0:T(8,128)(2,1)S(1)}, u32[]{:S(2)}, u32[]{:S(2)}) %collective-permute-start.10) | collective-permute-done | bytes 196640 | tf_op jit(solution)/shard_map/ppermute | solution.py:32
  27.3 2.5 %collective-permute-start.11 = (bf16[256,384]{1,0:T(8,128)(2,1)S(1)}, bf16[256,384]{1,0:T(8,128)(2,1)S(1)}, u32[]{:S(2)}, u32[]{:S(2)}) collective-permute-start(bf16[256,384]{1,0:T(8,128)(2,1)S(1)} %collective-permute-done.10.refs_6_.refs_8_), channel_id=1, source_target_pairs={{0,8},{4,12},{8,0},{12,4},{16,24},{20,28},{24,16},{28,20},{1,9},{5... | collective-permute-start | bytes 589832 | tf_op jit(solution)/shard_map/ppermute | solution.py:32
  29.8 2.3 %multiply_sine_fusion = (f32[32,3072]{1,0:T(8,128)}, f32[32,3072]{1,0:T(8,128)}) fusion(f32[3072]{0:T(1024)S(1)} %bitcast.19, f32[32]{0:T(128)S(1)} %negate_power_fusion), kind=kLoop, calls=%fused_computation | loop fusion | flops 98304 | bytes 798848 | tf_op jit(solution)/shard_map/sin | solution.py:569
  32.1 1.5 collective-permute-done.11.refs_7_.refs_9_
  33.6 2.6 %collective-permute-done.6.refs_2_ = bf16[400,1024]{1,0:T(8,128)(2,1)S(1)} collective-permute-done((bf16[400,1024]{1,0:T(8,128)(2,1)}, bf16[400,1024]{1,0:T(8,128)(2,1)S(1)}, u32[]{:S(2)}, u32[]{:S(2)}) %collective-permute-start.6) | collective-permute-done | bytes 819232 | tf_op jit(solution)/shard_map/ppermute | solution.py:32
  38.6 1.3 collective-permute-start.14
  40.2 1.9 %collective-permute-start.17 = (bf16[256,256]{1,0:T(8,128)(2,1)S(1)}, bf16[256,256]{1,0:T(8,128)(2,1)S(1)}, u32[]{:S(2)}, u32[]{:S(2)}) collective-permute-start(bf16[256,256]{1,0:T(8,128)(2,1)S(1)} %constant_dynamic-update-slice_fusion), channel_id=1, source_target_pairs={{0,16},{4,20},{8,24},{12,28},{16,0},{20,4},{24,8},{28,12},{1,17},{... | collective-permute-start | bytes 393224 | tf_op jit(solution)/shard_map/ppermute | solution.py:32
  42.1 8.2 %project.2 = (bf16[3072,128]{1,0:T(8,128)(2,1)}, bf16[3072,256]{1,0:T(8,128)(2,1)}, bf16[8,4,24,1024]{3,2,1,0:T(8,128)(2,1)}) custom-call(s32[5]{0:T(128)} %stack.29.meta, bf16[400,1024]{1,0:T(8,128)(2,1)} %layer_norm.1.refs_0_, bf16[400,1024]{1,0:T(8,128)(2,1)} %copy-done.16, bf16[400,1024]{1,0:T(8,128)(2,1)} %copy-done.6, ...), custom_call_target="tpu_custom_call" | custom-call | flops 9663676416 | bytes 6291456 | tf_op jit(solution)/shard_map/project/pallas_call | solution.py:172
  51.7 5.3 %all-to-all-start = ((bf16[32,24,1024]{2,1,0:T(8,128)(2,1)}), bf16[32,24,1024]{2,1,0:T(8,128)(2,1)S(1)}, u32[]{:S(2)}, u32[]{:S(2)}) async-start(bf16[32,24,1024]{2,1,0:T(8,128)(2,1)} %bitcast.18), calls=%async_computation | async-start | bytes 3145728 | tf_op jit(solution)/shard_map/all_to_all | solution.py:701
  61.3 8.2 %project.3 = (bf16[3072,128]{1,0:T(8,128)(2,1)}, bf16[3072,256]{1,0:T(8,128)(2,1)}, bf16[8,4,24,1024]{3,2,1,0:T(8,128)(2,1)}) custom-call(s32[5]{0:T(128)} %stack.29.meta, bf16[400,1024]{1,0:T(8,128)(2,1)} %copy-done.4, bf16[400,1024]{1,0:T(8,128)(2,1)} %copy-done.15, ...), custom_call_target="tpu_custom_call", output_to_operand_aliasing={{0}: (13, {}), {1}: (14, {})} | custom-call | flops 9663676416 | bytes 6291456 | tf_op jit(solution)/shard_map/project/pallas_call | solution.py:172
  70.7 3.2 %collective-permute-start.20 = (bf16[1024,256]{1,0:T(8,128)(2,1)S(1)}, bf16[1024,256]{1,0:T(8,128)(2,1)}, u32[]{:S(2)}, u32[]{:S(2)}) collective-permute-start(bf16[1024,256]{1,0:T(8,128)(2,1)S(1)} %get-tuple-element.109), channel_id=1, source_target_pairs={{0,8},{4,12},{8,16},{12,20},{16,24},{20,28},{1,9},{5,13},{9,17},{1... | collective-permute-start | bytes 1572872 | tf_op jit(solution)/shard_map/ppermute | solution.py:38
  73.9 2.1 %collective-permute-start.21 = (bf16[1024,256]{1,0:T(8,128)(2,1)S(1)}, bf16[1024,256]{1,0:T(8,128)(2,1)}, u32[]{:S(2)}, u32[]{:S(2)}) collective-permute-start(bf16[1024,256]{1,0:T(8,128)(2,1)S(1)} %get-tuple-element.108), channel_id=1, source_target_pairs={{8,0},{12,4},{16,8},{20,12},{24,16},{28,20},{9,1},{13,5},{17,9},{2... | collective-permute-start | bytes 1572872 | tf_op jit(solution)/shard_map/ppermute | solution.py:38
  76.0 23.8 %attend_edges.1 = (f32[5,160,256]{2,1,0:T(8,128)}, f32[5,160,256]{2,1,0:T(8,128)}, f32[5,8,256]{2,1,0:T(8,128)}, f32[5,8,256]{2,1,0:T(8,128)}) custom-call(s32[5]{0:T(128)} %stack.29.meta, s32[1,128]{1,0:T(1,128)} %get-tuple-element.60.ranges, bf16[3072,128]{1,0:T(8,128)(2,1)} %get-tuple-element.78.refs_0_.refs_3_, ...), custom_call_target="tpu_custom_call" | custom-call | flops 6442450944 | bytes 5242880 | tf_op jit(solution)/shard_map/attend_edges/pallas_call | solution.py:425
  99.9 4.0 %collective-permute-done.20.refs_7_ = bf16[1024,256]{1,0:T(8,128)(2,1)} collective-permute-done((bf16[1024,256]{1,0:T(8,128)(2,1)S(1)}, bf16[1024,256]{1,0:T(8,128)(2,1)}, u32[]{:S(2)}, u32[]{:S(2)}) %collective-permute-start.20) | collective-permute-done | bytes 524320 | tf_op jit(solution)/shard_map/ppermute | solution.py:38
  103.9 5.1 %all-to-all-start.1 = ((bf16[32,24,1024]{2,1,0:T(8,128)(2,1)}), bf16[32,24,1024]{2,1,0:T(8,128)(2,1)S(1)}, u32[]{:S(2)}, u32[]{:S(2)}) async-start(bf16[32,24,1024]{2,1,0:T(8,128)(2,1)} %bitcast.17), calls=%async_computation.1 | async-start | bytes 3145728 | tf_op jit(solution)/shard_map/all_to_all | solution.py:701
  109.8 1.7 %constant_dynamic-update-slice_fusion.6 = bf16[2048,256]{1,0:T(8,128)(2,1)} fusion(bf16[2048,256]{1,0:T(8,128)(2,1)} %constant_dynamic-update-slice_fusion.7, bf16[512,256]{1,0:T(8,128)(2,1)} %copy-done), kind=kLoop, calls=%fused_computation.20 | loop fusion | bytes 524288
  111.5 1.7 %constant_dynamic-update-slice_fusion.5 = bf16[2048,256]{1,0:T(8,128)(2,1)} fusion(bf16[2048,256]{1,0:T(8,128)(2,1)} %constant_dynamic-update-slice_fusion.6, bf16[512,256]{1,0:T(8,128)(2,1)} %copy-done.1), kind=kLoop, calls=%fused_computation.19 | loop fusion | bytes 524288
  114.2 16.4 %attend_finish.1 = (bf16[384,128]{1,0:T(8,128)(2,1)}, bf16[384,128]{1,0:T(8,128)(2,1)}, bf16[384,128]{1,0:T(8,128)(2,1)}, bf16[384,128]{1,0:T(8,128)(2,1)}, bf16...) custom-call(s32[5]{0:T(128)} %stack.29.meta, ...), custom_call_target="tpu_custom_call" | custom-call | flops 6442450944 | bytes 5242880 | tf_op jit(solution)/shard_map/attend_finish/pallas_call | solution.py:453
  134.4 3.1 %collective-permute-done.26.refs_2_ = bf16[384,128]{1,0:T(8,128)(2,1)S(1)} collective-permute-done((bf16[384,128]{1,0:T(8,128)(2,1)}, bf16[384,128]{1,0:T(8,128)(2,1)S(1)}, u32[]{:S(2)}, u32[]{:S(2)}) %collective-permute-start.26) | collective-permute-done | bytes 98336 | tf_op jit(solution)/shard_map/ppermute | solution.py:747
  137.5 1.4 collective-permute-start.30
  138.9 2.8 %collective-permute-done.27.refs_3_ = bf16[384,128]{1,0:T(8,128)(2,1)S(1)} collective-permute-done((bf16[384,128]{1,0:T(8,128)(2,1)}, bf16[384,128]{1,0:T(8,128)(2,1)S(1)}, u32[]{:S(2)}, u32[]{:S(2)}) %collective-permute-start.27) | collective-permute-done | bytes 98336 | tf_op jit(solution)/shard_map/ppermute | solution.py:747
  141.7 1.3 collective-permute-start.31
  144.6 2.7 %collective-permute-done.31.refs_7_ = bf16[384,128]{1,0:T(8,128)(2,1)S(1)} collective-permute-done((bf16[384,128]{1,0:T(8,128)(2,1)}, bf16[384,128]{1,0:T(8,128)(2,1)S(1)}, u32[]{:S(2)}, u32[]{:S(2)}) %collective-permute-start.31) | collective-permute-done | bytes 98336 | tf_op jit(solution)/shard_map/ppermute | solution.py:747
  147.9 4.7 %output_projection.1 = bf16[384,1024]{1,0:T(8,128)(2,1)} custom-call(s32[2]{0:T(128)} %pad_add_fusion.meta, bf16[384,128]{1,0:T(8,128)(2,1)} %get-tuple-element.94.refs_0_, bf16[384,128]{1,0:T(8,128)(2,1)} %copy-done.7, bf16[384,128]{1,0:T(8,128)(2,1)} %copy-done.8, bf16[384,128]{1,0:T(8,128)(2,1)} %copy-done.9, bf16[384,128]{1,0:T(8,128)(2,1)} %copy-done.10, ...), custom_call_target="tpu_custom_call" | custom-call | flops 805306368 | bytes 4194304 | tf_op jit(solution)/shard_map/output_projection/pallas_call | solution.py:513
  152.6 2.4 %unpack.1 = bf16[8,24,8192]{2,1,0:T(8,128)(2,1)} custom-call(bf16[4,2,4,24,1024]{4,3,2,1,0:T(8,128)(2,1)S(1)} %bitcast.14, bf16[4,2,4,24,1024]{4,3,2,1,0:T(8,128)(2,1)S(1)} %bitcast.15), custom_call_target="tpu_custom_call" | custom-call | bytes 6291456 | tf_op jit(solution)/shard_map/unpack/pallas_call | solution.py:551
  (113 shorter events, 24.6 us)
Async XLA Ops:
  1.5 8.3 %collective-permute-start.5 = (bf16[128,128]{1,0:T(8,128)(2,1)S(1)}, bf16[128,128]{1,0:T(8,128)(2,1)S(1)}, u32[]{:S(2)}, u32[]{:S(2)}) collective-permute-start(bf16[128,128]{1,0:T(8,128)(2,1)S(1)} %get-tuple-element.113), channel_id=1, source_target_pairs={{0,6},{1,5},{2,4},{3,7},{4,2},{5,1},{6,0},{7,3},{8,14},{9,13},{10,... | collective-permute-start | bytes 98312 | tf_op jit(solution)/shard_map/ppermute | solution.py:641
  2.8 12.8 %collective-permute-start.4 = (bf16[128,128]{1,0:T(8,128)(2,1)S(1)}, bf16[128,128]{1,0:T(8,128)(2,1)S(1)}, u32[]{:S(2)}, u32[]{:S(2)}) collective-permute-start(bf16[128,128]{1,0:T(8,128)(2,1)S(1)} %get-tuple-element.111), channel_id=1, source_target_pairs={{0,5},{1,4},{2,7},{3,6},{4,1},{5,0},{6,3},{7,2},{8,13},{9,12},{10,... | collective-permute-start | bytes 98312 | tf_op jit(solution)/shard_map/ppermute | solution.py:641
  4.8 12.1 %collective-permute-start.3 = (bf16[128,128]{1,0:T(8,128)(2,1)S(1)}, bf16[128,128]{1,0:T(8,128)(2,1)S(1)}, u32[]{:S(2)}, u32[]{:S(2)}) collective-permute-start(bf16[128,128]{1,0:T(8,128)(2,1)S(1)} %get-tuple-element.112), channel_id=1, source_target_pairs={{0,4},{1,7},{2,6},{3,5},{4,0},{5,3},{6,2},{7,1},{8,12},{9,15},{10,... | collective-permute-start | bytes 98312 | tf_op jit(solution)/shard_map/ppermute | solution.py:641
  6.0 10.8 %collective-permute-start.2 = (bf16[128,128]{1,0:T(8,128)(2,1)S(1)}, bf16[128,128]{1,0:T(8,128)(2,1)S(1)}, u32[]{:S(2)}, u32[]{:S(2)}) collective-permute-start(bf16[128,128]{1,0:T(8,128)(2,1)S(1)} %get-tuple-element.115), channel_id=1, source_target_pairs={{0,2},{1,1},{2,0},{3,3},{4,6},{5,5},{6,4},{7,7},{8,10},{9,9},{10,8... | collective-permute-start | bytes 98312 | tf_op jit(solution)/shard_map/ppermute | solution.py:641
  6.7 10.2 %collective-permute-start.1 = (bf16[128,128]{1,0:T(8,128)(2,1)S(1)}, bf16[128,128]{1,0:T(8,128)(2,1)S(1)}, u32[]{:S(2)}, u32[]{:S(2)}) collective-permute-start(bf16[128,128]{1,0:T(8,128)(2,1)S(1)} %get-tuple-element.114), channel_id=1, source_target_pairs={{0,1},{1,0},{2,3},{3,2},{4,5},{5,4},{6,7},{7,6},{8,9},{9,8},{10,11... | collective-permute-start | bytes 98312 | tf_op jit(solution)/shard_map/ppermute | solution.py:641
  9.8 7.1 %collective-permute-start = (bf16[128,128]{1,0:T(8,128)(2,1)S(1)}, bf16[128,128]{1,0:T(8,128)(2,1)S(1)}, u32[]{:S(2)}, u32[]{:S(2)}) collective-permute-start(bf16[128,128]{1,0:T(8,128)(2,1)S(1)} %get-tuple-element.110), channel_id=1, source_target_pairs={{0,0},{1,3},{2,2},{3,1},{4,4},{5,7},{6,6},{7,5},{8,8},{9,11},{10,1... | collective-permute-start | bytes 98312 | tf_op jit(solution)/shard_map/ppermute | solution.py:641
  15.6 6.2 %collective-permute-start.12 = (bf16[128,256]{1,0:T(8,128)(2,1)S(1)}, bf16[128,256]{1,0:T(8,128)(2,1)S(1)}, u32[]{:S(2)}, u32[]{:S(2)}) collective-permute-start(bf16[128,256]{1,0:T(8,128)(2,1)S(1)} %copy-done.14), channel_id=1, source_target_pairs={{0,8},{4,12},{8,0},{12,4},{16,24},{20,28},{24,16},{28,20},{1,9},{5... | collective-permute-start | bytes 196616 | tf_op jit(solution)/shard_map/ppermute | solution.py:32
  16.9 19.3 %collective-permute-start.6 = (bf16[400,1024]{1,0:T(8,128)(2,1)}, bf16[400,1024]{1,0:T(8,128)(2,1)S(1)}, u32[]{:S(2)}, u32[]{:S(2)}) collective-permute-start(bf16[400,1024]{1,0:T(8,128)(2,1)} %layer_norm.1.refs_0_), channel_id=1, source_target_pairs={{0,2},{1,3},{2,0},{3,1},{4,6},{5,7},{6,4},{7,5},{8,10},{9,11},{10,... | collective-permute-start | bytes 2457608 | tf_op jit(solution)/shard_map/ppermute | solution.py:32
  17.9 19.1 %collective-permute-start.7 = (bf16[400,1024]{1,0:T(8,128)(2,1)}, bf16[400,1024]{1,0:T(8,128)(2,1)S(1)}, u32[]{:S(2)}, u32[]{:S(2)}) collective-permute-start(bf16[400,1024]{1,0:T(8,128)(2,1)} %layer_norm.1.refs_0_), channel_id=1, source_target_pairs={{0,4},{4,0},{8,12},{12,8},{16,20},{20,16},{24,28},{28,24},{1,5},{5... | collective-permute-start | bytes 2457608 | tf_op jit(solution)/shard_map/ppermute | solution.py:32
  18.5 18.5 %collective-permute-start.8 = (bf16[400,1024]{1,0:T(8,128)(2,1)}, bf16[400,1024]{1,0:T(8,128)(2,1)S(1)}, u32[]{:S(2)}, u32[]{:S(2)}) collective-permute-start(bf16[400,1024]{1,0:T(8,128)(2,1)} %layer_norm.1.refs_0_), channel_id=1, source_target_pairs={{0,1},{1,0},{2,3},{3,2},{4,5},{5,4},{6,7},{7,6},{8,9},{9,8},{10,11... | collective-permute-start | bytes 2457608 | tf_op jit(solution)/shard_map/ppermute | solution.py:32
  18.5 8.8 %collective-permute-start.10 = (bf16[256,384]{1,0:T(8,128)(2,1)S(1)}, bf16[256,384]{1,0:T(8,128)(2,1)S(1)}, u32[]{:S(2)}, u32[]{:S(2)}) collective-permute-start(bf16[256,384]{1,0:T(8,128)(2,1)S(1)} %maximum_maximum_fusion.refs_4_.refs_6_), channel_id=1, source_target_pairs={{0,16},{4,20},{8,24},{12,28},{16,0},{20,4},{24,8},{28,12},{1,17},{... | collective-permute-start | bytes 589832 | tf_op jit(solution)/shard_map/ppermute | solution.py:32
  21.8 10.3 %collective-permute-start.9 = (bf16[256,384]{1,0:T(8,128)(2,1)S(1)}, bf16[256,384]{1,0:T(8,128)(2,1)S(1)}, u32[]{:S(2)}, u32[]{:S(2)}) collective-permute-start(bf16[256,384]{1,0:T(8,128)(2,1)S(1)} %maximum_maximum_fusion.refs_4_.refs_6_), channel_id=1, source_target_pairs={{0,8},{4,12},{8,0},{12,4},{16,24},{20,28},{24,16},{28,20},{1,9},{5... | collective-permute-start | bytes 589832 | tf_op jit(solution)/shard_map/ppermute | solution.py:32
  27.3 6.3 %collective-permute-start.11 = (bf16[256,384]{1,0:T(8,128)(2,1)S(1)}, bf16[256,384]{1,0:T(8,128)(2,1)S(1)}, u32[]{:S(2)}, u32[]{:S(2)}) collective-permute-start(bf16[256,384]{1,0:T(8,128)(2,1)S(1)} %collective-permute-done.10.refs_6_.refs_8_), channel_id=1, source_target_pairs={{0,8},{4,12},{8,0},{12,4},{16,24},{20,28},{24,16},{28,20},{1,9},{5... | collective-permute-start | bytes 589832 | tf_op jit(solution)/shard_map/ppermute | solution.py:32
  38.0 4.1 %collective-permute-start.13 = (bf16[400,1024]{1,0:T(8,128)(2,1)S(1)}, bf16[400,1024]{1,0:T(8,128)(2,1)}, u32[]{:S(2)}, u32[]{:S(2)}) collective-permute-start(bf16[400,1024]{1,0:T(8,128)(2,1)S(1)} %collective-permute-done.6.refs_2_), channel_id=1, source_target_pairs={{0,1},{1,0},{2,3},{3,2},{4,5},{5,4},{6,7},{7,6},{8,9},{9,8},{10,11... | collective-permute-start | bytes 2457608 | tf_op jit(solution)/shard_map/ppermute | solution.py:32
  38.0 12.6 %collective-permute-start.16 = (bf16[400,1024]{1,0:T(8,128)(2,1)S(1)}, bf16[400,1024]{1,0:T(8,128)(2,1)S(1)}, u32[]{:S(2)}, u32[]{:S(2)}) collective-permute-start(bf16[400,1024]{1,0:T(8,128)(2,1)S(1)} %collective-permute-done.7.refs_0_), channel_id=1, source_target_pairs={{0,1},{1,0},{2,3},{3,2},{4,5},{5,4},{6,7},{7,6},{8,9},{9,8},{10,11... | collective-permute-start | bytes 2457608 | tf_op jit(solution)/shard_map/ppermute | solution.py:32
  38.6 11.7 %collective-permute-start.14 = (bf16[192,1024]{1,0:T(8,128)(2,1)S(1)}, bf16[192,1024]{1,0:T(8,128)(2,1)}, u32[]{:S(2)}, u32[]{:S(2)}) collective-permute-start(bf16[192,1024]{1,0:T(8,128)(2,1)S(1)} %slice.42), channel_id=1, source_target_pairs={{0,4},{4,0},{8,12},{12,8},{16,20},{20,16},{24,28},{28,24},{1,5},{5... | collective-permute-start | bytes 1179656 | tf_op jit(solution)/shard_map/ppermute | solution.py:32
  39.9 10.7 %collective-permute-start.15 = (bf16[208,1024]{1,0:T(8,128)(2,1)S(1)}, bf16[208,1024]{1,0:T(8,128)(2,1)S(1)}, u32[]{:S(2)}, u32[]{:S(2)}) collective-permute-start(bf16[208,1024]{1,0:T(8,128)(2,1)S(1)} %slice.43), channel_id=1, source_target_pairs={{0,2},{1,3},{2,0},{3,1},{4,6},{5,7},{6,4},{7,5},{8,10},{9,11},{10,... | collective-permute-start | bytes 1277960 | tf_op jit(solution)/shard_map/ppermute | solution.py:32
  40.2 10.1 %collective-permute-start.17 = (bf16[256,256]{1,0:T(8,128)(2,1)S(1)}, bf16[256,256]{1,0:T(8,128)(2,1)S(1)}, u32[]{:S(2)}, u32[]{:S(2)}) collective-permute-start(bf16[256,256]{1,0:T(8,128)(2,1)S(1)} %constant_dynamic-update-slice_fusion), channel_id=1, source_target_pairs={{0,16},{4,20},{8,24},{12,28},{16,0},{20,4},{24,8},{28,12},{1,17},{... | collective-permute-start | bytes 393224 | tf_op jit(solution)/shard_map/ppermute | solution.py:32
  51.7 52.2 %all-to-all-start = ((bf16[32,24,1024]{2,1,0:T(8,128)(2,1)}), bf16[32,24,1024]{2,1,0:T(8,128)(2,1)S(1)}, u32[]{:S(2)}, u32[]{:S(2)}) async-start(bf16[32,24,1024]{2,1,0:T(8,128)(2,1)} %bitcast.18), calls=%async_computation | async-start | bytes 3145728 | tf_op jit(solution)/shard_map/all_to_all | solution.py:701
  57.7 42.2 %collective-permute-start.22 = (bf16[512,256]{1,0:T(8,128)(2,1)S(1)}, bf16[512,256]{1,0:T(8,128)(2,1)S(1)}, u32[]{:S(2)}, u32[]{:S(2)}) collective-permute-start(bf16[512,256]{1,0:T(8,128)(2,1)S(1)} %constant_dynamic-update-slice_fusion.2), channel_id=1, source_target_pairs={{0,4},{4,0},{8,12},{12,8},{16,20},{20,16},{24,28},{28,24},{1,5},{5... | collective-permute-start | bytes 786440 | tf_op jit(solution)/shard_map/ppermute | solution.py:32
  58.9 40.9 %collective-permute-start.23 = (bf16[512,256]{1,0:T(8,128)(2,1)S(1)}, bf16[512,256]{1,0:T(8,128)(2,1)S(1)}, u32[]{:S(2)}, u32[]{:S(2)}) collective-permute-start(bf16[512,256]{1,0:T(8,128)(2,1)S(1)} %constant_dynamic-update-slice_fusion.2), channel_id=1, source_target_pairs={{0,2},{1,3},{2,0},{3,1},{4,6},{5,7},{6,4},{7,5},{8,10},{9,11},{10,... | collective-permute-start | bytes 786440 | tf_op jit(solution)/shard_map/ppermute | solution.py:32
  60.1 39.8 %collective-permute-start.24 = (bf16[512,256]{1,0:T(8,128)(2,1)S(1)}, bf16[512,256]{1,0:T(8,128)(2,1)S(1)}, u32[]{:S(2)}, u32[]{:S(2)}) collective-permute-start(bf16[512,256]{1,0:T(8,128)(2,1)S(1)} %constant_dynamic-update-slice_fusion.2), channel_id=1, source_target_pairs={{0,6},{1,7},{2,4},{3,5},{4,2},{5,3},{6,0},{7,1},{8,14},{9,15},{10,... | collective-permute-start | bytes 786440 | tf_op jit(solution)/shard_map/ppermute | solution.py:723
  70.7 33.2 %collective-permute-start.20 = (bf16[1024,256]{1,0:T(8,128)(2,1)S(1)}, bf16[1024,256]{1,0:T(8,128)(2,1)}, u32[]{:S(2)}, u32[]{:S(2)}) collective-permute-start(bf16[1024,256]{1,0:T(8,128)(2,1)S(1)} %get-tuple-element.109), channel_id=1, source_target_pairs={{0,8},{4,12},{8,16},{12,20},{16,24},{20,28},{1,9},{5,13},{9,17},{1... | collective-permute-start | bytes 1572872 | tf_op jit(solution)/shard_map/ppermute | solution.py:38
  73.9 30.0 %collective-permute-start.21 = (bf16[1024,256]{1,0:T(8,128)(2,1)S(1)}, bf16[1024,256]{1,0:T(8,128)(2,1)}, u32[]{:S(2)}, u32[]{:S(2)}) collective-permute-start(bf16[1024,256]{1,0:T(8,128)(2,1)S(1)} %get-tuple-element.108), channel_id=1, source_target_pairs={{8,0},{12,4},{16,8},{20,12},{24,16},{28,20},{9,1},{13,5},{17,9},{2... | collective-permute-start | bytes 1572872 | tf_op jit(solution)/shard_map/ppermute | solution.py:38
  103.9 48.7 %all-to-all-start.1 = ((bf16[32,24,1024]{2,1,0:T(8,128)(2,1)}), bf16[32,24,1024]{2,1,0:T(8,128)(2,1)S(1)}, u32[]{:S(2)}, u32[]{:S(2)}) async-start(bf16[32,24,1024]{2,1,0:T(8,128)(2,1)} %bitcast.17), calls=%async_computation.1 | async-start | bytes 3145728 | tf_op jit(solution)/shard_map/all_to_all | solution.py:701
  113.9 33.4 %collective-permute-start.32 = (bf16[2048,256]{1,0:T(8,128)(2,1)}, bf16[2048,256]{1,0:T(8,128)(2,1)}, u32[]{:S(2)}, u32[]{:S(2)}) collective-permute-start(bf16[2048,256]{1,0:T(8,128)(2,1)} %constant_dynamic-update-slice_fusion.4.refs_8_), channel_id=1, source_target_pairs={{0,1},{1,0},{2,3},{3,2},{4,5},{5,4},{6,7},{7,6},{8,9},{9,8},{10,11... | collective-permute-start | bytes 3145736 | tf_op jit(solution)/shard_map/ppermute | solution.py:32
  130.9 6.6 %collective-permute-start.26 = (bf16[384,128]{1,0:T(8,128)(2,1)}, bf16[384,128]{1,0:T(8,128)(2,1)S(1)}, u32[]{:S(2)}, u32[]{:S(2)}) collective-permute-start(bf16[384,128]{1,0:T(8,128)(2,1)} %get-tuple-element.96), channel_id=1, source_target_pairs={{0,2},{1,3},{2,0},{3,1},{4,6},{5,7},{6,4},{7,5},{8,10},{9,11},{10,... | collective-permute-start | bytes 294920 | tf_op jit(solution)/shard_map/ppermute | solution.py:747
  132.1 9.6 %collective-permute-start.27 = (bf16[384,128]{1,0:T(8,128)(2,1)}, bf16[384,128]{1,0:T(8,128)(2,1)S(1)}, u32[]{:S(2)}, u32[]{:S(2)}) collective-permute-start(bf16[384,128]{1,0:T(8,128)(2,1)} %get-tuple-element.97), channel_id=1, source_target_pairs={{0,3},{1,2},{2,1},{3,0},{4,7},{5,6},{6,5},{7,4},{8,11},{9,10},{10,... | collective-permute-start | bytes 294920 | tf_op jit(solution)/shard_map/ppermute | solution.py:747
  132.9 10.8 %collective-permute-start.28 = (bf16[384,128]{1,0:T(8,128)(2,1)}, bf16[384,128]{1,0:T(8,128)(2,1)S(1)}, u32[]{:S(2)}, u32[]{:S(2)}) collective-permute-start(bf16[384,128]{1,0:T(8,128)(2,1)} %get-tuple-element.98), channel_id=1, source_target_pairs={{0,4},{1,5},{2,6},{3,7},{4,0},{5,1},{6,2},{7,3},{8,12},{9,13},{10,... | collective-permute-start | bytes 294920 | tf_op jit(solution)/shard_map/ppermute | solution.py:747
  134.1 10.5 %collective-permute-start.29 = (bf16[384,128]{1,0:T(8,128)(2,1)}, bf16[384,128]{1,0:T(8,128)(2,1)S(1)}, u32[]{:S(2)}, u32[]{:S(2)}) collective-permute-start(bf16[384,128]{1,0:T(8,128)(2,1)} %get-tuple-element.99), channel_id=1, source_target_pairs={{0,5},{1,4},{2,7},{3,6},{4,1},{5,0},{6,3},{7,2},{8,13},{9,12},{10,... | collective-permute-start | bytes 294920 | tf_op jit(solution)/shard_map/ppermute | solution.py:747
  137.5 7.1 %collective-permute-start.30 = (bf16[384,128]{1,0:T(8,128)(2,1)}, bf16[384,128]{1,0:T(8,128)(2,1)S(1)}, u32[]{:S(2)}, u32[]{:S(2)}) collective-permute-start(bf16[384,128]{1,0:T(8,128)(2,1)} %get-tuple-element.100), channel_id=1, source_target_pairs={{0,6},{1,7},{2,4},{3,5},{4,2},{5,3},{6,0},{7,1},{8,14},{9,15},{10,... | collective-permute-start | bytes 294920 | tf_op jit(solution)/shard_map/ppermute | solution.py:747
  141.7 5.6 %collective-permute-start.31 = (bf16[384,128]{1,0:T(8,128)(2,1)}, bf16[384,128]{1,0:T(8,128)(2,1)S(1)}, u32[]{:S(2)}, u32[]{:S(2)}) collective-permute-start(bf16[384,128]{1,0:T(8,128)(2,1)} %get-tuple-element.101), channel_id=1, source_target_pairs={{0,7},{1,6},{2,5},{3,4},{4,3},{5,2},{6,1},{7,0},{8,15},{9,14},{10,... | collective-permute-start | bytes 294920 | tf_op jit(solution)/shard_map/ppermute | solution.py:747
  (26 other events, 130.3 us)

commit v11 on v10

--- a/solution.py
+++ b/solution.py
@@ -531,6 +531,33 @@
     )(meta, *parts, *weights)
 
 
+def stack_kernel(count, *refs):
+    blocks, result, sems = refs[:count], refs[count], refs[count + 1]
+    rows = blocks[0].shape[0]
+    copies = [
+        pltpu.make_async_copy(block, result.at[pl.ds(number * rows, rows), :], sems.at[number])
+        for number, block in enumerate(blocks)
+    ]
+    for copy in copies:
+        copy.start()
+    for copy in copies:
+        copy.wait()
+
+
+def stacked(blocks):
+    rows, width = blocks[0].shape
+    return pl.pallas_call(
+        functools.partial(stack_kernel, len(blocks)),
+        in_specs=[pl.BlockSpec(memory_space=pl.ANY)] * len(blocks),
+        out_specs=pl.BlockSpec(memory_space=pl.ANY),
+        out_shape=jax.ShapeDtypeStruct((len(blocks) * rows, width), blocks[0].dtype),
+        scratch_shapes=[pltpu.SemaphoreType.DMA((len(blocks),))],
+        compiler_params=PARAMS,
+        cost_estimate=pl.CostEstimate(flops=0, bytes_accessed=2 << 20, transcendentals=0),
+        name="stacked",
+    )(*blocks)
+
+
 def unpack_kernel(own_row, other_row, pages):
     _, pair, members, capacity, part = own_row.shape
     width = part // (2 * PAGE)
@@ -658,6 +685,7 @@
     weights = [planes[distance] for distance in range(0, peers, PAIR)]
 
     first_row = place // PAIR * group_rows
+    segment_ids, plane = lax.optimization_barrier((segment_ids, plane))
     padded_ids = jnp.concatenate(
         [
             jnp.full((SPAN,), -1, jnp.int32),
@@ -666,7 +694,6 @@
         ]
     )
     window_ids = lax.dynamic_slice_in_dim(padded_ids, first_row, group_rows + 2 * SPAN, 0)
-    window_ids, plane = lax.optimization_barrier((window_ids, plane))
     *bounds, ranges = document_bounds(window_ids, group_rows)
     positions = SPAN + jnp.arange(group_rows, dtype=jnp.int32) - bounds[0][0]
     order = [(number * members + column) % PARTS for number in range(PARTS)]
@@ -733,7 +760,7 @@
         )
     )
     other_row = to_owners(send)
-    columns = jnp.concatenate([last_rows, other_rows, across_rows, corner_rows], axis=0)
+    columns = stacked([last_rows, other_rows, across_rows, corner_rows])
     row_order = place
     if output_weight.shape[0] != width:
         wanted = jnp.arange(peers) ^ place

time: 156 us -> 181 us (1.16)
  Pallas kernels: 68.9 us -> 99.2 us
  local copies, waits for them, and re-layouts: 10.3 us -> 5.97 us
    pallas_call x0 -> x1, Pallas kernels: none -> 32.9 us  [stacked(): pl.pallas_call(functools.partial(stack_kernel, len(blocks)), in_specs=[pl...]
    ppermute x7, waiting for transfers between devices: 9.47 us -> 5.08 us  [per_device(): lax.ppermute(mixed[distance], ('tok', 'grp'), [(source, source ^ distance...]
    pallas_call x1, Pallas kernels: 23.8 us -> 19.9 us  [attend_edges(): pl.pallas_call(functools.partial(edge_kernel, edge), grid_spec=pltpu.Pref...]
    unnamed x51 -> x48, local copies, waits for them, and re-layouts: 7.54 us -> 4.01 us
    ppermute x2, waiting for transfers between devices: 3.99 us -> 7.27 us  [shifted(): lax.ppermute(value, axis, [(source, source + steps) for source in range(i...]
  transfers between devices with their start and end apart: 35 -> 35, of which waited for: 10 -> 10; matrix products, arithmetic and copies ran while one was open for 8% -> 3% of each run, Pallas kernels for 43% -> 54%
where the time goes in v11:
time: 181 us; the launch traced here: 180 us
  Pallas kernels  99.2 us (55%)
  starting transfers between devices  45.9 us (25%)
  waiting for transfers between devices  22.3 us (12%)
  local copies, waits for them, and re-layouts  5.97 us (3%)
  other arithmetic  5.16 us (3%)
    pallas_call x1, Pallas kernels, stacked(): pl.pallas_call(functools.partial(stack_kernel, len(blocks)), in_specs=[pl...  32.9 us
    pallas_call x1, Pallas kernels, attend_edges(): pl.pallas_call(functools.partial(edge_kernel, edge), grid_spec=pltpu.Pref...  19.9 us
    pallas_call x1, Pallas kernels, attend_finish(): pl.pallas_call(functools.partial(finish_kernel, edge), grid_spec=pltpu.Pr...  17.7 us
    pallas_call x2, Pallas kernels, project(): pl.pallas_call(functools.partial(project_kernel, first, layout, len(weigh...  16.4 us
    ppermute x17, starting transfers between devices, flipped(): lax.ppermute(value, axis, [(source, source ^ bit) for source in range(cou...  13.1 us
    all_to_all x2, starting transfers between devices, to_owners(): lax.all_to_all(send.reshape((flat,) + send.shape[2:]), ('tok', 'grp'), sp...  10.5 us
    ppermute x17, waiting for transfers between devices, flipped(): lax.ppermute(value, axis, [(source, source ^ bit) for source in range(cou...  9.96 us
    ppermute x6, starting transfers between devices, per_device(): pieces.append(lax.ppermute(piece, ('tok', 'grp'), route))  9.33 us
  transfers between devices with their start and end apart: 35, of which 10 were waited for; matrix products, arithmetic and copies ran while one was open for 3% of the time, Pallas kernels for 54%

profile of v11, /device:TPU:17, one launch (start us, length us, event | category | flops | bytes accessed | tf_op | source)
XLA Modules:
  0.0 179.7 jit_solution(7220349795549311985)
XLA Ops:
  1.5 1.3 collective-permute-start.5
  2.8 2.0 %collective-permute-start.4 = (bf16[128,128]{1,0:T(8,128)(2,1)S(1)}, bf16[128,128]{1,0:T(8,128)(2,1)S(1)}, u32[]{:S(2)}, u32[]{:S(2)}) collective-permute-start(bf16[128,128]{1,0:T(8,128)(2,1)S(1)} %get-tuple-element.111), channel_id=1, source_target_pairs={{0,5},{1,4},{2,7},{3,6},{4,1},{5,0},{6,3},{7,2},{8,13},{9,12},{10,... | collective-permute-start | bytes 98312 | tf_op jit(solution)/shard_map/ppermute | solution.py:668
  4.8 1.2 collective-permute-start.3
  6.7 1.7 collective-permute-start.1
  8.5 2.4 %collective-permute-start = (bf16[128,128]{1,0:T(8,128)(2,1)S(1)}, bf16[128,128]{1,0:T(8,128)(2,1)S(1)}, u32[]{:S(2)}, u32[]{:S(2)}) collective-permute-start(bf16[128,128]{1,0:T(8,128)(2,1)S(1)} %get-tuple-element.110), channel_id=1, source_target_pairs={{0,0},{1,3},{2,2},{3,1},{4,4},{5,7},{6,6},{7,5},{8,8},{9,11},{10,1... | collective-permute-start | bytes 98312 | tf_op jit(solution)/shard_map/ppermute | solution.py:668
  11.0 2.6 %layer_norm.1.refs_0_ = bf16[400,1024]{1,0:T(8,128)(2,1)} custom-call(bf16[384,1024]{1,0:T(8,128)(2,1)} %tokens.1, f32[1,1024]{1,0:T(1,128)} %bitcast.21, s32[1,96]{1,0:T(1,128)} %bitcast.22), custom_call_target="tpu_custom_call" | custom-call | tf_op jit(solution)/shard_map/layer_norm/pallas_call | solution.py:65
  14.2 1.3 collective-permute-start.12
  17.8 2.5 %document_bounds.1 = (s32[1,3072]{1,0:T(1,128)}, s32[1,3072]{1,0:T(1,128)}, s32[1,128]{1,0:T(1,128)}) custom-call(s32[1,5120]{1,0:T(1,128)} %bitcast.20), custom_call_target="tpu_custom_call" | custom-call | flops 17179869184 | tf_op jit(solution)/shard_map/document_bounds/pallas_call | solution.py:632
  21.3 4.7 %collective-permute-done.10.refs_6_.refs_8_ = bf16[256,384]{1,0:T(8,128)(2,1)S(1)} collective-permute-done((bf16[256,384]{1,0:T(8,128)(2,1)S(1)}, bf16[256,384]{1,0:T(8,128)(2,1)S(1)}, u32[]{:S(2)}, u32[]{:S(2)}) %collective-permute-start.10) | collective-permute-done | bytes 196640 | tf_op jit(solution)/shard_map/ppermute | solution.py:32
  26.0 2.5 %collective-permute-start.11 = (bf16[256,384]{1,0:T(8,128)(2,1)S(1)}, bf16[256,384]{1,0:T(8,128)(2,1)S(1)}, u32[]{:S(2)}, u32[]{:S(2)}) collective-permute-start(bf16[256,384]{1,0:T(8,128)(2,1)S(1)} %collective-permute-done.10.refs_6_.refs_8_), channel_id=1, source_target_pairs={{0,8},{4,12},{8,0},{12,4},{16,24},{20,28},{24,16},{28,20},{1,9},{5... | collective-permute-start | bytes 589832 | tf_op jit(solution)/shard_map/ppermute | solution.py:32
  28.4 2.3 %multiply_sine_fusion = (f32[32,3072]{1,0:T(8,128)}, f32[32,3072]{1,0:T(8,128)}) fusion(f32[3072]{0:T(1024)S(1)} %bitcast.19, f32[32]{0:T(128)S(1)} %negate_power_fusion), kind=kLoop, calls=%fused_computation | loop fusion | flops 98304 | bytes 798848 | tf_op jit(solution)/shard_map/sin | solution.py:596
  30.8 1.5 collective-permute-done.11.refs_7_.refs_9_
  32.2 2.6 %collective-permute-done.6.refs_2_ = bf16[400,1024]{1,0:T(8,128)(2,1)S(1)} collective-permute-done((bf16[400,1024]{1,0:T(8,128)(2,1)}, bf16[400,1024]{1,0:T(8,128)(2,1)S(1)}, u32[]{:S(2)}, u32[]{:S(2)}) %collective-permute-start.6) | collective-permute-done | bytes 819232 | tf_op jit(solution)/shard_map/ppermute | solution.py:32
  37.2 1.2 collective-permute-start.14
  38.7 1.9 %collective-permute-start.17 = (bf16[256,256]{1,0:T(8,128)(2,1)S(1)}, bf16[256,256]{1,0:T(8,128)(2,1)S(1)}, u32[]{:S(2)}, u32[]{:S(2)}) collective-permute-start(bf16[256,256]{1,0:T(8,128)(2,1)S(1)} %constant_dynamic-update-slice_fusion), channel_id=1, source_target_pairs={{0,16},{4,20},{8,24},{12,28},{16,0},{20,4},{24,8},{28,12},{1,17},{... | collective-permute-start | bytes 393224 | tf_op jit(solution)/shard_map/ppermute | solution.py:32
  40.7 8.2 %project.2 = (bf16[3072,128]{1,0:T(8,128)(2,1)}, bf16[3072,256]{1,0:T(8,128)(2,1)}, bf16[8,4,24,1024]{3,2,1,0:T(8,128)(2,1)}) custom-call(s32[5]{0:T(128)} %stack.29.meta, bf16[400,1024]{1,0:T(8,128)(2,1)} %layer_norm.1.refs_0_, bf16[400,1024]{1,0:T(8,128)(2,1)} %copy-done.17, bf16[400,1024]{1,0:T(8,128)(2,1)} %copy-done.6, ...), custom_call_target="tpu_custom_call" | custom-call | flops 9663676416 | bytes 6291456 | tf_op jit(solution)/shard_map/project/pallas_call | solution.py:172
  50.2 5.4 %all-to-all-start = ((bf16[32,24,1024]{2,1,0:T(8,128)(2,1)}), bf16[32,24,1024]{2,1,0:T(8,128)(2,1)S(1)}, u32[]{:S(2)}, u32[]{:S(2)}) async-start(bf16[32,24,1024]{2,1,0:T(8,128)(2,1)} %bitcast.18), calls=%async_computation | async-start | bytes 3145728 | tf_op jit(solution)/shard_map/all_to_all | solution.py:728
  56.3 1.3 collective-permute-start.22
  60.5 8.2 %project.3 = (bf16[3072,128]{1,0:T(8,128)(2,1)}, bf16[3072,256]{1,0:T(8,128)(2,1)}, bf16[8,4,24,1024]{3,2,1,0:T(8,128)(2,1)}) custom-call(s32[5]{0:T(128)} %stack.29.meta, bf16[400,1024]{1,0:T(8,128)(2,1)} %copy-done.4, bf16[400,1024]{1,0:T(8,128)(2,1)} %copy-done.16, ...), custom_call_target="tpu_custom_call", output_to_operand_aliasing={{0}: (13, {}), {1}: (14, {})} | custom-call | flops 9663676416 | bytes 6291456 | tf_op jit(solution)/shard_map/project/pallas_call | solution.py:172
  68.7 1.3 fusion.2
  70.0 3.2 %collective-permute-start.20 = (bf16[1024,256]{1,0:T(8,128)(2,1)S(1)}, bf16[1024,256]{1,0:T(8,128)(2,1)}, u32[]{:S(2)}, u32[]{:S(2)}) collective-permute-start(bf16[1024,256]{1,0:T(8,128)(2,1)S(1)} %get-tuple-element.109), channel_id=1, source_target_pairs={{0,8},{4,12},{8,16},{12,20},{16,24},{20,28},{1,9},{5,13},{9,17},{1... | collective-permute-start | bytes 1572872 | tf_op jit(solution)/shard_map/ppermute | solution.py:38
  73.2 2.1 %collective-permute-start.21 = (bf16[1024,256]{1,0:T(8,128)(2,1)S(1)}, bf16[1024,256]{1,0:T(8,128)(2,1)}, u32[]{:S(2)}, u32[]{:S(2)}) collective-permute-start(bf16[1024,256]{1,0:T(8,128)(2,1)S(1)} %get-tuple-element.108), channel_id=1, source_target_pairs={{8,0},{12,4},{16,8},{20,12},{24,16},{28,20},{9,1},{13,5},{17,9},{2... | collective-permute-start | bytes 1572872 | tf_op jit(solution)/shard_map/ppermute | solution.py:38
  75.3 19.9 %attend_edges.1 = (f32[5,160,256]{2,1,0:T(8,128)}, f32[5,160,256]{2,1,0:T(8,128)}, f32[5,8,256]{2,1,0:T(8,128)}, f32[5,8,256]{2,1,0:T(8,128)}) custom-call(s32[5]{0:T(128)} %stack.29.meta, s32[1,128]{1,0:T(1,128)} %get-tuple-element.60.ranges, bf16[3072,128]{1,0:T(8,128)(2,1)} %get-tuple-element.78.refs_0_.refs_3_, ...), custom_call_target="tpu_custom_call" | custom-call | flops 6442450944 | bytes 5242880 | tf_op jit(solution)/shard_map/attend_edges/pallas_call | solution.py:425
  95.2 7.3 %collective-permute-done.20.refs_7_ = bf16[1024,256]{1,0:T(8,128)(2,1)} collective-permute-done((bf16[1024,256]{1,0:T(8,128)(2,1)S(1)}, bf16[1024,256]{1,0:T(8,128)(2,1)}, u32[]{:S(2)}, u32[]{:S(2)}) %collective-permute-start.20) | collective-permute-done | bytes 524320 | tf_op jit(solution)/shard_map/ppermute | solution.py:38
  102.5 5.1 %all-to-all-start.1 = ((bf16[32,24,1024]{2,1,0:T(8,128)(2,1)}), bf16[32,24,1024]{2,1,0:T(8,128)(2,1)S(1)}, u32[]{:S(2)}, u32[]{:S(2)}) async-start(bf16[32,24,1024]{2,1,0:T(8,128)(2,1)} %bitcast.17), calls=%async_computation.1 | async-start | bytes 3145728 | tf_op jit(solution)/shard_map/all_to_all | solution.py:728
  107.7 32.9 %stacked.1.refs_8_ = bf16[2048,256]{1,0:T(8,128)(2,1)} custom-call(bf16[512,256]{1,0:T(8,128)(2,1)} %copy-done, bf16[512,256]{1,0:T(8,128)(2,1)} %copy-done.1, bf16[512,256]{1,0:T(8,128)(2,1)} %copy-done.2, bf16[512,256]{1,0:T(8,128)(2,1)} %copy-done.3), custom_call_target="tpu_custom_call" | custom-call | bytes 2097152 | tf_op jit(solution)/shard_map/stacked/pallas_call | solution.py:549
  141.0 17.7 %attend_finish.1 = (bf16[384,128]{1,0:T(8,128)(2,1)}, bf16[384,128]{1,0:T(8,128)(2,1)}, bf16[384,128]{1,0:T(8,128)(2,1)}, bf16[384,128]{1,0:T(8,128)(2,1)}, bf16...) custom-call(s32[5]{0:T(128)} %stack.29.meta, ...), custom_call_target="tpu_custom_call" | custom-call | flops 6442450944 | bytes 5242880 | tf_op jit(solution)/shard_map/attend_finish/pallas_call | solution.py:453
  163.2 2.1 %collective-permute-start.30 = (bf16[384,128]{1,0:T(8,128)(2,1)}, bf16[384,128]{1,0:T(8,128)(2,1)S(1)}, u32[]{:S(2)}, u32[]{:S(2)}) collective-permute-start(bf16[384,128]{1,0:T(8,128)(2,1)} %get-tuple-element.100), channel_id=1, source_target_pairs={{0,6},{1,7},{2,4},{3,5},{4,2},{5,3},{6,0},{7,1},{8,14},{9,15},{10,... | collective-permute-start | bytes 294920 | tf_op jit(solution)/shard_map/ppermute | solution.py:774
  166.1 1.6 collective-permute-start.31
  169.2 2.7 %collective-permute-done.31.refs_7_ = bf16[384,128]{1,0:T(8,128)(2,1)S(1)} collective-permute-done((bf16[384,128]{1,0:T(8,128)(2,1)}, bf16[384,128]{1,0:T(8,128)(2,1)S(1)}, u32[]{:S(2)}, u32[]{:S(2)}) %collective-permute-start.31) | collective-permute-done | bytes 98336 | tf_op jit(solution)/shard_map/ppermute | solution.py:774
  172.5 4.7 %output_projection.1 = bf16[384,1024]{1,0:T(8,128)(2,1)} custom-call(s32[2]{0:T(128)} %pad_add_fusion.meta, bf16[384,128]{1,0:T(8,128)(2,1)} %get-tuple-element.94.refs_0_, bf16[384,128]{1,0:T(8,128)(2,1)} %copy-done.7, bf16[384,128]{1,0:T(8,128)(2,1)} %copy-done.8, bf16[384,128]{1,0:T(8,128)(2,1)} %copy-done.9, bf16[384,128]{1,0:T(8,128)(2,1)} %copy-done.10, ...), custom_call_target="tpu_custom_call" | custom-call | flops 805306368 | bytes 4194304 | tf_op jit(solution)/shard_map/output_projection/pallas_call | solution.py:513
  177.2 2.4 %unpack.1 = bf16[8,24,8192]{2,1,0:T(8,128)(2,1)} custom-call(bf16[4,2,4,24,1024]{4,3,2,1,0:T(8,128)(2,1)S(1)} %bitcast.14, bf16[4,2,4,24,1024]{4,3,2,1,0:T(8,128)(2,1)S(1)} %bitcast.15), custom_call_target="tpu_custom_call" | custom-call | bytes 6291456 | tf_op jit(solution)/shard_map/unpack/pallas_call | solution.py:578
  (110 shorter events, 20.7 us)
Async XLA Ops:
  1.5 6.9 %collective-permute-start.5 = (bf16[128,128]{1,0:T(8,128)(2,1)S(1)}, bf16[128,128]{1,0:T(8,128)(2,1)S(1)}, u32[]{:S(2)}, u32[]{:S(2)}) collective-permute-start(bf16[128,128]{1,0:T(8,128)(2,1)S(1)} %get-tuple-element.113), channel_id=1, source_target_pairs={{0,6},{1,5},{2,4},{3,7},{4,2},{5,1},{6,0},{7,3},{8,14},{9,13},{10,... | collective-permute-start | bytes 98312 | tf_op jit(solution)/shard_map/ppermute | solution.py:668
  2.8 11.4 %collective-permute-start.4 = (bf16[128,128]{1,0:T(8,128)(2,1)S(1)}, bf16[128,128]{1,0:T(8,128)(2,1)S(1)}, u32[]{:S(2)}, u32[]{:S(2)}) collective-permute-start(bf16[128,128]{1,0:T(8,128)(2,1)S(1)} %get-tuple-element.111), channel_id=1, source_target_pairs={{0,5},{1,4},{2,7},{3,6},{4,1},{5,0},{6,3},{7,2},{8,13},{9,12},{10,... | collective-permute-start | bytes 98312 | tf_op jit(solution)/shard_map/ppermute | solution.py:668
  4.8 10.7 %collective-permute-start.3 = (bf16[128,128]{1,0:T(8,128)(2,1)S(1)}, bf16[128,128]{1,0:T(8,128)(2,1)S(1)}, u32[]{:S(2)}, u32[]{:S(2)}) collective-permute-start(bf16[128,128]{1,0:T(8,128)(2,1)S(1)} %get-tuple-element.112), channel_id=1, source_target_pairs={{0,4},{1,7},{2,6},{3,5},{4,0},{5,3},{6,2},{7,1},{8,12},{9,15},{10,... | collective-permute-start | bytes 98312 | tf_op jit(solution)/shard_map/ppermute | solution.py:668
  6.1 9.5 %collective-permute-start.2 = (bf16[128,128]{1,0:T(8,128)(2,1)S(1)}, bf16[128,128]{1,0:T(8,128)(2,1)S(1)}, u32[]{:S(2)}, u32[]{:S(2)}) collective-permute-start(bf16[128,128]{1,0:T(8,128)(2,1)S(1)} %get-tuple-element.115), channel_id=1, source_target_pairs={{0,2},{1,1},{2,0},{3,3},{4,6},{5,5},{6,4},{7,7},{8,10},{9,9},{10,8... | collective-permute-start | bytes 98312 | tf_op jit(solution)/shard_map/ppermute | solution.py:668
  6.7 8.8 %collective-permute-start.1 = (bf16[128,128]{1,0:T(8,128)(2,1)S(1)}, bf16[128,128]{1,0:T(8,128)(2,1)S(1)}, u32[]{:S(2)}, u32[]{:S(2)}) collective-permute-start(bf16[128,128]{1,0:T(8,128)(2,1)S(1)} %get-tuple-element.114), channel_id=1, source_target_pairs={{0,1},{1,0},{2,3},{3,2},{4,5},{5,4},{6,7},{7,6},{8,9},{9,8},{10,11... | collective-permute-start | bytes 98312 | tf_op jit(solution)/shard_map/ppermute | solution.py:668
  8.5 7.1 %collective-permute-start = (bf16[128,128]{1,0:T(8,128)(2,1)S(1)}, bf16[128,128]{1,0:T(8,128)(2,1)S(1)}, u32[]{:S(2)}, u32[]{:S(2)}) collective-permute-start(bf16[128,128]{1,0:T(8,128)(2,1)S(1)} %get-tuple-element.110), channel_id=1, source_target_pairs={{0,0},{1,3},{2,2},{3,1},{4,4},{5,7},{6,6},{7,5},{8,8},{9,11},{10,1... | collective-permute-start | bytes 98312 | tf_op jit(solution)/shard_map/ppermute | solution.py:668
  14.2 6.8 %collective-permute-start.12 = (bf16[128,256]{1,0:T(8,128)(2,1)S(1)}, bf16[128,256]{1,0:T(8,128)(2,1)S(1)}, u32[]{:S(2)}, u32[]{:S(2)}) collective-permute-start(bf16[128,256]{1,0:T(8,128)(2,1)S(1)} %copy-done.14), channel_id=1, source_target_pairs={{0,8},{4,12},{8,0},{12,4},{16,24},{20,28},{24,16},{28,20},{1,9},{5... | collective-permute-start | bytes 196616 | tf_op jit(solution)/shard_map/ppermute | solution.py:32
  15.6 19.2 %collective-permute-start.6 = (bf16[400,1024]{1,0:T(8,128)(2,1)}, bf16[400,1024]{1,0:T(8,128)(2,1)S(1)}, u32[]{:S(2)}, u32[]{:S(2)}) collective-permute-start(bf16[400,1024]{1,0:T(8,128)(2,1)} %layer_norm.1.refs_0_), channel_id=1, source_target_pairs={{0,2},{1,3},{2,0},{3,1},{4,6},{5,7},{6,4},{7,5},{8,10},{9,11},{10,... | collective-permute-start | bytes 2457608 | tf_op jit(solution)/shard_map/ppermute | solution.py:32
  16.6 19.1 %collective-permute-start.7 = (bf16[400,1024]{1,0:T(8,128)(2,1)}, bf16[400,1024]{1,0:T(8,128)(2,1)S(1)}, u32[]{:S(2)}, u32[]{:S(2)}) collective-permute-start(bf16[400,1024]{1,0:T(8,128)(2,1)} %layer_norm.1.refs_0_), channel_id=1, source_target_pairs={{0,4},{4,0},{8,12},{12,8},{16,20},{20,16},{24,28},{28,24},{1,5},{5... | collective-permute-start | bytes 2457608 | tf_op jit(solution)/shard_map/ppermute | solution.py:32
  17.1 18.5 %collective-permute-start.8 = (bf16[400,1024]{1,0:T(8,128)(2,1)}, bf16[400,1024]{1,0:T(8,128)(2,1)S(1)}, u32[]{:S(2)}, u32[]{:S(2)}) collective-permute-start(bf16[400,1024]{1,0:T(8,128)(2,1)} %layer_norm.1.refs_0_), channel_id=1, source_target_pairs={{0,1},{1,0},{2,3},{3,2},{4,5},{5,4},{6,7},{7,6},{8,9},{9,8},{10,11... | collective-permute-start | bytes 2457608 | tf_op jit(solution)/shard_map/ppermute | solution.py:32
  17.1 8.8 %collective-permute-start.10 = (bf16[256,384]{1,0:T(8,128)(2,1)S(1)}, bf16[256,384]{1,0:T(8,128)(2,1)S(1)}, u32[]{:S(2)}, u32[]{:S(2)}) collective-permute-start(bf16[256,384]{1,0:T(8,128)(2,1)S(1)} %maximum_maximum_fusion.refs_4_.refs_6_), channel_id=1, source_target_pairs={{0,16},{4,20},{8,24},{12,28},{16,0},{20,4},{24,8},{28,12},{1,17},{... | collective-permute-start | bytes 589832 | tf_op jit(solution)/shard_map/ppermute | solution.py:32
  21.1 9.7 %collective-permute-start.9 = (bf16[256,384]{1,0:T(8,128)(2,1)S(1)}, bf16[256,384]{1,0:T(8,128)(2,1)S(1)}, u32[]{:S(2)}, u32[]{:S(2)}) collective-permute-start(bf16[256,384]{1,0:T(8,128)(2,1)S(1)} %maximum_maximum_fusion.refs_4_.refs_6_), channel_id=1, source_target_pairs={{0,8},{4,12},{8,0},{12,4},{16,24},{20,28},{24,16},{28,20},{1,9},{5... | collective-permute-start | bytes 589832 | tf_op jit(solution)/shard_map/ppermute | solution.py:32
  26.0 6.2 %collective-permute-start.11 = (bf16[256,384]{1,0:T(8,128)(2,1)S(1)}, bf16[256,384]{1,0:T(8,128)(2,1)S(1)}, u32[]{:S(2)}, u32[]{:S(2)}) collective-permute-start(bf16[256,384]{1,0:T(8,128)(2,1)S(1)} %collective-permute-done.10.refs_6_.refs_8_), channel_id=1, source_target_pairs={{0,8},{4,12},{8,0},{12,4},{16,24},{20,28},{24,16},{28,20},{1,9},{5... | collective-permute-start | bytes 589832 | tf_op jit(solution)/shard_map/ppermute | solution.py:32
  36.6 4.1 %collective-permute-start.13 = (bf16[400,1024]{1,0:T(8,128)(2,1)S(1)}, bf16[400,1024]{1,0:T(8,128)(2,1)}, u32[]{:S(2)}, u32[]{:S(2)}) collective-permute-start(bf16[400,1024]{1,0:T(8,128)(2,1)S(1)} %collective-permute-done.6.refs_2_), channel_id=1, source_target_pairs={{0,1},{1,0},{2,3},{3,2},{4,5},{5,4},{6,7},{7,6},{8,9},{9,8},{10,11... | collective-permute-start | bytes 2457608 | tf_op jit(solution)/shard_map/ppermute | solution.py:32
  36.6 12.7 %collective-permute-start.16 = (bf16[400,1024]{1,0:T(8,128)(2,1)S(1)}, bf16[400,1024]{1,0:T(8,128)(2,1)S(1)}, u32[]{:S(2)}, u32[]{:S(2)}) collective-permute-start(bf16[400,1024]{1,0:T(8,128)(2,1)S(1)} %collective-permute-done.7.refs_0_), channel_id=1, source_target_pairs={{0,1},{1,0},{2,3},{3,2},{4,5},{5,4},{6,7},{7,6},{8,9},{9,8},{10,11... | collective-permute-start | bytes 2457608 | tf_op jit(solution)/shard_map/ppermute | solution.py:32
  37.2 11.7 %collective-permute-start.14 = (bf16[192,1024]{1,0:T(8,128)(2,1)S(1)}, bf16[192,1024]{1,0:T(8,128)(2,1)}, u32[]{:S(2)}, u32[]{:S(2)}) collective-permute-start(bf16[192,1024]{1,0:T(8,128)(2,1)S(1)} %slice.42), channel_id=1, source_target_pairs={{0,4},{4,0},{8,12},{12,8},{16,20},{20,16},{24,28},{28,24},{1,5},{5... | collective-permute-start | bytes 1179656 | tf_op jit(solution)/shard_map/ppermute | solution.py:32
  38.5 10.9 %collective-permute-start.15 = (bf16[208,1024]{1,0:T(8,128)(2,1)S(1)}, bf16[208,1024]{1,0:T(8,128)(2,1)}, u32[]{:S(2)}, u32[]{:S(2)}) collective-permute-start(bf16[208,1024]{1,0:T(8,128)(2,1)S(1)} %slice.43), channel_id=1, source_target_pairs={{0,2},{1,3},{2,0},{3,1},{4,6},{5,7},{6,4},{7,5},{8,10},{9,11},{10,... | collective-permute-start | bytes 1277960 | tf_op jit(solution)/shard_map/ppermute | solution.py:32
  38.7 10.2 %collective-permute-start.17 = (bf16[256,256]{1,0:T(8,128)(2,1)S(1)}, bf16[256,256]{1,0:T(8,128)(2,1)S(1)}, u32[]{:S(2)}, u32[]{:S(2)}) collective-permute-start(bf16[256,256]{1,0:T(8,128)(2,1)S(1)} %constant_dynamic-update-slice_fusion), channel_id=1, source_target_pairs={{0,16},{4,20},{8,24},{12,28},{16,0},{20,4},{24,8},{28,12},{1,17},{... | collective-permute-start | bytes 393224 | tf_op jit(solution)/shard_map/ppermute | solution.py:32
  50.2 52.3 %all-to-all-start = ((bf16[32,24,1024]{2,1,0:T(8,128)(2,1)}), bf16[32,24,1024]{2,1,0:T(8,128)(2,1)S(1)}, u32[]{:S(2)}, u32[]{:S(2)}) async-start(bf16[32,24,1024]{2,1,0:T(8,128)(2,1)} %bitcast.18), calls=%async_computation | async-start | bytes 3145728 | tf_op jit(solution)/shard_map/all_to_all | solution.py:728
  56.3 38.9 %collective-permute-start.22 = (bf16[512,256]{1,0:T(8,128)(2,1)S(1)}, bf16[512,256]{1,0:T(8,128)(2,1)S(1)}, u32[]{:S(2)}, u32[]{:S(2)}) collective-permute-start(bf16[512,256]{1,0:T(8,128)(2,1)S(1)} %constant_dynamic-update-slice_fusion.2.refs_0_), channel_id=1, source_target_pairs={{0,4},{4,0},{8,12},{12,8},{16,20},{20,16},{24,28},{28,24},{1,5},{5... | collective-permute-start | bytes 786440 | tf_op jit(solution)/shard_map/ppermute | solution.py:32
  57.6 37.7 %collective-permute-start.23 = (bf16[512,256]{1,0:T(8,128)(2,1)S(1)}, bf16[512,256]{1,0:T(8,128)(2,1)S(1)}, u32[]{:S(2)}, u32[]{:S(2)}) collective-permute-start(bf16[512,256]{1,0:T(8,128)(2,1)S(1)} %constant_dynamic-update-slice_fusion.2.refs_0_), channel_id=1, source_target_pairs={{0,2},{1,3},{2,0},{3,1},{4,6},{5,7},{6,4},{7,5},{8,10},{9,11},{10,... | collective-permute-start | bytes 786440 | tf_op jit(solution)/shard_map/ppermute | solution.py:32
  58.8 36.5 %collective-permute-start.24 = (bf16[512,256]{1,0:T(8,128)(2,1)S(1)}, bf16[512,256]{1,0:T(8,128)(2,1)S(1)}, u32[]{:S(2)}, u32[]{:S(2)}) collective-permute-start(bf16[512,256]{1,0:T(8,128)(2,1)S(1)} %constant_dynamic-update-slice_fusion.2.refs_0_), channel_id=1, source_target_pairs={{0,6},{1,7},{2,4},{3,5},{4,2},{5,3},{6,0},{7,1},{8,14},{9,15},{10,... | collective-permute-start | bytes 786440 | tf_op jit(solution)/shard_map/ppermute | solution.py:750
  70.0 32.5 %collective-permute-start.20 = (bf16[1024,256]{1,0:T(8,128)(2,1)S(1)}, bf16[1024,256]{1,0:T(8,128)(2,1)}, u32[]{:S(2)}, u32[]{:S(2)}) collective-permute-start(bf16[1024,256]{1,0:T(8,128)(2,1)S(1)} %get-tuple-element.109), channel_id=1, source_target_pairs={{0,8},{4,12},{8,16},{12,20},{16,24},{20,28},{1,9},{5,13},{9,17},{1... | collective-permute-start | bytes 1572872 | tf_op jit(solution)/shard_map/ppermute | solution.py:38
  73.2 29.3 %collective-permute-start.21 = (bf16[1024,256]{1,0:T(8,128)(2,1)S(1)}, bf16[1024,256]{1,0:T(8,128)(2,1)}, u32[]{:S(2)}, u32[]{:S(2)}) collective-permute-start(bf16[1024,256]{1,0:T(8,128)(2,1)S(1)} %get-tuple-element.108), channel_id=1, source_target_pairs={{8,0},{12,4},{16,8},{20,12},{24,16},{28,20},{9,1},{13,5},{17,9},{2... | collective-permute-start | bytes 1572872 | tf_op jit(solution)/shard_map/ppermute | solution.py:38
  102.5 74.7 %all-to-all-start.1 = ((bf16[32,24,1024]{2,1,0:T(8,128)(2,1)}), bf16[32,24,1024]{2,1,0:T(8,128)(2,1)S(1)}, u32[]{:S(2)}, u32[]{:S(2)}) async-start(bf16[32,24,1024]{2,1,0:T(8,128)(2,1)} %bitcast.17), calls=%async_computation.1 | async-start | bytes 3145728 | tf_op jit(solution)/shard_map/all_to_all | solution.py:728
  140.6 31.3 %collective-permute-start.32 = (bf16[2048,256]{1,0:T(8,128)(2,1)}, bf16[2048,256]{1,0:T(8,128)(2,1)}, u32[]{:S(2)}, u32[]{:S(2)}) collective-permute-start(bf16[2048,256]{1,0:T(8,128)(2,1)} %stacked.1.refs_8_), channel_id=1, source_target_pairs={{0,1},{1,0},{2,3},{3,2},{4,5},{5,4},{6,7},{7,6},{8,9},{9,8},{10,11... | collective-permute-start | bytes 3145736 | tf_op jit(solution)/shard_map/ppermute | solution.py:32
  159.0 4.2 %collective-permute-start.26 = (bf16[384,128]{1,0:T(8,128)(2,1)}, bf16[384,128]{1,0:T(8,128)(2,1)S(1)}, u32[]{:S(2)}, u32[]{:S(2)}) collective-permute-start(bf16[384,128]{1,0:T(8,128)(2,1)} %get-tuple-element.96), channel_id=1, source_target_pairs={{0,2},{1,3},{2,0},{3,1},{4,6},{5,7},{6,4},{7,5},{8,10},{9,11},{10,... | collective-permute-start | bytes 294920 | tf_op jit(solution)/shard_map/ppermute | solution.py:774
  160.2 5.9 %collective-permute-start.27 = (bf16[384,128]{1,0:T(8,128)(2,1)}, bf16[384,128]{1,0:T(8,128)(2,1)S(1)}, u32[]{:S(2)}, u32[]{:S(2)}) collective-permute-start(bf16[384,128]{1,0:T(8,128)(2,1)} %get-tuple-element.97), channel_id=1, source_target_pairs={{0,3},{1,2},{2,1},{3,0},{4,7},{5,6},{6,5},{7,4},{8,11},{9,10},{10,... | collective-permute-start | bytes 294920 | tf_op jit(solution)/shard_map/ppermute | solution.py:774
  161.0 7.3 %collective-permute-start.28 = (bf16[384,128]{1,0:T(8,128)(2,1)}, bf16[384,128]{1,0:T(8,128)(2,1)S(1)}, u32[]{:S(2)}, u32[]{:S(2)}) collective-permute-start(bf16[384,128]{1,0:T(8,128)(2,1)} %get-tuple-element.98), channel_id=1, source_target_pairs={{0,4},{1,5},{2,6},{3,7},{4,0},{5,1},{6,2},{7,3},{8,12},{9,13},{10,... | collective-permute-start | bytes 294920 | tf_op jit(solution)/shard_map/ppermute | solution.py:774
  162.2 7.0 %collective-permute-start.29 = (bf16[384,128]{1,0:T(8,128)(2,1)}, bf16[384,128]{1,0:T(8,128)(2,1)S(1)}, u32[]{:S(2)}, u32[]{:S(2)}) collective-permute-start(bf16[384,128]{1,0:T(8,128)(2,1)} %get-tuple-element.99), channel_id=1, source_target_pairs={{0,5},{1,4},{2,7},{3,6},{4,1},{5,0},{6,3},{7,2},{8,13},{9,12},{10,... | collective-permute-start | bytes 294920 | tf_op jit(solution)/shard_map/ppermute | solution.py:774
  163.2 6.0 %collective-permute-start.30 = (bf16[384,128]{1,0:T(8,128)(2,1)}, bf16[384,128]{1,0:T(8,128)(2,1)S(1)}, u32[]{:S(2)}, u32[]{:S(2)}) collective-permute-start(bf16[384,128]{1,0:T(8,128)(2,1)} %get-tuple-element.100), channel_id=1, source_target_pairs={{0,6},{1,7},{2,4},{3,5},{4,2},{5,3},{6,0},{7,1},{8,14},{9,15},{10,... | collective-permute-start | bytes 294920 | tf_op jit(solution)/shard_map/ppermute | solution.py:774
  166.1 5.7 %collective-permute-start.31 = (bf16[384,128]{1,0:T(8,128)(2,1)}, bf16[384,128]{1,0:T(8,128)(2,1)S(1)}, u32[]{:S(2)}, u32[]{:S(2)}) collective-permute-start(bf16[384,128]{1,0:T(8,128)(2,1)} %get-tuple-element.101), channel_id=1, source_target_pairs={{0,7},{1,6},{2,5},{3,4},{4,3},{5,2},{6,1},{7,0},{8,15},{9,14},{10,... | collective-permute-start | bytes 294920 | tf_op jit(solution)/shard_map/ppermute | solution.py:774
  (26 other events, 162.8 us)

commit v12 on v10

--- a/solution.py
+++ b/solution.py
@@ -531,6 +531,29 @@
     )(meta, *parts, *weights)
 
 
+def stack_kernel(*refs):
+    result = refs[-1]
+    for number, block in enumerate(refs[:-1]):
+
+        @pl.when(pl.program_id(0) == number)
+        def _():
+            result[...] = block[...]
+
+
+def stacked(blocks):
+    rows, width = blocks[0].shape
+    return pl.pallas_call(
+        stack_kernel,
+        grid=(len(blocks),),
+        in_specs=[pl.BlockSpec((rows, width), lambda i: (0, 0))] * len(blocks),
+        out_specs=pl.BlockSpec((rows, width), lambda i: (i, 0)),
+        out_shape=jax.ShapeDtypeStruct((len(blocks) * rows, width), blocks[0].dtype),
+        compiler_params=PARAMS,
+        cost_estimate=pl.CostEstimate(flops=0, bytes_accessed=2 << 20, transcendentals=0),
+        name="stacked",
+    )(*blocks)
+
+
 def unpack_kernel(own_row, other_row, pages):
     _, pair, members, capacity, part = own_row.shape
     width = part // (2 * PAGE)
@@ -658,6 +681,7 @@
     weights = [planes[distance] for distance in range(0, peers, PAIR)]
 
     first_row = place // PAIR * group_rows
+    segment_ids, plane = lax.optimization_barrier((segment_ids, plane))
     padded_ids = jnp.concatenate(
         [
             jnp.full((SPAN,), -1, jnp.int32),
@@ -666,7 +690,6 @@
         ]
     )
     window_ids = lax.dynamic_slice_in_dim(padded_ids, first_row, group_rows + 2 * SPAN, 0)
-    window_ids, plane = lax.optimization_barrier((window_ids, plane))
     *bounds, ranges = document_bounds(window_ids, group_rows)
     positions = SPAN + jnp.arange(group_rows, dtype=jnp.int32) - bounds[0][0]
     order = [(number * members + column) % PARTS for number in range(PARTS)]
@@ -733,7 +756,7 @@
         )
     )
     other_row = to_owners(send)
-    columns = jnp.concatenate([last_rows, other_rows, across_rows, corner_rows], axis=0)
+    columns = stacked([last_rows, other_rows, across_rows, corner_rows])
     row_order = place
     if output_weight.shape[0] != width:
         wanted = jnp.arange(peers) ^ place

time: 156 us -> 158 us (1.013)
  waiting for transfers between devices: 24.1 us -> 31.7 us
  local copies, waits for them, and re-layouts: 10.3 us -> 5.97 us
  Pallas kernels: 68.9 us -> 66.4 us
  starting transfers between devices: 44.8 us -> 46.6 us
    ppermute x7, waiting for transfers between devices: 9.47 us -> 14.4 us  [per_device(): lax.ppermute(mixed[distance], ('tok', 'grp'), [(source, source ^ distance...]
    all_to_all x2, starting transfers between devices: 10.5 us -> 14.9 us  [to_owners(): lax.all_to_all(send.reshape((flat,) + send.shape[2:]), ('tok', 'grp'), sp...]
    pallas_call x1, Pallas kernels: 23.8 us -> 19.9 us  [attend_edges(): pl.pallas_call(functools.partial(edge_kernel, edge), grid_spec=pltpu.Pref...]
    unnamed x51 -> x48, local copies, waits for them, and re-layouts: 7.54 us -> 4.01 us
    ppermute x2, waiting for transfers between devices: 3.99 us -> 7.28 us  [shifted(): lax.ppermute(value, axis, [(source, source + steps) for source in range(i...]
    pallas_call x0 -> x1, Pallas kernels: none -> 2.78 us  [stacked(): pl.pallas_call(stack_kernel, grid=(len(blocks),), in_specs=[pl.BlockSpec(...]
    ppermute x7, starting transfers between devices: 6.46 us -> 3.73 us  [per_device(): lax.ppermute(mixed[distance], ('tok', 'grp'), [(source, source ^ distance...]
  transfers between devices with their start and end apart: 35 -> 35, of which waited for: 10 -> 9; matrix products, arithmetic and copies ran while one was open for 8% -> 4% of each run, Pallas kernels for 43% -> 41%
where the time goes in v12:
time: 158 us; the launch traced here: 157 us
  Pallas kernels  66.4 us (42%)
  starting transfers between devices  46.6 us (29%)
  waiting for transfers between devices  31.7 us (20%)
  local copies, waits for them, and re-layouts  5.97 us (4%)
  other arithmetic  5.17 us (3%)
    pallas_call x1, Pallas kernels, attend_edges(): pl.pallas_call(functools.partial(edge_kernel, edge), grid_spec=pltpu.Pref...  19.9 us
    pallas_call x2, Pallas kernels, project(): pl.pallas_call(functools.partial(project_kernel, first, layout, len(weigh...  16.4 us
    pallas_call x1, Pallas kernels, attend_finish(): pl.pallas_call(functools.partial(finish_kernel, edge), grid_spec=pltpu.Pr...  15.1 us
    all_to_all x2, starting transfers between devices, to_owners(): lax.all_to_all(send.reshape((flat,) + send.shape[2:]), ('tok', 'grp'), sp...  14.9 us
    ppermute x7, waiting for transfers between devices, per_device(): lax.ppermute(mixed[distance], ('tok', 'grp'), [(source, source ^ distance...  14.4 us
    ppermute x17, starting transfers between devices, flipped(): lax.ppermute(value, axis, [(source, source ^ bit) for source in range(cou...  13 us
    ppermute x17, waiting for transfers between devices, flipped(): lax.ppermute(value, axis, [(source, source ^ bit) for source in range(cou...  9.96 us
    ppermute x6, starting transfers between devices, per_device(): pieces.append(lax.ppermute(piece, ('tok', 'grp'), route))  9.33 us
  transfers between devices with their start and end apart: 35, of which 9 were waited for; matrix products, arithmetic and copies ran while one was open for 4% of the time, Pallas kernels for 41%

profile of v12, /device:TPU:17, one launch (start us, length us, event | category | flops | bytes accessed | tf_op | source)
XLA Modules:
  0.0 156.9 jit_solution(6852543864632796363)
XLA Ops:
  1.5 1.3 collective-permute-start.5
  2.8 2.0 %collective-permute-start.4 = (bf16[128,128]{1,0:T(8,128)(2,1)S(1)}, bf16[128,128]{1,0:T(8,128)(2,1)S(1)}, u32[]{:S(2)}, u32[]{:S(2)}) collective-permute-start(bf16[128,128]{1,0:T(8,128)(2,1)S(1)} %get-tuple-element.111), channel_id=1, source_target_pairs={{0,5},{1,4},{2,7},{3,6},{4,1},{5,0},{6,3},{7,2},{8,13},{9,12},{10,... | collective-permute-start | bytes 98312 | tf_op jit(solution)/shard_map/ppermute | solution.py:664
  4.8 1.2 collective-permute-start.3
  6.7 1.7 %collective-permute-start.1 = (bf16[128,128]{1,0:T(8,128)(2,1)S(1)}, bf16[128,128]{1,0:T(8,128)(2,1)S(1)}, u32[]{:S(2)}, u32[]{:S(2)}) collective-permute-start(bf16[128,128]{1,0:T(8,128)(2,1)S(1)} %get-tuple-element.114), channel_id=1, source_target_pairs={{0,1},{1,0},{2,3},{3,2},{4,5},{5,4},{6,7},{7,6},{8,9},{9,8},{10,11... | collective-permute-start | bytes 98312 | tf_op jit(solution)/shard_map/ppermute | solution.py:664
  8.5 2.4 %collective-permute-start = (bf16[128,128]{1,0:T(8,128)(2,1)S(1)}, bf16[128,128]{1,0:T(8,128)(2,1)S(1)}, u32[]{:S(2)}, u32[]{:S(2)}) collective-permute-start(bf16[128,128]{1,0:T(8,128)(2,1)S(1)} %get-tuple-element.110), channel_id=1, source_target_pairs={{0,0},{1,3},{2,2},{3,1},{4,4},{5,7},{6,6},{7,5},{8,8},{9,11},{10,1... | collective-permute-start | bytes 98312 | tf_op jit(solution)/shard_map/ppermute | solution.py:664
  11.0 2.6 %layer_norm.1.refs_0_ = bf16[400,1024]{1,0:T(8,128)(2,1)} custom-call(bf16[384,1024]{1,0:T(8,128)(2,1)} %tokens.1, f32[1,1024]{1,0:T(1,128)} %bitcast.21, s32[1,96]{1,0:T(1,128)} %bitcast.22), custom_call_target="tpu_custom_call" | custom-call | tf_op jit(solution)/shard_map/layer_norm/pallas_call | solution.py:65
  14.2 1.3 collective-permute-start.12
  17.8 2.5 %document_bounds.1 = (s32[1,3072]{1,0:T(1,128)}, s32[1,3072]{1,0:T(1,128)}, s32[1,128]{1,0:T(1,128)}) custom-call(s32[1,5120]{1,0:T(1,128)} %bitcast.20), custom_call_target="tpu_custom_call" | custom-call | flops 17179869184 | tf_op jit(solution)/shard_map/document_bounds/pallas_call | solution.py:628
  21.3 4.7 %collective-permute-done.10.refs_6_.refs_8_ = bf16[256,384]{1,0:T(8,128)(2,1)S(1)} collective-permute-done((bf16[256,384]{1,0:T(8,128)(2,1)S(1)}, bf16[256,384]{1,0:T(8,128)(2,1)S(1)}, u32[]{:S(2)}, u32[]{:S(2)}) %collective-permute-start.10) | collective-permute-done | bytes 196640 | tf_op jit(solution)/shard_map/ppermute | solution.py:32
  26.0 2.5 %collective-permute-start.11 = (bf16[256,384]{1,0:T(8,128)(2,1)S(1)}, bf16[256,384]{1,0:T(8,128)(2,1)S(1)}, u32[]{:S(2)}, u32[]{:S(2)}) collective-permute-start(bf16[256,384]{1,0:T(8,128)(2,1)S(1)} %collective-permute-done.10.refs_6_.refs_8_), channel_id=1, source_target_pairs={{0,8},{4,12},{8,0},{12,4},{16,24},{20,28},{24,16},{28,20},{1,9},{5... | collective-permute-start | bytes 589832 | tf_op jit(solution)/shard_map/ppermute | solution.py:32
  28.4 2.3 %multiply_sine_fusion = (f32[32,3072]{1,0:T(8,128)}, f32[32,3072]{1,0:T(8,128)}) fusion(f32[3072]{0:T(1024)S(1)} %bitcast.19, f32[32]{0:T(128)S(1)} %negate_power_fusion), kind=kLoop, calls=%fused_computation | loop fusion | flops 98304 | bytes 798848 | tf_op jit(solution)/shard_map/sin | solution.py:592
  30.8 1.5 collective-permute-done.11.refs_7_.refs_9_
  32.2 2.6 %collective-permute-done.6.refs_2_ = bf16[400,1024]{1,0:T(8,128)(2,1)S(1)} collective-permute-done((bf16[400,1024]{1,0:T(8,128)(2,1)}, bf16[400,1024]{1,0:T(8,128)(2,1)S(1)}, u32[]{:S(2)}, u32[]{:S(2)}) %collective-permute-start.6) | collective-permute-done | bytes 819232 | tf_op jit(solution)/shard_map/ppermute | solution.py:32
  37.2 1.2 collective-permute-start.14
  38.7 1.9 %collective-permute-start.17 = (bf16[256,256]{1,0:T(8,128)(2,1)S(1)}, bf16[256,256]{1,0:T(8,128)(2,1)S(1)}, u32[]{:S(2)}, u32[]{:S(2)}) collective-permute-start(bf16[256,256]{1,0:T(8,128)(2,1)S(1)} %constant_dynamic-update-slice_fusion), channel_id=1, source_target_pairs={{0,16},{4,20},{8,24},{12,28},{16,0},{20,4},{24,8},{28,12},{1,17},{... | collective-permute-start | bytes 393224 | tf_op jit(solution)/shard_map/ppermute | solution.py:32
  40.7 8.2 %project.2 = (bf16[3072,128]{1,0:T(8,128)(2,1)}, bf16[3072,256]{1,0:T(8,128)(2,1)}, bf16[8,4,24,1024]{3,2,1,0:T(8,128)(2,1)}) custom-call(s32[5]{0:T(128)} %stack.29.meta, bf16[400,1024]{1,0:T(8,128)(2,1)} %layer_norm.1.refs_0_, bf16[400,1024]{1,0:T(8,128)(2,1)} %copy-done.17, bf16[400,1024]{1,0:T(8,128)(2,1)} %copy-done.6, ...), custom_call_target="tpu_custom_call" | custom-call | flops 9663676416 | bytes 6291456 | tf_op jit(solution)/shard_map/project/pallas_call | solution.py:172
  50.2 5.4 %all-to-all-start = ((bf16[32,24,1024]{2,1,0:T(8,128)(2,1)}), bf16[32,24,1024]{2,1,0:T(8,128)(2,1)S(1)}, u32[]{:S(2)}, u32[]{:S(2)}) async-start(bf16[32,24,1024]{2,1,0:T(8,128)(2,1)} %bitcast.18), calls=%async_computation | async-start | bytes 3145728 | tf_op jit(solution)/shard_map/all_to_all | solution.py:724
  56.3 1.3 collective-permute-start.22
  60.5 8.2 %project.3 = (bf16[3072,128]{1,0:T(8,128)(2,1)}, bf16[3072,256]{1,0:T(8,128)(2,1)}, bf16[8,4,24,1024]{3,2,1,0:T(8,128)(2,1)}) custom-call(s32[5]{0:T(128)} %stack.29.meta, bf16[400,1024]{1,0:T(8,128)(2,1)} %copy-done.4, bf16[400,1024]{1,0:T(8,128)(2,1)} %copy-done.16, ...), custom_call_target="tpu_custom_call", output_to_operand_aliasing={{0}: (13, {}), {1}: (14, {})} | custom-call | flops 9663676416 | bytes 6291456 | tf_op jit(solution)/shard_map/project/pallas_call | solution.py:172
  68.7 1.3 fusion.2
  70.0 3.2 %collective-permute-start.20 = (bf16[1024,256]{1,0:T(8,128)(2,1)S(1)}, bf16[1024,256]{1,0:T(8,128)(2,1)}, u32[]{:S(2)}, u32[]{:S(2)}) collective-permute-start(bf16[1024,256]{1,0:T(8,128)(2,1)S(1)} %get-tuple-element.109), channel_id=1, source_target_pairs={{0,8},{4,12},{8,16},{12,20},{16,24},{20,28},{1,9},{5,13},{9,17},{1... | collective-permute-start | bytes 1572872 | tf_op jit(solution)/shard_map/ppermute | solution.py:38
  73.2 2.1 %collective-permute-start.21 = (bf16[1024,256]{1,0:T(8,128)(2,1)S(1)}, bf16[1024,256]{1,0:T(8,128)(2,1)}, u32[]{:S(2)}, u32[]{:S(2)}) collective-permute-start(bf16[1024,256]{1,0:T(8,128)(2,1)S(1)} %get-tuple-element.108), channel_id=1, source_target_pairs={{8,0},{12,4},{16,8},{20,12},{24,16},{28,20},{9,1},{13,5},{17,9},{2... | collective-permute-start | bytes 1572872 | tf_op jit(solution)/shard_map/ppermute | solution.py:38
  75.3 19.9 %attend_edges.1 = (f32[5,160,256]{2,1,0:T(8,128)}, f32[5,160,256]{2,1,0:T(8,128)}, f32[5,8,256]{2,1,0:T(8,128)}, f32[5,8,256]{2,1,0:T(8,128)}) custom-call(s32[5]{0:T(128)} %stack.29.meta, s32[1,128]{1,0:T(1,128)} %get-tuple-element.60.ranges, bf16[3072,128]{1,0:T(8,128)(2,1)} %get-tuple-element.78.refs_0_.refs_3_, ...), custom_call_target="tpu_custom_call" | custom-call | flops 6442450944 | bytes 5242880 | tf_op jit(solution)/shard_map/attend_edges/pallas_call | solution.py:425
  95.2 7.3 %collective-permute-done.20.refs_7_ = bf16[1024,256]{1,0:T(8,128)(2,1)} collective-permute-done((bf16[1024,256]{1,0:T(8,128)(2,1)S(1)}, bf16[1024,256]{1,0:T(8,128)(2,1)}, u32[]{:S(2)}, u32[]{:S(2)}) %collective-permute-start.20) | collective-permute-done | bytes 524320 | tf_op jit(solution)/shard_map/ppermute | solution.py:38
  102.5 9.6 %all-to-all-start.1 = ((bf16[32,24,1024]{2,1,0:T(8,128)(2,1)}), bf16[32,24,1024]{2,1,0:T(8,128)(2,1)S(1)}, u32[]{:S(2)}, u32[]{:S(2)}) async-start(bf16[32,24,1024]{2,1,0:T(8,128)(2,1)} %bitcast.17), calls=%async_computation.1 | async-start | bytes 3145728 | tf_op jit(solution)/shard_map/all_to_all | solution.py:724
  112.1 2.8 %stacked.1.refs_8_ = bf16[2048,256]{1,0:T(8,128)(2,1)} custom-call(bf16[512,256]{1,0:T(8,128)(2,1)} %copy-done, bf16[512,256]{1,0:T(8,128)(2,1)} %copy-done.1, bf16[512,256]{1,0:T(8,128)(2,1)} %copy-done.2, bf16[512,256]{1,0:T(8,128)(2,1)} %copy-done.3), custom_call_target="tpu_custom_call" | custom-call | bytes 2097152 | tf_op jit(solution)/shard_map/stacked/pallas_call | solution.py:545
  115.2 15.1 %attend_finish.1 = (bf16[384,128]{1,0:T(8,128)(2,1)}, bf16[384,128]{1,0:T(8,128)(2,1)}, bf16[384,128]{1,0:T(8,128)(2,1)}, bf16[384,128]{1,0:T(8,128)(2,1)}, bf16...) custom-call(s32[5]{0:T(128)} %stack.29.meta, ...), custom_call_target="tpu_custom_call" | custom-call | flops 6442450944 | bytes 5242880 | tf_op jit(solution)/shard_map/attend_finish/pallas_call | solution.py:453
  134.1 4.9 %collective-permute-done.26.refs_2_ = bf16[384,128]{1,0:T(8,128)(2,1)S(1)} collective-permute-done((bf16[384,128]{1,0:T(8,128)(2,1)}, bf16[384,128]{1,0:T(8,128)(2,1)S(1)}, u32[]{:S(2)}, u32[]{:S(2)}) %collective-permute-start.26) | collective-permute-done | bytes 98336 | tf_op jit(solution)/shard_map/ppermute | solution.py:770
  139.0 4.7 %collective-permute-done.27.refs_3_ = bf16[384,128]{1,0:T(8,128)(2,1)S(1)} collective-permute-done((bf16[384,128]{1,0:T(8,128)(2,1)}, bf16[384,128]{1,0:T(8,128)(2,1)S(1)}, u32[]{:S(2)}, u32[]{:S(2)}) %collective-permute-start.27) | collective-permute-done | bytes 98336 | tf_op jit(solution)/shard_map/ppermute | solution.py:770
  144.4 4.8 %collective-permute-done.31.refs_7_ = bf16[384,128]{1,0:T(8,128)(2,1)S(1)} collective-permute-done((bf16[384,128]{1,0:T(8,128)(2,1)}, bf16[384,128]{1,0:T(8,128)(2,1)S(1)}, u32[]{:S(2)}, u32[]{:S(2)}) %collective-permute-start.31) | collective-permute-done | bytes 98336 | tf_op jit(solution)/shard_map/ppermute | solution.py:770
  149.8 4.7 %output_projection.1 = bf16[384,1024]{1,0:T(8,128)(2,1)} custom-call(s32[2]{0:T(128)} %pad_add_fusion.meta, bf16[384,128]{1,0:T(8,128)(2,1)} %get-tuple-element.94.refs_0_, bf16[384,128]{1,0:T(8,128)(2,1)} %copy-done.7, bf16[384,128]{1,0:T(8,128)(2,1)} %copy-done.8, bf16[384,128]{1,0:T(8,128)(2,1)} %copy-done.9, bf16[384,128]{1,0:T(8,128)(2,1)} %copy-done.10, ...), custom_call_target="tpu_custom_call" | custom-call | flops 805306368 | bytes 4194304 | tf_op jit(solution)/shard_map/output_projection/pallas_call | solution.py:513
  154.5 2.4 %unpack.1 = bf16[8,24,8192]{2,1,0:T(8,128)(2,1)} custom-call(bf16[4,2,4,24,1024]{4,3,2,1,0:T(8,128)(2,1)S(1)} %bitcast.14, bf16[4,2,4,24,1024]{4,3,2,1,0:T(8,128)(2,1)S(1)} %bitcast.15), custom_call_target="tpu_custom_call" | custom-call | bytes 6291456 | tf_op jit(solution)/shard_map/unpack/pallas_call | solution.py:574
  (110 shorter events, 18.2 us)
Async XLA Ops:
  1.5 6.9 %collective-permute-start.5 = (bf16[128,128]{1,0:T(8,128)(2,1)S(1)}, bf16[128,128]{1,0:T(8,128)(2,1)S(1)}, u32[]{:S(2)}, u32[]{:S(2)}) collective-permute-start(bf16[128,128]{1,0:T(8,128)(2,1)S(1)} %get-tuple-element.113), channel_id=1, source_target_pairs={{0,6},{1,5},{2,4},{3,7},{4,2},{5,1},{6,0},{7,3},{8,14},{9,13},{10,... | collective-permute-start | bytes 98312 | tf_op jit(solution)/shard_map/ppermute | solution.py:664
  2.8 11.4 %collective-permute-start.4 = (bf16[128,128]{1,0:T(8,128)(2,1)S(1)}, bf16[128,128]{1,0:T(8,128)(2,1)S(1)}, u32[]{:S(2)}, u32[]{:S(2)}) collective-permute-start(bf16[128,128]{1,0:T(8,128)(2,1)S(1)} %get-tuple-element.111), channel_id=1, source_target_pairs={{0,5},{1,4},{2,7},{3,6},{4,1},{5,0},{6,3},{7,2},{8,13},{9,12},{10,... | collective-permute-start | bytes 98312 | tf_op jit(solution)/shard_map/ppermute | solution.py:664
  4.8 10.7 %collective-permute-start.3 = (bf16[128,128]{1,0:T(8,128)(2,1)S(1)}, bf16[128,128]{1,0:T(8,128)(2,1)S(1)}, u32[]{:S(2)}, u32[]{:S(2)}) collective-permute-start(bf16[128,128]{1,0:T(8,128)(2,1)S(1)} %get-tuple-element.112), channel_id=1, source_target_pairs={{0,4},{1,7},{2,6},{3,5},{4,0},{5,3},{6,2},{7,1},{8,12},{9,15},{10,... | collective-permute-start | bytes 98312 | tf_op jit(solution)/shard_map/ppermute | solution.py:664
  6.1 9.5 %collective-permute-start.2 = (bf16[128,128]{1,0:T(8,128)(2,1)S(1)}, bf16[128,128]{1,0:T(8,128)(2,1)S(1)}, u32[]{:S(2)}, u32[]{:S(2)}) collective-permute-start(bf16[128,128]{1,0:T(8,128)(2,1)S(1)} %get-tuple-element.115), channel_id=1, source_target_pairs={{0,2},{1,1},{2,0},{3,3},{4,6},{5,5},{6,4},{7,7},{8,10},{9,9},{10,8... | collective-permute-start | bytes 98312 | tf_op jit(solution)/shard_map/ppermute | solution.py:664
  6.7 8.8 %collective-permute-start.1 = (bf16[128,128]{1,0:T(8,128)(2,1)S(1)}, bf16[128,128]{1,0:T(8,128)(2,1)S(1)}, u32[]{:S(2)}, u32[]{:S(2)}) collective-permute-start(bf16[128,128]{1,0:T(8,128)(2,1)S(1)} %get-tuple-element.114), channel_id=1, source_target_pairs={{0,1},{1,0},{2,3},{3,2},{4,5},{5,4},{6,7},{7,6},{8,9},{9,8},{10,11... | collective-permute-start | bytes 98312 | tf_op jit(solution)/shard_map/ppermute | solution.py:664
  8.5 7.1 %collective-permute-start = (bf16[128,128]{1,0:T(8,128)(2,1)S(1)}, bf16[128,128]{1,0:T(8,128)(2,1)S(1)}, u32[]{:S(2)}, u32[]{:S(2)}) collective-permute-start(bf16[128,128]{1,0:T(8,128)(2,1)S(1)} %get-tuple-element.110), channel_id=1, source_target_pairs={{0,0},{1,3},{2,2},{3,1},{4,4},{5,7},{6,6},{7,5},{8,8},{9,11},{10,1... | collective-permute-start | bytes 98312 | tf_op jit(solution)/shard_map/ppermute | solution.py:664
  14.2 6.8 %collective-permute-start.12 = (bf16[128,256]{1,0:T(8,128)(2,1)S(1)}, bf16[128,256]{1,0:T(8,128)(2,1)S(1)}, u32[]{:S(2)}, u32[]{:S(2)}) collective-permute-start(bf16[128,256]{1,0:T(8,128)(2,1)S(1)} %copy-done.14), channel_id=1, source_target_pairs={{0,8},{4,12},{8,0},{12,4},{16,24},{20,28},{24,16},{28,20},{1,9},{5... | collective-permute-start | bytes 196616 | tf_op jit(solution)/shard_map/ppermute | solution.py:32
  15.6 19.2 %collective-permute-start.6 = (bf16[400,1024]{1,0:T(8,128)(2,1)}, bf16[400,1024]{1,0:T(8,128)(2,1)S(1)}, u32[]{:S(2)}, u32[]{:S(2)}) collective-permute-start(bf16[400,1024]{1,0:T(8,128)(2,1)} %layer_norm.1.refs_0_), channel_id=1, source_target_pairs={{0,2},{1,3},{2,0},{3,1},{4,6},{5,7},{6,4},{7,5},{8,10},{9,11},{10,... | collective-permute-start | bytes 2457608 | tf_op jit(solution)/shard_map/ppermute | solution.py:32
  16.6 19.1 %collective-permute-start.7 = (bf16[400,1024]{1,0:T(8,128)(2,1)}, bf16[400,1024]{1,0:T(8,128)(2,1)S(1)}, u32[]{:S(2)}, u32[]{:S(2)}) collective-permute-start(bf16[400,1024]{1,0:T(8,128)(2,1)} %layer_norm.1.refs_0_), channel_id=1, source_target_pairs={{0,4},{4,0},{8,12},{12,8},{16,20},{20,16},{24,28},{28,24},{1,5},{5... | collective-permute-start | bytes 2457608 | tf_op jit(solution)/shard_map/ppermute | solution.py:32
  17.1 18.5 %collective-permute-start.8 = (bf16[400,1024]{1,0:T(8,128)(2,1)}, bf16[400,1024]{1,0:T(8,128)(2,1)S(1)}, u32[]{:S(2)}, u32[]{:S(2)}) collective-permute-start(bf16[400,1024]{1,0:T(8,128)(2,1)} %layer_norm.1.refs_0_), channel_id=1, source_target_pairs={{0,1},{1,0},{2,3},{3,2},{4,5},{5,4},{6,7},{7,6},{8,9},{9,8},{10,11... | collective-permute-start | bytes 2457608 | tf_op jit(solution)/shard_map/ppermute | solution.py:32
  17.1 8.8 %collective-permute-start.10 = (bf16[256,384]{1,0:T(8,128)(2,1)S(1)}, bf16[256,384]{1,0:T(8,128)(2,1)S(1)}, u32[]{:S(2)}, u32[]{:S(2)}) collective-permute-start(bf16[256,384]{1,0:T(8,128)(2,1)S(1)} %maximum_maximum_fusion.refs_4_.refs_6_), channel_id=1, source_target_pairs={{0,16},{4,20},{8,24},{12,28},{16,0},{20,4},{24,8},{28,12},{1,17},{... | collective-permute-start | bytes 589832 | tf_op jit(solution)/shard_map/ppermute | solution.py:32
  21.1 9.7 %collective-permute-start.9 = (bf16[256,384]{1,0:T(8,128)(2,1)S(1)}, bf16[256,384]{1,0:T(8,128)(2,1)S(1)}, u32[]{:S(2)}, u32[]{:S(2)}) collective-permute-start(bf16[256,384]{1,0:T(8,128)(2,1)S(1)} %maximum_maximum_fusion.refs_4_.refs_6_), channel_id=1, source_target_pairs={{0,8},{4,12},{8,0},{12,4},{16,24},{20,28},{24,16},{28,20},{1,9},{5... | collective-permute-start | bytes 589832 | tf_op jit(solution)/shard_map/ppermute | solution.py:32
  26.0 6.2 %collective-permute-start.11 = (bf16[256,384]{1,0:T(8,128)(2,1)S(1)}, bf16[256,384]{1,0:T(8,128)(2,1)S(1)}, u32[]{:S(2)}, u32[]{:S(2)}) collective-permute-start(bf16[256,384]{1,0:T(8,128)(2,1)S(1)} %collective-permute-done.10.refs_6_.refs_8_), channel_id=1, source_target_pairs={{0,8},{4,12},{8,0},{12,4},{16,24},{20,28},{24,16},{28,20},{1,9},{5... | collective-permute-start | bytes 589832 | tf_op jit(solution)/shard_map/ppermute | solution.py:32
  36.6 4.1 %collective-permute-start.13 = (bf16[400,1024]{1,0:T(8,128)(2,1)S(1)}, bf16[400,1024]{1,0:T(8,128)(2,1)}, u32[]{:S(2)}, u32[]{:S(2)}) collective-permute-start(bf16[400,1024]{1,0:T(8,128)(2,1)S(1)} %collective-permute-done.6.refs_2_), channel_id=1, source_target_pairs={{0,1},{1,0},{2,3},{3,2},{4,5},{5,4},{6,7},{7,6},{8,9},{9,8},{10,11... | collective-permute-start | bytes 2457608 | tf_op jit(solution)/shard_map/ppermute | solution.py:32
  36.6 12.7 %collective-permute-start.16 = (bf16[400,1024]{1,0:T(8,128)(2,1)S(1)}, bf16[400,1024]{1,0:T(8,128)(2,1)S(1)}, u32[]{:S(2)}, u32[]{:S(2)}) collective-permute-start(bf16[400,1024]{1,0:T(8,128)(2,1)S(1)} %collective-permute-done.7.refs_0_), channel_id=1, source_target_pairs={{0,1},{1,0},{2,3},{3,2},{4,5},{5,4},{6,7},{7,6},{8,9},{9,8},{10,11... | collective-permute-start | bytes 2457608 | tf_op jit(solution)/shard_map/ppermute | solution.py:32
  37.2 11.7 %collective-permute-start.14 = (bf16[192,1024]{1,0:T(8,128)(2,1)S(1)}, bf16[192,1024]{1,0:T(8,128)(2,1)}, u32[]{:S(2)}, u32[]{:S(2)}) collective-permute-start(bf16[192,1024]{1,0:T(8,128)(2,1)S(1)} %slice.42), channel_id=1, source_target_pairs={{0,4},{4,0},{8,12},{12,8},{16,20},{20,16},{24,28},{28,24},{1,5},{5... | collective-permute-start | bytes 1179656 | tf_op jit(solution)/shard_map/ppermute | solution.py:32
  38.5 10.9 %collective-permute-start.15 = (bf16[208,1024]{1,0:T(8,128)(2,1)S(1)}, bf16[208,1024]{1,0:T(8,128)(2,1)}, u32[]{:S(2)}, u32[]{:S(2)}) collective-permute-start(bf16[208,1024]{1,0:T(8,128)(2,1)S(1)} %slice.43), channel_id=1, source_target_pairs={{0,2},{1,3},{2,0},{3,1},{4,6},{5,7},{6,4},{7,5},{8,10},{9,11},{10,... | collective-permute-start | bytes 1277960 | tf_op jit(solution)/shard_map/ppermute | solution.py:32
  38.7 10.2 %collective-permute-start.17 = (bf16[256,256]{1,0:T(8,128)(2,1)S(1)}, bf16[256,256]{1,0:T(8,128)(2,1)S(1)}, u32[]{:S(2)}, u32[]{:S(2)}) collective-permute-start(bf16[256,256]{1,0:T(8,128)(2,1)S(1)} %constant_dynamic-update-slice_fusion), channel_id=1, source_target_pairs={{0,16},{4,20},{8,24},{12,28},{16,0},{20,4},{24,8},{28,12},{1,17},{... | collective-permute-start | bytes 393224 | tf_op jit(solution)/shard_map/ppermute | solution.py:32
  50.2 52.3 %all-to-all-start = ((bf16[32,24,1024]{2,1,0:T(8,128)(2,1)}), bf16[32,24,1024]{2,1,0:T(8,128)(2,1)S(1)}, u32[]{:S(2)}, u32[]{:S(2)}) async-start(bf16[32,24,1024]{2,1,0:T(8,128)(2,1)} %bitcast.18), calls=%async_computation | async-start | bytes 3145728 | tf_op jit(solution)/shard_map/all_to_all | solution.py:724
  56.3 38.9 %collective-permute-start.22 = (bf16[512,256]{1,0:T(8,128)(2,1)S(1)}, bf16[512,256]{1,0:T(8,128)(2,1)S(1)}, u32[]{:S(2)}, u32[]{:S(2)}) collective-permute-start(bf16[512,256]{1,0:T(8,128)(2,1)S(1)} %constant_dynamic-update-slice_fusion.2.refs_0_), channel_id=1, source_target_pairs={{0,4},{4,0},{8,12},{12,8},{16,20},{20,16},{24,28},{28,24},{1,5},{5... | collective-permute-start | bytes 786440 | tf_op jit(solution)/shard_map/ppermute | solution.py:32
  57.6 37.6 %collective-permute-start.23 = (bf16[512,256]{1,0:T(8,128)(2,1)S(1)}, bf16[512,256]{1,0:T(8,128)(2,1)S(1)}, u32[]{:S(2)}, u32[]{:S(2)}) collective-permute-start(bf16[512,256]{1,0:T(8,128)(2,1)S(1)} %constant_dynamic-update-slice_fusion.2.refs_0_), channel_id=1, source_target_pairs={{0,2},{1,3},{2,0},{3,1},{4,6},{5,7},{6,4},{7,5},{8,10},{9,11},{10,... | collective-permute-start | bytes 786440 | tf_op jit(solution)/shard_map/ppermute | solution.py:32
  58.8 36.5 %collective-permute-start.24 = (bf16[512,256]{1,0:T(8,128)(2,1)S(1)}, bf16[512,256]{1,0:T(8,128)(2,1)S(1)}, u32[]{:S(2)}, u32[]{:S(2)}) collective-permute-start(bf16[512,256]{1,0:T(8,128)(2,1)S(1)} %constant_dynamic-update-slice_fusion.2.refs_0_), channel_id=1, source_target_pairs={{0,6},{1,7},{2,4},{3,5},{4,2},{5,3},{6,0},{7,1},{8,14},{9,15},{10,... | collective-permute-start | bytes 786440 | tf_op jit(solution)/shard_map/ppermute | solution.py:746
  70.0 32.5 %collective-permute-start.20 = (bf16[1024,256]{1,0:T(8,128)(2,1)S(1)}, bf16[1024,256]{1,0:T(8,128)(2,1)}, u32[]{:S(2)}, u32[]{:S(2)}) collective-permute-start(bf16[1024,256]{1,0:T(8,128)(2,1)S(1)} %get-tuple-element.109), channel_id=1, source_target_pairs={{0,8},{4,12},{8,16},{12,20},{16,24},{20,28},{1,9},{5,13},{9,17},{1... | collective-permute-start | bytes 1572872 | tf_op jit(solution)/shard_map/ppermute | solution.py:38
  73.2 29.3 %collective-permute-start.21 = (bf16[1024,256]{1,0:T(8,128)(2,1)S(1)}, bf16[1024,256]{1,0:T(8,128)(2,1)}, u32[]{:S(2)}, u32[]{:S(2)}) collective-permute-start(bf16[1024,256]{1,0:T(8,128)(2,1)S(1)} %get-tuple-element.108), channel_id=1, source_target_pairs={{8,0},{12,4},{16,8},{20,12},{24,16},{28,20},{9,1},{13,5},{17,9},{2... | collective-permute-start | bytes 1572872 | tf_op jit(solution)/shard_map/ppermute | solution.py:38
  102.5 52.0 %all-to-all-start.1 = ((bf16[32,24,1024]{2,1,0:T(8,128)(2,1)}), bf16[32,24,1024]{2,1,0:T(8,128)(2,1)S(1)}, u32[]{:S(2)}, u32[]{:S(2)}) async-start(bf16[32,24,1024]{2,1,0:T(8,128)(2,1)} %bitcast.17), calls=%async_computation.1 | async-start | bytes 3145728 | tf_op jit(solution)/shard_map/all_to_all | solution.py:724
  114.9 34.3 %collective-permute-start.32 = (bf16[2048,256]{1,0:T(8,128)(2,1)}, bf16[2048,256]{1,0:T(8,128)(2,1)}, u32[]{:S(2)}, u32[]{:S(2)}) collective-permute-start(bf16[2048,256]{1,0:T(8,128)(2,1)} %stacked.1.refs_8_), channel_id=1, source_target_pairs={{0,1},{1,0},{2,3},{3,2},{4,5},{5,4},{6,7},{7,6},{8,9},{9,8},{10,11... | collective-permute-start | bytes 3145736 | tf_op jit(solution)/shard_map/ppermute | solution.py:32
  130.6 8.4 %collective-permute-start.26 = (bf16[384,128]{1,0:T(8,128)(2,1)}, bf16[384,128]{1,0:T(8,128)(2,1)S(1)}, u32[]{:S(2)}, u32[]{:S(2)}) collective-permute-start(bf16[384,128]{1,0:T(8,128)(2,1)} %get-tuple-element.96), channel_id=1, source_target_pairs={{0,2},{1,3},{2,0},{3,1},{4,6},{5,7},{6,4},{7,5},{8,10},{9,11},{10,... | collective-permute-start | bytes 294920 | tf_op jit(solution)/shard_map/ppermute | solution.py:770
  131.8 11.9 %collective-permute-start.27 = (bf16[384,128]{1,0:T(8,128)(2,1)}, bf16[384,128]{1,0:T(8,128)(2,1)S(1)}, u32[]{:S(2)}, u32[]{:S(2)}) collective-permute-start(bf16[384,128]{1,0:T(8,128)(2,1)} %get-tuple-element.97), channel_id=1, source_target_pairs={{0,3},{1,2},{2,1},{3,0},{4,7},{5,6},{6,5},{7,4},{8,11},{9,10},{10,... | collective-permute-start | bytes 294920 | tf_op jit(solution)/shard_map/ppermute | solution.py:770
  132.6 11.7 %collective-permute-start.28 = (bf16[384,128]{1,0:T(8,128)(2,1)}, bf16[384,128]{1,0:T(8,128)(2,1)S(1)}, u32[]{:S(2)}, u32[]{:S(2)}) collective-permute-start(bf16[384,128]{1,0:T(8,128)(2,1)} %get-tuple-element.98), channel_id=1, source_target_pairs={{0,4},{1,5},{2,6},{3,7},{4,0},{5,1},{6,2},{7,3},{8,12},{9,13},{10,... | collective-permute-start | bytes 294920 | tf_op jit(solution)/shard_map/ppermute | solution.py:770
  133.8 10.5 %collective-permute-start.29 = (bf16[384,128]{1,0:T(8,128)(2,1)}, bf16[384,128]{1,0:T(8,128)(2,1)S(1)}, u32[]{:S(2)}, u32[]{:S(2)}) collective-permute-start(bf16[384,128]{1,0:T(8,128)(2,1)} %get-tuple-element.99), channel_id=1, source_target_pairs={{0,5},{1,4},{2,7},{3,6},{4,1},{5,0},{6,3},{7,2},{8,13},{9,12},{10,... | collective-permute-start | bytes 294920 | tf_op jit(solution)/shard_map/ppermute | solution.py:770
  139.0 5.3 %collective-permute-start.30 = (bf16[384,128]{1,0:T(8,128)(2,1)}, bf16[384,128]{1,0:T(8,128)(2,1)S(1)}, u32[]{:S(2)}, u32[]{:S(2)}) collective-permute-start(bf16[384,128]{1,0:T(8,128)(2,1)} %get-tuple-element.100), channel_id=1, source_target_pairs={{0,6},{1,7},{2,4},{3,5},{4,2},{5,3},{6,0},{7,1},{8,14},{9,15},{10,... | collective-permute-start | bytes 294920 | tf_op jit(solution)/shard_map/ppermute | solution.py:770
  143.7 5.4 %collective-permute-start.31 = (bf16[384,128]{1,0:T(8,128)(2,1)}, bf16[384,128]{1,0:T(8,128)(2,1)S(1)}, u32[]{:S(2)}, u32[]{:S(2)}) collective-permute-start(bf16[384,128]{1,0:T(8,128)(2,1)} %get-tuple-element.101), channel_id=1, source_target_pairs={{0,7},{1,6},{2,5},{3,4},{4,3},{5,2},{6,1},{7,0},{8,15},{9,14},{10,... | collective-permute-start | bytes 294920 | tf_op jit(solution)/shard_map/ppermute | solution.py:770
  (26 other events, 175.3 us)

commit v13 on v12

--- a/solution.py
+++ b/solution.py
@@ -483,52 +483,93 @@
 
 
 def output_kernel(members, meta, *refs):
-    parts, weights, result, mixed = refs[:members], refs[members:-2], refs[-2], refs[-1]
+    parts, weights, received = refs[:members], refs[members : members + 2], refs[members + 2 : -4]
+    result, pages, mixed, chosen = refs[-4:]
+    step = pl.program_id(0)
     width = parts[0].shape[1]
-    tile = weights[0].shape[1]
-    for distance in range(members):
-        source = meta[0] ^ distance
-        head_pair = PAIR * (source % (members // PAIR)) + source // (members // PAIR)
-        shard = head_pair ^ meta[1]
-        shard = jnp.where(meta[1] < 0, head_pair, shard // PAIR + shard % PAIR * (members // PAIR))
-        columns = pl.ds(pl.multiple_of(shard * width, width), width)
-        mixed[:, columns] = parts[distance][...]
-    depth = mixed.shape[1]
-    groups = len(weights) * (weights[0].shape[0] // depth)
-    for distance in range(groups):
-        columns = pl.ds(pl.multiple_of((meta[0] % groups ^ distance) * tile, tile), tile)
-        start = distance // len(weights) * depth
-        result[:, columns] = jnp.dot(
-            mixed[...],
-            weights[distance % len(weights)][start : start + depth, :],
-            preferred_element_type=jnp.float32,
-        ).astype(jnp.bfloat16)
-
-
-def output_projection(meta, parts, weights):
+    half = members // PAIR // 2
+
+    @pl.when(step == 0)
+    def _():
+        for distance in range(members):
+            source = meta[0] ^ distance
+            head_pair = PAIR * (source % (members // PAIR)) + source // (members // PAIR)
+            shard = head_pair ^ meta[1]
+            shard = jnp.where(
+                meta[1] < 0, head_pair, shard // PAIR + shard % PAIR * (members // PAIR)
+            )
+            columns = pl.ds(pl.multiple_of(shard * width, width), width)
+            mixed[:, columns] = parts[distance][...]
+
+    @pl.when(step < half)
+    def _():
+        chosen[...] = weights[0][...]
+
+    @pl.when(step >= half)
+    def _():
+        chosen[...] = weights[1][...]
+
+    result[...] = jnp.dot(
+        mixed[...], chosen[...], preferred_element_type=jnp.float32
+    ).astype(jnp.bfloat16)
+    _, pair, count, _, part = received[0].shape
+    piece = part // (2 * PAGE)
+    for source in range(pair):
+        for low in range(pair):
+            block = received[0 if source == low else 1]
+            for high in range(count):
+                for turn in range(2 * PAGE):
+                    start = (turn * pair * count + PAIR * high + low) * piece
+                    pages[source, :, start : start + piece] = block[
+                        0, low, high, :, turn * piece : (turn + 1) * piece
+                    ]
+
+
+def outputs(meta, parts, weights, own_row, other_row):
     rows, width = parts[0].shape
     depth, tile = width * len(parts), weights[0].shape[1]
-    columns = sum(weight.shape[0] for weight in weights) // depth * tile
+    groups = len(parts) // PAIR
+    half = groups // 2
+    planes, pair, members, capacity, part = own_row.shape
+    place = lambda i: jnp.minimum(i, groups - 1)
     whole = lambda shape: pl.BlockSpec(shape, lambda i, m: (0, 0))
+    row_block = pl.BlockSpec((1,) + own_row.shape[1:], lambda i, m: (i, 0, 0, 0, 0))
     return pl.pallas_call(
         functools.partial(output_kernel, len(parts)),
         grid_spec=pltpu.PrefetchScalarGridSpec(
             num_scalar_prefetch=1,
-            grid=(1,),
+            grid=(planes,),
             in_specs=[whole(parts[0].shape)] * len(parts)
-            + [whole(weight.shape) for weight in weights],
-            out_specs=whole((rows, columns)),
-            scratch_shapes=[pltpu.VMEM((rows, depth), jnp.bfloat16)],
+            + [
+                pl.BlockSpec((depth, tile), lambda i, m: (jnp.minimum(i, half - 1), 0)),
+                pl.BlockSpec((depth, tile), lambda i, m: (jnp.maximum(place(i) - half, 0), 0)),
+                row_block,
+                row_block,
+            ],
+            out_specs=[
+                pl.BlockSpec(
+                    (rows, tile),
+                    lambda i, m: (0, (m[0] % groups) ^ (2 * (place(i) % half) + place(i) // half)),
+                ),
+                pl.BlockSpec((pair, capacity, pair * members * part), lambda i, m: (i, 0, 0)),
+            ],
+            scratch_shapes=[
+                pltpu.VMEM((rows, depth), jnp.bfloat16),
+                pltpu.VMEM((depth, tile), jnp.bfloat16),
+            ],
         ),
-        out_shape=jax.ShapeDtypeStruct((rows, columns), jnp.bfloat16),
-        compiler_params=PARAMS,
+        out_shape=[
+            jax.ShapeDtypeStruct((rows, groups * tile), jnp.bfloat16),
+            jax.ShapeDtypeStruct(
+                (planes * pair, capacity, pair * members * part), jnp.bfloat16
+            ),
+        ],
+        compiler_params=pltpu.CompilerParams(vmem_limit_bytes=32 * 1024 * 1024),
         cost_estimate=pl.CostEstimate(
-            flops=2 * rows * depth * columns,
-            bytes_accessed=4 << 20,
-            transcendentals=0,
+            flops=2 * rows * depth * groups * tile, bytes_accessed=10 << 20, transcendentals=0
         ),
-        name="output_projection",
-    )(meta, *parts, *weights)
+        name="outputs",
+    )(meta, *parts, *weights, own_row, other_row)
 
 
 def stack_kernel(*refs):
@@ -552,37 +593,6 @@
         cost_estimate=pl.CostEstimate(flops=0, bytes_accessed=2 << 20, transcendentals=0),
         name="stacked",
     )(*blocks)
-
-
-def unpack_kernel(own_row, other_row, pages):
-    _, pair, members, capacity, part = own_row.shape
-    width = part // (2 * PAGE)
-    for source in range(pair):
-        for low in range(pair):
-            received = own_row if source == low else other_row
-            for high in range(members):
-                for turn in range(2 * PAGE):
-                    start = (turn * pair * members + PAIR * high + low) * width
-                    pages[source, :, start : start + width] = received[
-                        0, low, high, :, turn * width : (turn + 1) * width
-                    ]
-
-
-def unpack(own_row, other_row):
-    planes, pair, members, capacity, part = own_row.shape
-    block = pl.BlockSpec((1,) + own_row.shape[1:], lambda i: (i, 0, 0, 0, 0))
-    return pl.pallas_call(
-        unpack_kernel,
-        grid=(planes,),
-        in_specs=[block, block],
-        out_specs=pl.BlockSpec((pair, capacity, pair * members * part), lambda i: (i, 0, 0)),
-        out_shape=jax.ShapeDtypeStruct(
-            (planes * pair, capacity, pair * members * part), jnp.bfloat16
-        ),
-        compiler_params=pltpu.CompilerParams(vmem_limit_bytes=24 * 1024 * 1024),
-        cost_estimate=pl.CostEstimate(flops=0, bytes_accessed=6 << 20, transcendentals=0),
-        name="unpack",
-    )(own_row, other_row)
 
 
 def rope_tables(positions):
@@ -775,10 +785,8 @@
         for distance in range(1, blocks)
     ]
     output_meta = jnp.stack([member, row_order]).astype(jnp.int32)
-    attended = output_projection(output_meta, parts, last_weights)
-    cache_pages = unpack(own_row, other_row).reshape(
-        peers * capacity, 2 * PAGE * model_width
-    )
+    attended, cache_pages = outputs(output_meta, parts, last_weights, own_row, other_row)
+    cache_pages = cache_pages.reshape(peers * capacity, 2 * PAGE * model_width)
     return attended, cache_pages
 
 

time: 158 us -> 159 us (level)
  waiting for transfers between devices: 31.7 us -> 25.9 us
  local copies, waits for them, and re-layouts: 5.97 us -> 11.5 us
  Pallas kernels: 66.4 us -> 69 us
  starting transfers between devices: 46.6 us -> 44.5 us
    unnamed x48 -> x52, local copies, waits for them, and re-layouts: 4.01 us -> 9.52 us
    ppermute x7, waiting for transfers between devices: 14.4 us -> 9.28 us  [per_device(): lax.ppermute(mixed[distance], ('tok', 'grp'), [(source, source ^ distance...]
    all_to_all x2, starting transfers between devices: 14.9 us -> 10.5 us  [to_owners(): lax.all_to_all(send.reshape((flat,) + send.shape[2:]), ('tok', 'grp'), sp...]
    pallas_call x1, Pallas kernels: 15.1 us -> 17.7 us  [attend_finish(): pl.pallas_call(functools.partial(finish_kernel, edge), grid_spec=pltpu.Pr...]
    ppermute x7, starting transfers between devices: 3.73 us -> 6.13 us  [per_device(): lax.ppermute(mixed[distance], ('tok', 'grp'), [(source, source ^ distance...]
    pallas_call x2 -> x1, Pallas kernels: 7.17 us -> 5.79 us  [outputs(): pl.pallas_call(functools.partial(output_kernel, len(parts)), grid_spec=pl...]
  transfers between devices with their start and end apart: 35 -> 35, of which waited for: 9 -> 9; matrix products, arithmetic and copies ran while one was open for 4% -> 4% of each run, Pallas kernels for 41% -> 40%
where the time goes in v13:
time: 159 us; the launch traced here: 157 us
  Pallas kernels  69 us (43%)
  starting transfers between devices  44.5 us (28%)
  waiting for transfers between devices  25.9 us (16%)
  local copies, waits for them, and re-layouts  11.5 us (7%)
  other arithmetic  4.64 us (3%)
    pallas_call x1, Pallas kernels, attend_edges(): pl.pallas_call(functools.partial(edge_kernel, edge), grid_spec=pltpu.Pref...  21.2 us
    pallas_call x1, Pallas kernels, attend_finish(): pl.pallas_call(functools.partial(finish_kernel, edge), grid_spec=pltpu.Pr...  17.7 us
    pallas_call x2, Pallas kernels, project(): pl.pallas_call(functools.partial(project_kernel, first, layout, len(weigh...  16.4 us
    ppermute x17, starting transfers between devices, flipped(): lax.ppermute(value, axis, [(source, source ^ bit) for source in range(cou...  13 us
    all_to_all x2, starting transfers between devices, to_owners(): lax.all_to_all(send.reshape((flat,) + send.shape[2:]), ('tok', 'grp'), sp...  10.5 us
    ppermute x17, waiting for transfers between devices, flipped(): lax.ppermute(value, axis, [(source, source ^ bit) for source in range(cou...  10 us
    unnamed x52, local copies, waits for them, and re-layouts  9.52 us
    ppermute x6, starting transfers between devices, per_device(): pieces.append(lax.ppermute(piece, ('tok', 'grp'), route))  9.33 us
  transfers between devices with their start and end apart: 35, of which 9 were waited for; matrix products, arithmetic and copies ran while one was open for 4% of the time, Pallas kernels for 40%

profile of v13, /device:TPU:17, one launch (start us, length us, event | category | flops | bytes accessed | tf_op | source)
XLA Modules:
  0.0 156.7 jit_solution(1082051193233162669)
XLA Ops:
  1.5 1.3 collective-permute-start.5
  2.8 2.0 %collective-permute-start.4 = (bf16[128,128]{1,0:T(8,128)(2,1)S(1)}, bf16[128,128]{1,0:T(8,128)(2,1)S(1)}, u32[]{:S(2)}, u32[]{:S(2)}) collective-permute-start(bf16[128,128]{1,0:T(8,128)(2,1)S(1)} %get-tuple-element.115), channel_id=1, source_target_pairs={{0,5},{1,4},{2,7},{3,6},{4,1},{5,0},{6,3},{7,2},{8,13},{9,12},{10,... | collective-permute-start | bytes 98312 | tf_op jit(solution)/shard_map/ppermute | solution.py:674
  6.7 1.7 %collective-permute-start.1 = (bf16[128,128]{1,0:T(8,128)(2,1)S(1)}, bf16[128,128]{1,0:T(8,128)(2,1)S(1)}, u32[]{:S(2)}, u32[]{:S(2)}) collective-permute-start(bf16[128,128]{1,0:T(8,128)(2,1)S(1)} %get-tuple-element.118), channel_id=1, source_target_pairs={{0,1},{1,0},{2,3},{3,2},{4,5},{5,4},{6,7},{7,6},{8,9},{9,8},{10,11... | collective-permute-start | bytes 98312 | tf_op jit(solution)/shard_map/ppermute | solution.py:674
  8.5 2.4 %collective-permute-start = (bf16[128,128]{1,0:T(8,128)(2,1)S(1)}, bf16[128,128]{1,0:T(8,128)(2,1)S(1)}, u32[]{:S(2)}, u32[]{:S(2)}) collective-permute-start(bf16[128,128]{1,0:T(8,128)(2,1)S(1)} %get-tuple-element.114), channel_id=1, source_target_pairs={{0,0},{1,3},{2,2},{3,1},{4,4},{5,7},{6,6},{7,5},{8,8},{9,11},{10,1... | collective-permute-start | bytes 98312 | tf_op jit(solution)/shard_map/ppermute | solution.py:674
  11.0 2.6 %layer_norm.1.refs_0_ = bf16[400,1024]{1,0:T(8,128)(2,1)} custom-call(bf16[384,1024]{1,0:T(8,128)(2,1)} %tokens.1, f32[1,1024]{1,0:T(1,128)} %bitcast.20, s32[1,96]{1,0:T(1,128)} %bitcast.21), custom_call_target="tpu_custom_call" | custom-call | tf_op jit(solution)/shard_map/layer_norm/pallas_call | solution.py:65
  14.3 1.3 collective-permute-start.12
  17.9 2.5 %document_bounds.1 = (s32[1,3072]{1,0:T(1,128)}, s32[1,3072]{1,0:T(1,128)}, s32[1,128]{1,0:T(1,128)}) custom-call(s32[1,5120]{1,0:T(1,128)} %bitcast.19), custom_call_target="tpu_custom_call" | custom-call | flops 17179869184 | tf_op jit(solution)/shard_map/document_bounds/pallas_call | solution.py:638
  21.3 4.7 %collective-permute-done.10.refs_6_.refs_8_ = bf16[256,384]{1,0:T(8,128)(2,1)S(1)} collective-permute-done((bf16[256,384]{1,0:T(8,128)(2,1)S(1)}, bf16[256,384]{1,0:T(8,128)(2,1)S(1)}, u32[]{:S(2)}, u32[]{:S(2)}) %collective-permute-start.10) | collective-permute-done | bytes 196640 | tf_op jit(solution)/shard_map/ppermute | solution.py:32
  26.0 2.5 %collective-permute-start.11 = (bf16[256,384]{1,0:T(8,128)(2,1)S(1)}, bf16[256,384]{1,0:T(8,128)(2,1)S(1)}, u32[]{:S(2)}, u32[]{:S(2)}) collective-permute-start(bf16[256,384]{1,0:T(8,128)(2,1)S(1)} %collective-permute-done.10.refs_6_.refs_8_), channel_id=1, source_target_pairs={{0,8},{4,12},{8,0},{12,4},{16,24},{20,28},{24,16},{28,20},{1,9},{5... | collective-permute-start | bytes 589832 | tf_op jit(solution)/shard_map/ppermute | solution.py:32
  28.5 2.3 %multiply_sine_fusion = (f32[32,3072]{1,0:T(8,128)}, f32[32,3072]{1,0:T(8,128)}) fusion(f32[3072]{0:T(1024)S(1)} %bitcast.18, f32[32]{0:T(128)S(1)} %negate_power_fusion), kind=kLoop, calls=%fused_computation | loop fusion | flops 98304 | bytes 798848 | tf_op jit(solution)/shard_map/sin | solution.py:602
  30.8 1.5 collective-permute-done.11.refs_7_.refs_9_
  32.3 2.6 %collective-permute-done.6.refs_2_ = bf16[400,1024]{1,0:T(8,128)(2,1)S(1)} collective-permute-done((bf16[400,1024]{1,0:T(8,128)(2,1)}, bf16[400,1024]{1,0:T(8,128)(2,1)S(1)}, u32[]{:S(2)}, u32[]{:S(2)}) %collective-permute-start.6) | collective-permute-done | bytes 819232 | tf_op jit(solution)/shard_map/ppermute | solution.py:32
  37.3 1.2 collective-permute-start.14
  38.8 1.9 %collective-permute-start.17 = (bf16[256,256]{1,0:T(8,128)(2,1)S(1)}, bf16[256,256]{1,0:T(8,128)(2,1)S(1)}, u32[]{:S(2)}, u32[]{:S(2)}) collective-permute-start(bf16[256,256]{1,0:T(8,128)(2,1)S(1)} %constant_dynamic-update-slice_fusion), channel_id=1, source_target_pairs={{0,16},{4,20},{8,24},{12,28},{16,0},{20,4},{24,8},{28,12},{1,17},{... | collective-permute-start | bytes 393224 | tf_op jit(solution)/shard_map/ppermute | solution.py:32
  40.8 8.2 %project.2 = (bf16[3072,128]{1,0:T(8,128)(2,1)}, bf16[3072,256]{1,0:T(8,128)(2,1)}, bf16[8,4,24,1024]{3,2,1,0:T(8,128)(2,1)}) custom-call(s32[5]{0:T(128)} %stack.29.meta, bf16[400,1024]{1,0:T(8,128)(2,1)} %layer_norm.1.refs_0_, bf16[400,1024]{1,0:T(8,128)(2,1)} %copy-done.18, bf16[400,1024]{1,0:T(8,128)(2,1)} %copy-done.14, ...), custom_call_target="tpu_custom_call" | custom-call | flops 9663676416 | bytes 6291456 | tf_op jit(solution)/shard_map/project/pallas_call | solution.py:172
  50.4 5.4 %all-to-all-start = ((bf16[32,24,1024]{2,1,0:T(8,128)(2,1)}), bf16[32,24,1024]{2,1,0:T(8,128)(2,1)S(1)}, u32[]{:S(2)}, u32[]{:S(2)}) async-start(bf16[32,24,1024]{2,1,0:T(8,128)(2,1)} %bitcast.17), calls=%async_computation | async-start | bytes 3145728 | tf_op jit(solution)/shard_map/all_to_all | solution.py:734
  56.4 1.3 collective-permute-start.22
  60.0 8.2 %project.3 = (bf16[3072,128]{1,0:T(8,128)(2,1)}, bf16[3072,256]{1,0:T(8,128)(2,1)}, bf16[8,4,24,1024]{3,2,1,0:T(8,128)(2,1)}) custom-call(s32[5]{0:T(128)} %stack.29.meta, bf16[400,1024]{1,0:T(8,128)(2,1)} %copy-done.12, bf16[400,1024]{1,0:T(8,128)(2,1)} %copy-done.17, bf16[192,1024]{1,0:T(8,128)(2,1)} %copy-done.20, ...), custom_call_target="tpu_custom_call", output_to_operand_aliasing={{0}: (13, {}), {1}: (14, {})} | custom-call | flops 9663676416 | bytes 6291456 | tf_op jit(solution)/shard_map/project/pallas_call | solution.py:172
  68.2 1.3 fusion.2
  69.5 3.2 %collective-permute-start.20 = (bf16[1024,256]{1,0:T(8,128)(2,1)S(1)}, bf16[1024,256]{1,0:T(8,128)(2,1)}, u32[]{:S(2)}, u32[]{:S(2)}) collective-permute-start(bf16[1024,256]{1,0:T(8,128)(2,1)S(1)} %get-tuple-element.113), channel_id=1, source_target_pairs={{0,8},{4,12},{8,16},{12,20},{16,24},{20,28},{1,9},{5,13},{9,17},{1... | collective-permute-start | bytes 1572872 | tf_op jit(solution)/shard_map/ppermute | solution.py:38
  72.6 2.1 %collective-permute-start.21 = (bf16[1024,256]{1,0:T(8,128)(2,1)S(1)}, bf16[1024,256]{1,0:T(8,128)(2,1)}, u32[]{:S(2)}, u32[]{:S(2)}) collective-permute-start(bf16[1024,256]{1,0:T(8,128)(2,1)S(1)} %get-tuple-element.112), channel_id=1, source_target_pairs={{8,0},{12,4},{16,8},{20,12},{24,16},{28,20},{9,1},{13,5},{17,9},{2... | collective-permute-start | bytes 1572872 | tf_op jit(solution)/shard_map/ppermute | solution.py:38
  74.8 21.2 %attend_edges.1 = (f32[5,160,256]{2,1,0:T(8,128)}, f32[5,160,256]{2,1,0:T(8,128)}, f32[5,8,256]{2,1,0:T(8,128)}, f32[5,8,256]{2,1,0:T(8,128)}) custom-call(s32[5]{0:T(128)} %stack.29.meta, s32[1,128]{1,0:T(1,128)} %get-tuple-element.62.ranges, bf16[3072,128]{1,0:T(8,128)(2,1)} %get-tuple-element.80.refs_0_.refs_3_, ...), custom_call_target="tpu_custom_call" | custom-call | flops 6442450944 | bytes 5242880 | tf_op jit(solution)/shard_map/attend_edges/pallas_call | solution.py:425
  96.1 6.5 %collective-permute-done.20.refs_7_ = bf16[1024,256]{1,0:T(8,128)(2,1)} collective-permute-done((bf16[1024,256]{1,0:T(8,128)(2,1)S(1)}, bf16[1024,256]{1,0:T(8,128)(2,1)}, u32[]{:S(2)}, u32[]{:S(2)}) %collective-permute-start.20) | collective-permute-done | bytes 524320 | tf_op jit(solution)/shard_map/ppermute | solution.py:38
  102.6 5.1 %all-to-all-start.1 = ((bf16[32,24,1024]{2,1,0:T(8,128)(2,1)}), bf16[32,24,1024]{2,1,0:T(8,128)(2,1)S(1)}, u32[]{:S(2)}, u32[]{:S(2)}) async-start(bf16[32,24,1024]{2,1,0:T(8,128)(2,1)} %bitcast.16), calls=%async_computation.1 | async-start | bytes 3145728 | tf_op jit(solution)/shard_map/all_to_all | solution.py:734
  107.8 2.8 %stacked.1.refs_8_ = bf16[2048,256]{1,0:T(8,128)(2,1)} custom-call(bf16[512,256]{1,0:T(8,128)(2,1)} %copy-done.8, bf16[512,256]{1,0:T(8,128)(2,1)} %copy-done.9, bf16[512,256]{1,0:T(8,128)(2,1)} %copy-done.10, bf16[512,256]{1,0:T(8,128)(2,1)} %copy-done.11), custom_call_target="tpu_custom_call" | custom-call | bytes 2097152 | tf_op jit(solution)/shard_map/stacked/pallas_call | solution.py:586
  110.9 17.7 %attend_finish.1 = (bf16[384,128]{1,0:T(8,128)(2,1)}, bf16[384,128]{1,0:T(8,128)(2,1)}, bf16[384,128]{1,0:T(8,128)(2,1)}, bf16[384,128]{1,0:T(8,128)(2,1)}, bf16...) custom-call(s32[5]{0:T(128)} %stack.29.meta, ...), custom_call_target="tpu_custom_call" | custom-call | flops 6442450944 | bytes 5242880 | tf_op jit(solution)/shard_map/attend_finish/pallas_call | solution.py:453
  132.4 3.0 %collective-permute-done.26.refs_2_ = bf16[384,128]{1,0:T(8,128)(2,1)S(1)} collective-permute-done((bf16[384,128]{1,0:T(8,128)(2,1)}, bf16[384,128]{1,0:T(8,128)(2,1)S(1)}, u32[]{:S(2)}, u32[]{:S(2)}) %collective-permute-start.26) | collective-permute-done | bytes 98336 | tf_op jit(solution)/shard_map/ppermute | solution.py:780
  135.4 1.4 collective-permute-start.30
  136.7 3.4 %collective-permute-done.27.refs_3_ = bf16[384,128]{1,0:T(8,128)(2,1)S(1)} collective-permute-done((bf16[384,128]{1,0:T(8,128)(2,1)}, bf16[384,128]{1,0:T(8,128)(2,1)S(1)}, u32[]{:S(2)}, u32[]{:S(2)}) %collective-permute-start.27) | collective-permute-done | bytes 98336 | tf_op jit(solution)/shard_map/ppermute | solution.py:780
  142.6 2.9 %collective-permute-done.31.refs_7_ = bf16[384,128]{1,0:T(8,128)(2,1)S(1)} collective-permute-done((bf16[384,128]{1,0:T(8,128)(2,1)}, bf16[384,128]{1,0:T(8,128)(2,1)S(1)}, u32[]{:S(2)}, u32[]{:S(2)}) %collective-permute-start.31) | collective-permute-done | bytes 98336 | tf_op jit(solution)/shard_map/ppermute | solution.py:780
  146.1 1.2 copy-done
  150.9 5.8 %outputs.1 = (bf16[384,1024]{1,0:T(8,128)(2,1)}, bf16[8,24,8192]{2,1,0:T(8,128)(2,1)}) custom-call(s32[2]{0:T(128)S(1)} %pad_add_fusion.meta, bf16[384,128]{1,0:T(8,128)(2,1)S(1)} %copy-done.1, bf16[384,128]{1,0:T(8,128)(2,1)S(1)} %collective-permute-done.25.refs_1_, bf16[384,128]{1,0:T(8,128)(2,1)S(1)} %collective-permute-done.26.refs_2_, ...), custom_call_target="tpu_custom_call" | custom-call | flops 805306368 | bytes 10485760 | tf_op jit(solution)/shard_map/outputs/pallas_call | solution.py:537
  (113 shorter events, 24.4 us)
Async XLA Ops:
  1.5 6.9 %collective-permute-start.5 = (bf16[128,128]{1,0:T(8,128)(2,1)S(1)}, bf16[128,128]{1,0:T(8,128)(2,1)S(1)}, u32[]{:S(2)}, u32[]{:S(2)}) collective-permute-start(bf16[128,128]{1,0:T(8,128)(2,1)S(1)} %get-tuple-element.117), channel_id=1, source_target_pairs={{0,6},{1,5},{2,4},{3,7},{4,2},{5,1},{6,0},{7,3},{8,14},{9,13},{10,... | collective-permute-start | bytes 98312 | tf_op jit(solution)/shard_map/ppermute | solution.py:674
  2.8 11.4 %collective-permute-start.4 = (bf16[128,128]{1,0:T(8,128)(2,1)S(1)}, bf16[128,128]{1,0:T(8,128)(2,1)S(1)}, u32[]{:S(2)}, u32[]{:S(2)}) collective-permute-start(bf16[128,128]{1,0:T(8,128)(2,1)S(1)} %get-tuple-element.115), channel_id=1, source_target_pairs={{0,5},{1,4},{2,7},{3,6},{4,1},{5,0},{6,3},{7,2},{8,13},{9,12},{10,... | collective-permute-start | bytes 98312 | tf_op jit(solution)/shard_map/ppermute | solution.py:674
  4.8 10.7 %collective-permute-start.3 = (bf16[128,128]{1,0:T(8,128)(2,1)S(1)}, bf16[128,128]{1,0:T(8,128)(2,1)S(1)}, u32[]{:S(2)}, u32[]{:S(2)}) collective-permute-start(bf16[128,128]{1,0:T(8,128)(2,1)S(1)} %get-tuple-element.116), channel_id=1, source_target_pairs={{0,4},{1,7},{2,6},{3,5},{4,0},{5,3},{6,2},{7,1},{8,12},{9,15},{10,... | collective-permute-start | bytes 98312 | tf_op jit(solution)/shard_map/ppermute | solution.py:674
  6.1 9.5 %collective-permute-start.2 = (bf16[128,128]{1,0:T(8,128)(2,1)S(1)}, bf16[128,128]{1,0:T(8,128)(2,1)S(1)}, u32[]{:S(2)}, u32[]{:S(2)}) collective-permute-start(bf16[128,128]{1,0:T(8,128)(2,1)S(1)} %get-tuple-element.119), channel_id=1, source_target_pairs={{0,2},{1,1},{2,0},{3,3},{4,6},{5,5},{6,4},{7,7},{8,10},{9,9},{10,8... | collective-permute-start | bytes 98312 | tf_op jit(solution)/shard_map/ppermute | solution.py:674
  6.7 8.9 %collective-permute-start.1 = (bf16[128,128]{1,0:T(8,128)(2,1)S(1)}, bf16[128,128]{1,0:T(8,128)(2,1)S(1)}, u32[]{:S(2)}, u32[]{:S(2)}) collective-permute-start(bf16[128,128]{1,0:T(8,128)(2,1)S(1)} %get-tuple-element.118), channel_id=1, source_target_pairs={{0,1},{1,0},{2,3},{3,2},{4,5},{5,4},{6,7},{7,6},{8,9},{9,8},{10,11... | collective-permute-start | bytes 98312 | tf_op jit(solution)/shard_map/ppermute | solution.py:674
  8.5 7.1 %collective-permute-start = (bf16[128,128]{1,0:T(8,128)(2,1)S(1)}, bf16[128,128]{1,0:T(8,128)(2,1)S(1)}, u32[]{:S(2)}, u32[]{:S(2)}) collective-permute-start(bf16[128,128]{1,0:T(8,128)(2,1)S(1)} %get-tuple-element.114), channel_id=1, source_target_pairs={{0,0},{1,3},{2,2},{3,1},{4,4},{5,7},{6,6},{7,5},{8,8},{9,11},{10,1... | collective-permute-start | bytes 98312 | tf_op jit(solution)/shard_map/ppermute | solution.py:674
  14.3 6.8 %collective-permute-start.12 = (bf16[128,256]{1,0:T(8,128)(2,1)S(1)}, bf16[128,256]{1,0:T(8,128)(2,1)S(1)}, u32[]{:S(2)}, u32[]{:S(2)}) collective-permute-start(bf16[128,256]{1,0:T(8,128)(2,1)S(1)} %copy-done.15), channel_id=1, source_target_pairs={{0,8},{4,12},{8,0},{12,4},{16,24},{20,28},{24,16},{28,20},{1,9},{5... | collective-permute-start | bytes 196616 | tf_op jit(solution)/shard_map/ppermute | solution.py:32
  15.6 19.2 %collective-permute-start.6 = (bf16[400,1024]{1,0:T(8,128)(2,1)}, bf16[400,1024]{1,0:T(8,128)(2,1)S(1)}, u32[]{:S(2)}, u32[]{:S(2)}) collective-permute-start(bf16[400,1024]{1,0:T(8,128)(2,1)} %layer_norm.1.refs_0_), channel_id=1, source_target_pairs={{0,2},{1,3},{2,0},{3,1},{4,6},{5,7},{6,4},{7,5},{8,10},{9,11},{10,... | collective-permute-start | bytes 2457608 | tf_op jit(solution)/shard_map/ppermute | solution.py:32
  16.6 19.1 %collective-permute-start.7 = (bf16[400,1024]{1,0:T(8,128)(2,1)}, bf16[400,1024]{1,0:T(8,128)(2,1)S(1)}, u32[]{:S(2)}, u32[]{:S(2)}) collective-permute-start(bf16[400,1024]{1,0:T(8,128)(2,1)} %layer_norm.1.refs_0_), channel_id=1, source_target_pairs={{0,4},{4,0},{8,12},{12,8},{16,20},{20,16},{24,28},{28,24},{1,5},{5... | collective-permute-start | bytes 2457608 | tf_op jit(solution)/shard_map/ppermute | solution.py:32
  17.2 18.5 %collective-permute-start.8 = (bf16[400,1024]{1,0:T(8,128)(2,1)}, bf16[400,1024]{1,0:T(8,128)(2,1)S(1)}, u32[]{:S(2)}, u32[]{:S(2)}) collective-permute-start(bf16[400,1024]{1,0:T(8,128)(2,1)} %layer_norm.1.refs_0_), channel_id=1, source_target_pairs={{0,1},{1,0},{2,3},{3,2},{4,5},{5,4},{6,7},{7,6},{8,9},{9,8},{10,11... | collective-permute-start | bytes 2457608 | tf_op jit(solution)/shard_map/ppermute | solution.py:32
  17.2 8.8 %collective-permute-start.10 = (bf16[256,384]{1,0:T(8,128)(2,1)S(1)}, bf16[256,384]{1,0:T(8,128)(2,1)S(1)}, u32[]{:S(2)}, u32[]{:S(2)}) collective-permute-start(bf16[256,384]{1,0:T(8,128)(2,1)S(1)} %maximum_maximum_fusion.refs_4_.refs_6_), channel_id=1, source_target_pairs={{0,16},{4,20},{8,24},{12,28},{16,0},{20,4},{24,8},{28,12},{1,17},{... | collective-permute-start | bytes 589832 | tf_op jit(solution)/shard_map/ppermute | solution.py:32
  21.1 9.7 %collective-permute-start.9 = (bf16[256,384]{1,0:T(8,128)(2,1)S(1)}, bf16[256,384]{1,0:T(8,128)(2,1)S(1)}, u32[]{:S(2)}, u32[]{:S(2)}) collective-permute-start(bf16[256,384]{1,0:T(8,128)(2,1)S(1)} %maximum_maximum_fusion.refs_4_.refs_6_), channel_id=1, source_target_pairs={{0,8},{4,12},{8,0},{12,4},{16,24},{20,28},{24,16},{28,20},{1,9},{5... | collective-permute-start | bytes 589832 | tf_op jit(solution)/shard_map/ppermute | solution.py:32
  26.0 6.3 %collective-permute-start.11 = (bf16[256,384]{1,0:T(8,128)(2,1)S(1)}, bf16[256,384]{1,0:T(8,128)(2,1)S(1)}, u32[]{:S(2)}, u32[]{:S(2)}) collective-permute-start(bf16[256,384]{1,0:T(8,128)(2,1)S(1)} %collective-permute-done.10.refs_6_.refs_8_), channel_id=1, source_target_pairs={{0,8},{4,12},{8,0},{12,4},{16,24},{20,28},{24,16},{28,20},{1,9},{5... | collective-permute-start | bytes 589832 | tf_op jit(solution)/shard_map/ppermute | solution.py:32
  36.6 4.1 %collective-permute-start.13 = (bf16[400,1024]{1,0:T(8,128)(2,1)S(1)}, bf16[400,1024]{1,0:T(8,128)(2,1)}, u32[]{:S(2)}, u32[]{:S(2)}) collective-permute-start(bf16[400,1024]{1,0:T(8,128)(2,1)S(1)} %collective-permute-done.6.refs_2_), channel_id=1, source_target_pairs={{0,1},{1,0},{2,3},{3,2},{4,5},{5,4},{6,7},{7,6},{8,9},{9,8},{10,11... | collective-permute-start | bytes 2457608 | tf_op jit(solution)/shard_map/ppermute | solution.py:32
  36.7 12.7 %collective-permute-start.16 = (bf16[400,1024]{1,0:T(8,128)(2,1)S(1)}, bf16[400,1024]{1,0:T(8,128)(2,1)S(1)}, u32[]{:S(2)}, u32[]{:S(2)}) collective-permute-start(bf16[400,1024]{1,0:T(8,128)(2,1)S(1)} %collective-permute-done.7.refs_0_), channel_id=1, source_target_pairs={{0,1},{1,0},{2,3},{3,2},{4,5},{5,4},{6,7},{7,6},{8,9},{9,8},{10,11... | collective-permute-start | bytes 2457608 | tf_op jit(solution)/shard_map/ppermute | solution.py:32
  37.3 11.7 %collective-permute-start.14 = (bf16[192,1024]{1,0:T(8,128)(2,1)S(1)}, bf16[192,1024]{1,0:T(8,128)(2,1)S(1)}, u32[]{:S(2)}, u32[]{:S(2)}) collective-permute-start(bf16[192,1024]{1,0:T(8,128)(2,1)S(1)} %slice.42), channel_id=1, source_target_pairs={{0,4},{4,0},{8,12},{12,8},{16,20},{20,16},{24,28},{28,24},{1,5},{5... | collective-permute-start | bytes 1179656 | tf_op jit(solution)/shard_map/ppermute | solution.py:32
  38.6 10.9 %collective-permute-start.15 = (bf16[208,1024]{1,0:T(8,128)(2,1)S(1)}, bf16[208,1024]{1,0:T(8,128)(2,1)}, u32[]{:S(2)}, u32[]{:S(2)}) collective-permute-start(bf16[208,1024]{1,0:T(8,128)(2,1)S(1)} %slice.43), channel_id=1, source_target_pairs={{0,2},{1,3},{2,0},{3,1},{4,6},{5,7},{6,4},{7,5},{8,10},{9,11},{10,... | collective-permute-start | bytes 1277960 | tf_op jit(solution)/shard_map/ppermute | solution.py:32
  38.8 10.1 %collective-permute-start.17 = (bf16[256,256]{1,0:T(8,128)(2,1)S(1)}, bf16[256,256]{1,0:T(8,128)(2,1)S(1)}, u32[]{:S(2)}, u32[]{:S(2)}) collective-permute-start(bf16[256,256]{1,0:T(8,128)(2,1)S(1)} %constant_dynamic-update-slice_fusion), channel_id=1, source_target_pairs={{0,16},{4,20},{8,24},{12,28},{16,0},{20,4},{24,8},{28,12},{1,17},{... | collective-permute-start | bytes 393224 | tf_op jit(solution)/shard_map/ppermute | solution.py:32
  50.4 52.2 %all-to-all-start = ((bf16[32,24,1024]{2,1,0:T(8,128)(2,1)}), bf16[32,24,1024]{2,1,0:T(8,128)(2,1)S(1)}, u32[]{:S(2)}, u32[]{:S(2)}) async-start(bf16[32,24,1024]{2,1,0:T(8,128)(2,1)} %bitcast.17), calls=%async_computation | async-start | bytes 3145728 | tf_op jit(solution)/shard_map/all_to_all | solution.py:734
  56.4 39.7 %collective-permute-start.22 = (bf16[512,256]{1,0:T(8,128)(2,1)S(1)}, bf16[512,256]{1,0:T(8,128)(2,1)S(1)}, u32[]{:S(2)}, u32[]{:S(2)}) collective-permute-start(bf16[512,256]{1,0:T(8,128)(2,1)S(1)} %constant_dynamic-update-slice_fusion.2.refs_0_), channel_id=1, source_target_pairs={{0,4},{4,0},{8,12},{12,8},{16,20},{20,16},{24,28},{28,24},{1,5},{5... | collective-permute-start | bytes 786440 | tf_op jit(solution)/shard_map/ppermute | solution.py:32
  57.6 38.4 %collective-permute-start.23 = (bf16[512,256]{1,0:T(8,128)(2,1)S(1)}, bf16[512,256]{1,0:T(8,128)(2,1)S(1)}, u32[]{:S(2)}, u32[]{:S(2)}) collective-permute-start(bf16[512,256]{1,0:T(8,128)(2,1)S(1)} %constant_dynamic-update-slice_fusion.2.refs_0_), channel_id=1, source_target_pairs={{0,2},{1,3},{2,0},{3,1},{4,6},{5,7},{6,4},{7,5},{8,10},{9,11},{10,... | collective-permute-start | bytes 786440 | tf_op jit(solution)/shard_map/ppermute | solution.py:32
  58.8 37.2 %collective-permute-start.24 = (bf16[512,256]{1,0:T(8,128)(2,1)S(1)}, bf16[512,256]{1,0:T(8,128)(2,1)S(1)}, u32[]{:S(2)}, u32[]{:S(2)}) collective-permute-start(bf16[512,256]{1,0:T(8,128)(2,1)S(1)} %constant_dynamic-update-slice_fusion.2.refs_0_), channel_id=1, source_target_pairs={{0,6},{1,7},{2,4},{3,5},{4,2},{5,3},{6,0},{7,1},{8,14},{9,15},{10,... | collective-permute-start | bytes 786440 | tf_op jit(solution)/shard_map/ppermute | solution.py:756
  69.5 33.1 %collective-permute-start.20 = (bf16[1024,256]{1,0:T(8,128)(2,1)S(1)}, bf16[1024,256]{1,0:T(8,128)(2,1)}, u32[]{:S(2)}, u32[]{:S(2)}) collective-permute-start(bf16[1024,256]{1,0:T(8,128)(2,1)S(1)} %get-tuple-element.113), channel_id=1, source_target_pairs={{0,8},{4,12},{8,16},{12,20},{16,24},{20,28},{1,9},{5,13},{9,17},{1... | collective-permute-start | bytes 1572872 | tf_op jit(solution)/shard_map/ppermute | solution.py:38
  72.6 30.0 %collective-permute-start.21 = (bf16[1024,256]{1,0:T(8,128)(2,1)S(1)}, bf16[1024,256]{1,0:T(8,128)(2,1)}, u32[]{:S(2)}, u32[]{:S(2)}) collective-permute-start(bf16[1024,256]{1,0:T(8,128)(2,1)S(1)} %get-tuple-element.112), channel_id=1, source_target_pairs={{8,0},{12,4},{16,8},{20,12},{24,16},{28,20},{9,1},{13,5},{17,9},{2... | collective-permute-start | bytes 1572872 | tf_op jit(solution)/shard_map/ppermute | solution.py:38
  102.6 43.4 %all-to-all-start.1 = ((bf16[32,24,1024]{2,1,0:T(8,128)(2,1)}), bf16[32,24,1024]{2,1,0:T(8,128)(2,1)S(1)}, u32[]{:S(2)}, u32[]{:S(2)}) async-start(bf16[32,24,1024]{2,1,0:T(8,128)(2,1)} %bitcast.16), calls=%async_computation.1 | async-start | bytes 3145728 | tf_op jit(solution)/shard_map/all_to_all | solution.py:734
  110.5 35.5 %collective-permute-start.32 = (bf16[2048,256]{1,0:T(8,128)(2,1)}, bf16[2048,256]{1,0:T(8,128)(2,1)}, u32[]{:S(2)}, u32[]{:S(2)}) collective-permute-start(bf16[2048,256]{1,0:T(8,128)(2,1)} %stacked.1.refs_8_), channel_id=1, source_target_pairs={{0,1},{1,0},{2,3},{3,2},{4,5},{5,4},{6,7},{7,6},{8,9},{9,8},{10,11... | collective-permute-start | bytes 3145736 | tf_op jit(solution)/shard_map/ppermute | solution.py:32
  128.9 6.5 %collective-permute-start.26 = (bf16[384,128]{1,0:T(8,128)(2,1)}, bf16[384,128]{1,0:T(8,128)(2,1)S(1)}, u32[]{:S(2)}, u32[]{:S(2)}) collective-permute-start(bf16[384,128]{1,0:T(8,128)(2,1)} %get-tuple-element.98), channel_id=1, source_target_pairs={{0,2},{1,3},{2,0},{3,1},{4,6},{5,7},{6,4},{7,5},{8,10},{9,11},{10,... | collective-permute-start | bytes 294920 | tf_op jit(solution)/shard_map/ppermute | solution.py:780
  130.0 10.1 %collective-permute-start.27 = (bf16[384,128]{1,0:T(8,128)(2,1)}, bf16[384,128]{1,0:T(8,128)(2,1)S(1)}, u32[]{:S(2)}, u32[]{:S(2)}) collective-permute-start(bf16[384,128]{1,0:T(8,128)(2,1)} %get-tuple-element.99), channel_id=1, source_target_pairs={{0,3},{1,2},{2,1},{3,0},{4,7},{5,6},{6,5},{7,4},{8,11},{9,10},{10,... | collective-permute-start | bytes 294920 | tf_op jit(solution)/shard_map/ppermute | solution.py:780
  130.9 10.4 %collective-permute-start.28 = (bf16[384,128]{1,0:T(8,128)(2,1)}, bf16[384,128]{1,0:T(8,128)(2,1)S(1)}, u32[]{:S(2)}, u32[]{:S(2)}) collective-permute-start(bf16[384,128]{1,0:T(8,128)(2,1)} %get-tuple-element.100), channel_id=1, source_target_pairs={{0,4},{1,5},{2,6},{3,7},{4,0},{5,1},{6,2},{7,3},{8,12},{9,13},{10,... | collective-permute-start | bytes 294920 | tf_op jit(solution)/shard_map/ppermute | solution.py:780
  132.1 9.2 %collective-permute-start.29 = (bf16[384,128]{1,0:T(8,128)(2,1)}, bf16[384,128]{1,0:T(8,128)(2,1)S(1)}, u32[]{:S(2)}, u32[]{:S(2)}) collective-permute-start(bf16[384,128]{1,0:T(8,128)(2,1)} %get-tuple-element.101), channel_id=1, source_target_pairs={{0,5},{1,4},{2,7},{3,6},{4,1},{5,0},{6,3},{7,2},{8,13},{9,12},{10,... | collective-permute-start | bytes 294920 | tf_op jit(solution)/shard_map/ppermute | solution.py:780
  135.4 6.5 %collective-permute-start.30 = (bf16[384,128]{1,0:T(8,128)(2,1)}, bf16[384,128]{1,0:T(8,128)(2,1)S(1)}, u32[]{:S(2)}, u32[]{:S(2)}) collective-permute-start(bf16[384,128]{1,0:T(8,128)(2,1)} %get-tuple-element.102), channel_id=1, source_target_pairs={{0,6},{1,7},{2,4},{3,5},{4,2},{5,3},{6,0},{7,1},{8,14},{9,15},{10,... | collective-permute-start | bytes 294920 | tf_op jit(solution)/shard_map/ppermute | solution.py:780
  140.1 5.3 %collective-permute-start.31 = (bf16[384,128]{1,0:T(8,128)(2,1)}, bf16[384,128]{1,0:T(8,128)(2,1)S(1)}, u32[]{:S(2)}, u32[]{:S(2)}) collective-permute-start(bf16[384,128]{1,0:T(8,128)(2,1)} %get-tuple-element.103), channel_id=1, source_target_pairs={{0,7},{1,6},{2,5},{3,4},{4,3},{5,2},{6,1},{7,0},{8,15},{9,14},{10,... | collective-permute-start | bytes 294920 | tf_op jit(solution)/shard_map/ppermute | solution.py:780
  (28 other events, 128.1 us)

commit v14 on v13

--- a/solution.py
+++ b/solution.py
@@ -564,7 +564,7 @@
                 (planes * pair, capacity, pair * members * part), jnp.bfloat16
             ),
         ],
-        compiler_params=pltpu.CompilerParams(vmem_limit_bytes=32 * 1024 * 1024),
+        compiler_params=PARAMS,
         cost_estimate=pl.CostEstimate(
             flops=2 * rows * depth * groups * tile, bytes_accessed=10 << 20, transcendentals=0
         ),

time: 159 us -> 157 us (0.987)
  local copies, waits for them, and re-layouts: 11.5 us -> 8.16 us
    unnamed x52 -> x54, local copies, waits for them, and re-layouts: 9.52 us -> 6.13 us
    pallas_call x1, Pallas kernels: 17.7 us -> 14.5 us  [attend_finish(): pl.pallas_call(functools.partial(finish_kernel, edge), grid_spec=pltpu.Pr...]
    ppermute x2, waiting for transfers between devices: 6.52 us -> 3.3 us  [shifted(): lax.ppermute(value, axis, [(source, source + steps) for source in range(i...]
    ppermute x7, waiting for transfers between devices: 9.28 us -> 12.4 us  [per_device(): lax.ppermute(mixed[distance], ('tok', 'grp'), [(source, source ^ distance...]
    pallas_call x1, Pallas kernels: 21.2 us -> 23.8 us  [attend_edges(): pl.pallas_call(functools.partial(edge_kernel, edge), grid_spec=pltpu.Pref...]
  transfers between devices with their start and end apart: 35 -> 35, of which waited for: 9 -> 9; matrix products, arithmetic and copies ran while one was open for 4% -> 4% of each run, Pallas kernels for 40% -> 41%
where the time goes in v14:
time: 157 us; the launch traced here: 154 us
  Pallas kernels  69.4 us (44%)
  starting transfers between devices  44.2 us (28%)
  waiting for transfers between devices  25.9 us (16%)
  local copies, waits for them, and re-layouts  8.16 us (5%)
  other arithmetic  5.2 us (3%)
    pallas_call x1, Pallas kernels, attend_edges(): pl.pallas_call(functools.partial(edge_kernel, edge), grid_spec=pltpu.Pref...  23.8 us
    pallas_call x2, Pallas kernels, project(): pl.pallas_call(functools.partial(project_kernel, first, layout, len(weigh...  16.4 us
    pallas_call x1, Pallas kernels, attend_finish(): pl.pallas_call(functools.partial(finish_kernel, edge), grid_spec=pltpu.Pr...  14.5 us
    ppermute x17, starting transfers between devices, flipped(): lax.ppermute(value, axis, [(source, source ^ bit) for source in range(cou...  13 us
    ppermute x7, waiting for transfers between devices, per_device(): lax.ppermute(mixed[distance], ('tok', 'grp'), [(source, source ^ distance...  12.4 us
    all_to_all x2, starting transfers between devices, to_owners(): lax.all_to_all(send.reshape((flat,) + send.shape[2:]), ('tok', 'grp'), sp...  10.5 us
    ppermute x17, waiting for transfers between devices, flipped(): lax.ppermute(value, axis, [(source, source ^ bit) for source in range(cou...  10.1 us
    ppermute x6, starting transfers between devices, per_device(): pieces.append(lax.ppermute(piece, ('tok', 'grp'), route))  9.33 us
  transfers between devices with their start and end apart: 35, of which 9 were waited for; matrix products, arithmetic and copies ran while one was open for 4% of the time, Pallas kernels for 41%

profile of v14, /device:TPU:17, one launch (start us, length us, event | category | flops | bytes accessed | tf_op | source)
XLA Modules:
  0.0 154.0 jit_solution(18247336189652946250)
XLA Ops:
  1.5 1.3 collective-permute-start.5
  2.8 2.0 %collective-permute-start.4 = (bf16[128,128]{1,0:T(8,128)(2,1)S(1)}, bf16[128,128]{1,0:T(8,128)(2,1)S(1)}, u32[]{:S(2)}, u32[]{:S(2)}) collective-permute-start(bf16[128,128]{1,0:T(8,128)(2,1)S(1)} %get-tuple-element.115), channel_id=1, source_target_pairs={{0,5},{1,4},{2,7},{3,6},{4,1},{5,0},{6,3},{7,2},{8,13},{9,12},{10,... | collective-permute-start | bytes 98312 | tf_op jit(solution)/shard_map/ppermute | solution.py:674
  4.8 1.2 collective-permute-start.3
  6.7 1.7 %collective-permute-start.1 = (bf16[128,128]{1,0:T(8,128)(2,1)S(1)}, bf16[128,128]{1,0:T(8,128)(2,1)S(1)}, u32[]{:S(2)}, u32[]{:S(2)}) collective-permute-start(bf16[128,128]{1,0:T(8,128)(2,1)S(1)} %get-tuple-element.118), channel_id=1, source_target_pairs={{0,1},{1,0},{2,3},{3,2},{4,5},{5,4},{6,7},{7,6},{8,9},{9,8},{10,11... | collective-permute-start | bytes 98312 | tf_op jit(solution)/shard_map/ppermute | solution.py:674
  8.5 2.4 %collective-permute-start = (bf16[128,128]{1,0:T(8,128)(2,1)S(1)}, bf16[128,128]{1,0:T(8,128)(2,1)S(1)}, u32[]{:S(2)}, u32[]{:S(2)}) collective-permute-start(bf16[128,128]{1,0:T(8,128)(2,1)S(1)} %get-tuple-element.114), channel_id=1, source_target_pairs={{0,0},{1,3},{2,2},{3,1},{4,4},{5,7},{6,6},{7,5},{8,8},{9,11},{10,1... | collective-permute-start | bytes 98312 | tf_op jit(solution)/shard_map/ppermute | solution.py:674
  11.0 2.6 %layer_norm.1.refs_0_ = bf16[400,1024]{1,0:T(8,128)(2,1)} custom-call(bf16[384,1024]{1,0:T(8,128)(2,1)} %tokens.1, f32[1,1024]{1,0:T(1,128)} %bitcast.20, s32[1,96]{1,0:T(1,128)} %bitcast.21), custom_call_target="tpu_custom_call" | custom-call | tf_op jit(solution)/shard_map/layer_norm/pallas_call | solution.py:65
  14.3 1.3 collective-permute-start.12
  17.9 2.4 %document_bounds.1 = (s32[1,3072]{1,0:T(1,128)}, s32[1,3072]{1,0:T(1,128)}, s32[1,128]{1,0:T(1,128)}) custom-call(s32[1,5120]{1,0:T(1,128)} %bitcast.19), custom_call_target="tpu_custom_call" | custom-call | flops 17179869184 | tf_op jit(solution)/shard_map/document_bounds/pallas_call | solution.py:638
  21.3 4.8 %collective-permute-done.10.refs_6_.refs_8_ = bf16[256,384]{1,0:T(8,128)(2,1)S(1)} collective-permute-done((bf16[256,384]{1,0:T(8,128)(2,1)S(1)}, bf16[256,384]{1,0:T(8,128)(2,1)S(1)}, u32[]{:S(2)}, u32[]{:S(2)}) %collective-permute-start.10) | collective-permute-done | bytes 196640 | tf_op jit(solution)/shard_map/ppermute | solution.py:32
  26.1 2.5 %collective-permute-start.11 = (bf16[256,384]{1,0:T(8,128)(2,1)S(1)}, bf16[256,384]{1,0:T(8,128)(2,1)S(1)}, u32[]{:S(2)}, u32[]{:S(2)}) collective-permute-start(bf16[256,384]{1,0:T(8,128)(2,1)S(1)} %collective-permute-done.10.refs_6_.refs_8_), channel_id=1, source_target_pairs={{0,8},{4,12},{8,0},{12,4},{16,24},{20,28},{24,16},{28,20},{1,9},{5... | collective-permute-start | bytes 589832 | tf_op jit(solution)/shard_map/ppermute | solution.py:32
  28.5 2.3 %multiply_sine_fusion = (f32[32,3072]{1,0:T(8,128)}, f32[32,3072]{1,0:T(8,128)}) fusion(f32[3072]{0:T(1024)S(1)} %bitcast.18, f32[32]{0:T(128)S(1)} %negate_power_fusion), kind=kLoop, calls=%fused_computation | loop fusion | flops 98304 | bytes 798848 | tf_op jit(solution)/shard_map/sin | solution.py:602
  30.8 1.5 collective-permute-done.11.refs_7_.refs_9_
  32.3 2.6 %collective-permute-done.6.refs_2_ = bf16[400,1024]{1,0:T(8,128)(2,1)S(1)} collective-permute-done((bf16[400,1024]{1,0:T(8,128)(2,1)}, bf16[400,1024]{1,0:T(8,128)(2,1)S(1)}, u32[]{:S(2)}, u32[]{:S(2)}) %collective-permute-start.6) | collective-permute-done | bytes 819232 | tf_op jit(solution)/shard_map/ppermute | solution.py:32
  37.4 1.2 collective-permute-start.14
  38.9 1.9 %collective-permute-start.17 = (bf16[256,256]{1,0:T(8,128)(2,1)S(1)}, bf16[256,256]{1,0:T(8,128)(2,1)S(1)}, u32[]{:S(2)}, u32[]{:S(2)}) collective-permute-start(bf16[256,256]{1,0:T(8,128)(2,1)S(1)} %constant_dynamic-update-slice_fusion), channel_id=1, source_target_pairs={{0,16},{4,20},{8,24},{12,28},{16,0},{20,4},{24,8},{28,12},{1,17},{... | collective-permute-start | bytes 393224 | tf_op jit(solution)/shard_map/ppermute | solution.py:32
  40.8 8.2 %project.2 = (bf16[3072,128]{1,0:T(8,128)(2,1)}, bf16[3072,256]{1,0:T(8,128)(2,1)}, bf16[8,4,24,1024]{3,2,1,0:T(8,128)(2,1)}) custom-call(s32[5]{0:T(128)} %stack.29.meta, bf16[400,1024]{1,0:T(8,128)(2,1)} %layer_norm.1.refs_0_, bf16[400,1024]{1,0:T(8,128)(2,1)} %copy-done.20, bf16[400,1024]{1,0:T(8,128)(2,1)} %copy-done.9, ...), custom_call_target="tpu_custom_call" | custom-call | flops 9663676416 | bytes 6291456 | tf_op jit(solution)/shard_map/project/pallas_call | solution.py:172
  50.4 5.4 %all-to-all-start = ((bf16[32,24,1024]{2,1,0:T(8,128)(2,1)}), bf16[32,24,1024]{2,1,0:T(8,128)(2,1)S(1)}, u32[]{:S(2)}, u32[]{:S(2)}) async-start(bf16[32,24,1024]{2,1,0:T(8,128)(2,1)} %bitcast.17), calls=%async_computation | async-start | bytes 3145728 | tf_op jit(solution)/shard_map/all_to_all | solution.py:734
  56.4 1.3 collective-permute-start.22
  60.7 8.2 %project.3 = (bf16[3072,128]{1,0:T(8,128)(2,1)}, bf16[3072,256]{1,0:T(8,128)(2,1)}, bf16[8,4,24,1024]{3,2,1,0:T(8,128)(2,1)}) custom-call(s32[5]{0:T(128)} %stack.29.meta, bf16[400,1024]{1,0:T(8,128)(2,1)} %copy-done.7, bf16[400,1024]{1,0:T(8,128)(2,1)} %copy-done.19, ...), custom_call_target="tpu_custom_call", output_to_operand_aliasing={{0}: (13, {}), {1}: (14, {})} | custom-call | flops 9663676416 | bytes 6291456 | tf_op jit(solution)/shard_map/project/pallas_call | solution.py:172
  68.9 1.3 fusion.2
  70.2 3.2 %collective-permute-start.20 = (bf16[1024,256]{1,0:T(8,128)(2,1)S(1)}, bf16[1024,256]{1,0:T(8,128)(2,1)}, u32[]{:S(2)}, u32[]{:S(2)}) collective-permute-start(bf16[1024,256]{1,0:T(8,128)(2,1)S(1)} %get-tuple-element.113), channel_id=1, source_target_pairs={{0,8},{4,12},{8,16},{12,20},{16,24},{20,28},{1,9},{5,13},{9,17},{1... | collective-permute-start | bytes 1572872 | tf_op jit(solution)/shard_map/ppermute | solution.py:38
  73.3 2.1 %collective-permute-start.21 = (bf16[1024,256]{1,0:T(8,128)(2,1)S(1)}, bf16[1024,256]{1,0:T(8,128)(2,1)}, u32[]{:S(2)}, u32[]{:S(2)}) collective-permute-start(bf16[1024,256]{1,0:T(8,128)(2,1)S(1)} %get-tuple-element.112), channel_id=1, source_target_pairs={{8,0},{12,4},{16,8},{20,12},{24,16},{28,20},{9,1},{13,5},{17,9},{2... | collective-permute-start | bytes 1572872 | tf_op jit(solution)/shard_map/ppermute | solution.py:38
  75.5 23.8 %attend_edges.1 = (f32[5,160,256]{2,1,0:T(8,128)}, f32[5,160,256]{2,1,0:T(8,128)}, f32[5,8,256]{2,1,0:T(8,128)}, f32[5,8,256]{2,1,0:T(8,128)}) custom-call(s32[5]{0:T(128)} %stack.29.meta, s32[1,128]{1,0:T(1,128)} %get-tuple-element.62.ranges, bf16[3072,128]{1,0:T(8,128)(2,1)} %get-tuple-element.80.refs_0_.refs_3_, ...), custom_call_target="tpu_custom_call" | custom-call | flops 6442450944 | bytes 5242880 | tf_op jit(solution)/shard_map/attend_edges/pallas_call | solution.py:425
  99.4 3.3 %collective-permute-done.20.refs_7_ = bf16[1024,256]{1,0:T(8,128)(2,1)} collective-permute-done((bf16[1024,256]{1,0:T(8,128)(2,1)S(1)}, bf16[1024,256]{1,0:T(8,128)(2,1)}, u32[]{:S(2)}, u32[]{:S(2)}) %collective-permute-start.20) | collective-permute-done | bytes 524320 | tf_op jit(solution)/shard_map/ppermute | solution.py:38
  103.8 5.1 %all-to-all-start.1 = ((bf16[32,24,1024]{2,1,0:T(8,128)(2,1)}), bf16[32,24,1024]{2,1,0:T(8,128)(2,1)S(1)}, u32[]{:S(2)}, u32[]{:S(2)}) async-start(bf16[32,24,1024]{2,1,0:T(8,128)(2,1)} %bitcast.16), calls=%async_computation.1 | async-start | bytes 3145728 | tf_op jit(solution)/shard_map/all_to_all | solution.py:734
  109.0 2.8 %stacked.1.refs_8_ = bf16[2048,256]{1,0:T(8,128)(2,1)} custom-call(bf16[512,256]{1,0:T(8,128)(2,1)} %copy-done.3, bf16[512,256]{1,0:T(8,128)(2,1)} %copy-done.4, bf16[512,256]{1,0:T(8,128)(2,1)} %copy-done.5, bf16[512,256]{1,0:T(8,128)(2,1)} %copy-done.6), custom_call_target="tpu_custom_call" | custom-call | bytes 2097152 | tf_op jit(solution)/shard_map/stacked/pallas_call | solution.py:586
  112.1 14.5 %attend_finish.1 = (bf16[384,128]{1,0:T(8,128)(2,1)}, bf16[384,128]{1,0:T(8,128)(2,1)}, bf16[384,128]{1,0:T(8,128)(2,1)}, bf16[384,128]{1,0:T(8,128)(2,1)}, bf16...) custom-call(s32[5]{0:T(128)} %stack.29.meta, ...), custom_call_target="tpu_custom_call" | custom-call | flops 6442450944 | bytes 5242880 | tf_op jit(solution)/shard_map/attend_finish/pallas_call | solution.py:453
  130.3 3.1 %collective-permute-done.26.refs_2_ = bf16[384,128]{1,0:T(8,128)(2,1)S(1)} collective-permute-done((bf16[384,128]{1,0:T(8,128)(2,1)}, bf16[384,128]{1,0:T(8,128)(2,1)S(1)}, u32[]{:S(2)}, u32[]{:S(2)}) %collective-permute-start.26) | collective-permute-done | bytes 98336 | tf_op jit(solution)/shard_map/ppermute | solution.py:780
  133.4 1.8 %collective-permute-start.30 = (bf16[384,128]{1,0:T(8,128)(2,1)}, bf16[384,128]{1,0:T(8,128)(2,1)S(1)}, u32[]{:S(2)}, u32[]{:S(2)}) collective-permute-start(bf16[384,128]{1,0:T(8,128)(2,1)} %get-tuple-element.102), channel_id=1, source_target_pairs={{0,6},{1,7},{2,4},{3,5},{4,2},{5,3},{6,0},{7,1},{8,14},{9,15},{10,... | collective-permute-start | bytes 294920 | tf_op jit(solution)/shard_map/ppermute | solution.py:780
  135.3 3.8 %collective-permute-done.27.refs_3_ = bf16[384,128]{1,0:T(8,128)(2,1)S(1)} collective-permute-done((bf16[384,128]{1,0:T(8,128)(2,1)}, bf16[384,128]{1,0:T(8,128)(2,1)S(1)}, u32[]{:S(2)}, u32[]{:S(2)}) %collective-permute-start.27) | collective-permute-done | bytes 98336 | tf_op jit(solution)/shard_map/ppermute | solution.py:780
  140.1 5.5 %collective-permute-done.31.refs_7_ = bf16[384,128]{1,0:T(8,128)(2,1)S(1)} collective-permute-done((bf16[384,128]{1,0:T(8,128)(2,1)}, bf16[384,128]{1,0:T(8,128)(2,1)S(1)}, u32[]{:S(2)}, u32[]{:S(2)}) %collective-permute-start.31) | collective-permute-done | bytes 98336 | tf_op jit(solution)/shard_map/ppermute | solution.py:780
  147.1 6.9 %outputs.1 = (bf16[384,1024]{1,0:T(8,128)(2,1)}, bf16[8,24,8192]{2,1,0:T(8,128)(2,1)}) custom-call(s32[2]{0:T(128)} %pad_add_fusion.meta, bf16[384,128]{1,0:T(8,128)(2,1)} %get-tuple-element.96.refs_0_, bf16[384,128]{1,0:T(8,128)(2,1)} %copy-done.10, bf16[384,128]{1,0:T(8,128)(2,1)} %copy-done.11, bf16[384,128]{1,0:T(8,128)(2,1)} %copy-done.12, ...), custom_call_target="tpu_custom_call" | custom-call | flops 805306368 | bytes 10485760 | tf_op jit(solution)/shard_map/outputs/pallas_call | solution.py:537
  (115 shorter events, 20.9 us)
Async XLA Ops:
  1.5 6.9 %collective-permute-start.5 = (bf16[128,128]{1,0:T(8,128)(2,1)S(1)}, bf16[128,128]{1,0:T(8,128)(2,1)S(1)}, u32[]{:S(2)}, u32[]{:S(2)}) collective-permute-start(bf16[128,128]{1,0:T(8,128)(2,1)S(1)} %get-tuple-element.117), channel_id=1, source_target_pairs={{0,6},{1,5},{2,4},{3,7},{4,2},{5,1},{6,0},{7,3},{8,14},{9,13},{10,... | collective-permute-start | bytes 98312 | tf_op jit(solution)/shard_map/ppermute | solution.py:674
  2.8 11.5 %collective-permute-start.4 = (bf16[128,128]{1,0:T(8,128)(2,1)S(1)}, bf16[128,128]{1,0:T(8,128)(2,1)S(1)}, u32[]{:S(2)}, u32[]{:S(2)}) collective-permute-start(bf16[128,128]{1,0:T(8,128)(2,1)S(1)} %get-tuple-element.115), channel_id=1, source_target_pairs={{0,5},{1,4},{2,7},{3,6},{4,1},{5,0},{6,3},{7,2},{8,13},{9,12},{10,... | collective-permute-start | bytes 98312 | tf_op jit(solution)/shard_map/ppermute | solution.py:674
  4.8 10.8 %collective-permute-start.3 = (bf16[128,128]{1,0:T(8,128)(2,1)S(1)}, bf16[128,128]{1,0:T(8,128)(2,1)S(1)}, u32[]{:S(2)}, u32[]{:S(2)}) collective-permute-start(bf16[128,128]{1,0:T(8,128)(2,1)S(1)} %get-tuple-element.116), channel_id=1, source_target_pairs={{0,4},{1,7},{2,6},{3,5},{4,0},{5,3},{6,2},{7,1},{8,12},{9,15},{10,... | collective-permute-start | bytes 98312 | tf_op jit(solution)/shard_map/ppermute | solution.py:674
  6.1 9.6 %collective-permute-start.2 = (bf16[128,128]{1,0:T(8,128)(2,1)S(1)}, bf16[128,128]{1,0:T(8,128)(2,1)S(1)}, u32[]{:S(2)}, u32[]{:S(2)}) collective-permute-start(bf16[128,128]{1,0:T(8,128)(2,1)S(1)} %get-tuple-element.119), channel_id=1, source_target_pairs={{0,2},{1,1},{2,0},{3,3},{4,6},{5,5},{6,4},{7,7},{8,10},{9,9},{10,8... | collective-permute-start | bytes 98312 | tf_op jit(solution)/shard_map/ppermute | solution.py:674
  6.7 8.9 %collective-permute-start.1 = (bf16[128,128]{1,0:T(8,128)(2,1)S(1)}, bf16[128,128]{1,0:T(8,128)(2,1)S(1)}, u32[]{:S(2)}, u32[]{:S(2)}) collective-permute-start(bf16[128,128]{1,0:T(8,128)(2,1)S(1)} %get-tuple-element.118), channel_id=1, source_target_pairs={{0,1},{1,0},{2,3},{3,2},{4,5},{5,4},{6,7},{7,6},{8,9},{9,8},{10,11... | collective-permute-start | bytes 98312 | tf_op jit(solution)/shard_map/ppermute | solution.py:674
  8.5 7.2 %collective-permute-start = (bf16[128,128]{1,0:T(8,128)(2,1)S(1)}, bf16[128,128]{1,0:T(8,128)(2,1)S(1)}, u32[]{:S(2)}, u32[]{:S(2)}) collective-permute-start(bf16[128,128]{1,0:T(8,128)(2,1)S(1)} %get-tuple-element.114), channel_id=1, source_target_pairs={{0,0},{1,3},{2,2},{3,1},{4,4},{5,7},{6,6},{7,5},{8,8},{9,11},{10,1... | collective-permute-start | bytes 98312 | tf_op jit(solution)/shard_map/ppermute | solution.py:674
  14.3 6.7 %collective-permute-start.12 = (bf16[128,256]{1,0:T(8,128)(2,1)S(1)}, bf16[128,256]{1,0:T(8,128)(2,1)S(1)}, u32[]{:S(2)}, u32[]{:S(2)}) collective-permute-start(bf16[128,256]{1,0:T(8,128)(2,1)S(1)} %copy-done.17), channel_id=1, source_target_pairs={{0,8},{4,12},{8,0},{12,4},{16,24},{20,28},{24,16},{28,20},{1,9},{5... | collective-permute-start | bytes 196616 | tf_op jit(solution)/shard_map/ppermute | solution.py:32
  15.7 19.2 %collective-permute-start.6 = (bf16[400,1024]{1,0:T(8,128)(2,1)}, bf16[400,1024]{1,0:T(8,128)(2,1)S(1)}, u32[]{:S(2)}, u32[]{:S(2)}) collective-permute-start(bf16[400,1024]{1,0:T(8,128)(2,1)} %layer_norm.1.refs_0_), channel_id=1, source_target_pairs={{0,2},{1,3},{2,0},{3,1},{4,6},{5,7},{6,4},{7,5},{8,10},{9,11},{10,... | collective-permute-start | bytes 2457608 | tf_op jit(solution)/shard_map/ppermute | solution.py:32
  16.7 19.1 %collective-permute-start.7 = (bf16[400,1024]{1,0:T(8,128)(2,1)}, bf16[400,1024]{1,0:T(8,128)(2,1)S(1)}, u32[]{:S(2)}, u32[]{:S(2)}) collective-permute-start(bf16[400,1024]{1,0:T(8,128)(2,1)} %layer_norm.1.refs_0_), channel_id=1, source_target_pairs={{0,4},{4,0},{8,12},{12,8},{16,20},{20,16},{24,28},{28,24},{1,5},{5... | collective-permute-start | bytes 2457608 | tf_op jit(solution)/shard_map/ppermute | solution.py:32
  17.2 18.5 %collective-permute-start.8 = (bf16[400,1024]{1,0:T(8,128)(2,1)}, bf16[400,1024]{1,0:T(8,128)(2,1)S(1)}, u32[]{:S(2)}, u32[]{:S(2)}) collective-permute-start(bf16[400,1024]{1,0:T(8,128)(2,1)} %layer_norm.1.refs_0_), channel_id=1, source_target_pairs={{0,1},{1,0},{2,3},{3,2},{4,5},{5,4},{6,7},{7,6},{8,9},{9,8},{10,11... | collective-permute-start | bytes 2457608 | tf_op jit(solution)/shard_map/ppermute | solution.py:32
  17.2 8.8 %collective-permute-start.10 = (bf16[256,384]{1,0:T(8,128)(2,1)S(1)}, bf16[256,384]{1,0:T(8,128)(2,1)S(1)}, u32[]{:S(2)}, u32[]{:S(2)}) collective-permute-start(bf16[256,384]{1,0:T(8,128)(2,1)S(1)} %maximum_maximum_fusion.refs_4_.refs_6_), channel_id=1, source_target_pairs={{0,16},{4,20},{8,24},{12,28},{16,0},{20,4},{24,8},{28,12},{1,17},{... | collective-permute-start | bytes 589832 | tf_op jit(solution)/shard_map/ppermute | solution.py:32
  21.1 9.8 %collective-permute-start.9 = (bf16[256,384]{1,0:T(8,128)(2,1)S(1)}, bf16[256,384]{1,0:T(8,128)(2,1)S(1)}, u32[]{:S(2)}, u32[]{:S(2)}) collective-permute-start(bf16[256,384]{1,0:T(8,128)(2,1)S(1)} %maximum_maximum_fusion.refs_4_.refs_6_), channel_id=1, source_target_pairs={{0,8},{4,12},{8,0},{12,4},{16,24},{20,28},{24,16},{28,20},{1,9},{5... | collective-permute-start | bytes 589832 | tf_op jit(solution)/shard_map/ppermute | solution.py:32
  26.1 6.2 %collective-permute-start.11 = (bf16[256,384]{1,0:T(8,128)(2,1)S(1)}, bf16[256,384]{1,0:T(8,128)(2,1)S(1)}, u32[]{:S(2)}, u32[]{:S(2)}) collective-permute-start(bf16[256,384]{1,0:T(8,128)(2,1)S(1)} %collective-permute-done.10.refs_6_.refs_8_), channel_id=1, source_target_pairs={{0,8},{4,12},{8,0},{12,4},{16,24},{20,28},{24,16},{28,20},{1,9},{5... | collective-permute-start | bytes 589832 | tf_op jit(solution)/shard_map/ppermute | solution.py:32
  36.7 4.1 %collective-permute-start.13 = (bf16[400,1024]{1,0:T(8,128)(2,1)S(1)}, bf16[400,1024]{1,0:T(8,128)(2,1)}, u32[]{:S(2)}, u32[]{:S(2)}) collective-permute-start(bf16[400,1024]{1,0:T(8,128)(2,1)S(1)} %collective-permute-done.6.refs_2_), channel_id=1, source_target_pairs={{0,1},{1,0},{2,3},{3,2},{4,5},{5,4},{6,7},{7,6},{8,9},{9,8},{10,11... | collective-permute-start | bytes 2457608 | tf_op jit(solution)/shard_map/ppermute | solution.py:32
  36.8 12.7 %collective-permute-start.16 = (bf16[400,1024]{1,0:T(8,128)(2,1)S(1)}, bf16[400,1024]{1,0:T(8,128)(2,1)S(1)}, u32[]{:S(2)}, u32[]{:S(2)}) collective-permute-start(bf16[400,1024]{1,0:T(8,128)(2,1)S(1)} %collective-permute-done.7.refs_0_), channel_id=1, source_target_pairs={{0,1},{1,0},{2,3},{3,2},{4,5},{5,4},{6,7},{7,6},{8,9},{9,8},{10,11... | collective-permute-start | bytes 2457608 | tf_op jit(solution)/shard_map/ppermute | solution.py:32
  37.4 11.7 %collective-permute-start.14 = (bf16[192,1024]{1,0:T(8,128)(2,1)S(1)}, bf16[192,1024]{1,0:T(8,128)(2,1)}, u32[]{:S(2)}, u32[]{:S(2)}) collective-permute-start(bf16[192,1024]{1,0:T(8,128)(2,1)S(1)} %slice.42), channel_id=1, source_target_pairs={{0,4},{4,0},{8,12},{12,8},{16,20},{20,16},{24,28},{28,24},{1,5},{5... | collective-permute-start | bytes 1179656 | tf_op jit(solution)/shard_map/ppermute | solution.py:32
  38.6 10.9 %collective-permute-start.15 = (bf16[208,1024]{1,0:T(8,128)(2,1)S(1)}, bf16[208,1024]{1,0:T(8,128)(2,1)}, u32[]{:S(2)}, u32[]{:S(2)}) collective-permute-start(bf16[208,1024]{1,0:T(8,128)(2,1)S(1)} %slice.43), channel_id=1, source_target_pairs={{0,2},{1,3},{2,0},{3,1},{4,6},{5,7},{6,4},{7,5},{8,10},{9,11},{10,... | collective-permute-start | bytes 1277960 | tf_op jit(solution)/shard_map/ppermute | solution.py:32
  38.9 10.1 %collective-permute-start.17 = (bf16[256,256]{1,0:T(8,128)(2,1)S(1)}, bf16[256,256]{1,0:T(8,128)(2,1)S(1)}, u32[]{:S(2)}, u32[]{:S(2)}) collective-permute-start(bf16[256,256]{1,0:T(8,128)(2,1)S(1)} %constant_dynamic-update-slice_fusion), channel_id=1, source_target_pairs={{0,16},{4,20},{8,24},{12,28},{16,0},{20,4},{24,8},{28,12},{1,17},{... | collective-permute-start | bytes 393224 | tf_op jit(solution)/shard_map/ppermute | solution.py:32
  50.4 52.2 %all-to-all-start = ((bf16[32,24,1024]{2,1,0:T(8,128)(2,1)}), bf16[32,24,1024]{2,1,0:T(8,128)(2,1)S(1)}, u32[]{:S(2)}, u32[]{:S(2)}) async-start(bf16[32,24,1024]{2,1,0:T(8,128)(2,1)} %bitcast.17), calls=%async_computation | async-start | bytes 3145728 | tf_op jit(solution)/shard_map/all_to_all | solution.py:734
  56.4 42.9 %collective-permute-start.22 = (bf16[512,256]{1,0:T(8,128)(2,1)S(1)}, bf16[512,256]{1,0:T(8,128)(2,1)S(1)}, u32[]{:S(2)}, u32[]{:S(2)}) collective-permute-start(bf16[512,256]{1,0:T(8,128)(2,1)S(1)} %constant_dynamic-update-slice_fusion.2.refs_0_), channel_id=1, source_target_pairs={{0,4},{4,0},{8,12},{12,8},{16,20},{20,16},{24,28},{28,24},{1,5},{5... | collective-permute-start | bytes 786440 | tf_op jit(solution)/shard_map/ppermute | solution.py:32
  57.7 41.6 %collective-permute-start.23 = (bf16[512,256]{1,0:T(8,128)(2,1)S(1)}, bf16[512,256]{1,0:T(8,128)(2,1)S(1)}, u32[]{:S(2)}, u32[]{:S(2)}) collective-permute-start(bf16[512,256]{1,0:T(8,128)(2,1)S(1)} %constant_dynamic-update-slice_fusion.2.refs_0_), channel_id=1, source_target_pairs={{0,2},{1,3},{2,0},{3,1},{4,6},{5,7},{6,4},{7,5},{8,10},{9,11},{10,... | collective-permute-start | bytes 786440 | tf_op jit(solution)/shard_map/ppermute | solution.py:32
  58.9 40.4 %collective-permute-start.24 = (bf16[512,256]{1,0:T(8,128)(2,1)S(1)}, bf16[512,256]{1,0:T(8,128)(2,1)S(1)}, u32[]{:S(2)}, u32[]{:S(2)}) collective-permute-start(bf16[512,256]{1,0:T(8,128)(2,1)S(1)} %constant_dynamic-update-slice_fusion.2.refs_0_), channel_id=1, source_target_pairs={{0,6},{1,7},{2,4},{3,5},{4,2},{5,3},{6,0},{7,1},{8,14},{9,15},{10,... | collective-permute-start | bytes 786440 | tf_op jit(solution)/shard_map/ppermute | solution.py:756
  70.2 32.5 %collective-permute-start.20 = (bf16[1024,256]{1,0:T(8,128)(2,1)S(1)}, bf16[1024,256]{1,0:T(8,128)(2,1)}, u32[]{:S(2)}, u32[]{:S(2)}) collective-permute-start(bf16[1024,256]{1,0:T(8,128)(2,1)S(1)} %get-tuple-element.113), channel_id=1, source_target_pairs={{0,8},{4,12},{8,16},{12,20},{16,24},{20,28},{1,9},{5,13},{9,17},{1... | collective-permute-start | bytes 1572872 | tf_op jit(solution)/shard_map/ppermute | solution.py:38
  73.3 29.3 %collective-permute-start.21 = (bf16[1024,256]{1,0:T(8,128)(2,1)S(1)}, bf16[1024,256]{1,0:T(8,128)(2,1)}, u32[]{:S(2)}, u32[]{:S(2)}) collective-permute-start(bf16[1024,256]{1,0:T(8,128)(2,1)S(1)} %get-tuple-element.112), channel_id=1, source_target_pairs={{8,0},{12,4},{16,8},{20,12},{24,16},{28,20},{9,1},{13,5},{17,9},{2... | collective-permute-start | bytes 1572872 | tf_op jit(solution)/shard_map/ppermute | solution.py:38
  103.8 41.8 %all-to-all-start.1 = ((bf16[32,24,1024]{2,1,0:T(8,128)(2,1)}), bf16[32,24,1024]{2,1,0:T(8,128)(2,1)S(1)}, u32[]{:S(2)}, u32[]{:S(2)}) async-start(bf16[32,24,1024]{2,1,0:T(8,128)(2,1)} %bitcast.16), calls=%async_computation.1 | async-start | bytes 3145728 | tf_op jit(solution)/shard_map/all_to_all | solution.py:734
  111.7 33.9 %collective-permute-start.32 = (bf16[2048,256]{1,0:T(8,128)(2,1)}, bf16[2048,256]{1,0:T(8,128)(2,1)S(1)}, u32[]{:S(2)}, u32[]{:S(2)}) collective-permute-start(bf16[2048,256]{1,0:T(8,128)(2,1)} %stacked.1.refs_8_), channel_id=1, source_target_pairs={{0,1},{1,0},{2,3},{3,2},{4,5},{5,4},{6,7},{7,6},{8,9},{9,8},{10,11... | collective-permute-start | bytes 3145736 | tf_op jit(solution)/shard_map/ppermute | solution.py:32
  126.8 6.7 %collective-permute-start.26 = (bf16[384,128]{1,0:T(8,128)(2,1)}, bf16[384,128]{1,0:T(8,128)(2,1)S(1)}, u32[]{:S(2)}, u32[]{:S(2)}) collective-permute-start(bf16[384,128]{1,0:T(8,128)(2,1)} %get-tuple-element.98), channel_id=1, source_target_pairs={{0,2},{1,3},{2,0},{3,1},{4,6},{5,7},{6,4},{7,5},{8,10},{9,11},{10,... | collective-permute-start | bytes 294920 | tf_op jit(solution)/shard_map/ppermute | solution.py:780
  128.0 11.1 %collective-permute-start.27 = (bf16[384,128]{1,0:T(8,128)(2,1)}, bf16[384,128]{1,0:T(8,128)(2,1)S(1)}, u32[]{:S(2)}, u32[]{:S(2)}) collective-permute-start(bf16[384,128]{1,0:T(8,128)(2,1)} %get-tuple-element.99), channel_id=1, source_target_pairs={{0,3},{1,2},{2,1},{3,0},{4,7},{5,6},{6,5},{7,4},{8,11},{9,10},{10,... | collective-permute-start | bytes 294920 | tf_op jit(solution)/shard_map/ppermute | solution.py:780
  128.8 11.3 %collective-permute-start.28 = (bf16[384,128]{1,0:T(8,128)(2,1)}, bf16[384,128]{1,0:T(8,128)(2,1)S(1)}, u32[]{:S(2)}, u32[]{:S(2)}) collective-permute-start(bf16[384,128]{1,0:T(8,128)(2,1)} %get-tuple-element.100), channel_id=1, source_target_pairs={{0,4},{1,5},{2,6},{3,7},{4,0},{5,1},{6,2},{7,3},{8,12},{9,13},{10,... | collective-permute-start | bytes 294920 | tf_op jit(solution)/shard_map/ppermute | solution.py:780
  130.0 10.1 %collective-permute-start.29 = (bf16[384,128]{1,0:T(8,128)(2,1)}, bf16[384,128]{1,0:T(8,128)(2,1)S(1)}, u32[]{:S(2)}, u32[]{:S(2)}) collective-permute-start(bf16[384,128]{1,0:T(8,128)(2,1)} %get-tuple-element.101), channel_id=1, source_target_pairs={{0,5},{1,4},{2,7},{3,6},{4,1},{5,0},{6,3},{7,2},{8,13},{9,12},{10,... | collective-permute-start | bytes 294920 | tf_op jit(solution)/shard_map/ppermute | solution.py:780
  133.4 6.7 %collective-permute-start.30 = (bf16[384,128]{1,0:T(8,128)(2,1)}, bf16[384,128]{1,0:T(8,128)(2,1)S(1)}, u32[]{:S(2)}, u32[]{:S(2)}) collective-permute-start(bf16[384,128]{1,0:T(8,128)(2,1)} %get-tuple-element.102), channel_id=1, source_target_pairs={{0,6},{1,7},{2,4},{3,5},{4,2},{5,3},{6,0},{7,1},{8,14},{9,15},{10,... | collective-permute-start | bytes 294920 | tf_op jit(solution)/shard_map/ppermute | solution.py:780
  139.0 6.5 %collective-permute-start.31 = (bf16[384,128]{1,0:T(8,128)(2,1)}, bf16[384,128]{1,0:T(8,128)(2,1)S(1)}, u32[]{:S(2)}, u32[]{:S(2)}) collective-permute-start(bf16[384,128]{1,0:T(8,128)(2,1)} %get-tuple-element.103), channel_id=1, source_target_pairs={{0,7},{1,6},{2,5},{3,4},{4,3},{5,2},{6,1},{7,0},{8,15},{9,14},{10,... | collective-permute-start | bytes 294920 | tf_op jit(solution)/shard_map/ppermute | solution.py:780
  (29 other events, 173.0 us)
